TPU v7x, 32 devices: a whole 2x2x4 slice. The times are simulated.
32 devices in a mesh: freq: 4 (over x, core), frames: 8 (over z, y).
Axes of the slice: x: 2, y: 2, z: 4, core: 2. Of those that a mesh axis runs over, the one named last changes fastest.
Arguments:
- signal: float32 [8, 4, 1048576], P('frames', 'freq'), may hold values from -6 to 6
- templates: float32 [64, 32768], P(None, ('freq', 'frames')), may hold values from 0.03 to 3.6, as said below
- activations: float32 [64, 1024], P('freq', 'frames'), may hold values from 0.3 to 36, as said below
Outputs:
- final_activations: float32 [64, 1024], P('freq', 'frames')
- final_templates: float32 [64, 32768], P(None, ('freq', 'frames'))
Inputs may be any that keep to these rules, and one draw needn't show every extreme that they name: `templates`: all entries are positive. `activations`: all entries are positive.
All inputs are finite; a program needn't handle non-finite values.
Results may differ from a plain program's by a relative error of at most 0.00011.
Values sent between devices are 32-bit elements; how exact they have to be, the bound alone decides.
No kernel may reach another device: no remote copies, remote signals or barrier semaphores. Data moves between devices by JAX's collectives and lax.ppermute only.
A program may use at most 64 MiB of HBM per device.

v0:
```python
import math

import jax
import jax.numpy as jnp
from jax import lax
from jax.sharding import PartitionSpec as P

FRAME_LEN = 65536
SPLIT = 256


PRECISE = lax.Precision.HIGHEST


def passed_along(block, axis, distance):
    devices = range(lax.axis_size(axis))
    route = [((i - distance) % len(devices), i) for i in devices]
    return lax.ppermute(block, axis, route)


def from_behind(value, axis, steps):
    count = lax.axis_size(axis)
    leading, last = (max(0, -steps), min(count, count - steps))
    return lax.ppermute(value, axis, [(source, source + steps) for source in range(leading, last)])


def hann_window():
    positions = jnp.arange(FRAME_LEN, dtype=jnp.int32).astype(jnp.float32)
    return 0.5 - 0.5 * jnp.cos(2.0 * math.pi / FRAME_LEN * positions)


def fourier_tables(split_len):
    indices = jnp.arange(split_len, dtype=jnp.int32)
    products = indices[:, None] * indices[None, :] % split_len
    angles = 2.0 * math.pi / split_len * products.astype(jnp.float32)
    cosine_table = jnp.cos(angles)
    sine_table = jnp.sin(angles)
    first_section = jnp.concatenate([cosine_table, -sine_table], 0)
    half_split = split_len // 2
    cos_half = cosine_table[:half_split]
    sin_half = sine_table[:half_split]
    second_section = jnp.concatenate(
        [jnp.concatenate([cos_half, sin_half], 1), jnp.concatenate([-sin_half, cos_half], 1)], 0
    )
    twiddle = (
        2.0
        * math.pi
        / (split_len * split_len)
        * (indices[:, None] * indices[None, :]).astype(jnp.float32)
    )
    return (first_section, second_section, jnp.cos(twiddle), jnp.sin(twiddle))


def frame_magnitudes(extended, frame_count):
    first_section, second_section, twiddle_cos, twiddle_sin = fourier_tables(SPLIT)
    window = hann_window()
    group_size = math.gcd(frame_count, 4)
    half_split = SPLIT // 2

    def per_block(offset):
        first_half = lax.dynamic_slice_in_dim(extended, offset, group_size, 0)
        second_half = lax.dynamic_slice_in_dim(extended, offset + 1, group_size, 0)
        frames = jnp.concatenate([first_half, second_half], 1) * window
        samples = frames.reshape(group_size, SPLIT, SPLIT)
        section_one = jnp.einsum(
            "oq,gqp->gop",
            first_section,
            samples,
            precision=PRECISE,
            preferred_element_type=jnp.float32,
        )
        real_one = section_one[:, :SPLIT]
        imag_one = section_one[:, SPLIT:]
        twisted = jnp.concatenate(
            [
                real_one * twiddle_cos + imag_one * twiddle_sin,
                imag_one * twiddle_cos - real_one * twiddle_sin,
            ],
            2,
        )
        section_two = jnp.einsum(
            "oc,gjc->goj",
            second_section,
            twisted,
            precision=PRECISE,
            preferred_element_type=jnp.float32,
        )
        real_two = section_two[:, :half_split]
        imag_two = section_two[:, half_split:]
        magnitude = jnp.sqrt(real_two * real_two + imag_two * imag_two) * (8.0 / SPLIT)
        return magnitude.reshape(group_size, half_split * SPLIT)

    offsets = jnp.arange(frame_count // group_size, dtype=jnp.int32) * group_size
    return lax.map(per_block, offsets).reshape(frame_count, half_split * SPLIT)


def gather_basis(own_columns):
    return lax.all_gather(own_columns, "frames", axis=1, tiled=True)


def gather_activity(own_rows):
    return lax.all_gather(own_rows, "freq", axis=0, tiled=True)


def quotient(spectrum, basis_full, act_full):
    approx = lax.dot_general(
        act_full,
        basis_full,
        (((0,), (0,)), ((), ())),
        precision=PRECISE,
        preferred_element_type=jnp.float32,
    )
    return spectrum / approx


def update_activity(spectrum, basis_full, act_full, act_own):
    ratio_rows = quotient(spectrum, basis_full, act_full)
    numerator = lax.dot_general(
        basis_full,
        ratio_rows,
        (((1,), (1,)), ((), ())),
        precision=PRECISE,
        preferred_element_type=jnp.float32,
    )
    totals = jnp.sum(basis_full, axis=1)
    numerator, totals = lax.psum((numerator, totals), "freq")
    new_full = act_full * (numerator / totals[:, None])
    rank_rows = act_own.shape[0]
    new_own = lax.dynamic_slice_in_dim(new_full, lax.axis_index("freq") * rank_rows, rank_rows, 0)
    return (new_own, new_full)


def on_device(signal, templates, activations):
    hop_len = FRAME_LEN // 2
    sample_rows = signal.reshape(-1, hop_len)
    frame_count = sample_rows.shape[0]
    leading = sample_rows[:1]
    from_next = passed_along(leading, "freq", -1)
    from_later = from_behind(from_next, "frames", -1)
    last_sub = lax.axis_index("freq") == lax.axis_size("freq") - 1
    trailing = jnp.where(last_sub, from_later, from_next)
    extended = jnp.concatenate([sample_rows, trailing], 0)
    spectrum = frame_magnitudes(extended, frame_count)
    spectrum = lax.all_to_all(spectrum, "freq", split_axis=1, concat_axis=0, tiled=True)
    basis_full = gather_basis(templates)
    act_full = gather_activity(activations)
    middle_own, middle_full = update_activity(spectrum, basis_full, act_full, activations)
    second_ratio = quotient(spectrum, basis_full, middle_full)
    numerator = jnp.dot(
        middle_full, second_ratio, precision=PRECISE, preferred_element_type=jnp.float32
    )
    totals = jnp.sum(middle_full, axis=1)
    numerator = lax.psum_scatter(numerator, "frames", scatter_dimension=1, tiled=True)
    totals = lax.psum(totals, "frames")
    basis_own = templates * (numerator / totals[:, None])
    new_basis = gather_basis(basis_own)
    final_own, unused = update_activity(spectrum, new_basis, middle_full, middle_own)
    return (final_own, basis_own)


def solution(mesh):
    return jax.shard_map(
        on_device,
        mesh=mesh,
        in_specs=(P("frames", "freq", None), P(None, ("freq", "frames")), P("freq", "frames")),
        out_specs=(P("freq", "frames"), P(None, ("freq", "frames"))),
        check_vma=False,
    )
```

profile of v0, /device:TPU:0, one launch (start us, length us, event | category | flops | bytes accessed | tf_op | source)
XLA Modules:
  0.0 450.9 jit_solution(15451722020676664964)
XLA Ops:
  7.2 0.9 slice_bitcast_fusion
  8.1 2.4 collective-permute-start
  10.6 1.0 fusion.31
  11.6 1.0 fusion.32
  13.1 1.3 collective-permute-start.1
  14.9 34.1 %reduce.3 = f32[1048576]{0:T(1024)} reduce(f32[1,1,1048576]{2,1,0:T(1,128)} %param.5, f32[]{:T(128)} %broadcast.50), dimensions={0,1}, to_apply=%param.5.reduce_sub_computation.3 | reduce | bytes 8388612 | tf_op args[0]
  49.0 5.0 %reshape.38 = f32[32,32768]{1,0:T(8,128)} reshape(f32[1048576]{0:T(1024)} %reduce.3) | data formatting | bytes 8388608 | tf_op jit(solution)/shard_map/reshape | solution.py:135
  54.3 4.9 %pad_maximum_fusion = f32[33,32768]{1,0:T(8,128)} fusion(f32[1,32768]{1,0:T(1,128)S(1)} %broadcast_select_fusion, f32[32,32768]{1,0:T(8,128)} %reshape.38), kind=kLoop, calls=%fused_computation.36 | loop fusion | flops 1081344 | bytes 8650752 | tf_op jit(solution)/shard_map/concatenate | solution.py:142
  59.2 137.4 %while.14 = (s32[]{:T(128)}, f32[8,4,32768]{2,1,0:T(4,128)}, s32[8]{0:T(128)S(1)}, f32[33,32768]{1,0:T(8,128)}, f32[512,256]{1,0:T(8,128)S(1)}, /*index=5*/f32[2...) while((s32[]{:T(128)}, f32[8,4,32768]{2,1,0:T(4,128)}, ...), condition=%wide.region_1.2_spmd.clone.clone, body=%wide.region_0.1_spmd.clone.clone.sunk | while | flops 3224829952 | bytes 22545096 | solution.py:94
  63.1 2.4 constant_dynamic-slice_fusion.3
  65.8 0.9 multiply_subtract_fusion.3
  66.8 3.4 convolution_bitcast_fusion.3
  70.2 0.9 fusion.59
  71.4 3.5 fusion.60
  80.3 2.4 constant_dynamic-slice_fusion.3
  83.0 0.9 multiply_subtract_fusion.3
  83.9 3.4 convolution_bitcast_fusion.3
  87.4 0.9 fusion.59
  88.6 3.5 fusion.60
  97.4 2.4 constant_dynamic-slice_fusion.3
  100.1 0.9 multiply_subtract_fusion.3
  101.1 3.4 convolution_bitcast_fusion.3
  104.5 0.9 fusion.59
  105.7 3.5 fusion.60
  114.6 2.4 constant_dynamic-slice_fusion.3
  117.2 0.9 multiply_subtract_fusion.3
  118.2 3.4 convolution_bitcast_fusion.3
  121.7 0.9 fusion.59
  122.9 3.5 fusion.60
  131.7 2.4 constant_dynamic-slice_fusion.3
  134.4 0.9 multiply_subtract_fusion.3
  135.4 3.4 convolution_bitcast_fusion.3
  138.8 0.9 fusion.59
  140.0 3.5 fusion.60
  148.9 2.4 constant_dynamic-slice_fusion.3
  151.5 0.9 multiply_subtract_fusion.3
  152.5 3.4 convolution_bitcast_fusion.3
  155.9 0.9 fusion.59
  157.1 3.5 fusion.60
  166.0 2.4 constant_dynamic-slice_fusion.3
  169.7 3.4 convolution_bitcast_fusion.3
  173.1 0.9 fusion.59
  174.3 3.5 fusion.60
  183.2 2.4 constant_dynamic-slice_fusion.3
  186.8 3.4 convolution_bitcast_fusion.3
  190.3 0.9 fusion.59
  191.5 3.5 fusion.60
  195.7 0.9 constant_dynamic-update-slice_fusion.2
  196.6 6.8 %all_to_all.14 = f32[32,4,8192]{2,1,0:T(4,128)} reshape(f32[8,4,32768]{2,1,0:T(4,128)} %get-tuple-element.121) | data formatting | bytes 8388608 | tf_op jit(solution)/shard_map/all_to_all | solution.py:144
  203.4 6.6 %copy.16 = f32[32,4,8192]{2,0,1:T(8,128)} copy(f32[32,4,8192]{2,1,0:T(4,128)} %all_to_all.14) | data formatting | bytes 8388608 | tf_op jit(solution)/shard_map/all_to_all | solution.py:144
  210.0 5.0 %all-to-all-start = ((f32[32,4,8192]{2,0,1:T(8,128)}), f32[32,4,8192]{2,0,1:T(8,128)}, u32[]{:S(2)}, u32[]{:S(2)}) async-start(f32[32,4,8192]{2,0,1:T(8,128)} %copy.16), calls=%async_computation | async-start | bytes 8388608 | tf_op jit(solution)/shard_map/all_to_all | solution.py:144
  215.0 49.2 %all_gather.9 = f32[64,128]{1,0:T(8,128)S(1)} all-gather(f32[16,128]{1,0:T(8,128)S(1)} %copy-done.3), channel_id=1, replica_groups=mesh['freq'=4,'frames'=8] {'freq'}, dimensions={0}, use_global_device_ids=true | all-gather | bytes 40960 | tf_op jit(solution)/shard_map/all_gather | solution.py:102
  264.3 6.7 %convolution_divide_fusion.2 = f32[128,8192]{1,0:T(8,128)S(1)} fusion(f32[128,8192]{1,0:T(8,128)} %bitcast.2, f32[64,128]{1,0:T(8,128)S(1)} %all_gather.9, f32[64,8192]{1,0:T(8,128)} %all-gather.3.cloned.1.call-done), kind=kOutput, calls=%fused_computation.35 | convolution fusion | flops 806354944 | bytes 10518528 | tf_op jit(solution)/shard_map/dot_general | solution.py:106
  271.0 4.4 convolution_bitcast_fusion.1
  275.6 11.0 %all-reduce.1 = (f32[64,128]{1,0:T(8,128)S(1)}, f32[64]{0:T(128)S(1)}) all-reduce(f32[64,128]{1,0:T(8,128)S(1)} %convolution_bitcast_fusion.1, f32[64]{0:T(128)S(1)} %reduce_sum.27), channel_id=1, replica_groups=mesh['freq'=4,'frames'=8] {'freq'}, use_global_device_ids=true, to_apply=%region_2.3 | all-reduce | flops 8256 | bytes 66048 | tf_op jit(solution)/shard_map/psum | solution.py:126
  286.8 5.5 %convolution_divide_fusion.1 = f32[128,8192]{1,0:T(8,128)S(1)} fusion(f32[128,8192]{1,0:T(8,128)} %bitcast.2, f32[64,128]{1,0:T(8,128)S(1)} %get-tuple-element.180, f32[64,8192]{1,0:T(8,128)S(1)} %copy-done), kind=kOutput, calls=%fused_computation.34 | convolution fusion | flops 806354944 | bytes 10518528 | tf_op jit(solution)/shard_map/dot_general | solution.py:106
  292.4 3.6 fusion.36
  296.1 22.9 %psum.37 = f32[64]{0:T(128)S(1)} all-reduce(f32[64]{0:T(128)S(1)} %get-tuple-element.179), channel_id=1, replica_groups=mesh['freq'=4,'frames'=8] {'frames'}, use_global_device_ids=true, to_apply=%region_7.8 | all-reduce | flops 64 | bytes 512 | tf_op jit(solution)/shard_map/psum | solution.py:154
  319.0 47.6 %reduce-scatter.2.cloned.1.call-done = f32[64,1024]{1,0:T(8,128)} async-done(((f32[64,8192]{1,0:T(8,128)}), f32[64,1024]{1,0:T(8,128)}) %reduce-scatter.2.cloned.1.call-update) | async-done | bytes 262160 | tf_op jit(solution)/shard_map/reduce_scatter | solution.py:153
  366.5 1.8 divide_multiply_fusion
  368.3 49.4 %all-gather.5.cloned.1.call-done = f32[64,8192]{1,0:T(8,128)} async-done(((f32[64,1024]{1,0:T(8,128)}), f32[64,8192]{1,0:T(8,128)}) %all-gather.5.cloned.1.call-update) | async-done | bytes 2097168 | tf_op jit(solution)/shard_map/all_gather | solution.py:98
  417.7 8.5 %convolution_divide_fusion = f32[128,8192]{1,0:T(8,128)} fusion(f32[128,8192]{1,0:T(8,128)} %bitcast.2, f32[64,128]{1,0:T(8,128)S(1)} %get-tuple-element.180, f32[64,8192]{1,0:T(8,128)} %all-gather.5.cloned.1.call-done), kind=kOutput, calls=%fused_computation.33 | convolution fusion | flops 806354944 | bytes 10518528 | tf_op jit(solution)/shard_map/dot_general | solution.py:106
  426.5 6.2 %fusion.37 = f32[64,128]{1,0:T(8,128)S(1)} fusion(f32[64,8192]{1,0:T(8,128)S(1)} %copy-done.1, f32[128,8192]{1,0:T(8,128)} %convolution_divide_fusion), kind=kOutput, calls=%fused_computation.63 | convolution fusion | flops 805306368 | bytes 6324224 | tf_op jit(solution)/shard_map/dot_general | solution.py:118
  432.7 10.5 %all-reduce = (f32[64,128]{1,0:T(8,128)S(1)}, f32[64]{0:T(128)S(1)}) all-reduce(f32[64,128]{1,0:T(8,128)S(1)} %fusion.37, f32[64]{0:T(128)S(1)} %reduce_sum.29), channel_id=1, replica_groups=mesh['freq'=4,'frames'=8] {'freq'}, use_global_device_ids=true, to_apply=%region_8.9 | all-reduce | flops 8256 | bytes 66048 | tf_op jit(solution)/shard_map/psum | solution.py:126
  (96 shorter events, 24.6 us)
Async XLA Ops:
  7.2 257.1 %all-gather.3.cloned.1.call-start = ((), (), s32[]{:S(2)}) async-start(), calls=%async_computation.2 | async-start | bytes 2359296 | tf_op jit(solution)/shard_map/all_gather | solution.py:98
  8.1 5.0 %collective-permute-start = (f32[1,32768]{1,0:T(1,128)S(1)}, f32[1,32768]{1,0:T(1,128)S(1)}, u32[]{:S(2)}, u32[]{:S(2)}) collective-permute-start(f32[1,32768]{1,0:T(1,128)S(1)} %slice_bitcast_fusion), channel_id=1, source_target_pairs={{8,0},{16,8},{24,16},{0,24},{9,1},{17,9},{25,17},{1,25},{10,2},{18... | collective-permute-start | bytes 393224 | tf_op jit(solution)/shard_map/ppermute | solution.py:18
  13.1 41.1 %collective-permute-start.1 = (f32[1,32768]{1,0:T(1,128)S(1)}, f32[1,32768]{1,0:T(1,128)S(1)}, u32[]{:S(2)}, u32[]{:S(2)}) collective-permute-start(f32[1,32768]{1,0:T(1,128)S(1)} %collective-permute-done), channel_id=1, source_target_pairs={{1,0},{2,1},{3,2},{4,3},{5,4},{6,5},{7,6},{9,8},{10,9},{11,10},{12... | collective-permute-start | bytes 393224 | tf_op jit(solution)/shard_map/ppermute | solution.py:24
  210.0 5.0 %copy-start.3 = (f32[16,128]{1,0:T(8,128)S(1)}, f32[16,128]{1,0:T(8,128)}, u32[]{:S(2)}) copy-start(f32[16,128]{1,0:T(8,128)} %param.7) | copy-start | bytes 24580
  210.0 54.3 %all-to-all-start = ((f32[32,4,8192]{2,0,1:T(8,128)}), f32[32,4,8192]{2,0,1:T(8,128)}, u32[]{:S(2)}, u32[]{:S(2)}) async-start(f32[32,4,8192]{2,0,1:T(8,128)} %copy.16), calls=%async_computation | async-start | bytes 8388608 | tf_op jit(solution)/shard_map/all_to_all | solution.py:144
  214.9 151.6 %reduce-scatter.2.cloned.1.call-start = ((), (), s32[]{:S(2)}) async-start(), calls=%async_computation.3 | async-start | bytes 2359296 | tf_op jit(solution)/shard_map/reduce_scatter | solution.py:153
  264.2 6.7 %copy-start = (f32[64,8192]{1,0:T(8,128)S(1)}, f32[64,8192]{1,0:T(8,128)}, u32[]{:S(2)}) copy-start(f32[64,8192]{1,0:T(8,128)} %all-gather.3.cloned.1.call-done) | copy-start | bytes 6291460
  292.4 74.2 %copy-start.2 = (f32[64,1024]{1,0:T(8,128)S(1)}, f32[64,1024]{1,0:T(8,128)}, u32[]{:S(2)}) copy-start(f32[64,1024]{1,0:T(8,128)} %param.6) | copy-start | bytes 786436
  296.0 121.7 %all-gather.5.cloned.1.call-start = ((), (), s32[]{:S(2)}) async-start(), calls=%async_computation.4 | async-start | bytes 2359296 | tf_op jit(solution)/shard_map/all_gather | solution.py:98
  417.7 8.5 %copy-start.1 = (f32[64,8192]{1,0:T(8,128)S(1)}, f32[64,8192]{1,0:T(8,128)}, u32[]{:S(2)}) copy-start(f32[64,8192]{1,0:T(8,128)} %all-gather.5.cloned.1.call-done) | copy-start | bytes 6291460
Sparse Core Ops, SparseCore 0:
  10.7 51.4 all-gather.2
  296.1 70.3 reduce-scatter.1
  369.3 48.3 all-gather.4
where the time goes:
time: 458 us; the launch traced here: 451 us
  waiting for transfers between devices  97.4 us (21%)
  blocking collectives  93.6 us (20%)
  matrix products  90.8 us (20%)
  other arithmetic  62.4 us (14%)
  local copies, waits for them, and re-layouts  56.8 us (12%)
  loops' own time  26.7 us (6%)
  between operations  14.4 us (3%)
  starting transfers between devices  8.8 us (2%)
    all_gather x2, waiting for transfers between devices, gather_basis(): return lax.all_gather(own_columns, 'frames', axis=1, tiled=True)  49.4 us
    all_gather x1, blocking collectives, gather_activity(): return lax.all_gather(own_rows, 'freq', axis=0, tiled=True)  49.2 us
    reduce_scatter x1, waiting for transfers between devices, on_device(): lax.psum_scatter(numerator, 'frames', scatter_dimension=1, tiled=True)  47.6 us
    unnamed x1, other arithmetic  34.1 us
    dot_general x8, matrix products, per_block(): jnp.einsum('oc,gjc->goj', second_section, twisted, precision=PRECISE, pre...  28.2 us
    dot_general x8, matrix products, per_block(): jnp.einsum('oq,gqp->gop', first_section, samples, precision=PRECISE, pref...  27.6 us
    another operation x1, loops' own time, frame_magnitudes(): return lax.map(per_block, offsets).reshape(frame_count, half_split * SPLIT)  26.7 us
    psum x1, blocking collectives, on_device(): totals = lax.psum(totals, 'frames')  22.9 us
  transfers between devices with their start and end apart: 6, of which 3 were waited for; matrix products, arithmetic and copies ran while one was open for 36% of the time, Pallas kernels for 0%

commit v1 on v0

v1 whole, which is shorter than its diff:
```python
import functools
import math

import jax
import jax.numpy as jnp
import ml_dtypes
import numpy as np
from jax import lax
from jax.experimental import pallas as pl
from jax.experimental.pallas import tpu as pltpu
from jax.sharding import Mesh
from jax.sharding import PartitionSpec as P

FRAME_LEN = 65536
SPLIT = 256
LANES = 128
GROUP = 8
HOP_ROWS = FRAME_LEN // 2 // LANES
VMEM = 56 * 1024 * 1024
NT = (((1,), (1,)), ((), ()))


def high_low(values):
    high = values.astype(np.float32).astype(ml_dtypes.bfloat16)
    low = (values - high.astype(np.float64)).astype(ml_dtypes.bfloat16)
    return high, low


def for_three_products(values):
    high, low = high_low(values)
    return np.concatenate([high, low, high], 1)


def units_of_member(units_here, member_blocks):
    order = list(range(units_here))
    if units_here % 8 == 0:
        order.sort(key=lambda r: (row_of_unit(r) % 2, r))
    kept = [(block, r) for block in member_blocks for r in order]
    if units_here % 8 == 0:
        kept.sort(key=lambda pair: row_of_unit(pair[1]) % 2)
    return kept


def row_of_unit(unit):
    return unit // 2 if unit % 2 == 0 else SPLIT - 1 - unit // 2


@functools.lru_cache(maxsize=None)
def tables(unit_order):
    half = SPLIT // 2
    index = np.arange(SPLIT, dtype=np.float64)
    slot = np.arange(half, dtype=np.float64)
    angle = 2.0 * np.pi / SPLIT * np.mod(np.outer(np.arange(half + 1), np.arange(SPLIT)), SPLIT)
    cosine, sine = np.cos(angle), np.sin(angle)
    first = np.concatenate([cosine[:half], cosine[half:], -sine[1:half]], 0)
    turn = 2.0 * np.pi / (SPLIT * SPLIT) * np.outer(slot, index)
    twiddle_cos, twiddle_sin = np.cos(turn), np.sin(turn)
    masked_cos = twiddle_cos.copy()
    masked_cos[0] = 0.0
    twiddle = np.stack([twiddle_cos, twiddle_sin, masked_cos]).astype(np.float32)
    middle = 2.0 * np.pi / (SPLIT * SPLIT) * half * index
    odd = 2.0 * np.pi / SPLIT * slot
    rows = np.zeros((8, SPLIT), np.float32)
    rows[0], rows[1] = np.cos(middle), -np.sin(middle)
    rows[2, :half], rows[3, :half] = np.cos(odd), np.sin(odd)
    seconds, mirrored, places = [], [], []
    for parity in range(2):
        here = [place for place, unit in enumerate(unit_order) if row_of_unit(unit) % 2 == parity]
        turns = np.array([row_of_unit(unit_order[place]) // 2 for place in here])
        phase = 2.0 * np.pi / half * np.mod(np.outer(turns, np.arange(half)), half)
        c, s = np.cos(phase), np.sin(phase)
        seconds.append(
            for_three_products(np.concatenate([np.concatenate([c, s], 1), np.concatenate([-s, c], 1)], 0))
        )
        flags = np.zeros((half, LANES), np.float32)
        flags[:, 0] = [unit_order[place] % 2 for place in here]
        mirrored.append(flags)
        places.append(tuple(here))
    position = np.arange(FRAME_LEN, dtype=np.float64)
    window = (0.5 - 0.5 * np.cos(2.0 * np.pi / FRAME_LEN * position)).astype(np.float32)
    window = window.reshape(SPLIT, 2, LANES).transpose(1, 0, 2)
    return (
        np.ascontiguousarray(window),
        for_three_products(first),
        twiddle,
        rows,
        np.stack(seconds),
        np.stack(mirrored),
        tuple(places),
    )


def split_values(values):
    high = values.astype(jnp.bfloat16)
    low = (values - high.astype(jnp.float32)).astype(jnp.bfloat16)
    return high, low


def dot(left, right):
    return jnp.dot(left, right, preferred_element_type=jnp.float32)


def dot_nt(left, right):
    return lax.dot_general(left, right, NT, preferred_element_type=jnp.float32)


def spectrum_kernel(
    places,
    per_member,
    main_ref,
    next_ref,
    window_ref,
    first_ref,
    twiddle_ref,
    rows_ref,
    second_ref,
    mirrored_ref,
    *rest,
):
    out_ref, parts_ref, middle_ref = rest[-3:]
    half = SPLIT // 2
    middle_ref[...] = jnp.zeros_like(middle_ref)

    def even_odd(real, imag):
        even = jnp.concatenate([real[:, :half] + real[:, half:], imag[:, :half] + imag[:, half:]], 1)
        real = real[:, :half] - real[:, half:]
        imag = imag[:, :half] - imag[:, half:]
        c, s = rows_ref[2:3, :half], rows_ref[3:4, :half]
        odd = jnp.concatenate([real * c + imag * s, imag * c - real * s], 1)
        return even, odd

    def three(values):
        high, low = split_values(values)
        return jnp.concatenate([high, high, low], 1)

    for g in range(GROUP):
        columns = []
        for side in range(2):
            top = main_ref[pl.ds(g * HOP_ROWS + side, half, stride=2), :]
            if g + 1 < GROUP:
                bottom = main_ref[pl.ds((g + 1) * HOP_ROWS + side, half, stride=2), :]
            else:
                bottom = next_ref[pl.ds(side, half, stride=2), :]
            columns.append(jnp.concatenate([top, bottom], 0) * window_ref[side])
        high, low = split_values(jnp.concatenate(columns, 1))
        section = dot(first_ref[...], jnp.concatenate([high, high, low], 0))
        a, b = section[:half], section[half:]
        real = a * twiddle_ref[0] + b * twiddle_ref[1]
        imag = b * twiddle_ref[2] - a * twiddle_ref[1]
        for parity, values in enumerate(even_odd(real, imag)):
            parts_ref[parity, g * half : (g + 1) * half, :] = three(values)
        nyquist = section[half : half + 1]
        for parity, values in enumerate(even_odd(nyquist * rows_ref[0:1], nyquist * rows_ref[1:2])):
            middle_ref[parity, g : g + 1, :] = values

    def magnitude(values):
        real, imag = values[:half], values[half:]
        return jnp.sqrt(real * real + imag * imag) * (8.0 / SPLIT)

    for parity in range(2):
        middle = magnitude(dot_nt(second_ref[parity], three(middle_ref[parity])))
        is_middle = mirrored_ref[parity] > 0.0
        for pair in range(GROUP // 2):
            values = magnitude(
                dot_nt(second_ref[parity], parts_ref[parity, pair * SPLIT : (pair + 1) * SPLIT, :])
            )
            for lane in range(2):
                g = 2 * pair + lane
                block = jnp.where(
                    is_middle, middle[:, g : g + 1], values[:, lane * LANES : (lane + 1) * LANES]
                )
                start = 0
                while start < half:
                    stop = start + 1
                    place = places[parity][start]
                    while (
                        stop < half
                        and stop - start < 8
                        and places[parity][stop] == place + stop - start
                        and places[parity][stop] // per_member == place // per_member
                    ):
                        stop += 1
                    member, row = divmod(place, per_member)
                    out_ref[member, 0, pl.ds(row * GROUP + g, stop - start, stride=GROUP), :] = block[start:stop]
                    start = stop


def spectrum_blocks(samples, trailing, unit_order, members):
    window, first, twiddle, rows, second, mirrored, places = tables(unit_order)
    per_member = SPLIT // members
    chunks = samples.shape[0] // (GROUP * HOP_ROWS)
    constants = [jnp.asarray(t) for t in (window, first, twiddle, rows, second, mirrored)]
    out_shape = jax.ShapeDtypeStruct((members, chunks, per_member * GROUP, LANES), jnp.float32)
    whole = [pl.BlockSpec(t.shape, lambda s, n=t.ndim: (0,) * n) for t in constants]
    kernel = functools.partial(spectrum_kernel, places, per_member)

    def call(first_chunk, count, following, following_spec, earlier):
        extra = [] if earlier is None else [earlier]
        return pl.pallas_call(
            kernel,
            grid=(count,),
            in_specs=[
                pl.BlockSpec((GROUP * HOP_ROWS, LANES), lambda s: (s + first_chunk, 0)),
                following_spec,
                *whole,
                *[pl.BlockSpec(memory_space=pl.ANY) for _ in extra],
            ],
            out_specs=pl.BlockSpec(
                (members, 1, per_member * GROUP, LANES), lambda s: (0, s + first_chunk, 0, 0)
            ),
            out_shape=out_shape,
            scratch_shapes=[
                pltpu.VMEM((2, GROUP * LANES, 3 * SPLIT), jnp.bfloat16),
                pltpu.VMEM((2, 16, SPLIT), jnp.float32),
            ],
            input_output_aliases={2 + len(constants): 0} if extra else {},
            compiler_params=pltpu.CompilerParams(vmem_limit_bytes=VMEM),
            cost_estimate=pl.CostEstimate(
                flops=count * GROUP * 6 * SPLIT * SPLIT * SPLIT * 2,
                bytes_accessed=count * GROUP * FRAME_LEN * 4,
                transcendentals=0,
            ),
        )(samples, following, *constants, *extra)

    ahead = pl.BlockSpec((HOP_ROWS, LANES), lambda s: (GROUP * (s + 1), 0))
    result = call(0, chunks - 1, samples, ahead, None)
    return call(chunks - 1, 1, trailing, pl.BlockSpec((HOP_ROWS, LANES), lambda s: (0, 0)), result)


def lanes_of_activity(activity):
    high, low = split_values(activity)
    return jnp.concatenate([high, high, low, low], 1)


def ratio_of(spectrum_ref, activity_lanes, basis):
    frames = activity_lanes.shape[0]
    splits = [split_values(block) for block in basis]
    stacked = jnp.concatenate([jnp.concatenate([h, l, h, l], 0) for h, l in splits], 1)
    approx = dot(activity_lanes, stacked)
    count = len(basis)
    values = jnp.concatenate(
        [
            spectrum_ref[:, :, row * GROUP : (row + 1) * GROUP, :].reshape(frames, LANES)
            for row in range(count)
        ],
        1,
    )
    return values / approx, splits


def add_to_activity(total_ref, ratio, splits):
    high, low = split_values(ratio)
    basis = jnp.concatenate([jnp.concatenate([h, l], 0) for h, l in splits], 1)
    total_ref[...] += dot_nt(jnp.concatenate([high, low], 1), jnp.concatenate([basis, basis], 1))


def first_kernel(rows, spectrum_ref, basis_ref, activity_ref, out_ref, lanes_ref, total_ref, sums_ref):
    step = pl.program_id(0)
    rank = activity_ref.shape[1]

    @pl.when(step == 0)
    def _():
        lanes_ref[...] = lanes_of_activity(activity_ref[...])
        total_ref[...] = jnp.zeros_like(total_ref)
        sums_ref[...] = jnp.zeros_like(sums_ref)

    basis = [basis_ref[row] for row in range(rows)]
    ratio, splits = ratio_of(spectrum_ref, lanes_ref[...], basis)
    add_to_activity(total_ref, ratio, splits)
    sums_ref[...] += sum(basis)

    @pl.when(step == pl.num_programs(0) - 1)
    def _():
        total = total_ref[...]
        total = total[:, :rank] + total[:, rank:]
        half = total.shape[0] // 2
        out_ref[:half, :] = jnp.concatenate([total[:half], total[half:]], 1)
        sums = jnp.sum(jnp.transpose(sums_ref[...]), axis=0, keepdims=True)
        out_ref[half:, :] = jnp.broadcast_to(jnp.concatenate([sums, sums], 1), (8, 2 * rank))


def by_owner(values, shape):
    subs, members, ranks, width = shape
    local = width // subs
    blocks = []
    for member in range(members):
        rows = [
            values[(sub * members + member) * local : (sub * members + member + 1) * local]
            for sub in range(subs)
        ]
        blocks.append(jnp.transpose(jnp.concatenate(rows, 0)).reshape(subs, ranks, width))
    return blocks


def second_kernel(
    rows, spectrum_ref, basis_ref, activity_ref, sums_ref, middle_ref, owned_ref, out_ref, lanes_ref, turned_ref
):
    step = pl.program_id(0)
    rank = activity_ref.shape[1]

    @pl.when(step == 0)
    def _():
        half = activity_ref.shape[0] // 2
        scale = sums_ref[:half, :] / sums_ref[half : half + 1, :]
        middle = activity_ref[...] * jnp.concatenate([scale[:, :rank], scale[:, rank:]], 0)
        middle_ref[...] = middle
        lanes_ref[...] = lanes_of_activity(middle)
        turned = jnp.transpose(middle)
        high, low = split_values(turned)
        turned_ref[...] = jnp.concatenate([high, low], 0)
        totals = jnp.sum(turned, axis=1, keepdims=True)
        out_ref[out_ref.shape[0] - 1] = jnp.broadcast_to(totals, (rank, LANES))
        subs, members, ranks, width = owned_ref.shape
        for member, block in enumerate(by_owner(middle, owned_ref.shape)):
            owned_ref[:, member] = block

    basis = [basis_ref[row] for row in range(rows)]
    ratio, _ = ratio_of(spectrum_ref, lanes_ref[...], basis)
    high, low = split_values(ratio)
    turned = turned_ref[...]
    total = dot(turned, high) + dot(turned, low)
    total = total[:rank] + total[rank:]
    for row in range(rows):
        out_ref[step * rows + row] = total[:, row * LANES : (row + 1) * LANES]


def third_kernel(
    rows,
    sources,
    spectrum_ref,
    basis_ref,
    middle_ref,
    *rest,
):
    numerators = rest[:sources]
    totals = rest[sources : 2 * sources]
    new_ref, out_ref, lanes_ref, total_ref, sums_ref = rest[2 * sources :]
    step = pl.program_id(0)
    rank = middle_ref.shape[1]

    @pl.when(step == 0)
    def _():
        lanes_ref[...] = lanes_of_activity(middle_ref[...])
        total_ref[...] = jnp.zeros_like(total_ref)
        sums_ref[...] = jnp.zeros_like(sums_ref)

    total = sum(ref[0] for ref in totals)
    basis = []
    for row in range(rows):
        block = basis_ref[row] * (sum(ref[row] for ref in numerators) / total)
        new_ref[row] = block
        basis.append(block)
    ratio, splits = ratio_of(spectrum_ref, lanes_ref[...], basis)
    add_to_activity(total_ref, ratio, splits)
    sums_ref[...] += sum(basis)

    @pl.when(step == pl.num_programs(0) - 1)
    def _():
        total = total_ref[...]
        total = total[:, :rank] + total[:, rank:]
        subs, members, _, ranks, width = out_ref.shape
        shape = (subs, members, ranks, width)
        sums = jnp.sum(sums_ref[...], axis=1, keepdims=True)
        sums = jnp.broadcast_to(sums, (rank, width)).reshape(subs, ranks, width)
        for member, block in enumerate(by_owner(total, shape)):
            out_ref[:, member, 0] = block
            out_ref[:, member, 1] = sums


def step_rows(per_member):
    return 2 if per_member % 2 == 0 else 1


def spectrum_spec(spectrum, rows):
    members, chunks = spectrum.shape[:2]
    return pl.BlockSpec((members, chunks, rows * GROUP, LANES), lambda s: (0, 0, s, 0))


def full(shape):
    return pl.BlockSpec(shape, lambda s: (0,) * len(shape))


def out_rank(operands):
    return operands[1].shape[1]


def update_call(kernel, spectrum, per_member, in_specs, out_specs, out_shape, scratch, operands):
    rows = step_rows(per_member)
    rank = out_rank(operands)
    return pl.pallas_call(
        kernel,
        grid=(per_member // rows,),
        in_specs=in_specs,
        out_specs=out_specs,
        out_shape=out_shape,
        scratch_shapes=scratch,
        compiler_params=pltpu.CompilerParams(vmem_limit_bytes=VMEM),
        cost_estimate=pl.CostEstimate(
            flops=spectrum.size * rank * 16, bytes_accessed=spectrum.size * 4, transcendentals=0
        ),
    )(*operands)


def turned_lanes(values):
    return jnp.roll(jnp.flip(values, -1), 1, -1)


def swap_by(value, axis, mask):
    count = lax.axis_size(axis)
    return lax.ppermute(value, axis, [(i, i ^ mask) for i in range(count)])


def sum_over(value, axes):
    for axis in axes:
        count = lax.axis_size(axis)
        if count & (count - 1):
            value = lax.psum(value, axis)
            continue
        mask = 1
        while mask < count:
            value = value + swap_by(value, axis, mask)
            mask *= 2
    return value


def on_device(signal, templates, activations):
    subs, groups, members = (lax.axis_size(axis) for axis in ("freq", "group", "member"))
    blocks = groups * members
    rank, bins_here = templates.shape
    ranks_here, width = activations.shape
    units_here = bins_here // LANES
    exchange = ("freq", "member")
    partners = subs * members
    per_member = units_here * groups
    rows = step_rows(per_member)
    me_sub, me_group, me_member = (lax.axis_index(axis) for axis in ("freq", "group", "member"))

    kept = units_of_member(units_here, range(groups))
    unit_order = tuple(
        units_here * (sub * blocks + group * members + member) + r
        for sub in range(subs)
        for member in range(members)
        for group, r in kept
    )

    samples = signal.reshape(-1, LANES)
    route = [
        (((sub + 1) % subs) * blocks + block + (sub + 1) // subs, sub * blocks + block)
        for sub in range(subs)
        for block in range(blocks)
        if block + (sub + 1) // subs < blocks
    ]
    trailing = lax.ppermute(samples[:HOP_ROWS], ("freq", "group", "member"), route)
    gathered = lax.all_gather(activations, exchange)
    other = [swap_by(templates, "group", 1)] if groups == 2 else []

    spectrum = spectrum_blocks(samples, trailing, unit_order, partners)
    spectrum, gathered, other, templates = lax.optimization_barrier(
        (spectrum, gathered, other, templates)
    )
    spectrum = lax.all_to_all(spectrum, exchange, 0, 0, tiled=True)

    local = width // subs
    activity = gathered.reshape(subs, members, ranks_here, subs, local)
    activity = activity.transpose(3, 1, 4, 0, 2).reshape(partners * local, rank)
    frames = partners * local

    own = templates.reshape(rank, units_here, LANES).transpose(1, 0, 2)
    if other:
        remote = other[0].reshape(rank, units_here, LANES).transpose(1, 0, 2)
        by_group = jnp.where(me_group == 0, jnp.stack([own, remote]), jnp.stack([remote, own]))
    else:
        by_group = own[None]
    unit_index = units_here * (
        me_sub * blocks + jnp.arange(groups)[:, None] * members + me_member
    ) + jnp.arange(units_here)[None, :]
    is_turned = (unit_index % 2 == 1)[:, :, None, None]
    by_group = jnp.where(is_turned, turned_lanes(by_group), by_group)
    basis = jnp.concatenate([by_group[group, r][None] for group, r in kept], 0)

    specs = spectrum_spec(spectrum, rows)
    basis_spec = pl.BlockSpec((rows, rank, LANES), lambda s: (s, 0, 0))
    lanes_scratch = pltpu.VMEM((frames, 4 * rank), jnp.bfloat16)
    total_scratch = pltpu.VMEM((frames, 2 * rank), jnp.float32)
    sums_scratch = pltpu.VMEM((rank, LANES), jnp.float32)
    sums_shape = (frames // 2 + 8, 2 * rank)
    sums = update_call(
        functools.partial(first_kernel, rows),
        spectrum,
        per_member,
        [specs, basis_spec, full((frames, rank))],
        full(sums_shape),
        jax.ShapeDtypeStruct(sums_shape, jnp.float32),
        [lanes_scratch, total_scratch, sums_scratch],
        (spectrum, basis, activity),
    )
    sums = sum_over(sums, exchange)

    owned_shape = (subs, members, ranks_here, width)
    numerator_shape = (per_member + 1, rank, LANES)
    middle, owned, numerator = update_call(
        functools.partial(second_kernel, rows),
        spectrum,
        per_member,
        [specs, basis_spec, full((frames, rank)), full(sums_shape)],
        [full((frames, rank)), full(owned_shape), full(numerator_shape)],
        [
            jax.ShapeDtypeStruct((frames, rank), jnp.float32),
            jax.ShapeDtypeStruct(owned_shape, jnp.float32),
            jax.ShapeDtypeStruct(numerator_shape, jnp.float32),
        ],
        [lanes_scratch, pltpu.VMEM((2 * rank, frames), jnp.bfloat16)],
        (spectrum, basis, activity, sums),
    )
    numerators = [numerator]
    if groups == 2:
        numerators.append(swap_by(numerator, "group", 1))
    payload_shape = (subs, members, 2, ranks_here, width)
    total_spec = pl.BlockSpec((1, rank, LANES), lambda s: (per_member, 0, 0))
    new_basis, payload = update_call(
        functools.partial(third_kernel, rows, len(numerators)),
        spectrum,
        per_member,
        [specs, basis_spec, full((frames, rank))]
        + [basis_spec] * len(numerators)
        + [total_spec] * len(numerators),
        [basis_spec, full(payload_shape)],
        [
            jax.ShapeDtypeStruct((per_member, rank, LANES), jnp.float32),
            jax.ShapeDtypeStruct(payload_shape, jnp.float32),
        ],
        [lanes_scratch, total_scratch, sums_scratch],
        (spectrum, basis, middle, *numerators, *numerators),
    )
    received = lax.all_to_all(
        payload.reshape(partners, 2, ranks_here, width), exchange, 0, 0, tiled=True
    )
    summed = jnp.sum(received, axis=0)
    mine = lax.dynamic_slice(
        owned, (me_sub, me_member, 0, 0), (1, 1, ranks_here, width)
    ).reshape(ranks_here, width)
    final_activations = mine * (summed[0] / summed[1])

    back = jnp.stack(
        [
            jnp.stack([new_basis[kept.index((group, r))] for r in range(units_here)])
            for group in range(groups)
        ]
    )
    back = lax.dynamic_index_in_dim(back, me_group, 0, keepdims=False)
    turned_here = lax.dynamic_index_in_dim(is_turned, me_group, 0, keepdims=False)
    back = jnp.where(turned_here, turned_lanes(back), back)
    final_templates = back.transpose(1, 0, 2).reshape(rank, bins_here)
    return (final_activations, final_templates)


def solution(mesh):
    subs, blocks = mesh.devices.shape
    groups = 2 if blocks % 2 == 0 else 1
    grid = Mesh(
        mesh.devices.reshape(subs, groups, blocks // groups), ("freq", "group", "member")
    )
    frames = ("group", "member")
    return jax.shard_map(
        on_device,
        mesh=grid,
        in_specs=(P(frames, "freq", None), P(None, ("freq", *frames)), P("freq", frames)),
        out_specs=(P("freq", frames), P(None, ("freq", *frames))),
        check_vma=False,
    )
```

time: 458 us -> 196 us (0.43); the launches traced: 451 us -> 195 us
  matrix products: 90.8 us -> 0 us
  blocking collectives: 93.6 us -> 27 us
  other arithmetic: 62.4 us -> 4.26 us
  local copies, waits for them, and re-layouts: 56.8 us -> 9.27 us
  Pallas kernels: 0 us -> 40.2 us
  loops' own time: 26.7 us -> 0 us
  between operations: 14.4 us -> 0.91 us
  starting transfers between devices: 8.8 us -> 20.3 us
  waiting for transfers between devices: 97.4 us -> 92.7 us
    dot_general x22 -> x0, matrix products: 90.8 us -> none  [the longest x8 28.2 us: per_block(): jnp.einsum('oc,gjc->goj', second_section, twisted, precision=PRECISE, pre...]
    all_to_all x1 -> x2, waiting for transfers between devices: 0.01 us -> 53 us  [the longest x1 51.3 us: on_device(): spectrum = lax.all_to_all(spectrum, exchange, 0, 0, tiled=True)]
    all_gather x2 -> x0, waiting for transfers between devices: 49.4 us -> none  [gather_basis(): return lax.all_gather(own_columns, 'frames', axis=1, tiled=True)]
    reduce_scatter x1 -> x0, waiting for transfers between devices: 47.6 us -> none  [on_device(): lax.psum_scatter(numerator, 'frames', scatter_dimension=1, tiled=True)]
    psum x3 -> x0, blocking collectives: 44.4 us -> none  [the longest x1 22.9 us: on_device(): totals = lax.psum(totals, 'frames')]
    pallas_call x0 -> x5, Pallas kernels: none -> 40.2 us  [the longest x3 24.3 us: update_call(): pl.pallas_call(kernel, grid=(per_member // rows,), in_specs=in_specs, out...]
    ppermute x2 -> x7, waiting for transfers between devices: 0.4 us -> 39.7 us  [the longest x6 39.7 us: swap_by(): return lax.ppermute(value, axis, [(i, i ^ mask) for i in range(count)])]
    unnamed x1 -> x0, other arithmetic: 34.1 us -> none
  transfers between devices with their start and end apart: 6 -> 9, of which waited for: 3 -> 7; matrix products, arithmetic and copies ran while one was open for 36% -> 4% of each run, Pallas kernels for 0% -> 8%
where the time goes in v1:
time: 196 us; the launch traced here: 195 us
  waiting for transfers between devices  92.7 us (47%)
  Pallas kernels  40.2 us (21%)
  blocking collectives  27 us (14%)
  starting transfers between devices  20.3 us (10%)
  local copies, waits for them, and re-layouts  9.27 us (5%)
  other arithmetic  4.26 us (2%)
    all_to_all x1, waiting for transfers between devices, on_device(): spectrum = lax.all_to_all(spectrum, exchange, 0, 0, tiled=True)  51.3 us
    ppermute x6, waiting for transfers between devices, swap_by(): return lax.ppermute(value, axis, [(i, i ^ mask) for i in range(count)])  39.7 us
    all_gather x1, blocking collectives, on_device(): gathered = lax.all_gather(activations, exchange)  27 us
    pallas_call x3, Pallas kernels, update_call(): pl.pallas_call(kernel, grid=(per_member // rows,), in_specs=in_specs, out...  24.3 us
    pallas_call x2, Pallas kernels, call(): pl.pallas_call(kernel, grid=(count,), in_specs=[pl.BlockSpec((GROUP * HOP...  15.9 us
    ppermute x6, starting transfers between devices, swap_by(): return lax.ppermute(value, axis, [(i, i ^ mask) for i in range(count)])  10.8 us
    unnamed x29, local copies, waits for them, and re-layouts  4.99 us
    all_to_all x1, starting transfers between devices, on_device(): spectrum = lax.all_to_all(spectrum, exchange, 0, 0, tiled=True)  4.68 us
  transfers between devices with their start and end apart: 9, of which 7 were waited for; matrix products, arithmetic and copies ran while one was open for 4% of the time, Pallas kernels for 8%

profile of v1, /device:TPU:0, one launch (start us, length us, event | category | flops | bytes accessed | tf_op | source)
XLA Modules:
  0.0 194.6 jit_solution(17659342575354839687)
XLA Ops:
  0.6 0.9 slice.126
  1.5 1.3 collective-permute-start
  2.8 6.5 %collective-permute-start.1 = (f32[64,1024]{1,0:T(8,128)}, f32[64,1024]{1,0:T(8,128)S(1)}, u32[]{:S(2)}, u32[]{:S(2)}) collective-permute-start(f32[64,1024]{1,0:T(8,128)} %param.10), channel_id=1, source_target_pairs={{0,4},{4,0},{1,5},{5,1},{2,6},{6,2},{3,7},{7,3},{8,12},{12,8},{9,1... | collective-permute-start | bytes 786440 | tf_op jit(solution)/shard_map/ppermute | solution.py:410
  9.3 0.0 copy-start.4
  9.3 10.5 %shard_map.104.rest_0_ = f32[16,4,128,128]{3,2,1,0:T(8,128)} custom-call(f32[8192,128]{1,0:T(8,128)} %bitcast.110, f32[8192,128]{1,0:T(8,128)} %bitcast.111, f32[2,256,128]{2,1,0:T(8,128)} %constant.60.clone.window_ref, bf16[256,768]{1,0:T(8,128)(2,1)} %constant.61.clone.first_ref, f32[3,128,256]{2,1,0:T(8,128)} %constant.62.clone.twiddle_ref, ...), custom_call_target="tpu_custom_call" | custom-call | flops 4831838208 | bytes 6291456 | tf_op jit(solution)/shard_map/pallas_call | solution.py:199
  19.9 0.0 copy-done.4
  19.9 27.0 %all-gather = f32[256,128]{1,0:T(8,128)S(1)} all-gather(f32[16,128]{1,0:T(8,128)S(1)} %copy-done.4), channel_id=2, replica_groups=mesh['freq'=4,'group'=2,'member'=4] {'freq','member'}, dimensions={0}, use_global_device_ids=true | all-gather | bytes 139264 | tf_op jit(solution)/shard_map/all_gather | solution.py:454
  46.9 0.0 collective-permute-done.next_ref
  46.9 0.0 copy-start.3
  46.9 0.7 copy-done.3
  47.5 5.4 %shard_map.105 = f32[16,4,128,128]{3,2,1,0:T(8,128)} custom-call(f32[8192,128]{1,0:T(8,128)} %bitcast.112, f32[256,128]{1,0:T(8,128)} %copy-done.3, f32[2,256,128]{2,1,0:T(8,128)} %constant.60.clone.window_ref, bf16[256,768]{1,0:T(8,128)(2,1)} %constant.61.clone.first_ref, ...), custom_call_target="tpu_custom_call", output_to_operand_aliasing={{}: (8, {})} | custom-call | flops 1610612736 | bytes 2097152 | tf_op jit(solution)/shard_map/pallas_call | solution.py:199
  52.9 0.0 collective-permute-done.1
  52.9 0.0 copy-start.2
  52.9 4.7 %all-to-all-start = ((f32[16,4,128,128]{3,2,1,0:T(8,128)}), f32[16,4,128,128]{3,2,1,0:T(8,128)}, u32[]{:S(2)}, u32[]{:S(2)}) async-start(f32[16,4,128,128]{3,2,1,0:T(8,128)} %shard_map.105), calls=%async_computation | async-start | bytes 8388608 | tf_op jit(solution)/shard_map/all_to_all | solution.py:461
  57.6 0.1 fusion.6
  57.7 0.0 copy-done.2
  57.8 0.2 slice.163
  58.0 0.2 slice.130
  58.2 0.3 reshape.79
  58.5 0.3 copy.22
  58.8 0.4 reshape.80
  59.3 0.8 copy.24.activity_ref
  60.1 0.2 maximum_select_fusion.1
  60.6 0.0 copy-start
  60.6 51.3 %all-to-all-done.spectrum_ref = f32[16,4,128,128]{3,2,1,0:T(8,128)} async-done(((f32[16,4,128,128]{3,2,1,0:T(8,128)}), f32[16,4,128,128]{3,2,1,0:T(8,128)}, u32[]{:S(2)}, u32[]{:S(2)}) %all-to-all-start) | async-done | bytes 4194336 | tf_op jit(solution)/shard_map/all_to_all | solution.py:461
  111.8 0.0 copy-done
  111.8 7.8 %shard_map.106 = f32[264,128]{1,0:T(8,128)} custom-call(f32[16,4,128,128]{3,2,1,0:T(8,128)} %all-to-all-done.spectrum_ref, f32[16,64,128]{2,1,0:T(8,128)} %copy-done, f32[512,64]{1,0:T(8,128)} %copy.24.activity_ref), custom_call_target="tpu_custom_call" | custom-call | flops 1073741824 | bytes 4194304 | tf_op jit(solution)/shard_map/pallas_call | solution.py:390
  119.6 2.2 %collective-permute-start.2 = (f32[264,128]{1,0:T(8,128)}, f32[264,128]{1,0:T(8,128)S(1)}, u32[]{:S(2)}, u32[]{:S(2)}) collective-permute-start(f32[264,128]{1,0:T(8,128)} %shard_map.106), channel_id=1, source_target_pairs={{0,8},{8,0},{16,24},{24,16},{1,9},{9,1},{17,25},{25,17},{2,10},{10... | collective-permute-start | bytes 405512 | tf_op jit(solution)/shard_map/ppermute | solution.py:410
  121.8 1.2 collective-permute-done.2
  123.0 0.9 add.81
  124.0 1.1 collective-permute-start.3
  125.0 4.8 %collective-permute-done.3 = f32[264,128]{1,0:T(8,128)S(1)} collective-permute-done((f32[264,128]{1,0:T(8,128)S(1)}, f32[264,128]{1,0:T(8,128)S(1)}, u32[]{:S(2)}, u32[]{:S(2)}) %collective-permute-start.3) | collective-permute-done | bytes 135200 | tf_op jit(solution)/shard_map/ppermute | solution.py:410
  129.9 0.6 collective-permute-start.4
  130.5 4.5 %collective-permute-done.4 = f32[264,128]{1,0:T(8,128)S(1)} collective-permute-done((f32[264,128]{1,0:T(8,128)S(1)}, f32[264,128]{1,0:T(8,128)S(1)}, u32[]{:S(2)}, u32[]{:S(2)}) %collective-permute-start.4) | collective-permute-done | bytes 135200 | tf_op jit(solution)/shard_map/ppermute | solution.py:410
  135.0 0.1 collective-permute-start.5
  135.1 5.0 %collective-permute-done.5 = f32[264,128]{1,0:T(8,128)S(1)} collective-permute-done((f32[264,128]{1,0:T(8,128)S(1)}, f32[264,128]{1,0:T(8,128)S(1)}, u32[]{:S(2)}, u32[]{:S(2)}) %collective-permute-start.5) | collective-permute-done | bytes 135200 | tf_op jit(solution)/shard_map/ppermute | solution.py:410
  140.1 0.7 add.84.sums_ref
  140.8 8.4 %shard_map.107 = (f32[512,64]{1,0:T(8,128)}, f32[4,4,16,128]{3,2,1,0:T(8,128)}, f32[17,64,128]{2,1,0:T(8,128)}) custom-call(f32[16,4,128,128]{3,2,1,0:T(8,128)} %all-to-all-done.spectrum_ref, f32[16,64,128]{2,1,0:T(8,128)} %copy-done, f32[512,64]{1,0:T(8,128)} %copy.24.activity_ref, f32[264,128]{1,0:T(8,128)} %add.84.sums_ref), custom_call_target="tpu_custom_call" | custom-call | flops 1073741824 | bytes 4194304 | tf_op jit(solution)/shard_map/pallas_call | solution.py:390
  149.2 0.4 collective-permute-start.6
  149.5 24.2 %collective-permute-done.6.rest_1_.rest_3_ = f32[17,64,128]{2,1,0:T(8,128)S(1)} collective-permute-done((f32[17,64,128]{2,1,0:T(8,128)}, f32[17,64,128]{2,1,0:T(8,128)S(1)}, u32[]{:S(2)}, u32[]{:S(2)}) %collective-permute-start.6) | collective-permute-done | bytes 557088 | tf_op jit(solution)/shard_map/ppermute | solution.py:410
  173.7 0.0 copy-start.1
  173.7 0.8 copy-done.1
  174.5 8.1 %shard_map.108 = (f32[16,64,128]{2,1,0:T(8,128)}, f32[4,4,2,16,128]{4,3,2,1,0:T(8,128)}) custom-call(f32[16,4,128,128]{3,2,1,0:T(8,128)} %all-to-all-done.spectrum_ref, f32[16,64,128]{2,1,0:T(8,128)} %copy-done, f32[512,64]{1,0:T(8,128)} %get-tuple-element.16.middle_ref, f32[17,64,128]{2,1,0:T(8,128)} %get-tuple-element.17.rest_0_.rest_2_, ...), custom_call_target="tpu_custom_call" | custom-call | flops 1073741824 | bytes 4194304 | tf_op jit(solution)/shard_map/pallas_call | solution.py:390
  182.6 3.5 %all-to-all-start.1 = ((f32[16,2,16,128]{3,2,1,0:T(8,128)}), f32[16,2,16,128]{3,2,1,0:T(8,128)S(1)}, u32[]{:S(2)}, u32[]{:S(2)}) async-start(f32[16,2,16,128]{3,2,1,0:T(8,128)} %bitcast.118), calls=%async_computation.1 | async-start | bytes 524288 | tf_op jit(solution)/shard_map/all_to_all | solution.py:535
  186.1 0.8 constant_dynamic-update-slice_fusion.19
  186.9 0.9 slice_dynamic-update-slice_fusion.2
  187.8 0.9 slice_dynamic-update-slice_fusion.1
  188.7 0.9 slice_dynamic-update-slice_fusion
  189.6 0.8 constant_dynamic-update-slice_fusion.18
  190.4 0.1 fusion.1
  190.4 0.1 slice.183
  190.6 0.1 slice.161
  190.7 0.9 copy_bitcast_fusion
  191.6 1.7 all-to-all-done.1
  193.3 1.3 fusion.4
  (23 shorter events, 0.2 us)
Async XLA Ops:
  1.5 45.3 %collective-permute-start = (f32[256,128]{1,0:T(8,128)S(1)}, f32[256,128]{1,0:T(8,128)S(1)}, u32[]{:S(2)}, u32[]{:S(2)}) collective-permute-start(f32[256,128]{1,0:T(8,128)S(1)} %bitcast.119), channel_id=1, source_target_pairs={{8,0},{9,1},{10,2},{11,3},{12,4},{13,5},{14,6},{15,7},{16,8},{17,9... | collective-permute-start | bytes 393224 | tf_op jit(solution)/shard_map/ppermute | solution.py:453
  2.8 50.1 %collective-permute-start.1 = (f32[64,1024]{1,0:T(8,128)}, f32[64,1024]{1,0:T(8,128)S(1)}, u32[]{:S(2)}, u32[]{:S(2)}) collective-permute-start(f32[64,1024]{1,0:T(8,128)} %param.10), channel_id=1, source_target_pairs={{0,4},{4,0},{1,5},{5,1},{2,6},{6,2},{3,7},{7,3},{8,12},{12,8},{9,1... | collective-permute-start | bytes 786440 | tf_op jit(solution)/shard_map/ppermute | solution.py:410
  9.3 10.6 %copy-start.4 = (f32[16,128]{1,0:T(8,128)S(1)}, f32[16,128]{1,0:T(8,128)}, u32[]{:S(2)}) copy-start(f32[16,128]{1,0:T(8,128)} %param.11) | copy-start | bytes 24580
  46.9 0.7 copy-start.3
  52.9 4.8 %copy-start.2 = (f32[64,1024]{1,0:T(8,128)S(1)}, f32[64,1024]{1,0:T(8,128)}, u32[]{:S(2)}) copy-start(f32[64,1024]{1,0:T(8,128)} %param.10) | copy-start | bytes 786436
  52.9 58.9 %all-to-all-start = ((f32[16,4,128,128]{3,2,1,0:T(8,128)}), f32[16,4,128,128]{3,2,1,0:T(8,128)}, u32[]{:S(2)}, u32[]{:S(2)}) async-start(f32[16,4,128,128]{3,2,1,0:T(8,128)} %shard_map.105), calls=%async_computation | async-start | bytes 8388608 | tf_op jit(solution)/shard_map/all_to_all | solution.py:461
  60.6 51.3 %copy-start = (f32[16,64,128]{2,1,0:T(8,128)}, f32[16,64,128]{2,1,0:T(8,128)S(1)}, u32[]{:S(2)}) copy-start(f32[16,64,128]{2,1,0:T(8,128)S(1)} %constant_dynamic-update-slice_fusion.basis_ref) | copy-start | bytes 1572868
  119.6 3.4 %collective-permute-start.2 = (f32[264,128]{1,0:T(8,128)}, f32[264,128]{1,0:T(8,128)S(1)}, u32[]{:S(2)}, u32[]{:S(2)}) collective-permute-start(f32[264,128]{1,0:T(8,128)} %shard_map.106), channel_id=1, source_target_pairs={{0,8},{8,0},{16,24},{24,16},{1,9},{9,1},{17,25},{25,17},{2,10},{10... | collective-permute-start | bytes 405512 | tf_op jit(solution)/shard_map/ppermute | solution.py:410
  124.0 5.9 %collective-permute-start.3 = (f32[264,128]{1,0:T(8,128)S(1)}, f32[264,128]{1,0:T(8,128)S(1)}, u32[]{:S(2)}, u32[]{:S(2)}) collective-permute-start(f32[264,128]{1,0:T(8,128)S(1)} %add.81), channel_id=1, source_target_pairs={{0,16},{8,24},{16,0},{24,8},{1,17},{9,25},{17,1},{25,9},{2,18},{10... | collective-permute-start | bytes 405512 | tf_op jit(solution)/shard_map/ppermute | solution.py:410
  129.9 5.1 %collective-permute-start.4 = (f32[264,128]{1,0:T(8,128)S(1)}, f32[264,128]{1,0:T(8,128)S(1)}, u32[]{:S(2)}, u32[]{:S(2)}) collective-permute-start(f32[264,128]{1,0:T(8,128)S(1)} %add.82), channel_id=1, source_target_pairs={{0,1},{1,0},{2,3},{3,2},{4,5},{5,4},{6,7},{7,6},{8,9},{9,8},{10,11... | collective-permute-start | bytes 405512 | tf_op jit(solution)/shard_map/ppermute | solution.py:410
  135.0 5.1 %collective-permute-start.5 = (f32[264,128]{1,0:T(8,128)S(1)}, f32[264,128]{1,0:T(8,128)S(1)}, u32[]{:S(2)}, u32[]{:S(2)}) collective-permute-start(f32[264,128]{1,0:T(8,128)S(1)} %add.83), channel_id=1, source_target_pairs={{0,2},{1,3},{2,0},{3,1},{4,6},{5,7},{6,4},{7,5},{8,10},{9,11},{10,... | collective-permute-start | bytes 405512 | tf_op jit(solution)/shard_map/ppermute | solution.py:410
  149.2 24.5 %collective-permute-start.6 = (f32[17,64,128]{2,1,0:T(8,128)}, f32[17,64,128]{2,1,0:T(8,128)S(1)}, u32[]{:S(2)}, u32[]{:S(2)}) collective-permute-start(f32[17,64,128]{2,1,0:T(8,128)} %get-tuple-element.17.rest_0_.rest_2_), channel_id=1, source_target_pairs={{0,4},{4,0},{1,5},{5,1},{2,6},{6,2},{3,7},{7,3},{8,12},{12,8},{9,1... | collective-permute-start | bytes 1671176 | tf_op jit(solution)/shard_map/ppermute | solution.py:410
  173.7 0.8 copy-start.1
  182.6 10.6 %all-to-all-start.1 = ((f32[16,2,16,128]{3,2,1,0:T(8,128)}), f32[16,2,16,128]{3,2,1,0:T(8,128)S(1)}, u32[]{:S(2)}, u32[]{:S(2)}) async-start(f32[16,2,16,128]{3,2,1,0:T(8,128)} %bitcast.118), calls=%async_computation.1 | async-start | bytes 524288 | tf_op jit(solution)/shard_map/all_to_all | solution.py:535

commit v2 on v1

--- a/solution.py
+++ b/solution.py
@@ -16,7 +16,8 @@
 LANES = 128
 GROUP = 8
 HOP_ROWS = FRAME_LEN // 2 // LANES
-VMEM = 56 * 1024 * 1024
+SPECTRUM_VMEM = 24 * 1024 * 1024
+UPDATE_VMEM = 24 * 1024 * 1024
 NT = (((1,), (1,)), ((), ()))
 
 
@@ -109,15 +110,17 @@
     per_member,
     main_ref,
     next_ref,
+    trailing_ref,
     window_ref,
     first_ref,
     twiddle_ref,
     rows_ref,
     second_ref,
     mirrored_ref,
-    *rest,
+    out_ref,
+    parts_ref,
+    middle_ref,
 ):
-    out_ref, parts_ref, middle_ref = rest[-3:]
     half = SPLIT // 2
     middle_ref[...] = jnp.zeros_like(middle_ref)
 
@@ -140,7 +143,11 @@
             if g + 1 < GROUP:
                 bottom = main_ref[pl.ds((g + 1) * HOP_ROWS + side, half, stride=2), :]
             else:
-                bottom = next_ref[pl.ds(side, half, stride=2), :]
+                bottom = jnp.where(
+                    pl.program_id(0) == pl.num_programs(0) - 1,
+                    trailing_ref[pl.ds(side, half, stride=2), :],
+                    next_ref[pl.ds(side, half, stride=2), :],
+                )
             columns.append(jnp.concatenate([top, bottom], 0) * window_ref[side])
         high, low = split_values(jnp.concatenate(columns, 1))
         section = dot(first_ref[...], jnp.concatenate([high, high, low], 0))
@@ -194,37 +201,29 @@
     whole = [pl.BlockSpec(t.shape, lambda s, n=t.ndim: (0,) * n) for t in constants]
     kernel = functools.partial(spectrum_kernel, places, per_member)
 
-    def call(first_chunk, count, following, following_spec, earlier):
-        extra = [] if earlier is None else [earlier]
-        return pl.pallas_call(
-            kernel,
-            grid=(count,),
-            in_specs=[
-                pl.BlockSpec((GROUP * HOP_ROWS, LANES), lambda s: (s + first_chunk, 0)),
-                following_spec,
-                *whole,
-                *[pl.BlockSpec(memory_space=pl.ANY) for _ in extra],
-            ],
-            out_specs=pl.BlockSpec(
-                (members, 1, per_member * GROUP, LANES), lambda s: (0, s + first_chunk, 0, 0)
-            ),
-            out_shape=out_shape,
-            scratch_shapes=[
-                pltpu.VMEM((2, GROUP * LANES, 3 * SPLIT), jnp.bfloat16),
-                pltpu.VMEM((2, 16, SPLIT), jnp.float32),
-            ],
-            input_output_aliases={2 + len(constants): 0} if extra else {},
-            compiler_params=pltpu.CompilerParams(vmem_limit_bytes=VMEM),
-            cost_estimate=pl.CostEstimate(
-                flops=count * GROUP * 6 * SPLIT * SPLIT * SPLIT * 2,
-                bytes_accessed=count * GROUP * FRAME_LEN * 4,
-                transcendentals=0,
-            ),
-        )(samples, following, *constants, *extra)
-
-    ahead = pl.BlockSpec((HOP_ROWS, LANES), lambda s: (GROUP * (s + 1), 0))
-    result = call(0, chunks - 1, samples, ahead, None)
-    return call(chunks - 1, 1, trailing, pl.BlockSpec((HOP_ROWS, LANES), lambda s: (0, 0)), result)
+    last = chunks * GROUP - 1
+    return pl.pallas_call(
+        functools.partial(spectrum_kernel, places, per_member),
+        grid=(chunks,),
+        in_specs=[
+            pl.BlockSpec((GROUP * HOP_ROWS, LANES), lambda s: (s, 0)),
+            pl.BlockSpec((HOP_ROWS, LANES), lambda s: (jnp.minimum(GROUP * (s + 1), last), 0)),
+            pl.BlockSpec((HOP_ROWS, LANES), lambda s: (0, 0)),
+            *whole,
+        ],
+        out_specs=pl.BlockSpec((members, 1, per_member * GROUP, LANES), lambda s: (0, s, 0, 0)),
+        out_shape=out_shape,
+        scratch_shapes=[
+            pltpu.VMEM((2, GROUP * LANES, 3 * SPLIT), jnp.bfloat16),
+            pltpu.VMEM((2, 16, SPLIT), jnp.float32),
+        ],
+        compiler_params=pltpu.CompilerParams(vmem_limit_bytes=SPECTRUM_VMEM),
+        cost_estimate=pl.CostEstimate(
+            flops=chunks * GROUP * 6 * SPLIT * SPLIT * SPLIT * 2,
+            bytes_accessed=chunks * GROUP * FRAME_LEN * 4,
+            transcendentals=0,
+        ),
+    )(samples, samples, trailing, *constants)
 
 
 def lanes_of_activity(activity):
@@ -232,51 +231,67 @@
     return jnp.concatenate([high, high, low, low], 1)
 
 
-def ratio_of(spectrum_ref, activity_lanes, basis):
+def ratio_of(spectrum_ref, start, activity_lanes, basis):
     frames = activity_lanes.shape[0]
     splits = [split_values(block) for block in basis]
     stacked = jnp.concatenate([jnp.concatenate([h, l, h, l], 0) for h, l in splits], 1)
     approx = dot(activity_lanes, stacked)
-    count = len(basis)
     values = jnp.concatenate(
         [
-            spectrum_ref[:, :, row * GROUP : (row + 1) * GROUP, :].reshape(frames, LANES)
-            for row in range(count)
+            spectrum_ref[:, :, (start + row) * GROUP : (start + row + 1) * GROUP, :].reshape(frames, LANES)
+            for row in range(len(basis))
         ],
         1,
     )
     return values / approx, splits
 
 
-def add_to_activity(total_ref, ratio, splits):
+def for_activity(ratio, splits):
     high, low = split_values(ratio)
     basis = jnp.concatenate([jnp.concatenate([h, l], 0) for h, l in splits], 1)
-    total_ref[...] += dot_nt(jnp.concatenate([high, low], 1), jnp.concatenate([basis, basis], 1))
-
-
-def first_kernel(rows, spectrum_ref, basis_ref, activity_ref, out_ref, lanes_ref, total_ref, sums_ref):
-    step = pl.program_id(0)
+    return dot_nt(jnp.concatenate([high, low], 1), jnp.concatenate([basis, basis], 1))
+
+
+def row_steps(per_member):
+    rows = math.gcd(per_member, 8)
+    return [range(start, start + rows) for start in range(0, per_member, rows)]
+
+
+def packed(values):
+    half = values.shape[0] // 2
+    return jnp.concatenate([values[:half], values[half:]], 1)
+
+
+def unpacked(values):
+    half = values.shape[1] // 2
+    return jnp.concatenate([values[:, :half], values[:, half:]], 0)
+
+
+def first_kernel(side_ref, spectrum_ref, basis_ref, activity_ref, mine_ref, other_ref, lanes_ref, total_ref):
     rank = activity_ref.shape[1]
-
-    @pl.when(step == 0)
-    def _():
-        lanes_ref[...] = lanes_of_activity(activity_ref[...])
-        total_ref[...] = jnp.zeros_like(total_ref)
-        sums_ref[...] = jnp.zeros_like(sums_ref)
-
-    basis = [basis_ref[row] for row in range(rows)]
-    ratio, splits = ratio_of(spectrum_ref, lanes_ref[...], basis)
-    add_to_activity(total_ref, ratio, splits)
-    sums_ref[...] += sum(basis)
-
-    @pl.when(step == pl.num_programs(0) - 1)
-    def _():
-        total = total_ref[...]
-        total = total[:, :rank] + total[:, rank:]
-        half = total.shape[0] // 2
-        out_ref[:half, :] = jnp.concatenate([total[:half], total[half:]], 1)
-        sums = jnp.sum(jnp.transpose(sums_ref[...]), axis=0, keepdims=True)
-        out_ref[half:, :] = jnp.broadcast_to(jnp.concatenate([sums, sums], 1), (8, 2 * rank))
+    lanes_ref[...] = lanes_of_activity(activity_ref[...])
+    sums = jnp.zeros((rank, LANES), jnp.float32)
+    for step, rows in enumerate(row_steps(basis_ref.shape[0])):
+        basis = [basis_ref[row] for row in rows]
+        ratio, splits = ratio_of(spectrum_ref, rows[0], lanes_ref[...], basis)
+        part = for_activity(ratio, splits)
+        if step == 0:
+            total_ref[...] = part
+        else:
+            total_ref[...] += part
+        sums += sum(basis)
+    total = total_ref[...]
+    total = total[:, :rank] + total[:, rank:]
+    half = total.shape[0] // 2
+    quarter = half // 2
+    early, late = packed(total[:half]), packed(total[half:])
+    first = side_ref[0] == 0
+    mine_ref[:quarter, :] = jnp.where(first, early, late)
+    other_ref[:quarter, :] = jnp.where(first, late, early)
+    sums = jnp.sum(jnp.transpose(sums), axis=0, keepdims=True)
+    sums = jnp.broadcast_to(jnp.concatenate([sums, sums], 1), (8, 2 * rank))
+    mine_ref[quarter:, :] = sums
+    other_ref[quarter:, :] = sums
 
 
 def by_owner(values, shape):
@@ -293,112 +308,75 @@
 
 
 def second_kernel(
-    rows, spectrum_ref, basis_ref, activity_ref, sums_ref, middle_ref, owned_ref, out_ref, lanes_ref, turned_ref
+    side_ref, spectrum_ref, basis_ref, activity_ref, mine_ref, other_ref, middle_ref, out_ref, lanes_ref, turned_ref
 ):
-    step = pl.program_id(0)
     rank = activity_ref.shape[1]
-
-    @pl.when(step == 0)
-    def _():
-        half = activity_ref.shape[0] // 2
-        scale = sums_ref[:half, :] / sums_ref[half : half + 1, :]
-        middle = activity_ref[...] * jnp.concatenate([scale[:, :rank], scale[:, rank:]], 0)
-        middle_ref[...] = middle
-        lanes_ref[...] = lanes_of_activity(middle)
-        turned = jnp.transpose(middle)
-        high, low = split_values(turned)
-        turned_ref[...] = jnp.concatenate([high, low], 0)
-        totals = jnp.sum(turned, axis=1, keepdims=True)
-        out_ref[out_ref.shape[0] - 1] = jnp.broadcast_to(totals, (rank, LANES))
-        subs, members, ranks, width = owned_ref.shape
-        for member, block in enumerate(by_owner(middle, owned_ref.shape)):
-            owned_ref[:, member] = block
-
-    basis = [basis_ref[row] for row in range(rows)]
-    ratio, _ = ratio_of(spectrum_ref, lanes_ref[...], basis)
-    high, low = split_values(ratio)
-    turned = turned_ref[...]
-    total = dot(turned, high) + dot(turned, low)
-    total = total[:rank] + total[rank:]
-    for row in range(rows):
-        out_ref[step * rows + row] = total[:, row * LANES : (row + 1) * LANES]
-
-
-def third_kernel(
-    rows,
-    sources,
-    spectrum_ref,
-    basis_ref,
-    middle_ref,
-    *rest,
-):
-    numerators = rest[:sources]
-    totals = rest[sources : 2 * sources]
-    new_ref, out_ref, lanes_ref, total_ref, sums_ref = rest[2 * sources :]
-    step = pl.program_id(0)
+    quarter = activity_ref.shape[0] // 4
+    first = side_ref[0] == 0
+    mine = mine_ref[:quarter, :] / mine_ref[quarter : quarter + 1, :]
+    other = other_ref[:quarter, :] / other_ref[quarter : quarter + 1, :]
+    early, late = jnp.where(first, mine, other), jnp.where(first, other, mine)
+    middle = activity_ref[...] * jnp.concatenate([unpacked(early), unpacked(late)], 0)
+    middle_ref[...] = middle
+    lanes_ref[...] = lanes_of_activity(middle)
+    turned = jnp.transpose(middle)
+    high, low = split_values(turned)
+    turned_ref[...] = jnp.concatenate([high, low], 0)
+    totals = jnp.sum(turned, axis=1, keepdims=True)
+    out_ref[out_ref.shape[0] - 1] = jnp.broadcast_to(totals, (rank, LANES))
+    for rows in row_steps(basis_ref.shape[0]):
+        ratio, _ = ratio_of(spectrum_ref, rows[0], lanes_ref[...], [basis_ref[row] for row in rows])
+        high, low = split_values(ratio)
+        total = dot(turned_ref[...], high) + dot(turned_ref[...], low)
+        total = total[:rank] + total[rank:]
+        for place, row in enumerate(rows):
+            out_ref[row] = total[:, place * LANES : (place + 1) * LANES]
+
+
+def third_kernel(spectrum_ref, basis_ref, middle_ref, *rest):
+    new_ref, out_ref, lanes_ref, total_ref = rest[-4:]
+    numerators = rest[:-4]
     rank = middle_ref.shape[1]
-
-    @pl.when(step == 0)
-    def _():
-        lanes_ref[...] = lanes_of_activity(middle_ref[...])
-        total_ref[...] = jnp.zeros_like(total_ref)
-        sums_ref[...] = jnp.zeros_like(sums_ref)
-
-    total = sum(ref[0] for ref in totals)
-    basis = []
-    for row in range(rows):
-        block = basis_ref[row] * (sum(ref[row] for ref in numerators) / total)
-        new_ref[row] = block
-        basis.append(block)
-    ratio, splits = ratio_of(spectrum_ref, lanes_ref[...], basis)
-    add_to_activity(total_ref, ratio, splits)
-    sums_ref[...] += sum(basis)
-
-    @pl.when(step == pl.num_programs(0) - 1)
-    def _():
-        total = total_ref[...]
-        total = total[:, :rank] + total[:, rank:]
-        subs, members, _, ranks, width = out_ref.shape
-        shape = (subs, members, ranks, width)
-        sums = jnp.sum(sums_ref[...], axis=1, keepdims=True)
-        sums = jnp.broadcast_to(sums, (rank, width)).reshape(subs, ranks, width)
-        for member, block in enumerate(by_owner(total, shape)):
-            out_ref[:, member, 0] = block
-            out_ref[:, member, 1] = sums
-
-
-def step_rows(per_member):
-    return 2 if per_member % 2 == 0 else 1
-
-
-def spectrum_spec(spectrum, rows):
-    members, chunks = spectrum.shape[:2]
-    return pl.BlockSpec((members, chunks, rows * GROUP, LANES), lambda s: (0, 0, s, 0))
-
-
-def full(shape):
-    return pl.BlockSpec(shape, lambda s: (0,) * len(shape))
-
-
-def out_rank(operands):
-    return operands[1].shape[1]
-
-
-def update_call(kernel, spectrum, per_member, in_specs, out_specs, out_shape, scratch, operands):
-    rows = step_rows(per_member)
-    rank = out_rank(operands)
+    per_member = basis_ref.shape[0]
+    lanes_ref[...] = lanes_of_activity(middle_ref[...])
+    scale = 1.0 / sum(ref[per_member] for ref in numerators)
+    sums = jnp.zeros((rank, LANES), jnp.float32)
+    for step, rows in enumerate(row_steps(per_member)):
+        basis = [basis_ref[row] * (sum(ref[row] for ref in numerators) * scale) for row in rows]
+        for row, block in zip(rows, basis):
+            new_ref[row] = block
+        ratio, splits = ratio_of(spectrum_ref, rows[0], lanes_ref[...], basis)
+        part = for_activity(ratio, splits)
+        if step == 0:
+            total_ref[...] = part
+        else:
+            total_ref[...] += part
+        sums += sum(basis)
+    total = total_ref[...]
+    total = total[:, :rank] + total[:, rank:]
+    subs, members, _, ranks, width = out_ref.shape
+    sums = jnp.sum(sums, axis=1, keepdims=True)
+    sums = jnp.broadcast_to(sums, (rank, width)).reshape(subs, ranks, width)
+    for member, block in enumerate(by_owner(total, (subs, members, ranks, width))):
+        out_ref[:, member, 0] = block
+        out_ref[:, member, 1] = sums
+
+
+def update_call(kernel, spectrum, out_shapes, scratch, operands, scalars=()):
+    in_vmem = pl.BlockSpec(memory_space=pltpu.VMEM)
+    rank = operands[0].shape[1]
     return pl.pallas_call(
         kernel,
-        grid=(per_member // rows,),
-        in_specs=in_specs,
-        out_specs=out_specs,
-        out_shape=out_shape,
+        in_specs=[pl.BlockSpec(memory_space=pltpu.SMEM) for _ in scalars]
+        + [in_vmem for _ in range(1 + len(operands))],
+        out_specs=[in_vmem for _ in out_shapes],
+        out_shape=[jax.ShapeDtypeStruct(shape, jnp.float32) for shape in out_shapes],
         scratch_shapes=scratch,
-        compiler_params=pltpu.CompilerParams(vmem_limit_bytes=VMEM),
+        compiler_params=pltpu.CompilerParams(vmem_limit_bytes=UPDATE_VMEM),
         cost_estimate=pl.CostEstimate(
             flops=spectrum.size * rank * 16, bytes_accessed=spectrum.size * 4, transcendentals=0
         ),
-    )(*operands)
+    )(*scalars, spectrum, *operands)
 
 
 def turned_lanes(values):
@@ -410,16 +388,10 @@
     return lax.ppermute(value, axis, [(i, i ^ mask) for i in range(count)])
 
 
-def sum_over(value, axes):
-    for axis in axes:
-        count = lax.axis_size(axis)
-        if count & (count - 1):
-            value = lax.psum(value, axis)
-            continue
-        mask = 1
-        while mask < count:
-            value = value + swap_by(value, axis, mask)
-            mask *= 2
+def sum_over(value, axis, mask):
+    while mask < lax.axis_size(axis):
+        value = value + swap_by(value, axis, mask)
+        mask *= 2
     return value
 
 
@@ -432,7 +404,6 @@
     exchange = ("freq", "member")
     partners = subs * members
     per_member = units_here * groups
-    rows = step_rows(per_member)
     me_sub, me_group, me_member = (lax.axis_index(axis) for axis in ("freq", "group", "member"))
 
     kept = units_of_member(units_here, range(groups))
@@ -451,7 +422,9 @@
         if block + (sub + 1) // subs < blocks
     ]
     trailing = lax.ppermute(samples[:HOP_ROWS], ("freq", "group", "member"), route)
-    gathered = lax.all_gather(activations, exchange)
+    gathered = lax.all_to_all(
+        jnp.broadcast_to(activations[None], (partners, ranks_here, width)), exchange, 0, 0, tiled=True
+    )
     other = [swap_by(templates, "group", 1)] if groups == 2 else []
 
     spectrum = spectrum_blocks(samples, trailing, unit_order, partners)
@@ -478,67 +451,46 @@
     by_group = jnp.where(is_turned, turned_lanes(by_group), by_group)
     basis = jnp.concatenate([by_group[group, r][None] for group, r in kept], 0)
 
-    specs = spectrum_spec(spectrum, rows)
-    basis_spec = pl.BlockSpec((rows, rank, LANES), lambda s: (s, 0, 0))
     lanes_scratch = pltpu.VMEM((frames, 4 * rank), jnp.bfloat16)
     total_scratch = pltpu.VMEM((frames, 2 * rank), jnp.float32)
-    sums_scratch = pltpu.VMEM((rank, LANES), jnp.float32)
-    sums_shape = (frames // 2 + 8, 2 * rank)
-    sums = update_call(
-        functools.partial(first_kernel, rows),
+    half_shape = (frames // 4 + 8, 2 * rank)
+    side = (me_sub % 2).astype(jnp.int32).reshape(1)
+    mine, other = update_call(
+        first_kernel, spectrum, [half_shape] * 2, [lanes_scratch, total_scratch], (basis, activity), (side,)
+    )
+    mine = mine + swap_by(other, "freq", 1)
+    mine = sum_over(mine, "freq", 2)
+    mine = sum_over(mine, "member", 1)
+    other = swap_by(mine, "freq", 1)
+
+    middle, numerator = update_call(
+        second_kernel,
         spectrum,
-        per_member,
-        [specs, basis_spec, full((frames, rank))],
-        full(sums_shape),
-        jax.ShapeDtypeStruct(sums_shape, jnp.float32),
-        [lanes_scratch, total_scratch, sums_scratch],
-        (spectrum, basis, activity),
-    )
-    sums = sum_over(sums, exchange)
-
-    owned_shape = (subs, members, ranks_here, width)
-    numerator_shape = (per_member + 1, rank, LANES)
-    middle, owned, numerator = update_call(
-        functools.partial(second_kernel, rows),
-        spectrum,
-        per_member,
-        [specs, basis_spec, full((frames, rank)), full(sums_shape)],
-        [full((frames, rank)), full(owned_shape), full(numerator_shape)],
-        [
-            jax.ShapeDtypeStruct((frames, rank), jnp.float32),
-            jax.ShapeDtypeStruct(owned_shape, jnp.float32),
-            jax.ShapeDtypeStruct(numerator_shape, jnp.float32),
-        ],
+        [(frames, rank), (per_member + 1, rank, LANES)],
         [lanes_scratch, pltpu.VMEM((2 * rank, frames), jnp.bfloat16)],
-        (spectrum, basis, activity, sums),
+        (basis, activity, mine, other),
+        (side,),
     )
     numerators = [numerator]
     if groups == 2:
         numerators.append(swap_by(numerator, "group", 1))
-    payload_shape = (subs, members, 2, ranks_here, width)
-    total_spec = pl.BlockSpec((1, rank, LANES), lambda s: (per_member, 0, 0))
     new_basis, payload = update_call(
-        functools.partial(third_kernel, rows, len(numerators)),
+        third_kernel,
         spectrum,
-        per_member,
-        [specs, basis_spec, full((frames, rank))]
-        + [basis_spec] * len(numerators)
-        + [total_spec] * len(numerators),
-        [basis_spec, full(payload_shape)],
-        [
-            jax.ShapeDtypeStruct((per_member, rank, LANES), jnp.float32),
-            jax.ShapeDtypeStruct(payload_shape, jnp.float32),
-        ],
-        [lanes_scratch, total_scratch, sums_scratch],
-        (spectrum, basis, middle, *numerators, *numerators),
+        [(per_member, rank, LANES), (subs, members, 2, ranks_here, width)],
+        [lanes_scratch, total_scratch],
+        (basis, middle, *numerators),
     )
     received = lax.all_to_all(
         payload.reshape(partners, 2, ranks_here, width), exchange, 0, 0, tiled=True
     )
     summed = jnp.sum(received, axis=0)
     mine = lax.dynamic_slice(
-        owned, (me_sub, me_member, 0, 0), (1, 1, ranks_here, width)
-    ).reshape(ranks_here, width)
+        middle.reshape(subs, members, local, rank),
+        (0, me_member, 0, me_sub * ranks_here),
+        (subs, 1, local, ranks_here),
+    )
+    mine = mine.reshape(width, ranks_here).T
     final_activations = mine * (summed[0] / summed[1])
 
     back = jnp.stack(

time: 196 us -> 165 us (0.84)
  blocking collectives: 27 us -> 0 us
  Pallas kernels: 40.2 us -> 24.9 us
  waiting for transfers between devices: 92.7 us -> 98.3 us
  local copies, waits for them, and re-layouts: 9.27 us -> 14.3 us
  starting transfers between devices: 20.3 us -> 24.2 us
  other arithmetic: 4.26 us -> 1.97 us
    all_gather x1 -> x0, blocking collectives: 27 us -> none  [on_device(): gathered = lax.all_gather(activations, exchange)]
    pallas_call x5 -> x4, Pallas kernels: 40.2 us -> 24.9 us  [the longest x3 14.4 us: update_call(): pl.pallas_call(kernel, in_specs=[pl.BlockSpec(memory_space=pltpu.SMEM) fo...]
    all_to_all x0 -> x1, starting transfers between devices: none -> 7.02 us  [on_device(): lax.all_to_all(jnp.broadcast_to(activations[None], (partners, ranks_here,...]
    unnamed x29 -> x37, local copies, waits for them, and re-layouts: 4.99 us -> 10 us
    all_to_all x1, waiting for transfers between devices: 1.69 us -> 5.81 us  [on_device(): lax.all_to_all(payload.reshape(partners, 2, ranks_here, width), exchange,...]
    ppermute x6 -> x7, starting transfers between devices: 10.8 us -> 7.2 us  [swap_by(): return lax.ppermute(value, axis, [(i, i ^ mask) for i in range(count)])]
    ppermute x6 -> x7, waiting for transfers between devices: 39.7 us -> 40.4 us  [swap_by(): return lax.ppermute(value, axis, [(i, i ^ mask) for i in range(count)])]
  transfers between devices with their start and end apart: 9 -> 11, of which waited for: 7 -> 8; matrix products, arithmetic and copies ran while one was open for 4% -> 3% of each run, Pallas kernels for 8% -> 6%
where the time goes in v2:
time: 165 us
  waiting for transfers between devices  98.3 us (60%)
  Pallas kernels  24.9 us (15%)
  starting transfers between devices  24.2 us (15%)
  local copies, waits for them, and re-layouts  14.3 us (9%)
  other arithmetic  1.97 us (1%)
    all_to_all x1, waiting for transfers between devices, on_device(): spectrum = lax.all_to_all(spectrum, exchange, 0, 0, tiled=True)  52.1 us
    ppermute x7, waiting for transfers between devices, swap_by(): return lax.ppermute(value, axis, [(i, i ^ mask) for i in range(count)])  40.4 us
    pallas_call x3, Pallas kernels, update_call(): pl.pallas_call(kernel, in_specs=[pl.BlockSpec(memory_space=pltpu.SMEM) fo...  14.4 us
    pallas_call x1, Pallas kernels, spectrum_blocks(): pl.pallas_call(functools.partial(spectrum_kernel, places, per_member), gr...  10.5 us
    unnamed x37, local copies, waits for them, and re-layouts  10 us
    ppermute x7, starting transfers between devices, swap_by(): return lax.ppermute(value, axis, [(i, i ^ mask) for i in range(count)])  7.2 us
    all_to_all x1, starting transfers between devices, on_device(): lax.all_to_all(jnp.broadcast_to(activations[None], (partners, ranks_here,...  7.02 us
    all_to_all x1, waiting for transfers between devices, on_device(): lax.all_to_all(payload.reshape(partners, 2, ranks_here, width), exchange,...  5.81 us
  transfers between devices with their start and end apart: 11, of which 8 were waited for; matrix products, arithmetic and copies ran while one was open for 3% of the time, Pallas kernels for 6%

profile of v2, /device:TPU:0, one launch (start us, length us, event | category | flops | bytes accessed | tf_op | source)
XLA Modules:
  0.0 164.7 jit_solution(4561666039809800025)
XLA Ops:
  0.6 0.9 slice.126
  1.5 1.3 collective-permute-start
  2.8 1.4 broadcast_in_dim.27
  4.2 7.0 %all-to-all-start = ((f32[16,16,128]{2,1,0:T(8,128)}), f32[16,16,128]{2,1,0:T(8,128)S(1)}, u32[]{:S(2)}, u32[]{:S(2)}) async-start(f32[16,16,128]{2,1,0:T(8,128)} %broadcast_in_dim.27), calls=%async_computation | async-start | bytes 262144 | tf_op jit(solution)/shard_map/all_to_all | solution.py:425
  11.2 3.0 %collective-permute-start.1 = (f32[64,1024]{1,0:T(8,128)}, f32[64,1024]{1,0:T(8,128)S(1)}, u32[]{:S(2)}, u32[]{:S(2)}) collective-permute-start(f32[64,1024]{1,0:T(8,128)} %param.10), channel_id=1, source_target_pairs={{0,4},{4,0},{1,5},{5,1},{2,6},{6,2},{3,7},{7,3},{8,12},{12,8},{9,1... | collective-permute-start | bytes 786440 | tf_op jit(solution)/shard_map/ppermute | solution.py:388
  14.2 0.0 collective-permute-done.trailing_ref
  14.2 0.0 copy-start.1
  14.2 2.2 %copy-done.1 = f32[1,1,1048576]{2,1,0:T(1,128)S(1)} copy-done((f32[1,1,1048576]{2,1,0:T(1,128)S(1)}, f32[1,1,1048576]{2,1,0:T(1,128)}, u32[]{:S(2)}) %copy-start.1) | copy-done | bytes 4194328
  16.4 0.0 copy-start.2
  16.4 1.1 copy-done.2
  17.5 0.0 copy-start.3
  17.6 1.0 copy-done.3
  18.5 0.0 copy-start.4
  18.5 1.0 copy-done.4
  19.5 0.0 copy-start.5
  19.5 0.9 copy-done.5
  20.5 0.0 copy-start.6
  20.5 0.9 copy-done.6
  21.4 0.0 copy-start.7
  21.4 0.7 copy-done.7
  22.1 10.5 %shard_map.104 = f32[16,4,128,128]{3,2,1,0:T(8,128)S(1)} custom-call(f32[8192,128]{1,0:T(8,128)S(1)} %bitcast.112, f32[8192,128]{1,0:T(8,128)S(1)} %bitcast.113, f32[256,128]{1,0:T(8,128)S(1)} %collective-permute-done.trailing_ref, f32[2,256,128]{2,1,0:T(8,128)S(1)} %copy-done.5, bf16[256,768]{1,0:T(8,128)(2,1)S(1)} %copy-done.3, ...), custom_call_target="tpu_custom_call" | custom-call | flops 6442450944 | bytes 8388608 | tf_op jit(solution)/shard_map/pallas_call | solution.py:205
  32.6 0.0 copy-start
  32.6 2.0 %copy-done = f32[16,4,128,128]{3,2,1,0:T(8,128)} copy-done((f32[16,4,128,128]{3,2,1,0:T(8,128)}, f32[16,4,128,128]{3,2,1,0:T(8,128)S(1)}, u32[]{:S(2)}) %copy-start) | copy-done | bytes 4194328
  34.6 0.0 copy-start.8
  34.6 0.0 all-to-all-done
  34.6 0.0 collective-permute-done.1
  34.6 5.2 %all-to-all-start.1 = ((f32[16,4,128,128]{3,2,1,0:T(8,128)}), f32[16,4,128,128]{3,2,1,0:T(8,128)}, u32[]{:S(2)}, u32[]{:S(2)}) async-start(f32[16,4,128,128]{3,2,1,0:T(8,128)} %copy-done), calls=%async_computation.1 | async-start | bytes 8388608 | tf_op jit(solution)/shard_map/all_to_all | solution.py:434
  39.9 0.1 fusion.6
  39.9 0.0 copy-done.8
  40.1 0.2 slice.163
  40.3 0.2 slice.130
  40.5 0.3 reshape.87
  40.7 0.3 copy.23
  41.1 0.4 reshape.88
  41.5 0.1 copy.25.activity_ref
  41.6 0.2 maximum_select_fusion.1
  42.1 52.1 %all-to-all-done.1.spectrum_ref = f32[16,4,128,128]{3,2,1,0:T(8,128)} async-done(((f32[16,4,128,128]{3,2,1,0:T(8,128)}), f32[16,4,128,128]{3,2,1,0:T(8,128)}, u32[]{:S(2)}, u32[]{:S(2)}) %all-to-all-start.1) | async-done | bytes 4194336 | tf_op jit(solution)/shard_map/all_to_all | solution.py:434
  94.2 5.0 %shard_map.105 = (f32[136,128]{1,0:T(8,128)S(1)}, f32[136,128]{1,0:T(8,128)S(1)}) custom-call(s32[1]{0:T(128)} %bitcast.side_ref, f32[16,4,128,128]{3,2,1,0:T(8,128)} %all-to-all-done.1.spectrum_ref, f32[16,64,128]{2,1,0:T(8,128)S(1)} %constant_dynamic-update-slice_fusion.basis_ref, f32[512,64]{1,0:T(8,128)S(1)} %copy.25.activity_ref), custom_call_target="tpu_custom_call" | custom-call | flops 1073741824 | bytes 4194304 | tf_op jit(solution)/shard_map/pallas_call | solution.py:368
  99.1 2.3 %collective-permute-start.2 = (f32[136,128]{1,0:T(8,128)S(1)}, f32[136,128]{1,0:T(8,128)S(1)}, u32[]{:S(2)}, u32[]{:S(2)}) collective-permute-start(f32[136,128]{1,0:T(8,128)S(1)} %get-tuple-element.17), channel_id=1, source_target_pairs={{0,8},{8,0},{16,24},{24,16},{1,9},{9,1},{17,25},{25,17},{2,10},{10... | collective-permute-start | bytes 208904 | tf_op jit(solution)/shard_map/ppermute | solution.py:388
  101.4 0.9 collective-permute-done.2
  102.3 1.1 collective-permute-start.3
  103.4 3.4 %collective-permute-done.3 = f32[136,128]{1,0:T(8,128)S(1)} collective-permute-done((f32[136,128]{1,0:T(8,128)S(1)}, f32[136,128]{1,0:T(8,128)S(1)}, u32[]{:S(2)}, u32[]{:S(2)}) %collective-permute-start.3) | collective-permute-done | bytes 69664 | tf_op jit(solution)/shard_map/ppermute | solution.py:388
  106.8 0.6 collective-permute-start.4
  107.5 3.7 %collective-permute-done.4 = f32[136,128]{1,0:T(8,128)S(1)} collective-permute-done((f32[136,128]{1,0:T(8,128)S(1)}, f32[136,128]{1,0:T(8,128)S(1)}, u32[]{:S(2)}, u32[]{:S(2)}) %collective-permute-start.4) | collective-permute-done | bytes 69664 | tf_op jit(solution)/shard_map/ppermute | solution.py:388
  111.2 0.1 collective-permute-start.5
  111.3 4.3 %collective-permute-done.5 = f32[136,128]{1,0:T(8,128)S(1)} collective-permute-done((f32[136,128]{1,0:T(8,128)S(1)}, f32[136,128]{1,0:T(8,128)S(1)}, u32[]{:S(2)}, u32[]{:S(2)}) %collective-permute-start.5) | collective-permute-done | bytes 69664 | tf_op jit(solution)/shard_map/ppermute | solution.py:388
  115.6 0.1 collective-permute-start.6
  115.7 1.2 collective-permute-done.6.other_ref
  116.9 3.9 %shard_map.106 = (f32[512,64]{1,0:T(8,128)S(1)}, f32[17,64,128]{2,1,0:T(8,128)S(1)}) custom-call(s32[1]{0:T(128)} %bitcast.side_ref, f32[16,4,128,128]{3,2,1,0:T(8,128)} %all-to-all-done.1.spectrum_ref, f32[16,64,128]{2,1,0:T(8,128)S(1)} %constant_dynamic-update-slice_fusion.basis_ref, f32[512,64]{1,0:T(8,128)S(1)} %copy.25.activity_ref, ...), custom_call_target="tpu_custom_call" | custom-call | flops 1073741824 | bytes 4194304 | tf_op jit(solution)/shard_map/pallas_call | solution.py:368
  120.8 0.1 collective-permute-start.7
  121.0 0.1 constant_dynamic-slice_fusion
  121.1 0.1 copy.28
  121.1 26.8 %collective-permute-done.7.rest_1_ = f32[17,64,128]{2,1,0:T(8,128)S(1)} collective-permute-done((f32[17,64,128]{2,1,0:T(8,128)S(1)}, f32[17,64,128]{2,1,0:T(8,128)S(1)}, u32[]{:S(2)}, u32[]{:S(2)}) %collective-permute-start.7) | collective-permute-done | bytes 557088 | tf_op jit(solution)/shard_map/ppermute | solution.py:388
  147.9 5.5 %shard_map.107 = (f32[16,64,128]{2,1,0:T(8,128)S(1)}, f32[4,4,2,16,128]{4,3,2,1,0:T(8,128)}) custom-call(f32[16,4,128,128]{3,2,1,0:T(8,128)} %all-to-all-done.1.spectrum_ref, f32[16,64,128]{2,1,0:T(8,128)S(1)} %constant_dynamic-update-slice_fusion.basis_ref, f32[512,64]{1,0:T(8,128)S(1)} %get-tuple-element.18.middle_ref, ...), custom_call_target="tpu_custom_call" | custom-call | flops 1073741824 | bytes 4194304 | tf_op jit(solution)/shard_map/pallas_call | solution.py:368
  153.4 3.5 %all-to-all-start.2 = ((f32[16,2,16,128]{3,2,1,0:T(8,128)}), f32[16,2,16,128]{3,2,1,0:T(8,128)S(1)}, u32[]{:S(2)}, u32[]{:S(2)}) async-start(f32[16,2,16,128]{3,2,1,0:T(8,128)} %bitcast.29), calls=%async_computation.2 | async-start | bytes 524288 | tf_op jit(solution)/shard_map/all_to_all | solution.py:484
  157.0 0.1 fusion.1
  157.1 0.1 slice.183
  157.2 0.1 slice.161
  157.4 0.9 copy_bitcast_fusion
  158.2 5.8 %all-to-all-done.2 = f32[16,2,16,128]{3,2,1,0:T(8,128)S(1)} async-done(((f32[16,2,16,128]{3,2,1,0:T(8,128)}), f32[16,2,16,128]{3,2,1,0:T(8,128)S(1)}, u32[]{:S(2)}, u32[]{:S(2)}) %all-to-all-start.2) | async-done | bytes 262176 | tf_op jit(solution)/shard_map/all_to_all | solution.py:484
  164.1 0.6 fusion.4
  (30 shorter events, 0.3 us)
Async XLA Ops:
  1.5 12.7 %collective-permute-start = (f32[256,128]{1,0:T(8,128)S(1)}, f32[256,128]{1,0:T(8,128)S(1)}, u32[]{:S(2)}, u32[]{:S(2)}) collective-permute-start(f32[256,128]{1,0:T(8,128)S(1)} %bitcast.120), channel_id=1, source_target_pairs={{8,0},{9,1},{10,2},{11,3},{12,4},{13,5},{14,6},{15,7},{16,8},{17,9... | collective-permute-start | bytes 393224 | tf_op jit(solution)/shard_map/ppermute | solution.py:424
  4.2 30.4 %all-to-all-start = ((f32[16,16,128]{2,1,0:T(8,128)}), f32[16,16,128]{2,1,0:T(8,128)S(1)}, u32[]{:S(2)}, u32[]{:S(2)}) async-start(f32[16,16,128]{2,1,0:T(8,128)} %broadcast_in_dim.27), calls=%async_computation | async-start | bytes 262144 | tf_op jit(solution)/shard_map/all_to_all | solution.py:425
  11.2 23.4 %collective-permute-start.1 = (f32[64,1024]{1,0:T(8,128)}, f32[64,1024]{1,0:T(8,128)S(1)}, u32[]{:S(2)}, u32[]{:S(2)}) collective-permute-start(f32[64,1024]{1,0:T(8,128)} %param.10), channel_id=1, source_target_pairs={{0,4},{4,0},{1,5},{5,1},{2,6},{6,2},{3,7},{7,3},{8,12},{12,8},{9,1... | collective-permute-start | bytes 786440 | tf_op jit(solution)/shard_map/ppermute | solution.py:388
  14.2 2.2 %copy-start.1 = (f32[1,1,1048576]{2,1,0:T(1,128)S(1)}, f32[1,1,1048576]{2,1,0:T(1,128)}, u32[]{:S(2)}) copy-start(f32[1,1,1048576]{2,1,0:T(1,128)} %param.9) | copy-start | bytes 12582916
  16.4 1.1 copy-start.2
  17.5 1.0 copy-start.3
  18.5 1.0 copy-start.4
  19.5 0.9 copy-start.5
  20.5 0.9 copy-start.6
  21.4 0.7 copy-start.7
  32.6 2.0 %copy-start = (f32[16,4,128,128]{3,2,1,0:T(8,128)}, f32[16,4,128,128]{3,2,1,0:T(8,128)S(1)}, u32[]{:S(2)}) copy-start(f32[16,4,128,128]{3,2,1,0:T(8,128)S(1)} %shard_map.104) | copy-start | bytes 12582916
  34.6 5.3 %copy-start.8 = (f32[64,1024]{1,0:T(8,128)S(1)}, f32[64,1024]{1,0:T(8,128)}, u32[]{:S(2)}) copy-start(f32[64,1024]{1,0:T(8,128)} %param.10) | copy-start | bytes 786436
  34.6 59.5 %all-to-all-start.1 = ((f32[16,4,128,128]{3,2,1,0:T(8,128)}), f32[16,4,128,128]{3,2,1,0:T(8,128)}, u32[]{:S(2)}, u32[]{:S(2)}) async-start(f32[16,4,128,128]{3,2,1,0:T(8,128)} %copy-done), calls=%async_computation.1 | async-start | bytes 8388608 | tf_op jit(solution)/shard_map/all_to_all | solution.py:434
  99.1 3.2 %collective-permute-start.2 = (f32[136,128]{1,0:T(8,128)S(1)}, f32[136,128]{1,0:T(8,128)S(1)}, u32[]{:S(2)}, u32[]{:S(2)}) collective-permute-start(f32[136,128]{1,0:T(8,128)S(1)} %get-tuple-element.17), channel_id=1, source_target_pairs={{0,8},{8,0},{16,24},{24,16},{1,9},{9,1},{17,25},{25,17},{2,10},{10... | collective-permute-start | bytes 208904 | tf_op jit(solution)/shard_map/ppermute | solution.py:388
  102.3 4.5 %collective-permute-start.3 = (f32[136,128]{1,0:T(8,128)S(1)}, f32[136,128]{1,0:T(8,128)S(1)}, u32[]{:S(2)}, u32[]{:S(2)}) collective-permute-start(f32[136,128]{1,0:T(8,128)S(1)} %add.86), channel_id=1, source_target_pairs={{0,16},{8,24},{16,0},{24,8},{1,17},{9,25},{17,1},{25,9},{2,18},{10... | collective-permute-start | bytes 208904 | tf_op jit(solution)/shard_map/ppermute | solution.py:388
  106.8 4.4 %collective-permute-start.4 = (f32[136,128]{1,0:T(8,128)S(1)}, f32[136,128]{1,0:T(8,128)S(1)}, u32[]{:S(2)}, u32[]{:S(2)}) collective-permute-start(f32[136,128]{1,0:T(8,128)S(1)} %add.87), channel_id=1, source_target_pairs={{0,1},{1,0},{2,3},{3,2},{4,5},{5,4},{6,7},{7,6},{8,9},{9,8},{10,11... | collective-permute-start | bytes 208904 | tf_op jit(solution)/shard_map/ppermute | solution.py:388
  111.2 4.4 %collective-permute-start.5 = (f32[136,128]{1,0:T(8,128)S(1)}, f32[136,128]{1,0:T(8,128)S(1)}, u32[]{:S(2)}, u32[]{:S(2)}) collective-permute-start(f32[136,128]{1,0:T(8,128)S(1)} %add.88), channel_id=1, source_target_pairs={{0,2},{1,3},{2,0},{3,1},{4,6},{5,7},{6,4},{7,5},{8,10},{9,11},{10,... | collective-permute-start | bytes 208904 | tf_op jit(solution)/shard_map/ppermute | solution.py:388
  115.6 1.3 collective-permute-start.6
  120.8 27.0 %collective-permute-start.7 = (f32[17,64,128]{2,1,0:T(8,128)S(1)}, f32[17,64,128]{2,1,0:T(8,128)S(1)}, u32[]{:S(2)}, u32[]{:S(2)}) collective-permute-start(f32[17,64,128]{2,1,0:T(8,128)S(1)} %get-tuple-element.19.rest_0_), channel_id=1, source_target_pairs={{0,4},{4,0},{1,5},{5,1},{2,6},{6,2},{3,7},{7,3},{8,12},{12,8},{9,1... | collective-permute-start | bytes 1671176 | tf_op jit(solution)/shard_map/ppermute | solution.py:388
  153.4 10.6 %all-to-all-start.2 = ((f32[16,2,16,128]{3,2,1,0:T(8,128)}), f32[16,2,16,128]{3,2,1,0:T(8,128)S(1)}, u32[]{:S(2)}, u32[]{:S(2)}) async-start(f32[16,2,16,128]{3,2,1,0:T(8,128)} %bitcast.29), calls=%async_computation.2 | async-start | bytes 524288 | tf_op jit(solution)/shard_map/all_to_all | solution.py:484

commit v3 on v2

--- a/solution.py
+++ b/solution.py
@@ -105,22 +105,8 @@
     return lax.dot_general(left, right, NT, preferred_element_type=jnp.float32)
 
 
-def spectrum_kernel(
-    places,
-    per_member,
-    main_ref,
-    next_ref,
-    trailing_ref,
-    window_ref,
-    first_ref,
-    twiddle_ref,
-    rows_ref,
-    second_ref,
-    mirrored_ref,
-    out_ref,
-    parts_ref,
-    middle_ref,
-):
+def transform_group(hop_rows, base, stride, places, per_member, table_refs, out_ref, parts_ref, middle_ref, ready):
+    window_ref, first_ref, twiddle_ref, rows_ref, second_ref, mirrored_ref = table_refs
     half = SPLIT // 2
     middle_ref[...] = jnp.zeros_like(middle_ref)
 
@@ -137,18 +123,10 @@
         return jnp.concatenate([high, high, low], 1)
 
     for g in range(GROUP):
-        columns = []
-        for side in range(2):
-            top = main_ref[pl.ds(g * HOP_ROWS + side, half, stride=2), :]
-            if g + 1 < GROUP:
-                bottom = main_ref[pl.ds((g + 1) * HOP_ROWS + side, half, stride=2), :]
-            else:
-                bottom = jnp.where(
-                    pl.program_id(0) == pl.num_programs(0) - 1,
-                    trailing_ref[pl.ds(side, half, stride=2), :],
-                    next_ref[pl.ds(side, half, stride=2), :],
-                )
-            columns.append(jnp.concatenate([top, bottom], 0) * window_ref[side])
+        columns = [
+            jnp.concatenate([hop_rows(g, side), hop_rows(g + 1, side)], 0) * window_ref[side]
+            for side in range(2)
+        ]
         high, low = split_values(jnp.concatenate(columns, 1))
         section = dot(first_ref[...], jnp.concatenate([high, high, low], 0))
         a, b = section[:half], section[half:]
@@ -159,6 +137,8 @@
         nyquist = section[half : half + 1]
         for parity, values in enumerate(even_odd(nyquist * rows_ref[0:1], nyquist * rows_ref[1:2])):
             middle_ref[parity, g : g + 1, :] = values
+
+    ready()
 
     def magnitude(values):
         real, imag = values[:half], values[half:]
@@ -188,42 +168,141 @@
                     ):
                         stop += 1
                     member, row = divmod(place, per_member)
-                    out_ref[member, 0, pl.ds(row * GROUP + g, stop - start, stride=GROUP), :] = block[start:stop]
+                    out_ref[member, pl.ds(row * stride + base + g, stop - start, stride=stride), :] = block[
+                        start:stop
+                    ]
                     start = stop
 
 
-def spectrum_blocks(samples, trailing, unit_order, members):
-    window, first, twiddle, rows, second, mirrored, places = tables(unit_order)
+def early_kernel(
+    places, per_member, frames, samples_ref, *rest
+):
+    table_refs, (out_ref, tail_ref) = rest[:6], rest[6:8]
+    copies_ref, (hops_ref, parts_ref, middle_ref, sem_ref) = rest[8:14], rest[14:]
+    groups = frames // GROUP - 1
+    group_rows = GROUP * HOP_ROWS
+    half = SPLIT // 2
+
+    def fetch(first, count, slot):
+        return pltpu.make_async_copy(
+            samples_ref.at[pl.ds(first, count), :], hops_ref.at[pl.ds(first, count), :], sem_ref.at[slot]
+        )
+
+    tables_in = [
+        pltpu.make_async_copy(table_refs[i], copies_ref[i], sem_ref.at[i]) for i in range(len(table_refs))
+    ]
+    lead = fetch(0, HOP_ROWS, 6)
+    tail = pltpu.make_async_copy(
+        samples_ref.at[pl.ds(groups * group_rows, group_rows), :], tail_ref, sem_ref.at[7]
+    )
+    hops = [fetch(HOP_ROWS + i * group_rows, group_rows, 8 + i) for i in range(groups)]
+    for copy in [tables_in[1], lead, hops[0], *tables_in[:1], *tables_in[2:], *hops[1:], tail]:
+        copy.start()
+    lead.wait()
+    for copy in tables_in[:4]:
+        copy.wait()
+
+    def body(i, carry):
+        first = pl.multiple_of(i * group_rows, group_rows)
+        pltpu.make_async_copy(
+            samples_ref.at[pl.ds(HOP_ROWS + first, group_rows), :],
+            hops_ref.at[pl.ds(HOP_ROWS + first, group_rows), :],
+            sem_ref.at[8 + i],
+        ).wait()
+
+        def ready():
+            @pl.when(i == 0)
+            def _():
+                for copy in tables_in[4:]:
+                    copy.wait()
+
+        transform_group(
+            lambda hop, side: hops_ref[pl.ds(first + hop * HOP_ROWS + side, half, stride=2), :],
+            i * GROUP,
+            frames,
+            places,
+            per_member,
+            copies_ref,
+            out_ref,
+            parts_ref,
+            middle_ref,
+            ready,
+        )
+        return carry
+
+    lax.fori_loop(0, groups, body, 0)
+    tail.wait()
+
+
+def late_kernel(places, per_member, frames, tail_ref, trailing_ref, activity_ref, *rest):
+    table_refs, (_, out_ref, parts_ref, middle_ref) = rest[:6], rest[6:]
+
+    def hop_rows(hop, side):
+        if hop == GROUP:
+            return trailing_ref[pl.ds(side, SPLIT // 2, stride=2), :]
+        return tail_ref[pl.ds(hop * HOP_ROWS + side, SPLIT // 2, stride=2), :]
+
+    for member in range(out_ref.shape[0]):
+        out_ref[member, per_member * frames :, :] = activity_ref[...]
+    transform_group(
+        hop_rows,
+        frames - GROUP,
+        frames,
+        places,
+        per_member,
+        table_refs,
+        out_ref,
+        parts_ref,
+        middle_ref,
+        lambda: None,
+    )
+
+
+def spectrum_blocks(samples, trailing, activity, unit_order, members):
+    *values, places = tables(unit_order)
     per_member = SPLIT // members
-    chunks = samples.shape[0] // (GROUP * HOP_ROWS)
-    constants = [jnp.asarray(t) for t in (window, first, twiddle, rows, second, mirrored)]
-    out_shape = jax.ShapeDtypeStruct((members, chunks, per_member * GROUP, LANES), jnp.float32)
-    whole = [pl.BlockSpec(t.shape, lambda s, n=t.ndim: (0,) * n) for t in constants]
-    kernel = functools.partial(spectrum_kernel, places, per_member)
-
-    last = chunks * GROUP - 1
+    frames = samples.shape[0] // HOP_ROWS
+    groups = frames // GROUP - 1
+    constants = [jnp.asarray(t) for t in values]
+    out_shape = jax.ShapeDtypeStruct((members, per_member * frames + activity.shape[0], LANES), jnp.float32)
+    tail_shape = jax.ShapeDtypeStruct((GROUP * HOP_ROWS, LANES), jnp.float32)
+    in_vmem = pl.BlockSpec(memory_space=pltpu.VMEM)
+    in_hbm = pl.BlockSpec(memory_space=pltpu.HBM)
+    scratch = [
+        pltpu.VMEM((2, GROUP * LANES, 3 * SPLIT), jnp.bfloat16),
+        pltpu.VMEM((2, 16, SPLIT), jnp.float32),
+    ]
+
+    def settings(count):
+        return dict(
+            compiler_params=pltpu.CompilerParams(vmem_limit_bytes=SPECTRUM_VMEM),
+            cost_estimate=pl.CostEstimate(
+                flops=count * GROUP * 6 * SPLIT * SPLIT * SPLIT * 2,
+                bytes_accessed=count * GROUP * FRAME_LEN * 4,
+                transcendentals=0,
+            ),
+        )
+
+    early, tail = pl.pallas_call(
+        functools.partial(early_kernel, places, per_member, frames),
+        in_specs=[in_hbm] * (1 + len(constants)),
+        out_specs=[in_vmem, in_vmem],
+        out_shape=[out_shape, tail_shape],
+        scratch_shapes=[pltpu.VMEM(t.shape, t.dtype) for t in constants]
+        + [pltpu.VMEM(((groups * GROUP + 1) * HOP_ROWS, LANES), jnp.float32)]
+        + scratch
+        + [pltpu.SemaphoreType.DMA((8 + groups,))],
+        **settings(groups),
+    )(samples, *constants)
     return pl.pallas_call(
-        functools.partial(spectrum_kernel, places, per_member),
-        grid=(chunks,),
-        in_specs=[
-            pl.BlockSpec((GROUP * HOP_ROWS, LANES), lambda s: (s, 0)),
-            pl.BlockSpec((HOP_ROWS, LANES), lambda s: (jnp.minimum(GROUP * (s + 1), last), 0)),
-            pl.BlockSpec((HOP_ROWS, LANES), lambda s: (0, 0)),
-            *whole,
-        ],
-        out_specs=pl.BlockSpec((members, 1, per_member * GROUP, LANES), lambda s: (0, s, 0, 0)),
+        functools.partial(late_kernel, places, per_member, frames),
+        in_specs=[in_vmem] * (4 + len(constants)),
+        out_specs=in_vmem,
         out_shape=out_shape,
-        scratch_shapes=[
-            pltpu.VMEM((2, GROUP * LANES, 3 * SPLIT), jnp.bfloat16),
-            pltpu.VMEM((2, 16, SPLIT), jnp.float32),
-        ],
-        compiler_params=pltpu.CompilerParams(vmem_limit_bytes=SPECTRUM_VMEM),
-        cost_estimate=pl.CostEstimate(
-            flops=chunks * GROUP * 6 * SPLIT * SPLIT * SPLIT * 2,
-            bytes_accessed=chunks * GROUP * FRAME_LEN * 4,
-            transcendentals=0,
-        ),
-    )(samples, samples, trailing, *constants)
+        scratch_shapes=scratch,
+        input_output_aliases={3 + len(constants): 0},
+        **settings(1),
+    )(tail, trailing, activity, *constants, early)
 
 
 def lanes_of_activity(activity):
@@ -233,23 +312,32 @@
 
 def ratio_of(spectrum_ref, start, activity_lanes, basis):
     frames = activity_lanes.shape[0]
+    local = frames // spectrum_ref.shape[0]
     splits = [split_values(block) for block in basis]
     stacked = jnp.concatenate([jnp.concatenate([h, l, h, l], 0) for h, l in splits], 1)
     approx = dot(activity_lanes, stacked)
     values = jnp.concatenate(
         [
-            spectrum_ref[:, :, (start + row) * GROUP : (start + row + 1) * GROUP, :].reshape(frames, LANES)
+            spectrum_ref[:, (start + row) * local : (start + row + 1) * local, :].reshape(frames, LANES)
             for row in range(len(basis))
         ],
         1,
     )
-    return values / approx, splits
-
-
-def for_activity(ratio, splits):
+    return values / approx, jnp.concatenate([jnp.concatenate([h, l], 0) for h, l in splits], 1)
+
+
+def for_activity(ratio, basis):
     high, low = split_values(ratio)
-    basis = jnp.concatenate([jnp.concatenate([h, l], 0) for h, l in splits], 1)
-    return dot_nt(jnp.concatenate([high, low], 1), jnp.concatenate([basis, basis], 1))
+    return dot_nt(high, basis) + dot_nt(low, basis)
+
+
+def both_parts(values):
+    half = values.shape[1] // 2
+    return values + pltpu.roll(values, half, 1)
+
+
+def row_sums(basis):
+    return dot_nt(jnp.ones((16, basis.shape[1]), jnp.bfloat16), basis)
 
 
 def row_steps(per_member):
@@ -258,8 +346,9 @@
 
 
 def packed(values):
-    half = values.shape[0] // 2
-    return jnp.concatenate([values[:half], values[half:]], 1)
+    rows, width = values.shape
+    lane = lax.broadcasted_iota(jnp.int32, (rows // 2, width), 1)
+    return jnp.where(lane < width // 2, values[: rows // 2], values[rows // 2 :])
 
 
 def unpacked(values):
@@ -267,29 +356,43 @@
     return jnp.concatenate([values[:, :half], values[:, half:]], 0)
 
 
-def first_kernel(side_ref, spectrum_ref, basis_ref, activity_ref, mine_ref, other_ref, lanes_ref, total_ref):
-    rank = activity_ref.shape[1]
-    lanes_ref[...] = lanes_of_activity(activity_ref[...])
-    sums = jnp.zeros((rank, LANES), jnp.float32)
+def gathered_activity(spectrum_ref, shape):
+    subs, members, ranks, width = shape
+    local = width // subs
+    frames_in = width // LANES
+    first = spectrum_ref.shape[1] - ranks * frames_in
+    pieces = {}
+    for member in range(members):
+        for part in range(frames_in):
+            start = first + part * ranks
+            rows = [spectrum_ref[sub * members + member, start : start + ranks, :] for sub in range(subs)]
+            block = jnp.transpose(jnp.concatenate(rows, 0))
+            for place in range(LANES // local):
+                pieces[part * (LANES // local) + place, member] = block[place * local : (place + 1) * local]
+    return jnp.concatenate([pieces[sub, member] for sub in range(subs) for member in range(members)], 0)
+
+
+def first_kernel(shape, side_ref, spectrum_ref, basis_ref, mine_ref, other_ref, activity_ref, lanes_ref, total_ref):
+    activity = gathered_activity(spectrum_ref, shape)
+    activity_ref[...] = activity
+    lanes_ref[...] = lanes_of_activity(activity)
+    sums = 0.0
     for step, rows in enumerate(row_steps(basis_ref.shape[0])):
-        basis = [basis_ref[row] for row in rows]
-        ratio, splits = ratio_of(spectrum_ref, rows[0], lanes_ref[...], basis)
-        part = for_activity(ratio, splits)
+        ratio, basis = ratio_of(spectrum_ref, rows[0], lanes_ref[...], [basis_ref[row] for row in rows])
+        part = for_activity(ratio, basis)
         if step == 0:
             total_ref[...] = part
         else:
             total_ref[...] += part
-        sums += sum(basis)
-    total = total_ref[...]
-    total = total[:, :rank] + total[:, rank:]
+        sums += row_sums(basis)
+    total = both_parts(total_ref[...])
     half = total.shape[0] // 2
     quarter = half // 2
     early, late = packed(total[:half]), packed(total[half:])
     first = side_ref[0] == 0
     mine_ref[:quarter, :] = jnp.where(first, early, late)
     other_ref[:quarter, :] = jnp.where(first, late, early)
-    sums = jnp.sum(jnp.transpose(sums), axis=0, keepdims=True)
-    sums = jnp.broadcast_to(jnp.concatenate([sums, sums], 1), (8, 2 * rank))
+    sums = both_parts(sums)[:8]
     mine_ref[quarter:, :] = sums
     other_ref[quarter:, :] = sums
 
@@ -340,23 +443,22 @@
     per_member = basis_ref.shape[0]
     lanes_ref[...] = lanes_of_activity(middle_ref[...])
     scale = 1.0 / sum(ref[per_member] for ref in numerators)
-    sums = jnp.zeros((rank, LANES), jnp.float32)
+    sums = 0.0
     for step, rows in enumerate(row_steps(per_member)):
-        basis = [basis_ref[row] * (sum(ref[row] for ref in numerators) * scale) for row in rows]
-        for row, block in zip(rows, basis):
+        blocks = [basis_ref[row] * (sum(ref[row] for ref in numerators) * scale) for row in rows]
+        for row, block in zip(rows, blocks):
             new_ref[row] = block
-        ratio, splits = ratio_of(spectrum_ref, rows[0], lanes_ref[...], basis)
-        part = for_activity(ratio, splits)
+        ratio, basis = ratio_of(spectrum_ref, rows[0], lanes_ref[...], blocks)
+        part = for_activity(ratio, basis)
         if step == 0:
             total_ref[...] = part
         else:
             total_ref[...] += part
-        sums += sum(basis)
-    total = total_ref[...]
-    total = total[:, :rank] + total[:, rank:]
+        sums += row_sums(basis)
+    total = both_parts(total_ref[...])[:, :rank]
     subs, members, _, ranks, width = out_ref.shape
-    sums = jnp.sum(sums, axis=1, keepdims=True)
-    sums = jnp.broadcast_to(sums, (rank, width)).reshape(subs, ranks, width)
+    sums = jnp.transpose(jnp.broadcast_to(both_parts(sums)[:1], (LANES, 2 * rank)))[:rank]
+    sums = jnp.concatenate([sums] * (width // LANES), 1).reshape(subs, ranks, width)
     for member, block in enumerate(by_owner(total, (subs, members, ranks, width))):
         out_ref[:, member, 0] = block
         out_ref[:, member, 1] = sums
@@ -422,20 +524,13 @@
         if block + (sub + 1) // subs < blocks
     ]
     trailing = lax.ppermute(samples[:HOP_ROWS], ("freq", "group", "member"), route)
-    gathered = lax.all_to_all(
-        jnp.broadcast_to(activations[None], (partners, ranks_here, width)), exchange, 0, 0, tiled=True
-    )
+    own_rows = activations.reshape(ranks_here, width // LANES, LANES).transpose(1, 0, 2)
+    own_rows = own_rows.reshape(ranks_here * width // LANES, LANES)
+    spectrum = spectrum_blocks(samples, trailing, own_rows, unit_order, partners)
+    spectrum, templates = lax.optimization_barrier((spectrum, templates))
     other = [swap_by(templates, "group", 1)] if groups == 2 else []
-
-    spectrum = spectrum_blocks(samples, trailing, unit_order, partners)
-    spectrum, gathered, other, templates = lax.optimization_barrier(
-        (spectrum, gathered, other, templates)
-    )
     spectrum = lax.all_to_all(spectrum, exchange, 0, 0, tiled=True)
-
     local = width // subs
-    activity = gathered.reshape(subs, members, ranks_here, subs, local)
-    activity = activity.transpose(3, 1, 4, 0, 2).reshape(partners * local, rank)
     frames = partners * local
 
     own = templates.reshape(rank, units_here, LANES).transpose(1, 0, 2)
@@ -455,8 +550,13 @@
     total_scratch = pltpu.VMEM((frames, 2 * rank), jnp.float32)
     half_shape = (frames // 4 + 8, 2 * rank)
     side = (me_sub % 2).astype(jnp.int32).reshape(1)
-    mine, other = update_call(
-        first_kernel, spectrum, [half_shape] * 2, [lanes_scratch, total_scratch], (basis, activity), (side,)
+    mine, other, activity = update_call(
+        functools.partial(first_kernel, (subs, members, ranks_here, width)),
+        spectrum,
+        [half_shape, half_shape, (frames, rank)],
+        [lanes_scratch, total_scratch],
+        (basis,),
+        (side,),
     )
     mine = mine + swap_by(other, "freq", 1)
     mine = sum_over(mine, "freq", 2)

time: 165 us -> 167 us (1.012)
  Pallas kernels: 24.9 us -> 28.7 us
  waiting for transfers between devices: 98.3 us -> 101 us
  local copies, waits for them, and re-layouts: 14.3 us -> 11.8 us
  starting transfers between devices: 24.2 us -> 22 us
    ppermute x7, waiting for transfers between devices: 40.4 us -> 88.8 us  [swap_by(): return lax.ppermute(value, axis, [(i, i ^ mask) for i in range(count)])]
    all_to_all x1, waiting for transfers between devices: 52.1 us -> 6.69 us  [on_device(): spectrum = lax.all_to_all(spectrum, exchange, 0, 0, tiled=True)]
    all_to_all x1 -> x0, starting transfers between devices: 7.02 us -> none  [on_device(): lax.all_to_all(jnp.broadcast_to(activations[None], (partners, ranks_here,...]
    pallas_call x1 -> x2, Pallas kernels: 10.5 us -> 14.2 us  [the longest x1 11.2 us: spectrum_blocks(): pl.pallas_call(functools.partial(early_kernel, places, per_member, frames...]
    ppermute x7, starting transfers between devices: 7.2 us -> 9.93 us  [swap_by(): return lax.ppermute(value, axis, [(i, i ^ mask) for i in range(count)])]
    all_to_all x1, starting transfers between devices: 5.19 us -> 7.2 us  [on_device(): spectrum = lax.all_to_all(spectrum, exchange, 0, 0, tiled=True)]
    unnamed x37 -> x39, local copies, waits for them, and re-layouts: 10 us -> 10 us
  transfers between devices with their start and end apart: 11 -> 10, of which waited for: 8 -> 9; matrix products, arithmetic and copies ran while one was open for 3% -> 1% of each run, Pallas kernels for 6% -> 7%
where the time goes in v3:
time: 167 us
  waiting for transfers between devices  101 us (60%)
  Pallas kernels  28.7 us (17%)
  starting transfers between devices  22 us (13%)
  local copies, waits for them, and re-layouts  11.8 us (7%)
  other arithmetic  1.97 us (1%)
    ppermute x7, waiting for transfers between devices, swap_by(): return lax.ppermute(value, axis, [(i, i ^ mask) for i in range(count)])  88.8 us
    pallas_call x3, Pallas kernels, update_call(): pl.pallas_call(kernel, in_specs=[pl.BlockSpec(memory_space=pltpu.SMEM) fo...  14.5 us
    pallas_call x1, Pallas kernels, spectrum_blocks(): pl.pallas_call(functools.partial(early_kernel, places, per_member, frames...  11.2 us
    unnamed x39, local copies, waits for them, and re-layouts  10 us
    ppermute x7, starting transfers between devices, swap_by(): return lax.ppermute(value, axis, [(i, i ^ mask) for i in range(count)])  9.93 us
    all_to_all x1, starting transfers between devices, on_device(): spectrum = lax.all_to_all(spectrum, exchange, 0, 0, tiled=True)  7.2 us
    all_to_all x1, waiting for transfers between devices, on_device(): spectrum = lax.all_to_all(spectrum, exchange, 0, 0, tiled=True)  6.69 us
    all_to_all x1, waiting for transfers between devices, on_device(): lax.all_to_all(payload.reshape(partners, 2, ranks_here, width), exchange,...  5.81 us
  transfers between devices with their start and end apart: 10, of which 9 were waited for; matrix products, arithmetic and copies ran while one was open for 1% of the time, Pallas kernels for 7%

profile of v3, /device:TPU:0, one launch (start us, length us, event | category | flops | bytes accessed | tf_op | source)
XLA Modules:
  0.0 166.7 jit_solution(8238618560041938631)
XLA Ops:
  0.6 0.9 slice.126
  1.5 1.3 collective-permute-start
  2.8 0.0 copy-start.1
  2.9 1.1 copy-done.1
  4.0 0.0 copy-start.2
  4.0 1.0 copy-done.2
  5.0 0.0 copy-start.3
  5.0 1.0 copy-done.3
  6.0 0.0 copy-start.4
  6.0 0.9 copy-done.4
  6.9 0.0 copy-start.5
  6.9 0.9 copy-done.5
  7.8 0.0 copy-start.7
  7.8 0.7 copy-done.7
  8.5 0.0 copy-start.8
  8.5 2.2 %copy-done.8 = f32[1,1,1048576]{2,1,0:T(1,128)S(1)} copy-done((f32[1,1,1048576]{2,1,0:T(1,128)S(1)}, f32[1,1,1048576]{2,1,0:T(1,128)}, u32[]{:S(2)}) %copy-start.8) | copy-done | bytes 4194328
  10.7 0.0 copy-start.6
  10.7 11.2 %shard_map.104 = (f32[16,528,128]{2,1,0:T(8,128)S(1)}, f32[2048,128]{1,0:T(8,128)S(1)}) custom-call(f32[8192,128]{1,0:T(8,128)S(1)} %bitcast.109, f32[2,256,128]{2,1,0:T(8,128)S(1)} %copy-done.4, bf16[256,768]{1,0:T(8,128)(2,1)S(1)} %copy-done.2, f32[3,128,256]{2,1,0:T(8,128)S(1)} %copy-done.3, f32[8,256]{1,0:T(8,128)S(1)} %copy-done.7, ...), custom_call_target="tpu_custom_call" | custom-call | flops 4831838208 | bytes 6291456 | tf_op jit(solution)/shard_map/pallas_call | solution.py:286
  21.9 0.0 collective-permute-done.trailing_ref
  21.9 0.0 copy-done.6
  22.0 3.0 %shard_map.105 = f32[16,528,128]{2,1,0:T(8,128)S(1)} custom-call(f32[2048,128]{1,0:T(8,128)S(1)} %get-tuple-element.13.tail_ref, f32[256,128]{1,0:T(8,128)S(1)} %collective-permute-done.trailing_ref, f32[16,128]{1,0:T(8,128)S(1)} %copy-done.6, f32[2,256,128]{2,1,0:T(8,128)S(1)} %copy-done.4, ...), custom_call_target="tpu_custom_call", output_to_operand_aliasing={{}: (9, {})} | custom-call | flops 1610612736 | bytes 2097152 | tf_op jit(solution)/shard_map/pallas_call | solution.py:297
  25.0 0.0 copy-start
  25.0 2.1 %copy-done = f32[16,528,128]{2,1,0:T(8,128)} copy-done((f32[16,528,128]{2,1,0:T(8,128)}, f32[16,528,128]{2,1,0:T(8,128)S(1)}, u32[]{:S(2)}) %copy-start) | copy-done | bytes 4325400
  27.1 0.0 copy-start.9
  27.1 7.2 %all-to-all-start = ((f32[16,528,128]{2,1,0:T(8,128)}), f32[16,528,128]{2,1,0:T(8,128)}, u32[]{:S(2)}, u32[]{:S(2)}) async-start(f32[16,528,128]{2,1,0:T(8,128)} %copy-done), calls=%async_computation | async-start | bytes 8650752 | tf_op jit(solution)/shard_map/all_to_all | solution.py:532
  34.3 0.0 copy-done.9
  34.3 4.1 %collective-permute-start.1 = (f32[64,1024]{1,0:T(8,128)S(1)}, f32[64,1024]{1,0:T(8,128)S(1)}, u32[]{:S(2)}, u32[]{:S(2)}) collective-permute-start(f32[64,1024]{1,0:T(8,128)S(1)} %copy-done.9), channel_id=1, source_target_pairs={{0,4},{4,0},{1,5},{5,1},{2,6},{6,2},{3,7},{7,3},{8,12},{12,8},{9,1... | collective-permute-start | bytes 786440 | tf_op jit(solution)/shard_map/ppermute | solution.py:490
  38.5 0.1 fusion.6
  38.6 49.7 %collective-permute-done.1 = f32[64,1024]{1,0:T(8,128)S(1)} collective-permute-done((f32[64,1024]{1,0:T(8,128)S(1)}, f32[64,1024]{1,0:T(8,128)S(1)}, u32[]{:S(2)}, u32[]{:S(2)}) %collective-permute-start.1) | collective-permute-done | bytes 262176 | tf_op jit(solution)/shard_map/ppermute | solution.py:490
  88.4 0.2 slice.163
  88.6 0.2 slice.130
  88.8 0.2 maximum_select_fusion.1
  89.2 6.7 %all-to-all-done.spectrum_ref = f32[16,528,128]{2,1,0:T(8,128)} async-done(((f32[16,528,128]{2,1,0:T(8,128)}), f32[16,528,128]{2,1,0:T(8,128)}, u32[]{:S(2)}, u32[]{:S(2)}) %all-to-all-start) | async-done | bytes 4325408 | tf_op jit(solution)/shard_map/all_to_all | solution.py:532
  95.9 4.9 %shard_map.106 = (f32[136,128]{1,0:T(8,128)S(1)}, f32[136,128]{1,0:T(8,128)S(1)}, f32[512,64]{1,0:T(8,128)S(1)}) custom-call(s32[1]{0:T(128)} %bitcast.side_ref, f32[16,528,128]{2,1,0:T(8,128)} %all-to-all-done.spectrum_ref, f32[16,64,128]{2,1,0:T(8,128)S(1)} %constant_dynamic-update-slice_fusion.basis_ref), custom_call_target="tpu_custom_call" | custom-call | flops 1107296256 | bytes 4325376 | tf_op jit(solution)/shard_map/pallas_call | solution.py:470
  100.9 0.1 collective-permute-start.2
  100.9 1.2 collective-permute-done.2
  102.2 0.6 collective-permute-start.3
  102.8 3.8 %collective-permute-done.3 = f32[136,128]{1,0:T(8,128)S(1)} collective-permute-done((f32[136,128]{1,0:T(8,128)S(1)}, f32[136,128]{1,0:T(8,128)S(1)}, u32[]{:S(2)}, u32[]{:S(2)}) %collective-permute-start.3) | collective-permute-done | bytes 69664 | tf_op jit(solution)/shard_map/ppermute | solution.py:490
  106.6 0.8 collective-permute-start.4
  107.4 3.6 %collective-permute-done.4 = f32[136,128]{1,0:T(8,128)S(1)} collective-permute-done((f32[136,128]{1,0:T(8,128)S(1)}, f32[136,128]{1,0:T(8,128)S(1)}, u32[]{:S(2)}, u32[]{:S(2)}) %collective-permute-start.4) | collective-permute-done | bytes 69664 | tf_op jit(solution)/shard_map/ppermute | solution.py:490
  111.0 3.7 %collective-permute-start.5 = (f32[136,128]{1,0:T(8,128)S(1)}, f32[136,128]{1,0:T(8,128)S(1)}, u32[]{:S(2)}, u32[]{:S(2)}) collective-permute-start(f32[136,128]{1,0:T(8,128)S(1)} %add.88), channel_id=1, source_target_pairs={{0,2},{1,3},{2,0},{3,1},{4,6},{5,7},{6,4},{7,5},{8,10},{9,11},{10,... | collective-permute-start | bytes 208904 | tf_op jit(solution)/shard_map/ppermute | solution.py:490
  114.7 2.3 %collective-permute-done.5 = f32[136,128]{1,0:T(8,128)S(1)} collective-permute-done((f32[136,128]{1,0:T(8,128)S(1)}, f32[136,128]{1,0:T(8,128)S(1)}, u32[]{:S(2)}, u32[]{:S(2)}) %collective-permute-start.5) | collective-permute-done | bytes 69664 | tf_op jit(solution)/shard_map/ppermute | solution.py:490
  117.0 0.1 collective-permute-start.6
  117.1 1.2 collective-permute-done.6.other_ref
  118.3 3.9 %shard_map.107 = (f32[512,64]{1,0:T(8,128)S(1)}, f32[17,64,128]{2,1,0:T(8,128)S(1)}) custom-call(s32[1]{0:T(128)} %bitcast.side_ref, f32[16,528,128]{2,1,0:T(8,128)} %all-to-all-done.spectrum_ref, f32[16,64,128]{2,1,0:T(8,128)S(1)} %constant_dynamic-update-slice_fusion.basis_ref, f32[512,64]{1,0:T(8,128)S(1)} %get-tuple-element.17.activity_ref, ...), custom_call_target="tpu_custom_call" | custom-call | flops 1107296256 | bytes 4325376 | tf_op jit(solution)/shard_map/pallas_call | solution.py:470
  122.2 0.6 collective-permute-start.7
  122.9 0.1 constant_dynamic-slice_fusion
  122.9 0.1 copy.23
  123.0 26.8 %collective-permute-done.7.rest_1_ = f32[17,64,128]{2,1,0:T(8,128)S(1)} collective-permute-done((f32[17,64,128]{2,1,0:T(8,128)S(1)}, f32[17,64,128]{2,1,0:T(8,128)S(1)}, u32[]{:S(2)}, u32[]{:S(2)}) %collective-permute-start.7) | collective-permute-done | bytes 557088 | tf_op jit(solution)/shard_map/ppermute | solution.py:490
  149.8 5.6 %shard_map.108 = (f32[16,64,128]{2,1,0:T(8,128)S(1)}, f32[4,4,2,16,128]{4,3,2,1,0:T(8,128)}) custom-call(f32[16,528,128]{2,1,0:T(8,128)} %all-to-all-done.spectrum_ref, f32[16,64,128]{2,1,0:T(8,128)S(1)} %constant_dynamic-update-slice_fusion.basis_ref, f32[512,64]{1,0:T(8,128)S(1)} %get-tuple-element.20.middle_ref, ...), custom_call_target="tpu_custom_call" | custom-call | flops 1107296256 | bytes 4325376 | tf_op jit(solution)/shard_map/pallas_call | solution.py:470
  155.4 3.5 %all-to-all-start.1 = ((f32[16,2,16,128]{3,2,1,0:T(8,128)}), f32[16,2,16,128]{3,2,1,0:T(8,128)S(1)}, u32[]{:S(2)}, u32[]{:S(2)}) async-start(f32[16,2,16,128]{3,2,1,0:T(8,128)} %bitcast.28), calls=%async_computation.1 | async-start | bytes 524288 | tf_op jit(solution)/shard_map/all_to_all | solution.py:584
  159.1 0.1 fusion.1
  159.1 0.1 slice.183
  159.3 0.1 slice.161
  159.4 0.9 copy_bitcast_fusion
  160.3 5.8 %all-to-all-done.1 = f32[16,2,16,128]{3,2,1,0:T(8,128)S(1)} async-done(((f32[16,2,16,128]{3,2,1,0:T(8,128)}), f32[16,2,16,128]{3,2,1,0:T(8,128)S(1)}, u32[]{:S(2)}, u32[]{:S(2)}) %all-to-all-start.1) | async-done | bytes 262176 | tf_op jit(solution)/shard_map/all_to_all | solution.py:584
  166.1 0.6 fusion.4
  (31 shorter events, 0.3 us)
Async XLA Ops:
  1.5 20.4 %collective-permute-start = (f32[256,128]{1,0:T(8,128)S(1)}, f32[256,128]{1,0:T(8,128)S(1)}, u32[]{:S(2)}, u32[]{:S(2)}) collective-permute-start(f32[256,128]{1,0:T(8,128)S(1)} %bitcast.115), channel_id=1, source_target_pairs={{8,0},{9,1},{10,2},{11,3},{12,4},{13,5},{14,6},{15,7},{16,8},{17,9... | collective-permute-start | bytes 393224 | tf_op jit(solution)/shard_map/ppermute | solution.py:526
  2.8 1.1 copy-start.1
  4.0 1.0 copy-start.2
  5.0 1.0 copy-start.3
  6.0 0.9 copy-start.4
  6.9 0.9 copy-start.5
  7.8 0.7 copy-start.7
  8.5 2.2 %copy-start.8 = (f32[1,1,1048576]{2,1,0:T(1,128)S(1)}, f32[1,1,1048576]{2,1,0:T(1,128)}, u32[]{:S(2)}) copy-start(f32[1,1,1048576]{2,1,0:T(1,128)} %param.9) | copy-start | bytes 12582916
  10.7 11.2 %copy-start.6 = (f32[16,128]{1,0:T(8,128)S(1)}, f32[16,128]{1,0:T(8,128)}, u32[]{:S(2)}) copy-start(f32[16,128]{1,0:T(8,128)} %activity_ref.1) | copy-start | bytes 24580
  25.0 2.1 %copy-start = (f32[16,528,128]{2,1,0:T(8,128)}, f32[16,528,128]{2,1,0:T(8,128)S(1)}, u32[]{:S(2)}) copy-start(f32[16,528,128]{2,1,0:T(8,128)S(1)} %shard_map.105) | copy-start | bytes 12976132
  27.1 7.2 %copy-start.9 = (f32[64,1024]{1,0:T(8,128)S(1)}, f32[64,1024]{1,0:T(8,128)}, u32[]{:S(2)}) copy-start(f32[64,1024]{1,0:T(8,128)} %param.10) | copy-start | bytes 786436
  27.1 68.9 %all-to-all-start = ((f32[16,528,128]{2,1,0:T(8,128)}), f32[16,528,128]{2,1,0:T(8,128)}, u32[]{:S(2)}, u32[]{:S(2)}) async-start(f32[16,528,128]{2,1,0:T(8,128)} %copy-done), calls=%async_computation | async-start | bytes 8650752 | tf_op jit(solution)/shard_map/all_to_all | solution.py:532
  34.3 54.0 %collective-permute-start.1 = (f32[64,1024]{1,0:T(8,128)S(1)}, f32[64,1024]{1,0:T(8,128)S(1)}, u32[]{:S(2)}, u32[]{:S(2)}) collective-permute-start(f32[64,1024]{1,0:T(8,128)S(1)} %copy-done.9), channel_id=1, source_target_pairs={{0,4},{4,0},{1,5},{5,1},{2,6},{6,2},{3,7},{7,3},{8,12},{12,8},{9,1... | collective-permute-start | bytes 786440 | tf_op jit(solution)/shard_map/ppermute | solution.py:490
  100.9 1.3 collective-permute-start.2
  102.2 4.4 %collective-permute-start.3 = (f32[136,128]{1,0:T(8,128)S(1)}, f32[136,128]{1,0:T(8,128)S(1)}, u32[]{:S(2)}, u32[]{:S(2)}) collective-permute-start(f32[136,128]{1,0:T(8,128)S(1)} %add.86), channel_id=1, source_target_pairs={{0,16},{8,24},{16,0},{24,8},{1,17},{9,25},{17,1},{25,9},{2,18},{10... | collective-permute-start | bytes 208904 | tf_op jit(solution)/shard_map/ppermute | solution.py:490
  106.6 4.4 %collective-permute-start.4 = (f32[136,128]{1,0:T(8,128)S(1)}, f32[136,128]{1,0:T(8,128)S(1)}, u32[]{:S(2)}, u32[]{:S(2)}) collective-permute-start(f32[136,128]{1,0:T(8,128)S(1)} %add.87), channel_id=1, source_target_pairs={{0,1},{1,0},{2,3},{3,2},{4,5},{5,4},{6,7},{7,6},{8,9},{9,8},{10,11... | collective-permute-start | bytes 208904 | tf_op jit(solution)/shard_map/ppermute | solution.py:490
  111.0 6.0 %collective-permute-start.5 = (f32[136,128]{1,0:T(8,128)S(1)}, f32[136,128]{1,0:T(8,128)S(1)}, u32[]{:S(2)}, u32[]{:S(2)}) collective-permute-start(f32[136,128]{1,0:T(8,128)S(1)} %add.88), channel_id=1, source_target_pairs={{0,2},{1,3},{2,0},{3,1},{4,6},{5,7},{6,4},{7,5},{8,10},{9,11},{10,... | collective-permute-start | bytes 208904 | tf_op jit(solution)/shard_map/ppermute | solution.py:490
  117.0 1.3 collective-permute-start.6
  122.2 27.6 %collective-permute-start.7 = (f32[17,64,128]{2,1,0:T(8,128)S(1)}, f32[17,64,128]{2,1,0:T(8,128)S(1)}, u32[]{:S(2)}, u32[]{:S(2)}) collective-permute-start(f32[17,64,128]{2,1,0:T(8,128)S(1)} %get-tuple-element.21.rest_0_), channel_id=1, source_target_pairs={{0,4},{4,0},{1,5},{5,1},{2,6},{6,2},{3,7},{7,3},{8,12},{12,8},{9,1... | collective-permute-start | bytes 1671176 | tf_op jit(solution)/shard_map/ppermute | solution.py:490
  155.4 10.6 %all-to-all-start.1 = ((f32[16,2,16,128]{3,2,1,0:T(8,128)}), f32[16,2,16,128]{3,2,1,0:T(8,128)S(1)}, u32[]{:S(2)}, u32[]{:S(2)}) async-start(f32[16,2,16,128]{3,2,1,0:T(8,128)} %bitcast.28), calls=%async_computation.1 | async-start | bytes 524288 | tf_op jit(solution)/shard_map/all_to_all | solution.py:584

commit v4 on v3

--- a/solution.py
+++ b/solution.py
@@ -283,17 +283,16 @@
             ),
         )
 
-    early, tail = pl.pallas_call(
+    early, tail, *copies = pl.pallas_call(
         functools.partial(early_kernel, places, per_member, frames),
         in_specs=[in_hbm] * (1 + len(constants)),
-        out_specs=[in_vmem, in_vmem],
-        out_shape=[out_shape, tail_shape],
-        scratch_shapes=[pltpu.VMEM(t.shape, t.dtype) for t in constants]
-        + [pltpu.VMEM(((groups * GROUP + 1) * HOP_ROWS, LANES), jnp.float32)]
+        out_specs=[in_vmem] * (2 + len(constants)),
+        out_shape=[out_shape, tail_shape] + [jax.ShapeDtypeStruct(t.shape, t.dtype) for t in constants],
+        scratch_shapes=[pltpu.VMEM(((groups * GROUP + 1) * HOP_ROWS, LANES), jnp.float32)]
         + scratch
         + [pltpu.SemaphoreType.DMA((8 + groups,))],
         **settings(groups),
-    )(samples, *constants)
+    )(*[pltpu.with_memory_space_constraint(value, pltpu.HBM) for value in (samples, *constants)])
     return pl.pallas_call(
         functools.partial(late_kernel, places, per_member, frames),
         in_specs=[in_vmem] * (4 + len(constants)),
@@ -302,7 +301,7 @@
         scratch_shapes=scratch,
         input_output_aliases={3 + len(constants): 0},
         **settings(1),
-    )(tail, trailing, activity, *constants, early)
+    )(tail, trailing, activity, *copies, early)
 
 
 def lanes_of_activity(activity):
@@ -524,11 +523,11 @@
         if block + (sub + 1) // subs < blocks
     ]
     trailing = lax.ppermute(samples[:HOP_ROWS], ("freq", "group", "member"), route)
+    other = [swap_by(templates, "group", 1)] if groups == 2 else []
     own_rows = activations.reshape(ranks_here, width // LANES, LANES).transpose(1, 0, 2)
     own_rows = own_rows.reshape(ranks_here * width // LANES, LANES)
     spectrum = spectrum_blocks(samples, trailing, own_rows, unit_order, partners)
-    spectrum, templates = lax.optimization_barrier((spectrum, templates))
-    other = [swap_by(templates, "group", 1)] if groups == 2 else []
+    spectrum, other = lax.optimization_barrier((spectrum, other))
     spectrum = lax.all_to_all(spectrum, exchange, 0, 0, tiled=True)
     local = width // subs
     frames = partners * local

time: 167 us -> 158 us (0.946)
  local copies, waits for them, and re-layouts: 11.8 us -> 3.95 us
    ppermute x7, waiting for transfers between devices: 88.8 us -> 40.4 us  [swap_by(): return lax.ppermute(value, axis, [(i, i ^ mask) for i in range(count)])]
    all_to_all x1, waiting for transfers between devices: 6.69 us -> 54.7 us  [on_device(): spectrum = lax.all_to_all(spectrum, exchange, 0, 0, tiled=True)]
    unnamed x39 -> x25, local copies, waits for them, and re-layouts: 10 us -> 2.18 us
    all_to_all x1, starting transfers between devices: 7.2 us -> 4.85 us  [on_device(): spectrum = lax.all_to_all(spectrum, exchange, 0, 0, tiled=True)]
  transfers between devices with their start and end apart: 10 -> 10, of which waited for: 9 -> 8; matrix products, arithmetic and copies ran while one was open for 1% -> 1% of each run, Pallas kernels for 7% -> 9%
where the time goes in v4:
time: 158 us; the launch traced here: 157 us
  waiting for transfers between devices  101 us (64%)
  Pallas kernels  29 us (18%)
  starting transfers between devices  20.4 us (13%)
  local copies, waits for them, and re-layouts  3.95 us (2%)
  other arithmetic  1.97 us (1%)
    all_to_all x1, waiting for transfers between devices, on_device(): spectrum = lax.all_to_all(spectrum, exchange, 0, 0, tiled=True)  54.7 us
    ppermute x7, waiting for transfers between devices, swap_by(): return lax.ppermute(value, axis, [(i, i ^ mask) for i in range(count)])  40.4 us
    pallas_call x3, Pallas kernels, update_call(): pl.pallas_call(kernel, in_specs=[pl.BlockSpec(memory_space=pltpu.SMEM) fo...  14.5 us
    pallas_call x1, Pallas kernels, spectrum_blocks(): pl.pallas_call(functools.partial(early_kernel, places, per_member, frames...  11.5 us
    ppermute x7, starting transfers between devices, swap_by(): return lax.ppermute(value, axis, [(i, i ^ mask) for i in range(count)])  10.7 us
    all_to_all x1, waiting for transfers between devices, on_device(): lax.all_to_all(payload.reshape(partners, 2, ranks_here, width), exchange,...  5.83 us
    all_to_all x1, starting transfers between devices, on_device(): spectrum = lax.all_to_all(spectrum, exchange, 0, 0, tiled=True)  4.85 us
    all_to_all x1, starting transfers between devices, on_device(): lax.all_to_all(payload.reshape(partners, 2, ranks_here, width), exchange,...  3.53 us
  transfers between devices with their start and end apart: 10, of which 8 were waited for; matrix products, arithmetic and copies ran while one was open for 1% of the time, Pallas kernels for 9%

profile of v4, /device:TPU:0, one launch (start us, length us, event | category | flops | bytes accessed | tf_op | source)
XLA Modules:
  0.0 157.2 jit_solution(13698510059936445763)
XLA Ops:
  0.6 0.9 slice.126
  1.5 1.3 collective-permute-start
  2.8 6.5 %collective-permute-start.1 = (f32[64,1024]{1,0:T(8,128)}, f32[64,1024]{1,0:T(8,128)S(1)}, u32[]{:S(2)}, u32[]{:S(2)}) collective-permute-start(f32[64,1024]{1,0:T(8,128)} %param.10), channel_id=1, source_target_pairs={{0,4},{4,0},{1,5},{5,1},{2,6},{6,2},{3,7},{7,3},{8,12},{12,8},{9,1... | collective-permute-start | bytes 786440 | tf_op jit(solution)/shard_map/ppermute | solution.py:489
  9.3 0.0 copy-start.1
  9.3 11.5 %shard_map.104 = (f32[16,528,128]{2,1,0:T(8,128)S(1)}, f32[2048,128]{1,0:T(8,128)S(1)}, f32[2,256,128]{2,1,0:T(8,128)S(1)}, bf16[256,768]{1,0:T(8,128)(2,1)S(1)}...) custom-call(f32[8192,128]{1,0:T(8,128)} %bitcast.115, ...), custom_call_target="tpu_custom_call" | custom-call | flops 4831838208 | bytes 6291456 | tf_op jit(solution)/shard_map/pallas_call | solution.py:286
  20.9 0.0 collective-permute-done.trailing_ref
  20.9 0.0 copy-done.1
  20.9 3.0 %shard_map.105 = f32[16,528,128]{2,1,0:T(8,128)S(1)} custom-call(f32[2048,128]{1,0:T(8,128)S(1)} %get-tuple-element.19.tail_ref, f32[256,128]{1,0:T(8,128)S(1)} %collective-permute-done.trailing_ref, f32[16,128]{1,0:T(8,128)S(1)} %copy-done.1, f32[2,256,128]{2,1,0:T(8,128)S(1)} %get-tuple-element.20.rest_0_, ...), custom_call_target="tpu_custom_call", output_to_operand_aliasing={{}: (9, {})} | custom-call | flops 1610612736 | bytes 2097152 | tf_op jit(solution)/shard_map/pallas_call | solution.py:296
  23.9 0.0 copy-start
  23.9 2.1 %copy-done = f32[16,528,128]{2,1,0:T(8,128)} copy-done((f32[16,528,128]{2,1,0:T(8,128)}, f32[16,528,128]{2,1,0:T(8,128)S(1)}, u32[]{:S(2)}) %copy-start) | copy-done | bytes 4325400
  26.0 0.0 copy-start.2
  26.0 0.0 collective-permute-done.1
  26.0 4.8 %all-to-all-start = ((f32[16,528,128]{2,1,0:T(8,128)}), f32[16,528,128]{2,1,0:T(8,128)}, u32[]{:S(2)}, u32[]{:S(2)}) async-start(f32[16,528,128]{2,1,0:T(8,128)} %copy-done), calls=%async_computation | async-start | bytes 8650752 | tf_op jit(solution)/shard_map/all_to_all | solution.py:531
  30.9 0.1 fusion.6
  31.0 0.0 copy-done.2
  31.1 0.2 slice.163
  31.3 0.2 slice.130
  31.5 0.2 maximum_select_fusion.1
  31.9 54.7 %all-to-all-done.spectrum_ref = f32[16,528,128]{2,1,0:T(8,128)} async-done(((f32[16,528,128]{2,1,0:T(8,128)}), f32[16,528,128]{2,1,0:T(8,128)}, u32[]{:S(2)}, u32[]{:S(2)}) %all-to-all-start) | async-done | bytes 4325408 | tf_op jit(solution)/shard_map/all_to_all | solution.py:531
  86.6 4.9 %shard_map.106 = (f32[136,128]{1,0:T(8,128)S(1)}, f32[136,128]{1,0:T(8,128)S(1)}, f32[512,64]{1,0:T(8,128)S(1)}) custom-call(s32[1]{0:T(128)} %bitcast.side_ref, f32[16,528,128]{2,1,0:T(8,128)} %all-to-all-done.spectrum_ref, f32[16,64,128]{2,1,0:T(8,128)S(1)} %constant_dynamic-update-slice_fusion.basis_ref), custom_call_target="tpu_custom_call" | custom-call | flops 1107296256 | bytes 4325376 | tf_op jit(solution)/shard_map/pallas_call | solution.py:469
  91.5 2.3 %collective-permute-start.2 = (f32[136,128]{1,0:T(8,128)S(1)}, f32[136,128]{1,0:T(8,128)S(1)}, u32[]{:S(2)}, u32[]{:S(2)}) collective-permute-start(f32[136,128]{1,0:T(8,128)S(1)} %get-tuple-element.31), channel_id=1, source_target_pairs={{0,8},{8,0},{16,24},{24,16},{1,9},{9,1},{17,25},{25,17},{2,10},{10... | collective-permute-start | bytes 208904 | tf_op jit(solution)/shard_map/ppermute | solution.py:489
  93.8 0.9 collective-permute-done.2
  94.7 1.1 collective-permute-start.3
  95.8 3.4 %collective-permute-done.3 = f32[136,128]{1,0:T(8,128)S(1)} collective-permute-done((f32[136,128]{1,0:T(8,128)S(1)}, f32[136,128]{1,0:T(8,128)S(1)}, u32[]{:S(2)}, u32[]{:S(2)}) %collective-permute-start.3) | collective-permute-done | bytes 69664 | tf_op jit(solution)/shard_map/ppermute | solution.py:489
  99.2 0.6 collective-permute-start.4
  99.8 3.7 %collective-permute-done.4 = f32[136,128]{1,0:T(8,128)S(1)} collective-permute-done((f32[136,128]{1,0:T(8,128)S(1)}, f32[136,128]{1,0:T(8,128)S(1)}, u32[]{:S(2)}, u32[]{:S(2)}) %collective-permute-start.4) | collective-permute-done | bytes 69664 | tf_op jit(solution)/shard_map/ppermute | solution.py:489
  103.6 0.1 collective-permute-start.5
  103.7 4.3 %collective-permute-done.5 = f32[136,128]{1,0:T(8,128)S(1)} collective-permute-done((f32[136,128]{1,0:T(8,128)S(1)}, f32[136,128]{1,0:T(8,128)S(1)}, u32[]{:S(2)}, u32[]{:S(2)}) %collective-permute-start.5) | collective-permute-done | bytes 69664 | tf_op jit(solution)/shard_map/ppermute | solution.py:489
  108.0 0.1 collective-permute-start.6
  108.1 1.2 collective-permute-done.6.other_ref
  109.3 3.9 %shard_map.107 = (f32[512,64]{1,0:T(8,128)S(1)}, f32[17,64,128]{2,1,0:T(8,128)S(1)}) custom-call(s32[1]{0:T(128)} %bitcast.side_ref, f32[16,528,128]{2,1,0:T(8,128)} %all-to-all-done.spectrum_ref, f32[16,64,128]{2,1,0:T(8,128)S(1)} %constant_dynamic-update-slice_fusion.basis_ref, f32[512,64]{1,0:T(8,128)S(1)} %get-tuple-element.29.activity_ref, ...), custom_call_target="tpu_custom_call" | custom-call | flops 1107296256 | bytes 4325376 | tf_op jit(solution)/shard_map/pallas_call | solution.py:469
  113.3 0.1 collective-permute-start.7
  113.4 0.1 constant_dynamic-slice_fusion
  113.5 0.1 copy.23
  113.5 26.8 %collective-permute-done.7.rest_1_ = f32[17,64,128]{2,1,0:T(8,128)S(1)} collective-permute-done((f32[17,64,128]{2,1,0:T(8,128)S(1)}, f32[17,64,128]{2,1,0:T(8,128)S(1)}, u32[]{:S(2)}, u32[]{:S(2)}) %collective-permute-start.7) | collective-permute-done | bytes 557088 | tf_op jit(solution)/shard_map/ppermute | solution.py:489
  140.3 5.6 %shard_map.108 = (f32[16,64,128]{2,1,0:T(8,128)S(1)}, f32[4,4,2,16,128]{4,3,2,1,0:T(8,128)}) custom-call(f32[16,528,128]{2,1,0:T(8,128)} %all-to-all-done.spectrum_ref, f32[16,64,128]{2,1,0:T(8,128)S(1)} %constant_dynamic-update-slice_fusion.basis_ref, f32[512,64]{1,0:T(8,128)S(1)} %get-tuple-element.32.middle_ref, ...), custom_call_target="tpu_custom_call" | custom-call | flops 1107296256 | bytes 4325376 | tf_op jit(solution)/shard_map/pallas_call | solution.py:469
  145.9 3.5 %all-to-all-start.1 = ((f32[16,2,16,128]{3,2,1,0:T(8,128)}), f32[16,2,16,128]{3,2,1,0:T(8,128)S(1)}, u32[]{:S(2)}, u32[]{:S(2)}) async-start(f32[16,2,16,128]{3,2,1,0:T(8,128)} %bitcast.28), calls=%async_computation.1 | async-start | bytes 524288 | tf_op jit(solution)/shard_map/all_to_all | solution.py:583
  149.5 0.1 fusion.1
  149.6 0.1 slice.183
  149.7 0.1 slice.161
  149.8 0.9 copy_bitcast_fusion
  150.7 5.8 %all-to-all-done.1 = f32[16,2,16,128]{3,2,1,0:T(8,128)S(1)} async-done(((f32[16,2,16,128]{3,2,1,0:T(8,128)}), f32[16,2,16,128]{3,2,1,0:T(8,128)S(1)}, u32[]{:S(2)}, u32[]{:S(2)}) %all-to-all-start.1) | async-done | bytes 262176 | tf_op jit(solution)/shard_map/all_to_all | solution.py:583
  156.6 0.6 fusion.4
  (31 shorter events, 0.3 us)
Async XLA Ops:
  1.5 19.3 %collective-permute-start = (f32[256,128]{1,0:T(8,128)S(1)}, f32[256,128]{1,0:T(8,128)S(1)}, u32[]{:S(2)}, u32[]{:S(2)}) collective-permute-start(f32[256,128]{1,0:T(8,128)S(1)} %bitcast.114), channel_id=1, source_target_pairs={{8,0},{9,1},{10,2},{11,3},{12,4},{13,5},{14,6},{15,7},{16,8},{17,9... | collective-permute-start | bytes 393224 | tf_op jit(solution)/shard_map/ppermute | solution.py:525
  2.8 23.1 %collective-permute-start.1 = (f32[64,1024]{1,0:T(8,128)}, f32[64,1024]{1,0:T(8,128)S(1)}, u32[]{:S(2)}, u32[]{:S(2)}) collective-permute-start(f32[64,1024]{1,0:T(8,128)} %param.10), channel_id=1, source_target_pairs={{0,4},{4,0},{1,5},{5,1},{2,6},{6,2},{3,7},{7,3},{8,12},{12,8},{9,1... | collective-permute-start | bytes 786440 | tf_op jit(solution)/shard_map/ppermute | solution.py:489
  9.3 11.6 %copy-start.1 = (f32[16,128]{1,0:T(8,128)S(1)}, f32[16,128]{1,0:T(8,128)}, u32[]{:S(2)}) copy-start(f32[16,128]{1,0:T(8,128)} %activity_ref.1) | copy-start | bytes 24580
  23.9 2.1 %copy-start = (f32[16,528,128]{2,1,0:T(8,128)}, f32[16,528,128]{2,1,0:T(8,128)S(1)}, u32[]{:S(2)}) copy-start(f32[16,528,128]{2,1,0:T(8,128)S(1)} %shard_map.105) | copy-start | bytes 12976132
  26.0 5.0 %copy-start.2 = (f32[64,1024]{1,0:T(8,128)S(1)}, f32[64,1024]{1,0:T(8,128)}, u32[]{:S(2)}) copy-start(f32[64,1024]{1,0:T(8,128)} %param.10) | copy-start | bytes 786436
  26.0 60.6 %all-to-all-start = ((f32[16,528,128]{2,1,0:T(8,128)}), f32[16,528,128]{2,1,0:T(8,128)}, u32[]{:S(2)}, u32[]{:S(2)}) async-start(f32[16,528,128]{2,1,0:T(8,128)} %copy-done), calls=%async_computation | async-start | bytes 8650752 | tf_op jit(solution)/shard_map/all_to_all | solution.py:531
  91.5 3.2 %collective-permute-start.2 = (f32[136,128]{1,0:T(8,128)S(1)}, f32[136,128]{1,0:T(8,128)S(1)}, u32[]{:S(2)}, u32[]{:S(2)}) collective-permute-start(f32[136,128]{1,0:T(8,128)S(1)} %get-tuple-element.31), channel_id=1, source_target_pairs={{0,8},{8,0},{16,24},{24,16},{1,9},{9,1},{17,25},{25,17},{2,10},{10... | collective-permute-start | bytes 208904 | tf_op jit(solution)/shard_map/ppermute | solution.py:489
  94.7 4.5 %collective-permute-start.3 = (f32[136,128]{1,0:T(8,128)S(1)}, f32[136,128]{1,0:T(8,128)S(1)}, u32[]{:S(2)}, u32[]{:S(2)}) collective-permute-start(f32[136,128]{1,0:T(8,128)S(1)} %add.86), channel_id=1, source_target_pairs={{0,16},{8,24},{16,0},{24,8},{1,17},{9,25},{17,1},{25,9},{2,18},{10... | collective-permute-start | bytes 208904 | tf_op jit(solution)/shard_map/ppermute | solution.py:489
  99.2 4.4 %collective-permute-start.4 = (f32[136,128]{1,0:T(8,128)S(1)}, f32[136,128]{1,0:T(8,128)S(1)}, u32[]{:S(2)}, u32[]{:S(2)}) collective-permute-start(f32[136,128]{1,0:T(8,128)S(1)} %add.87), channel_id=1, source_target_pairs={{0,1},{1,0},{2,3},{3,2},{4,5},{5,4},{6,7},{7,6},{8,9},{9,8},{10,11... | collective-permute-start | bytes 208904 | tf_op jit(solution)/shard_map/ppermute | solution.py:489
  103.6 4.4 %collective-permute-start.5 = (f32[136,128]{1,0:T(8,128)S(1)}, f32[136,128]{1,0:T(8,128)S(1)}, u32[]{:S(2)}, u32[]{:S(2)}) collective-permute-start(f32[136,128]{1,0:T(8,128)S(1)} %add.88), channel_id=1, source_target_pairs={{0,2},{1,3},{2,0},{3,1},{4,6},{5,7},{6,4},{7,5},{8,10},{9,11},{10,... | collective-permute-start | bytes 208904 | tf_op jit(solution)/shard_map/ppermute | solution.py:489
  108.0 1.3 collective-permute-start.6
  113.3 27.0 %collective-permute-start.7 = (f32[17,64,128]{2,1,0:T(8,128)S(1)}, f32[17,64,128]{2,1,0:T(8,128)S(1)}, u32[]{:S(2)}, u32[]{:S(2)}) collective-permute-start(f32[17,64,128]{2,1,0:T(8,128)S(1)} %get-tuple-element.33.rest_0_), channel_id=1, source_target_pairs={{0,4},{4,0},{1,5},{5,1},{2,6},{6,2},{3,7},{7,3},{8,12},{12,8},{9,1... | collective-permute-start | bytes 1671176 | tf_op jit(solution)/shard_map/ppermute | solution.py:489
  145.9 10.6 %all-to-all-start.1 = ((f32[16,2,16,128]{3,2,1,0:T(8,128)}), f32[16,2,16,128]{3,2,1,0:T(8,128)S(1)}, u32[]{:S(2)}, u32[]{:S(2)}) async-start(f32[16,2,16,128]{3,2,1,0:T(8,128)} %bitcast.28), calls=%async_computation.1 | async-start | bytes 524288 | tf_op jit(solution)/shard_map/all_to_all | solution.py:583

commit v5 on v4

--- a/solution.py
+++ b/solution.py
@@ -105,7 +105,7 @@
     return lax.dot_general(left, right, NT, preferred_element_type=jnp.float32)
 
 
-def transform_group(hop_rows, base, stride, places, per_member, table_refs, out_ref, parts_ref, middle_ref, ready):
+def transform_group(hop_rows, places, per_member, table_refs, out_ref, parts_ref, middle_ref, ready):
     window_ref, first_ref, twiddle_ref, rows_ref, second_ref, mirrored_ref = table_refs
     half = SPLIT // 2
     middle_ref[...] = jnp.zeros_like(middle_ref)
@@ -168,9 +168,7 @@
                     ):
                         stop += 1
                     member, row = divmod(place, per_member)
-                    out_ref[member, pl.ds(row * stride + base + g, stop - start, stride=stride), :] = block[
-                        start:stop
-                    ]
+                    out_ref[member, pl.ds(row * GROUP + g, stop - start, stride=GROUP), :] = block[start:stop]
                     start = stop
 
 
@@ -178,7 +176,7 @@
     places, per_member, frames, samples_ref, *rest
 ):
     table_refs, (out_ref, tail_ref) = rest[:6], rest[6:8]
-    copies_ref, (hops_ref, parts_ref, middle_ref, sem_ref) = rest[8:14], rest[14:]
+    copies_ref, (hops_ref, parts_ref, middle_ref, group_ref, sem_ref, out_sem_ref) = rest[8:14], rest[14:]
     groups = frames // GROUP - 1
     group_rows = GROUP * HOP_ROWS
     half = SPLIT // 2
@@ -218,24 +216,34 @@
 
         transform_group(
             lambda hop, side: hops_ref[pl.ds(first + hop * HOP_ROWS + side, half, stride=2), :],
-            i * GROUP,
-            frames,
             places,
             per_member,
             copies_ref,
-            out_ref,
+            group_ref.at[i],
             parts_ref,
             middle_ref,
             ready,
         )
+        send(i).start()
         return carry
+
+    def send(i):
+        count = group_ref.shape[2]
+        return pltpu.make_async_copy(
+            group_ref.at[i],
+            out_ref.at[:, pl.ds(pl.multiple_of(i * count, count), count), :],
+            out_sem_ref.at[i],
+        )
 
     lax.fori_loop(0, groups, body, 0)
     tail.wait()
+    for i in range(groups):
+        send(i).wait()
 
 
 def late_kernel(places, per_member, frames, tail_ref, trailing_ref, activity_ref, *rest):
-    table_refs, (_, out_ref, parts_ref, middle_ref) = rest[:6], rest[6:]
+    table_refs, (_, out_ref, parts_ref, middle_ref, group_ref, sem_ref) = rest[:6], rest[6:]
+    count = per_member * GROUP
 
     def hop_rows(hop, side):
         if hop == GROUP:
@@ -243,19 +251,21 @@
         return tail_ref[pl.ds(hop * HOP_ROWS + side, SPLIT // 2, stride=2), :]
 
     for member in range(out_ref.shape[0]):
-        out_ref[member, per_member * frames :, :] = activity_ref[...]
+        group_ref[member, count:, :] = activity_ref[...]
     transform_group(
         hop_rows,
-        frames - GROUP,
-        frames,
         places,
         per_member,
         table_refs,
-        out_ref,
+        group_ref,
         parts_ref,
         middle_ref,
         lambda: None,
     )
+    first = (frames // GROUP - 1) * count
+    send = pltpu.make_async_copy(group_ref, out_ref.at[:, pl.ds(first, group_ref.shape[1]), :], sem_ref)
+    send.start()
+    send.wait()
 
 
 def spectrum_blocks(samples, trailing, activity, unit_order, members):
@@ -264,7 +274,9 @@
     frames = samples.shape[0] // HOP_ROWS
     groups = frames // GROUP - 1
     constants = [jnp.asarray(t) for t in values]
-    out_shape = jax.ShapeDtypeStruct((members, per_member * frames + activity.shape[0], LANES), jnp.float32)
+    group_shape = (members, per_member * GROUP, LANES)
+    last_shape = (members, per_member * GROUP + activity.shape[0], LANES)
+    out_shape = pltpu.HBM((members, per_member * frames + activity.shape[0], LANES), jnp.float32)
     tail_shape = jax.ShapeDtypeStruct((GROUP * HOP_ROWS, LANES), jnp.float32)
     in_vmem = pl.BlockSpec(memory_space=pltpu.VMEM)
     in_hbm = pl.BlockSpec(memory_space=pltpu.HBM)
@@ -286,19 +298,23 @@
     early, tail, *copies = pl.pallas_call(
         functools.partial(early_kernel, places, per_member, frames),
         in_specs=[in_hbm] * (1 + len(constants)),
-        out_specs=[in_vmem] * (2 + len(constants)),
+        out_specs=[in_hbm] + [in_vmem] * (1 + len(constants)),
         out_shape=[out_shape, tail_shape] + [jax.ShapeDtypeStruct(t.shape, t.dtype) for t in constants],
         scratch_shapes=[pltpu.VMEM(((groups * GROUP + 1) * HOP_ROWS, LANES), jnp.float32)]
         + scratch
-        + [pltpu.SemaphoreType.DMA((8 + groups,))],
+        + [
+            pltpu.VMEM((groups, *group_shape), jnp.float32),
+            pltpu.SemaphoreType.DMA((8 + groups,)),
+            pltpu.SemaphoreType.DMA((groups,)),
+        ],
         **settings(groups),
     )(*[pltpu.with_memory_space_constraint(value, pltpu.HBM) for value in (samples, *constants)])
     return pl.pallas_call(
         functools.partial(late_kernel, places, per_member, frames),
-        in_specs=[in_vmem] * (4 + len(constants)),
-        out_specs=in_vmem,
+        in_specs=[in_vmem] * (3 + len(constants)) + [in_hbm],
+        out_specs=in_hbm,
         out_shape=out_shape,
-        scratch_shapes=scratch,
+        scratch_shapes=scratch + [pltpu.VMEM(last_shape, jnp.float32), pltpu.SemaphoreType.DMA],
         input_output_aliases={3 + len(constants): 0},
         **settings(1),
     )(tail, trailing, activity, *copies, early)
@@ -311,13 +327,21 @@
 
 def ratio_of(spectrum_ref, start, activity_lanes, basis):
     frames = activity_lanes.shape[0]
-    local = frames // spectrum_ref.shape[0]
+    members = spectrum_ref.shape[0]
+    groups = frames // (members * GROUP)
+    stride = spectrum_ref.shape[1] // groups
     splits = [split_values(block) for block in basis]
     stacked = jnp.concatenate([jnp.concatenate([h, l, h, l], 0) for h, l in splits], 1)
     approx = dot(activity_lanes, stacked)
     values = jnp.concatenate(
         [
-            spectrum_ref[:, (start + row) * local : (start + row + 1) * local, :].reshape(frames, LANES)
+            jnp.stack(
+                [
+                    spectrum_ref[:, pl.ds(group * stride + (start + row) * GROUP, GROUP), :]
+                    for group in range(groups)
+                ],
+                1,
+            ).reshape(frames, LANES)
             for row in range(len(basis))
         ],
         1,
@@ -355,28 +379,61 @@
     return jnp.concatenate([values[:, :half], values[:, half:]], 0)
 
 
-def gathered_activity(spectrum_ref, shape):
+def gathered_activity(rows_ref, shape):
     subs, members, ranks, width = shape
     local = width // subs
     frames_in = width // LANES
-    first = spectrum_ref.shape[1] - ranks * frames_in
     pieces = {}
     for member in range(members):
         for part in range(frames_in):
-            start = first + part * ranks
-            rows = [spectrum_ref[sub * members + member, start : start + ranks, :] for sub in range(subs)]
+            start = part * ranks
+            rows = [rows_ref[sub * members + member, start : start + ranks, :] for sub in range(subs)]
             block = jnp.transpose(jnp.concatenate(rows, 0))
             for place in range(LANES // local):
                 pieces[part * (LANES // local) + place, member] = block[place * local : (place + 1) * local]
     return jnp.concatenate([pieces[sub, member] for sub in range(subs) for member in range(members)], 0)
 
 
-def first_kernel(shape, side_ref, spectrum_ref, basis_ref, mine_ref, other_ref, activity_ref, lanes_ref, total_ref):
-    activity = gathered_activity(spectrum_ref, shape)
+def first_kernel(
+    shape,
+    side_ref,
+    received_ref,
+    basis_ref,
+    mine_ref,
+    other_ref,
+    activity_ref,
+    spectrum_ref,
+    lanes_ref,
+    total_ref,
+    rows_ref,
+    sem_ref,
+):
+    per_member = basis_ref.shape[0]
+    count = spectrum_ref.shape[1]
+    groups = count // (per_member * GROUP)
+    steps = row_steps(per_member)
+
+    def fetch(step, group):
+        place = pl.ds((group * per_member + steps[step][0]) * GROUP, len(steps[step]) * GROUP)
+        return pltpu.make_async_copy(
+            received_ref.at[:, place, :], spectrum_ref.at[:, place, :], sem_ref.at[1 + step * groups + group]
+        )
+
+    rows_copy = pltpu.make_async_copy(
+        received_ref.at[:, pl.ds(count, rows_ref.shape[1]), :], rows_ref, sem_ref.at[0]
+    )
+    rows_copy.start()
+    copies = [[fetch(step, group) for group in range(groups)] for step in range(len(steps))]
+    for copy in sum(copies, []):
+        copy.start()
+    rows_copy.wait()
+    activity = gathered_activity(rows_ref, shape)
     activity_ref[...] = activity
     lanes_ref[...] = lanes_of_activity(activity)
     sums = 0.0
-    for step, rows in enumerate(row_steps(basis_ref.shape[0])):
+    for step, rows in enumerate(steps):
+        for copy in copies[step]:
+            copy.wait()
         ratio, basis = ratio_of(spectrum_ref, rows[0], lanes_ref[...], [basis_ref[row] for row in rows])
         part = for_activity(ratio, basis)
         if step == 0:
@@ -463,13 +520,16 @@
         out_ref[:, member, 1] = sums
 
 
-def update_call(kernel, spectrum, out_shapes, scratch, operands, scalars=()):
+def update_call(kernel, spectrum, out_shapes, scratch, operands, scalars=(), place=pltpu.VMEM):
     in_vmem = pl.BlockSpec(memory_space=pltpu.VMEM)
+    if place == pltpu.HBM:
+        spectrum = pltpu.with_memory_space_constraint(spectrum, place)
     rank = operands[0].shape[1]
     return pl.pallas_call(
         kernel,
         in_specs=[pl.BlockSpec(memory_space=pltpu.SMEM) for _ in scalars]
-        + [in_vmem for _ in range(1 + len(operands))],
+        + [pl.BlockSpec(memory_space=place)]
+        + [in_vmem for _ in operands],
         out_specs=[in_vmem for _ in out_shapes],
         out_shape=[jax.ShapeDtypeStruct(shape, jnp.float32) for shape in out_shapes],
         scratch_shapes=scratch,
@@ -490,9 +550,11 @@
 
 
 def sum_over(value, axis, mask):
-    while mask < lax.axis_size(axis):
-        value = value + swap_by(value, axis, mask)
-        mask *= 2
+    count = lax.axis_size(axis)
+    while mask < count:
+        masks = [mask] if 2 * mask >= count else [mask, 2 * mask, 3 * mask]
+        value = sum([swap_by(value, axis, m) for m in masks], value)
+        mask *= 2 if len(masks) == 1 else 4
     return value
 
 
@@ -549,13 +611,22 @@
     total_scratch = pltpu.VMEM((frames, 2 * rank), jnp.float32)
     half_shape = (frames // 4 + 8, 2 * rank)
     side = (me_sub % 2).astype(jnp.int32).reshape(1)
-    mine, other, activity = update_call(
+    extra = ranks_here * width // LANES
+    spectrum_rows = spectrum.shape[1] - extra
+    row_groups = spectrum_rows // (per_member * GROUP)
+    mine, other, activity, spectrum = update_call(
         functools.partial(first_kernel, (subs, members, ranks_here, width)),
         spectrum,
-        [half_shape, half_shape, (frames, rank)],
-        [lanes_scratch, total_scratch],
+        [half_shape, half_shape, (frames, rank), (partners, spectrum_rows, LANES)],
+        [
+            lanes_scratch,
+            total_scratch,
+            pltpu.VMEM((partners, extra, LANES), jnp.float32),
+            pltpu.SemaphoreType.DMA((1 + len(row_steps(per_member)) * row_groups,)),
+        ],
         (basis,),
         (side,),
+        pltpu.HBM,
     )
     mine = mine + swap_by(other, "freq", 1)
     mine = sum_over(mine, "freq", 2)

time: 158 us -> 153 us (0.968)
  waiting for transfers between devices: 101 us -> 96.4 us
  Pallas kernels: 29 us -> 24.5 us
  starting transfers between devices: 20.4 us -> 23.2 us
  local copies, waits for them, and re-layouts: 3.95 us -> 6 us
    pallas_call x3, Pallas kernels: 14.5 us -> 9.44 us  [update_call(): pl.pallas_call(kernel, in_specs=[pl.BlockSpec(memory_space=pltpu.SMEM) fo...]
    ppermute x7 -> x8, waiting for transfers between devices: 40.4 us -> 36 us  [swap_by(): return lax.ppermute(value, axis, [(i, i ^ mask) for i in range(count)])]
    ppermute x7 -> x8, starting transfers between devices: 10.7 us -> 13.5 us  [swap_by(): return lax.ppermute(value, axis, [(i, i ^ mask) for i in range(count)])]
    unnamed x25 -> x27, local copies, waits for them, and re-layouts: 2.18 us -> 4.24 us
  transfers between devices with their start and end apart: 10 -> 11, of which waited for: 8 -> 8; matrix products, arithmetic and copies ran while one was open for 1% -> 1% of each run, Pallas kernels for 9% -> 10%
where the time goes in v5:
time: 153 us
  waiting for transfers between devices  96.4 us (63%)
  Pallas kernels  24.5 us (16%)
  starting transfers between devices  23.2 us (15%)
  local copies, waits for them, and re-layouts  6 us (4%)
  other arithmetic  1.98 us (1%)
    all_to_all x1, waiting for transfers between devices, on_device(): spectrum = lax.all_to_all(spectrum, exchange, 0, 0, tiled=True)  54.7 us
    ppermute x8, waiting for transfers between devices, swap_by(): return lax.ppermute(value, axis, [(i, i ^ mask) for i in range(count)])  36 us
    ppermute x8, starting transfers between devices, swap_by(): return lax.ppermute(value, axis, [(i, i ^ mask) for i in range(count)])  13.5 us
    pallas_call x1, Pallas kernels, spectrum_blocks(): pl.pallas_call(functools.partial(early_kernel, places, per_member, frames...  11.4 us
    pallas_call x3, Pallas kernels, update_call(): pl.pallas_call(kernel, in_specs=[pl.BlockSpec(memory_space=pltpu.SMEM) fo...  9.44 us
    all_to_all x1, waiting for transfers between devices, on_device(): lax.all_to_all(payload.reshape(partners, 2, ranks_here, width), exchange,...  5.83 us
    all_to_all x1, starting transfers between devices, on_device(): spectrum = lax.all_to_all(spectrum, exchange, 0, 0, tiled=True)  4.86 us
    unnamed x27, local copies, waits for them, and re-layouts  4.24 us
  transfers between devices with their start and end apart: 11, of which 8 were waited for; matrix products, arithmetic and copies ran while one was open for 1% of the time, Pallas kernels for 10%

profile of v5, /device:TPU:0, one launch (start us, length us, event | category | flops | bytes accessed | tf_op | source)
XLA Modules:
  0.0 153.1 jit_solution(17005004059066136047)
XLA Ops:
  0.6 0.9 slice.126
  1.5 1.3 collective-permute-start
  2.8 6.5 %collective-permute-start.1 = (f32[64,1024]{1,0:T(8,128)}, f32[64,1024]{1,0:T(8,128)S(1)}, u32[]{:S(2)}, u32[]{:S(2)}) collective-permute-start(f32[64,1024]{1,0:T(8,128)} %param.10), channel_id=1, source_target_pairs={{0,4},{4,0},{1,5},{5,1},{2,6},{6,2},{3,7},{7,3},{8,12},{12,8},{9,1... | collective-permute-start | bytes 786440 | tf_op jit(solution)/shard_map/ppermute | solution.py:549
  9.3 0.0 copy-start.2
  9.3 11.4 %shard_map.104 = (f32[16,528,128]{2,1,0:T(8,128)}, f32[2048,128]{1,0:T(8,128)S(1)}, f32[2,256,128]{2,1,0:T(8,128)S(1)}, bf16[256,768]{1,0:T(8,128)(2,1)S(1)}, f3...) custom-call(f32[8192,128]{1,0:T(8,128)} %bitcast.115, ...), custom_call_target="tpu_custom_call" | custom-call | flops 4831838208 | bytes 6291456 | tf_op jit(solution)/shard_map/pallas_call | solution.py:298
  20.8 0.0 collective-permute-done.trailing_ref
  20.8 0.0 copy-done.2
  20.8 3.6 %shard_map.105 = f32[16,528,128]{2,1,0:T(8,128)} custom-call(f32[2048,128]{1,0:T(8,128)S(1)} %get-tuple-element.20.tail_ref, f32[256,128]{1,0:T(8,128)S(1)} %collective-permute-done.trailing_ref, f32[16,128]{1,0:T(8,128)S(1)} %copy-done.2, f32[2,256,128]{2,1,0:T(8,128)S(1)} %get-tuple-element.21.rest_0_, ...), custom_call_target="tpu_custom_call", output_to_operand_aliasing={{}: (9, {})} | custom-call | flops 1610612736 | bytes 2097152 | tf_op jit(solution)/shard_map/pallas_call | solution.py:312
  24.4 0.0 copy-start.3
  24.4 0.0 collective-permute-done.1
  24.5 4.9 %all-to-all-start = ((f32[16,528,128]{2,1,0:T(8,128)}), f32[16,528,128]{2,1,0:T(8,128)}, u32[]{:S(2)}, u32[]{:S(2)}) async-start(f32[16,528,128]{2,1,0:T(8,128)} %shard_map.105), calls=%async_computation | async-start | bytes 8650752 | tf_op jit(solution)/shard_map/all_to_all | solution.py:593
  29.4 0.1 fusion.6
  29.4 0.0 copy-done.3
  29.5 0.2 slice.163
  29.7 0.2 slice.130
  29.9 0.2 maximum_select_fusion.1
  30.4 54.7 %all-to-all-done.received_ref = f32[16,528,128]{2,1,0:T(8,128)} async-done(((f32[16,528,128]{2,1,0:T(8,128)}), f32[16,528,128]{2,1,0:T(8,128)}, u32[]{:S(2)}, u32[]{:S(2)}) %all-to-all-start) | async-done | bytes 4325408 | tf_op jit(solution)/shard_map/all_to_all | solution.py:593
  85.1 4.4 %shard_map.106 = (f32[136,128]{1,0:T(8,128)S(1)}, f32[136,128]{1,0:T(8,128)S(1)}, f32[512,64]{1,0:T(8,128)S(1)}, f32[16,512,128]{2,1,0:T(8,128)S(1)}) custom-call(s32[1]{0:T(128)} %bitcast.side_ref, f32[16,528,128]{2,1,0:T(8,128)} %all-to-all-done.received_ref, f32[16,64,128]{2,1,0:T(8,128)S(1)} %constant_dynamic-update-slice_fusion.basis_ref), custom_call_target="tpu_custom_call" | custom-call | flops 1107296256 | bytes 4325376 | tf_op jit(solution)/shard_map/pallas_call | solution.py:528
  89.4 2.3 %collective-permute-start.2 = (f32[136,128]{1,0:T(8,128)S(1)}, f32[136,128]{1,0:T(8,128)S(1)}, u32[]{:S(2)}, u32[]{:S(2)}) collective-permute-start(f32[136,128]{1,0:T(8,128)S(1)} %get-tuple-element.33), channel_id=1, source_target_pairs={{0,8},{8,0},{16,24},{24,16},{1,9},{9,1},{17,25},{25,17},{2,10},{10... | collective-permute-start | bytes 208904 | tf_op jit(solution)/shard_map/ppermute | solution.py:549
  91.7 0.9 collective-permute-done.2
  92.6 1.1 collective-permute-start.3
  93.7 3.4 %collective-permute-done.3 = f32[136,128]{1,0:T(8,128)S(1)} collective-permute-done((f32[136,128]{1,0:T(8,128)S(1)}, f32[136,128]{1,0:T(8,128)S(1)}, u32[]{:S(2)}, u32[]{:S(2)}) %collective-permute-start.3) | collective-permute-done | bytes 69664 | tf_op jit(solution)/shard_map/ppermute | solution.py:549
  97.1 0.6 collective-permute-start.4
  97.8 0.0 collective-permute-start.5
  97.8 2.9 %collective-permute-start.6 = (f32[136,128]{1,0:T(8,128)S(1)}, f32[136,128]{1,0:T(8,128)S(1)}, u32[]{:S(2)}, u32[]{:S(2)}) collective-permute-start(f32[136,128]{1,0:T(8,128)S(1)} %add.90), channel_id=1, source_target_pairs={{0,3},{1,2},{2,1},{3,0},{4,7},{5,6},{6,5},{7,4},{8,11},{9,10},{10,... | collective-permute-start | bytes 208904 | tf_op jit(solution)/shard_map/ppermute | solution.py:549
  100.7 1.6 %collective-permute-done.4 = f32[136,128]{1,0:T(8,128)S(1)} collective-permute-done((f32[136,128]{1,0:T(8,128)S(1)}, f32[136,128]{1,0:T(8,128)S(1)}, u32[]{:S(2)}, u32[]{:S(2)}) %collective-permute-start.4) | collective-permute-done | bytes 69664 | tf_op jit(solution)/shard_map/ppermute | solution.py:549
  102.2 0.0 collective-permute-done.5
  102.3 1.5 collective-permute-done.6
  103.7 0.1 collective-permute-start.7
  103.8 1.2 collective-permute-done.7.other_ref
  105.1 1.7 %shard_map.107 = (f32[512,64]{1,0:T(8,128)S(1)}, f32[17,64,128]{2,1,0:T(8,128)S(1)}) custom-call(s32[1]{0:T(128)} %bitcast.side_ref, f32[16,512,128]{2,1,0:T(8,128)S(1)} %get-tuple-element.30.spectrum_ref, f32[16,64,128]{2,1,0:T(8,128)S(1)} %constant_dynamic-update-slice_fusion.basis_ref, f32[512,64]{1,0:T(8,128)S(1)} %get-tuple-element.31.activity_ref, ...), custom_call_target="tpu_custom_call" | custom-call | flops 1073741824 | bytes 4194304 | tf_op jit(solution)/shard_map/pallas_call | solution.py:528
  106.8 0.0 copy-start
  106.8 1.9 %copy-done = f32[16,512,128]{2,1,0:T(8,128)} copy-done((f32[16,512,128]{2,1,0:T(8,128)}, f32[16,512,128]{2,1,0:T(8,128)S(1)}, u32[]{:S(2)}) %copy-start) | copy-done | bytes 4194328
  108.7 0.0 collective-permute-start.8
  108.8 0.1 constant_dynamic-slice_fusion
  108.8 0.1 copy.23
  108.9 27.4 %collective-permute-done.8.rest_1_ = f32[17,64,128]{2,1,0:T(8,128)S(1)} collective-permute-done((f32[17,64,128]{2,1,0:T(8,128)S(1)}, f32[17,64,128]{2,1,0:T(8,128)S(1)}, u32[]{:S(2)}, u32[]{:S(2)}) %collective-permute-start.8) | collective-permute-done | bytes 557088 | tf_op jit(solution)/shard_map/ppermute | solution.py:549
  136.2 0.0 copy-start.1
  136.3 2.2 %copy-done.1 = f32[16,512,128]{2,1,0:T(8,128)S(1)} copy-done((f32[16,512,128]{2,1,0:T(8,128)S(1)}, f32[16,512,128]{2,1,0:T(8,128)}, u32[]{:S(2)}) %copy-start.1) | copy-done | bytes 4194328
  138.4 3.4 %shard_map.108 = (f32[16,64,128]{2,1,0:T(8,128)S(1)}, f32[4,4,2,16,128]{4,3,2,1,0:T(8,128)}) custom-call(f32[16,512,128]{2,1,0:T(8,128)S(1)} %copy-done.1, f32[16,64,128]{2,1,0:T(8,128)S(1)} %constant_dynamic-update-slice_fusion.basis_ref, f32[512,64]{1,0:T(8,128)S(1)} %get-tuple-element.34.middle_ref, f32[17,64,128]{2,1,0:T(8,128)S(1)} %get-tuple-element.35.rest_0_, ...), custom_call_target="tpu_custom_call" | custom-call | flops 1073741824 | bytes 4194304 | tf_op jit(solution)/shard_map/pallas_call | solution.py:528
  141.8 3.5 %all-to-all-start.1 = ((f32[16,2,16,128]{3,2,1,0:T(8,128)}), f32[16,2,16,128]{3,2,1,0:T(8,128)S(1)}, u32[]{:S(2)}, u32[]{:S(2)}) async-start(f32[16,2,16,128]{3,2,1,0:T(8,128)} %bitcast.28), calls=%async_computation.1 | async-start | bytes 524288 | tf_op jit(solution)/shard_map/all_to_all | solution.py:654
  145.4 0.1 fusion.1
  145.5 0.1 slice.183
  145.6 0.1 slice.161
  145.8 0.9 copy_bitcast_fusion
  146.6 5.8 %all-to-all-done.1 = f32[16,2,16,128]{3,2,1,0:T(8,128)S(1)} async-done(((f32[16,2,16,128]{3,2,1,0:T(8,128)}), f32[16,2,16,128]{3,2,1,0:T(8,128)S(1)}, u32[]{:S(2)}, u32[]{:S(2)}) %all-to-all-start.1) | async-done | bytes 262176 | tf_op jit(solution)/shard_map/all_to_all | solution.py:654
  152.5 0.6 fusion.4
  (30 shorter events, 0.3 us)
Async XLA Ops:
  1.5 19.2 %collective-permute-start = (f32[256,128]{1,0:T(8,128)S(1)}, f32[256,128]{1,0:T(8,128)S(1)}, u32[]{:S(2)}, u32[]{:S(2)}) collective-permute-start(f32[256,128]{1,0:T(8,128)S(1)} %bitcast.114), channel_id=1, source_target_pairs={{8,0},{9,1},{10,2},{11,3},{12,4},{13,5},{14,6},{15,7},{16,8},{17,9... | collective-permute-start | bytes 393224 | tf_op jit(solution)/shard_map/ppermute | solution.py:587
  2.8 21.6 %collective-permute-start.1 = (f32[64,1024]{1,0:T(8,128)}, f32[64,1024]{1,0:T(8,128)S(1)}, u32[]{:S(2)}, u32[]{:S(2)}) collective-permute-start(f32[64,1024]{1,0:T(8,128)} %param.10), channel_id=1, source_target_pairs={{0,4},{4,0},{1,5},{5,1},{2,6},{6,2},{3,7},{7,3},{8,12},{12,8},{9,1... | collective-permute-start | bytes 786440 | tf_op jit(solution)/shard_map/ppermute | solution.py:549
  9.3 11.4 %copy-start.2 = (f32[16,128]{1,0:T(8,128)S(1)}, f32[16,128]{1,0:T(8,128)}, u32[]{:S(2)}) copy-start(f32[16,128]{1,0:T(8,128)} %activity_ref.1) | copy-start | bytes 24580
  24.4 5.0 %copy-start.3 = (f32[64,1024]{1,0:T(8,128)S(1)}, f32[64,1024]{1,0:T(8,128)}, u32[]{:S(2)}) copy-start(f32[64,1024]{1,0:T(8,128)} %param.10) | copy-start | bytes 786436
  24.5 60.6 %all-to-all-start = ((f32[16,528,128]{2,1,0:T(8,128)}), f32[16,528,128]{2,1,0:T(8,128)}, u32[]{:S(2)}, u32[]{:S(2)}) async-start(f32[16,528,128]{2,1,0:T(8,128)} %shard_map.105), calls=%async_computation | async-start | bytes 8650752 | tf_op jit(solution)/shard_map/all_to_all | solution.py:593
  89.4 3.2 %collective-permute-start.2 = (f32[136,128]{1,0:T(8,128)S(1)}, f32[136,128]{1,0:T(8,128)S(1)}, u32[]{:S(2)}, u32[]{:S(2)}) collective-permute-start(f32[136,128]{1,0:T(8,128)S(1)} %get-tuple-element.33), channel_id=1, source_target_pairs={{0,8},{8,0},{16,24},{24,16},{1,9},{9,1},{17,25},{25,17},{2,10},{10... | collective-permute-start | bytes 208904 | tf_op jit(solution)/shard_map/ppermute | solution.py:549
  92.6 4.5 %collective-permute-start.3 = (f32[136,128]{1,0:T(8,128)S(1)}, f32[136,128]{1,0:T(8,128)S(1)}, u32[]{:S(2)}, u32[]{:S(2)}) collective-permute-start(f32[136,128]{1,0:T(8,128)S(1)} %add.89), channel_id=1, source_target_pairs={{0,16},{8,24},{16,0},{24,8},{1,17},{9,25},{17,1},{25,9},{2,18},{10... | collective-permute-start | bytes 208904 | tf_op jit(solution)/shard_map/ppermute | solution.py:549
  97.1 5.1 %collective-permute-start.4 = (f32[136,128]{1,0:T(8,128)S(1)}, f32[136,128]{1,0:T(8,128)S(1)}, u32[]{:S(2)}, u32[]{:S(2)}) collective-permute-start(f32[136,128]{1,0:T(8,128)S(1)} %add.90), channel_id=1, source_target_pairs={{0,1},{1,0},{2,3},{3,2},{4,5},{5,4},{6,7},{7,6},{8,9},{9,8},{10,11... | collective-permute-start | bytes 208904 | tf_op jit(solution)/shard_map/ppermute | solution.py:549
  97.8 4.5 %collective-permute-start.5 = (f32[136,128]{1,0:T(8,128)S(1)}, f32[136,128]{1,0:T(8,128)S(1)}, u32[]{:S(2)}, u32[]{:S(2)}) collective-permute-start(f32[136,128]{1,0:T(8,128)S(1)} %add.90), channel_id=1, source_target_pairs={{0,2},{1,3},{2,0},{3,1},{4,6},{5,7},{6,4},{7,5},{8,10},{9,11},{10,... | collective-permute-start | bytes 208904 | tf_op jit(solution)/shard_map/ppermute | solution.py:549
  97.8 6.0 %collective-permute-start.6 = (f32[136,128]{1,0:T(8,128)S(1)}, f32[136,128]{1,0:T(8,128)S(1)}, u32[]{:S(2)}, u32[]{:S(2)}) collective-permute-start(f32[136,128]{1,0:T(8,128)S(1)} %add.90), channel_id=1, source_target_pairs={{0,3},{1,2},{2,1},{3,0},{4,7},{5,6},{6,5},{7,4},{8,11},{9,10},{10,... | collective-permute-start | bytes 208904 | tf_op jit(solution)/shard_map/ppermute | solution.py:549
  103.7 1.3 collective-permute-start.7
  106.8 1.9 %copy-start = (f32[16,512,128]{2,1,0:T(8,128)}, f32[16,512,128]{2,1,0:T(8,128)S(1)}, u32[]{:S(2)}) copy-start(f32[16,512,128]{2,1,0:T(8,128)S(1)} %get-tuple-element.30.spectrum_ref) | copy-start | bytes 12582916
  108.7 27.5 %collective-permute-start.8 = (f32[17,64,128]{2,1,0:T(8,128)S(1)}, f32[17,64,128]{2,1,0:T(8,128)S(1)}, u32[]{:S(2)}, u32[]{:S(2)}) collective-permute-start(f32[17,64,128]{2,1,0:T(8,128)S(1)} %get-tuple-element.35.rest_0_), channel_id=1, source_target_pairs={{0,4},{4,0},{1,5},{5,1},{2,6},{6,2},{3,7},{7,3},{8,12},{12,8},{9,1... | collective-permute-start | bytes 1671176 | tf_op jit(solution)/shard_map/ppermute | solution.py:549
  136.2 2.2 %copy-start.1 = (f32[16,512,128]{2,1,0:T(8,128)S(1)}, f32[16,512,128]{2,1,0:T(8,128)}, u32[]{:S(2)}) copy-start(f32[16,512,128]{2,1,0:T(8,128)} %copy-done) | copy-start | bytes 12582916
  141.8 10.6 %all-to-all-start.1 = ((f32[16,2,16,128]{3,2,1,0:T(8,128)}), f32[16,2,16,128]{3,2,1,0:T(8,128)S(1)}, u32[]{:S(2)}, u32[]{:S(2)}) async-start(f32[16,2,16,128]{3,2,1,0:T(8,128)} %bitcast.28), calls=%async_computation.1 | async-start | bytes 524288 | tf_op jit(solution)/shard_map/all_to_all | solution.py:654

commit v6 on v5

--- a/solution.py
+++ b/solution.py
@@ -394,6 +394,23 @@
     return jnp.concatenate([pieces[sub, member] for sub in range(subs) for member in range(members)], 0)
 
 
+def start_fetches(received_ref, spectrum_ref, sem_ref, per_member):
+    count = spectrum_ref.shape[1]
+    groups = count // (per_member * GROUP)
+    copies = []
+    for step, rows in enumerate(row_steps(per_member)):
+        copies.append([])
+        for group in range(groups):
+            place = pl.ds((group * per_member + rows[0]) * GROUP, len(rows) * GROUP)
+            copies[-1].append(
+                pltpu.make_async_copy(
+                    received_ref.at[:, place, :], spectrum_ref.at[:, place, :], sem_ref.at[step * groups + group]
+                )
+            )
+            copies[-1][-1].start()
+    return copies
+
+
 def first_kernel(
     shape,
     side_ref,
@@ -406,26 +423,16 @@
     lanes_ref,
     total_ref,
     rows_ref,
+    rows_sem_ref,
     sem_ref,
 ):
-    per_member = basis_ref.shape[0]
+    steps = row_steps(basis_ref.shape[0])
     count = spectrum_ref.shape[1]
-    groups = count // (per_member * GROUP)
-    steps = row_steps(per_member)
-
-    def fetch(step, group):
-        place = pl.ds((group * per_member + steps[step][0]) * GROUP, len(steps[step]) * GROUP)
-        return pltpu.make_async_copy(
-            received_ref.at[:, place, :], spectrum_ref.at[:, place, :], sem_ref.at[1 + step * groups + group]
-        )
-
     rows_copy = pltpu.make_async_copy(
-        received_ref.at[:, pl.ds(count, rows_ref.shape[1]), :], rows_ref, sem_ref.at[0]
+        received_ref.at[:, pl.ds(count, rows_ref.shape[1]), :], rows_ref, rows_sem_ref
     )
     rows_copy.start()
-    copies = [[fetch(step, group) for group in range(groups)] for step in range(len(steps))]
-    for copy in sum(copies, []):
-        copy.start()
+    copies = start_fetches(received_ref, spectrum_ref, sem_ref, basis_ref.shape[0])
     rows_copy.wait()
     activity = gathered_activity(rows_ref, shape)
     activity_ref[...] = activity
@@ -481,29 +488,38 @@
     turned = jnp.transpose(middle)
     high, low = split_values(turned)
     turned_ref[...] = jnp.concatenate([high, low], 0)
-    totals = jnp.sum(turned, axis=1, keepdims=True)
-    out_ref[out_ref.shape[0] - 1] = jnp.broadcast_to(totals, (rank, LANES))
+    totals = jnp.sum(middle, axis=0, keepdims=True)
+    totals = jnp.broadcast_to(jnp.concatenate([totals] * (LANES // rank), 1), (8, LANES))
+    out_ref[out_ref.shape[0] - 8 :, :] = totals
     for rows in row_steps(basis_ref.shape[0]):
         ratio, _ = ratio_of(spectrum_ref, rows[0], lanes_ref[...], [basis_ref[row] for row in rows])
         high, low = split_values(ratio)
         total = dot(turned_ref[...], high) + dot(turned_ref[...], low)
         total = total[:rank] + total[rank:]
         for place, row in enumerate(rows):
-            out_ref[row] = total[:, place * LANES : (place + 1) * LANES]
-
-
-def third_kernel(spectrum_ref, basis_ref, middle_ref, *rest):
-    new_ref, out_ref, lanes_ref, total_ref = rest[-4:]
-    numerators = rest[:-4]
+            out_ref[row * rank : (row + 1) * rank, :] = total[:, place * LANES : (place + 1) * LANES]
+
+
+def third_kernel(received_ref, basis_ref, middle_ref, *rest):
+    new_ref, out_ref, lanes_ref, total_ref, spectrum_ref, sem_ref = rest[-6:]
+    numerators = rest[:-6]
     rank = middle_ref.shape[1]
     per_member = basis_ref.shape[0]
+    copies = start_fetches(received_ref, spectrum_ref, sem_ref, per_member)
     lanes_ref[...] = lanes_of_activity(middle_ref[...])
-    scale = 1.0 / sum(ref[per_member] for ref in numerators)
+    totals = sum(ref[per_member * rank :, :] for ref in numerators)
+    totals = jnp.transpose(jnp.concatenate([totals] * (LANES // 8), 0))[:rank]
+    scale = 1.0 / totals
     sums = 0.0
     for step, rows in enumerate(row_steps(per_member)):
-        blocks = [basis_ref[row] * (sum(ref[row] for ref in numerators) * scale) for row in rows]
+        blocks = [
+            basis_ref[row] * (sum(ref[row * rank : (row + 1) * rank, :] for ref in numerators) * scale)
+            for row in rows
+        ]
         for row, block in zip(rows, blocks):
             new_ref[row] = block
+        for copy in copies[step]:
+            copy.wait()
         ratio, basis = ratio_of(spectrum_ref, rows[0], lanes_ref[...], blocks)
         part = for_activity(ratio, basis)
         if step == 0:
@@ -614,15 +630,18 @@
     extra = ranks_here * width // LANES
     spectrum_rows = spectrum.shape[1] - extra
     row_groups = spectrum_rows // (per_member * GROUP)
+    fetch_sems = pltpu.SemaphoreType.DMA((len(row_steps(per_member)) * row_groups,))
+    received = spectrum
     mine, other, activity, spectrum = update_call(
         functools.partial(first_kernel, (subs, members, ranks_here, width)),
-        spectrum,
+        received,
         [half_shape, half_shape, (frames, rank), (partners, spectrum_rows, LANES)],
         [
             lanes_scratch,
             total_scratch,
             pltpu.VMEM((partners, extra, LANES), jnp.float32),
-            pltpu.SemaphoreType.DMA((1 + len(row_steps(per_member)) * row_groups,)),
+            pltpu.SemaphoreType.DMA,
+            fetch_sems,
         ],
         (basis,),
         (side,),
@@ -636,7 +655,7 @@
     middle, numerator = update_call(
         second_kernel,
         spectrum,
-        [(frames, rank), (per_member + 1, rank, LANES)],
+        [(frames, rank), (per_member * rank + 8, LANES)],
         [lanes_scratch, pltpu.VMEM((2 * rank, frames), jnp.bfloat16)],
         (basis, activity, mine, other),
         (side,),
@@ -646,15 +665,22 @@
         numerators.append(swap_by(numerator, "group", 1))
     new_basis, payload = update_call(
         third_kernel,
-        spectrum,
+        received,
         [(per_member, rank, LANES), (subs, members, 2, ranks_here, width)],
-        [lanes_scratch, total_scratch],
+        [
+            lanes_scratch,
+            total_scratch,
+            pltpu.VMEM((partners, spectrum_rows, LANES), jnp.float32),
+            fetch_sems,
+        ],
         (basis, middle, *numerators),
-    )
-    received = lax.all_to_all(
+        (),
+        pltpu.HBM,
+    )
+    parts = lax.all_to_all(
         payload.reshape(partners, 2, ranks_here, width), exchange, 0, 0, tiled=True
     )
-    summed = jnp.sum(received, axis=0)
+    summed = jnp.sum(parts, axis=0)
     mine = lax.dynamic_slice(
         middle.reshape(subs, members, local, rank),
         (0, me_member, 0, me_sub * ranks_here),

time: 153 us -> 151 us (0.987)
  local copies, waits for them, and re-layouts: 6 us -> 1.89 us
  Pallas kernels: 24.5 us -> 26.9 us
    unnamed x27 -> x23, local copies, waits for them, and re-layouts: 4.24 us -> 0.13 us
    pallas_call x3, Pallas kernels: 9.44 us -> 11.8 us  [update_call(): pl.pallas_call(kernel, in_specs=[pl.BlockSpec(memory_space=pltpu.SMEM) fo...]
  transfers between devices with their start and end apart: 11 -> 11, of which waited for: 8 -> 8; matrix products, arithmetic and copies ran while one was open for 1% -> 2% of each run, Pallas kernels for 10% -> 10%
where the time goes in v6:
time: 151 us; the launch traced here: 150 us
  waiting for transfers between devices  95.2 us (63%)
  Pallas kernels  26.9 us (18%)
  starting transfers between devices  23.2 us (15%)
  other arithmetic  1.98 us (1%)
  local copies, waits for them, and re-layouts  1.89 us (1%)
    all_to_all x1, waiting for transfers between devices, on_device(): spectrum = lax.all_to_all(spectrum, exchange, 0, 0, tiled=True)  54.7 us
    ppermute x8, waiting for transfers between devices, swap_by(): return lax.ppermute(value, axis, [(i, i ^ mask) for i in range(count)])  34.7 us
    ppermute x8, starting transfers between devices, swap_by(): return lax.ppermute(value, axis, [(i, i ^ mask) for i in range(count)])  13.5 us
    pallas_call x3, Pallas kernels, update_call(): pl.pallas_call(kernel, in_specs=[pl.BlockSpec(memory_space=pltpu.SMEM) fo...  11.8 us
    pallas_call x1, Pallas kernels, spectrum_blocks(): pl.pallas_call(functools.partial(early_kernel, places, per_member, frames...  11.4 us
    all_to_all x1, waiting for transfers between devices, on_device(): lax.all_to_all(payload.reshape(partners, 2, ranks_here, width), exchange,...  5.83 us
    all_to_all x1, starting transfers between devices, on_device(): spectrum = lax.all_to_all(spectrum, exchange, 0, 0, tiled=True)  4.86 us
    pallas_call x1, Pallas kernels, spectrum_blocks(): pl.pallas_call(functools.partial(late_kernel, places, per_member, frames)...  3.64 us
  transfers between devices with their start and end apart: 11, of which 8 were waited for; matrix products, arithmetic and copies ran while one was open for 2% of the time, Pallas kernels for 10%

profile of v6, /device:TPU:0, one launch (start us, length us, event | category | flops | bytes accessed | tf_op | source)
XLA Modules:
  0.0 150.3 jit_solution(4566238188337395247)
XLA Ops:
  0.6 0.9 slice.126
  1.5 1.3 collective-permute-start
  2.8 6.5 %collective-permute-start.1 = (f32[64,1024]{1,0:T(8,128)}, f32[64,1024]{1,0:T(8,128)S(1)}, u32[]{:S(2)}, u32[]{:S(2)}) collective-permute-start(f32[64,1024]{1,0:T(8,128)} %param.10), channel_id=1, source_target_pairs={{0,4},{4,0},{1,5},{5,1},{2,6},{6,2},{3,7},{7,3},{8,12},{12,8},{9,1... | collective-permute-start | bytes 786440 | tf_op jit(solution)/shard_map/ppermute | solution.py:565
  9.3 0.0 copy-start
  9.3 11.4 %shard_map.104 = (f32[16,528,128]{2,1,0:T(8,128)}, f32[2048,128]{1,0:T(8,128)S(1)}, f32[2,256,128]{2,1,0:T(8,128)S(1)}, bf16[256,768]{1,0:T(8,128)(2,1)S(1)}, f3...) custom-call(f32[8192,128]{1,0:T(8,128)} %bitcast.115, ...), custom_call_target="tpu_custom_call" | custom-call | flops 4831838208 | bytes 6291456 | tf_op jit(solution)/shard_map/pallas_call | solution.py:298
  20.8 0.0 collective-permute-done.trailing_ref
  20.8 0.0 copy-done
  20.8 3.6 %shard_map.105 = f32[16,528,128]{2,1,0:T(8,128)} custom-call(f32[2048,128]{1,0:T(8,128)S(1)} %get-tuple-element.20.tail_ref, f32[256,128]{1,0:T(8,128)S(1)} %collective-permute-done.trailing_ref, f32[16,128]{1,0:T(8,128)S(1)} %copy-done, f32[2,256,128]{2,1,0:T(8,128)S(1)} %get-tuple-element.21.rest_0_, ...), custom_call_target="tpu_custom_call", output_to_operand_aliasing={{}: (9, {})} | custom-call | flops 1610612736 | bytes 2097152 | tf_op jit(solution)/shard_map/pallas_call | solution.py:312
  24.5 0.0 copy-start.1
  24.5 0.0 collective-permute-done.1
  24.5 4.9 %all-to-all-start = ((f32[16,528,128]{2,1,0:T(8,128)}), f32[16,528,128]{2,1,0:T(8,128)}, u32[]{:S(2)}, u32[]{:S(2)}) async-start(f32[16,528,128]{2,1,0:T(8,128)} %shard_map.105), calls=%async_computation | async-start | bytes 8650752 | tf_op jit(solution)/shard_map/all_to_all | solution.py:609
  29.4 0.1 fusion.6
  29.5 0.0 copy-done.1
  29.6 0.2 slice.163
  29.8 0.2 slice.130
  30.0 0.2 maximum_select_fusion.1
  30.4 54.7 %all-to-all-done.received_ref = f32[16,528,128]{2,1,0:T(8,128)} async-done(((f32[16,528,128]{2,1,0:T(8,128)}), f32[16,528,128]{2,1,0:T(8,128)}, u32[]{:S(2)}, u32[]{:S(2)}) %all-to-all-start) | async-done | bytes 4325408 | tf_op jit(solution)/shard_map/all_to_all | solution.py:609
  85.1 5.0 %shard_map.106 = (f32[136,128]{1,0:T(8,128)S(1)}, f32[136,128]{1,0:T(8,128)S(1)}, f32[512,64]{1,0:T(8,128)S(1)}, f32[16,512,128]{2,1,0:T(8,128)S(1)}) custom-call(s32[1]{0:T(128)} %bitcast.side_ref, f32[16,528,128]{2,1,0:T(8,128)} %all-to-all-done.received_ref, f32[16,64,128]{2,1,0:T(8,128)S(1)} %constant_dynamic-update-slice_fusion.basis_ref), custom_call_target="tpu_custom_call" | custom-call | flops 1107296256 | bytes 4325376 | tf_op jit(solution)/shard_map/pallas_call | solution.py:544
  90.1 2.3 %collective-permute-start.2 = (f32[136,128]{1,0:T(8,128)S(1)}, f32[136,128]{1,0:T(8,128)S(1)}, u32[]{:S(2)}, u32[]{:S(2)}) collective-permute-start(f32[136,128]{1,0:T(8,128)S(1)} %get-tuple-element.33), channel_id=1, source_target_pairs={{0,8},{8,0},{16,24},{24,16},{1,9},{9,1},{17,25},{25,17},{2,10},{10... | collective-permute-start | bytes 208904 | tf_op jit(solution)/shard_map/ppermute | solution.py:565
  92.4 0.9 collective-permute-done.2
  93.3 1.1 collective-permute-start.3
  94.4 3.4 %collective-permute-done.3 = f32[136,128]{1,0:T(8,128)S(1)} collective-permute-done((f32[136,128]{1,0:T(8,128)S(1)}, f32[136,128]{1,0:T(8,128)S(1)}, u32[]{:S(2)}, u32[]{:S(2)}) %collective-permute-start.3) | collective-permute-done | bytes 69664 | tf_op jit(solution)/shard_map/ppermute | solution.py:565
  97.8 0.6 collective-permute-start.4
  98.5 0.0 collective-permute-start.5
  98.5 2.9 %collective-permute-start.6 = (f32[136,128]{1,0:T(8,128)S(1)}, f32[136,128]{1,0:T(8,128)S(1)}, u32[]{:S(2)}, u32[]{:S(2)}) collective-permute-start(f32[136,128]{1,0:T(8,128)S(1)} %add.90), channel_id=1, source_target_pairs={{0,3},{1,2},{2,1},{3,0},{4,7},{5,6},{6,5},{7,4},{8,11},{9,10},{10,... | collective-permute-start | bytes 208904 | tf_op jit(solution)/shard_map/ppermute | solution.py:565
  101.4 1.6 %collective-permute-done.4 = f32[136,128]{1,0:T(8,128)S(1)} collective-permute-done((f32[136,128]{1,0:T(8,128)S(1)}, f32[136,128]{1,0:T(8,128)S(1)}, u32[]{:S(2)}, u32[]{:S(2)}) %collective-permute-start.4) | collective-permute-done | bytes 69664 | tf_op jit(solution)/shard_map/ppermute | solution.py:565
  102.9 0.0 collective-permute-done.5
  103.0 1.5 collective-permute-done.6
  104.4 0.1 collective-permute-start.7
  104.5 1.2 collective-permute-done.7.other_ref
  105.8 1.7 %shard_map.107 = (f32[512,64]{1,0:T(8,128)S(1)}, f32[1032,128]{1,0:T(8,128)S(1)}) custom-call(s32[1]{0:T(128)} %bitcast.side_ref, f32[16,512,128]{2,1,0:T(8,128)S(1)} %get-tuple-element.30.spectrum_ref, f32[16,64,128]{2,1,0:T(8,128)S(1)} %constant_dynamic-update-slice_fusion.basis_ref, f32[512,64]{1,0:T(8,128)S(1)} %get-tuple-element.31.activity_ref, ...), custom_call_target="tpu_custom_call" | custom-call | flops 1073741824 | bytes 4194304 | tf_op jit(solution)/shard_map/pallas_call | solution.py:544
  107.5 0.1 collective-permute-start.8
  107.6 0.1 constant_dynamic-slice_fusion
  107.7 0.1 copy.23
  107.7 26.1 %collective-permute-done.8.rest_1_ = f32[1032,128]{1,0:T(8,128)S(1)} collective-permute-done((f32[1032,128]{1,0:T(8,128)S(1)}, f32[1032,128]{1,0:T(8,128)S(1)}, u32[]{:S(2)}, u32[]{:S(2)}) %collective-permute-start.8) | collective-permute-done | bytes 528416 | tf_op jit(solution)/shard_map/ppermute | solution.py:565
  133.9 5.1 %shard_map.108 = (f32[16,64,128]{2,1,0:T(8,128)S(1)}, f32[4,4,2,16,128]{4,3,2,1,0:T(8,128)}) custom-call(f32[16,528,128]{2,1,0:T(8,128)} %all-to-all-done.received_ref, f32[16,64,128]{2,1,0:T(8,128)S(1)} %constant_dynamic-update-slice_fusion.basis_ref, f32[512,64]{1,0:T(8,128)S(1)} %get-tuple-element.34.middle_ref, ...), custom_call_target="tpu_custom_call" | custom-call | flops 1107296256 | bytes 4325376 | tf_op jit(solution)/shard_map/pallas_call | solution.py:544
  139.0 3.5 %all-to-all-start.1 = ((f32[16,2,16,128]{3,2,1,0:T(8,128)}), f32[16,2,16,128]{3,2,1,0:T(8,128)S(1)}, u32[]{:S(2)}, u32[]{:S(2)}) async-start(f32[16,2,16,128]{3,2,1,0:T(8,128)} %bitcast.28), calls=%async_computation.1 | async-start | bytes 524288 | tf_op jit(solution)/shard_map/all_to_all | solution.py:680
  142.6 0.1 fusion.1
  142.7 0.1 slice.183
  142.8 0.1 slice.161
  142.9 0.9 copy_bitcast_fusion
  143.8 5.8 %all-to-all-done.1 = f32[16,2,16,128]{3,2,1,0:T(8,128)S(1)} async-done(((f32[16,2,16,128]{3,2,1,0:T(8,128)}), f32[16,2,16,128]{3,2,1,0:T(8,128)S(1)}, u32[]{:S(2)}, u32[]{:S(2)}) %all-to-all-start.1) | async-done | bytes 262176 | tf_op jit(solution)/shard_map/all_to_all | solution.py:680
  149.7 0.6 fusion.4
  (30 shorter events, 0.3 us)
Async XLA Ops:
  1.5 19.2 %collective-permute-start = (f32[256,128]{1,0:T(8,128)S(1)}, f32[256,128]{1,0:T(8,128)S(1)}, u32[]{:S(2)}, u32[]{:S(2)}) collective-permute-start(f32[256,128]{1,0:T(8,128)S(1)} %bitcast.114), channel_id=1, source_target_pairs={{8,0},{9,1},{10,2},{11,3},{12,4},{13,5},{14,6},{15,7},{16,8},{17,9... | collective-permute-start | bytes 393224 | tf_op jit(solution)/shard_map/ppermute | solution.py:603
  2.8 21.6 %collective-permute-start.1 = (f32[64,1024]{1,0:T(8,128)}, f32[64,1024]{1,0:T(8,128)S(1)}, u32[]{:S(2)}, u32[]{:S(2)}) collective-permute-start(f32[64,1024]{1,0:T(8,128)} %param.10), channel_id=1, source_target_pairs={{0,4},{4,0},{1,5},{5,1},{2,6},{6,2},{3,7},{7,3},{8,12},{12,8},{9,1... | collective-permute-start | bytes 786440 | tf_op jit(solution)/shard_map/ppermute | solution.py:565
  9.3 11.5 %copy-start = (f32[16,128]{1,0:T(8,128)S(1)}, f32[16,128]{1,0:T(8,128)}, u32[]{:S(2)}) copy-start(f32[16,128]{1,0:T(8,128)} %activity_ref.1) | copy-start | bytes 24580
  24.5 5.0 %copy-start.1 = (f32[64,1024]{1,0:T(8,128)S(1)}, f32[64,1024]{1,0:T(8,128)}, u32[]{:S(2)}) copy-start(f32[64,1024]{1,0:T(8,128)} %param.10) | copy-start | bytes 786436
  24.5 60.6 %all-to-all-start = ((f32[16,528,128]{2,1,0:T(8,128)}), f32[16,528,128]{2,1,0:T(8,128)}, u32[]{:S(2)}, u32[]{:S(2)}) async-start(f32[16,528,128]{2,1,0:T(8,128)} %shard_map.105), calls=%async_computation | async-start | bytes 8650752 | tf_op jit(solution)/shard_map/all_to_all | solution.py:609
  90.1 3.2 %collective-permute-start.2 = (f32[136,128]{1,0:T(8,128)S(1)}, f32[136,128]{1,0:T(8,128)S(1)}, u32[]{:S(2)}, u32[]{:S(2)}) collective-permute-start(f32[136,128]{1,0:T(8,128)S(1)} %get-tuple-element.33), channel_id=1, source_target_pairs={{0,8},{8,0},{16,24},{24,16},{1,9},{9,1},{17,25},{25,17},{2,10},{10... | collective-permute-start | bytes 208904 | tf_op jit(solution)/shard_map/ppermute | solution.py:565
  93.3 4.5 %collective-permute-start.3 = (f32[136,128]{1,0:T(8,128)S(1)}, f32[136,128]{1,0:T(8,128)S(1)}, u32[]{:S(2)}, u32[]{:S(2)}) collective-permute-start(f32[136,128]{1,0:T(8,128)S(1)} %add.89), channel_id=1, source_target_pairs={{0,16},{8,24},{16,0},{24,8},{1,17},{9,25},{17,1},{25,9},{2,18},{10... | collective-permute-start | bytes 208904 | tf_op jit(solution)/shard_map/ppermute | solution.py:565
  97.8 5.1 %collective-permute-start.4 = (f32[136,128]{1,0:T(8,128)S(1)}, f32[136,128]{1,0:T(8,128)S(1)}, u32[]{:S(2)}, u32[]{:S(2)}) collective-permute-start(f32[136,128]{1,0:T(8,128)S(1)} %add.90), channel_id=1, source_target_pairs={{0,1},{1,0},{2,3},{3,2},{4,5},{5,4},{6,7},{7,6},{8,9},{9,8},{10,11... | collective-permute-start | bytes 208904 | tf_op jit(solution)/shard_map/ppermute | solution.py:565
  98.5 4.5 %collective-permute-start.5 = (f32[136,128]{1,0:T(8,128)S(1)}, f32[136,128]{1,0:T(8,128)S(1)}, u32[]{:S(2)}, u32[]{:S(2)}) collective-permute-start(f32[136,128]{1,0:T(8,128)S(1)} %add.90), channel_id=1, source_target_pairs={{0,2},{1,3},{2,0},{3,1},{4,6},{5,7},{6,4},{7,5},{8,10},{9,11},{10,... | collective-permute-start | bytes 208904 | tf_op jit(solution)/shard_map/ppermute | solution.py:565
  98.5 6.0 %collective-permute-start.6 = (f32[136,128]{1,0:T(8,128)S(1)}, f32[136,128]{1,0:T(8,128)S(1)}, u32[]{:S(2)}, u32[]{:S(2)}) collective-permute-start(f32[136,128]{1,0:T(8,128)S(1)} %add.90), channel_id=1, source_target_pairs={{0,3},{1,2},{2,1},{3,0},{4,7},{5,6},{6,5},{7,4},{8,11},{9,10},{10,... | collective-permute-start | bytes 208904 | tf_op jit(solution)/shard_map/ppermute | solution.py:565
  104.4 1.3 collective-permute-start.7
  107.5 26.4 %collective-permute-start.8 = (f32[1032,128]{1,0:T(8,128)S(1)}, f32[1032,128]{1,0:T(8,128)S(1)}, u32[]{:S(2)}, u32[]{:S(2)}) collective-permute-start(f32[1032,128]{1,0:T(8,128)S(1)} %get-tuple-element.35.rest_0_), channel_id=1, source_target_pairs={{0,4},{4,0},{1,5},{5,1},{2,6},{6,2},{3,7},{7,3},{8,12},{12,8},{9,1... | collective-permute-start | bytes 1585160 | tf_op jit(solution)/shard_map/ppermute | solution.py:565
  139.0 10.7 %all-to-all-start.1 = ((f32[16,2,16,128]{3,2,1,0:T(8,128)}), f32[16,2,16,128]{3,2,1,0:T(8,128)S(1)}, u32[]{:S(2)}, u32[]{:S(2)}) async-start(f32[16,2,16,128]{3,2,1,0:T(8,128)} %bitcast.28), calls=%async_computation.1 | async-start | bytes 524288 | tf_op jit(solution)/shard_map/all_to_all | solution.py:680

commit v7 on v6

--- a/solution.py
+++ b/solution.py
@@ -27,9 +27,9 @@
     return high, low
 
 
-def for_three_products(values):
+def both_parts_below(values):
     high, low = high_low(values)
-    return np.concatenate([high, low, high], 1)
+    return np.concatenate([high, low], 0)
 
 
 def units_of_member(units_here, member_blocks):
@@ -71,7 +71,7 @@
         phase = 2.0 * np.pi / half * np.mod(np.outer(turns, np.arange(half)), half)
         c, s = np.cos(phase), np.sin(phase)
         seconds.append(
-            for_three_products(np.concatenate([np.concatenate([c, s], 1), np.concatenate([-s, c], 1)], 0))
+            both_parts_below(np.concatenate([np.concatenate([c, s], 1), np.concatenate([-s, c], 1)], 0))
         )
         flags = np.zeros((half, LANES), np.float32)
         flags[:, 0] = [unit_order[place] % 2 for place in here]
@@ -82,7 +82,7 @@
     window = window.reshape(SPLIT, 2, LANES).transpose(1, 0, 2)
     return (
         np.ascontiguousarray(window),
-        for_three_products(first),
+        both_parts_below(first),
         twiddle,
         rows,
         np.stack(seconds),
@@ -105,7 +105,7 @@
     return lax.dot_general(left, right, NT, preferred_element_type=jnp.float32)
 
 
-def transform_group(hop_rows, places, per_member, table_refs, out_ref, parts_ref, middle_ref, ready):
+def transform_group(hop_rows, places, per_member, table_refs, out_ref, parts_ref, middle_ref, written=None):
     window_ref, first_ref, twiddle_ref, rows_ref, second_ref, mirrored_ref = table_refs
     half = SPLIT // 2
     middle_ref[...] = jnp.zeros_like(middle_ref)
@@ -118,9 +118,12 @@
         odd = jnp.concatenate([real * c + imag * s, imag * c - real * s], 1)
         return even, odd
 
-    def three(values):
-        high, low = split_values(values)
-        return jnp.concatenate([high, high, low], 1)
+    def in_parts(values):
+        return jnp.concatenate(split_values(values), 1)
+
+    def second(parity, parts):
+        both = dot_nt(second_ref[parity], parts[:, :SPLIT])
+        return both[:SPLIT] + (both[SPLIT:] + dot_nt(second_ref[parity, :SPLIT, :], parts[:, SPLIT:]))
 
     for g in range(GROUP):
         columns = [
@@ -128,29 +131,26 @@
             for side in range(2)
         ]
         high, low = split_values(jnp.concatenate(columns, 1))
-        section = dot(first_ref[...], jnp.concatenate([high, high, low], 0))
+        section = dot(first_ref[...], high)
+        section = section[:SPLIT] + (section[SPLIT:] + dot(first_ref[:SPLIT, :], low))
         a, b = section[:half], section[half:]
         real = a * twiddle_ref[0] + b * twiddle_ref[1]
         imag = b * twiddle_ref[2] - a * twiddle_ref[1]
         for parity, values in enumerate(even_odd(real, imag)):
-            parts_ref[parity, g * half : (g + 1) * half, :] = three(values)
+            parts_ref[parity, g * half : (g + 1) * half, :] = in_parts(values)
         nyquist = section[half : half + 1]
         for parity, values in enumerate(even_odd(nyquist * rows_ref[0:1], nyquist * rows_ref[1:2])):
             middle_ref[parity, g : g + 1, :] = values
 
-    ready()
-
     def magnitude(values):
         real, imag = values[:half], values[half:]
         return jnp.sqrt(real * real + imag * imag) * (8.0 / SPLIT)
 
     for parity in range(2):
-        middle = magnitude(dot_nt(second_ref[parity], three(middle_ref[parity])))
+        middle = magnitude(second(parity, in_parts(middle_ref[parity])))
         is_middle = mirrored_ref[parity] > 0.0
         for pair in range(GROUP // 2):
-            values = magnitude(
-                dot_nt(second_ref[parity], parts_ref[parity, pair * SPLIT : (pair + 1) * SPLIT, :])
-            )
+            values = magnitude(second(parity, parts_ref[parity, pair * SPLIT : (pair + 1) * SPLIT, :]))
             for lane in range(2):
                 g = 2 * pair + lane
                 block = jnp.where(
@@ -170,13 +170,15 @@
                     member, row = divmod(place, per_member)
                     out_ref[member, pl.ds(row * GROUP + g, stop - start, stride=GROUP), :] = block[start:stop]
                     start = stop
+        if written is not None:
+            written(parity)
 
 
 def early_kernel(
     places, per_member, frames, samples_ref, *rest
 ):
-    table_refs, (out_ref, tail_ref) = rest[:6], rest[6:8]
-    copies_ref, (hops_ref, parts_ref, middle_ref, group_ref, sem_ref, out_sem_ref) = rest[8:14], rest[14:]
+    table_refs, (out_ref, tail_ref, group_ref) = rest[:6], rest[6:9]
+    copies_ref, (hops_ref, parts_ref, middle_ref, sem_ref, out_sem_ref) = rest[9:15], rest[15:]
     groups = frames // GROUP - 1
     group_rows = GROUP * HOP_ROWS
     half = SPLIT // 2
@@ -197,7 +199,7 @@
     for copy in [tables_in[1], lead, hops[0], *tables_in[:1], *tables_in[2:], *hops[1:], tail]:
         copy.start()
     lead.wait()
-    for copy in tables_in[:4]:
+    for copy in tables_in:
         copy.wait()
 
     def body(i, carry):
@@ -207,12 +209,6 @@
             hops_ref.at[pl.ds(HOP_ROWS + first, group_rows), :],
             sem_ref.at[8 + i],
         ).wait()
-
-        def ready():
-            @pl.when(i == 0)
-            def _():
-                for copy in tables_in[4:]:
-                    copy.wait()
 
         transform_group(
             lambda hop, side: hops_ref[pl.ds(first + hop * HOP_ROWS + side, half, stride=2), :],
@@ -222,9 +218,12 @@
             group_ref.at[i],
             parts_ref,
             middle_ref,
-            ready,
         )
-        send(i).start()
+
+        @pl.when(i < groups - 1)
+        def _():
+            send(i).start()
+
         return carry
 
     def send(i):
@@ -237,13 +236,18 @@
 
     lax.fori_loop(0, groups, body, 0)
     tail.wait()
-    for i in range(groups):
+    for i in range(groups - 1):
         send(i).wait()
 
 
-def late_kernel(places, per_member, frames, tail_ref, trailing_ref, activity_ref, *rest):
+def late_kernel(places, per_member, frames, done_ref, tail_ref, trailing_ref, activity_ref, *rest):
     table_refs, (_, out_ref, parts_ref, middle_ref, group_ref, sem_ref) = rest[:6], rest[6:]
     count = per_member * GROUP
+    before = frames // GROUP - 1
+    pass_on = pltpu.make_async_copy(
+        done_ref.at[before - 1], out_ref.at[:, pl.ds((before - 1) * count, count), :], sem_ref.at[0]
+    )
+    pass_on.start()
 
     def hop_rows(hop, side):
         if hop == GROUP:
@@ -252,6 +256,23 @@
 
     for member in range(out_ref.shape[0]):
         group_ref[member, count:, :] = activity_ref[...]
+    bounds = [0, group_ref.shape[1]]
+    if all(place % per_member < per_member // 2 for place in places[0]):
+        bounds.insert(1, count // 2)
+    sends = []
+
+    def written(parity):
+        if parity == 1 or len(bounds) == 3:
+            first, last = bounds[len(sends)], bounds[len(sends) + 1]
+            sends.append(
+                pltpu.make_async_copy(
+                    group_ref.at[:, pl.ds(first, last - first), :],
+                    out_ref.at[:, pl.ds(before * count + first, last - first), :],
+                    sem_ref.at[1 + len(sends)],
+                )
+            )
+            sends[-1].start()
+
     transform_group(
         hop_rows,
         places,
@@ -260,12 +281,11 @@
         group_ref,
         parts_ref,
         middle_ref,
-        lambda: None,
-    )
-    first = (frames // GROUP - 1) * count
-    send = pltpu.make_async_copy(group_ref, out_ref.at[:, pl.ds(first, group_ref.shape[1]), :], sem_ref)
-    send.start()
-    send.wait()
+        written,
+    )
+    pass_on.wait()
+    for send in sends:
+        send.wait()
 
 
 def spectrum_blocks(samples, trailing, activity, unit_order, members):
@@ -281,7 +301,7 @@
     in_vmem = pl.BlockSpec(memory_space=pltpu.VMEM)
     in_hbm = pl.BlockSpec(memory_space=pltpu.HBM)
     scratch = [
-        pltpu.VMEM((2, GROUP * LANES, 3 * SPLIT), jnp.bfloat16),
+        pltpu.VMEM((2, GROUP * LANES, 2 * SPLIT), jnp.bfloat16),
         pltpu.VMEM((2, 16, SPLIT), jnp.float32),
     ]
 
@@ -295,15 +315,15 @@
             ),
         )
 
-    early, tail, *copies = pl.pallas_call(
+    early, tail, done, *copies = pl.pallas_call(
         functools.partial(early_kernel, places, per_member, frames),
         in_specs=[in_hbm] * (1 + len(constants)),
-        out_specs=[in_hbm] + [in_vmem] * (1 + len(constants)),
-        out_shape=[out_shape, tail_shape] + [jax.ShapeDtypeStruct(t.shape, t.dtype) for t in constants],
+        out_specs=[in_hbm] + [in_vmem] * (2 + len(constants)),
+        out_shape=[out_shape, tail_shape, jax.ShapeDtypeStruct((groups, *group_shape), jnp.float32)]
+        + [jax.ShapeDtypeStruct(t.shape, t.dtype) for t in constants],
         scratch_shapes=[pltpu.VMEM(((groups * GROUP + 1) * HOP_ROWS, LANES), jnp.float32)]
         + scratch
         + [
-            pltpu.VMEM((groups, *group_shape), jnp.float32),
             pltpu.SemaphoreType.DMA((8 + groups,)),
             pltpu.SemaphoreType.DMA((groups,)),
         ],
@@ -311,13 +331,13 @@
     )(*[pltpu.with_memory_space_constraint(value, pltpu.HBM) for value in (samples, *constants)])
     return pl.pallas_call(
         functools.partial(late_kernel, places, per_member, frames),
-        in_specs=[in_vmem] * (3 + len(constants)) + [in_hbm],
+        in_specs=[in_vmem] * (4 + len(constants)) + [in_hbm],
         out_specs=in_hbm,
         out_shape=out_shape,
-        scratch_shapes=scratch + [pltpu.VMEM(last_shape, jnp.float32), pltpu.SemaphoreType.DMA],
-        input_output_aliases={3 + len(constants): 0},
+        scratch_shapes=scratch + [pltpu.VMEM(last_shape, jnp.float32), pltpu.SemaphoreType.DMA((3,))],
+        input_output_aliases={4 + len(constants): 0},
         **settings(1),
-    )(tail, trailing, activity, *copies, early)
+    )(done, tail, trailing, activity, *copies, early)
 
 
 def lanes_of_activity(activity):
@@ -363,8 +383,8 @@
     return dot_nt(jnp.ones((16, basis.shape[1]), jnp.bfloat16), basis)
 
 
-def row_steps(per_member):
-    rows = math.gcd(per_member, 8)
+def row_steps(per_member, most=8):
+    rows = math.gcd(per_member, most)
     return [range(start, start + rows) for start in range(0, per_member, rows)]
 
 
@@ -394,11 +414,11 @@
     return jnp.concatenate([pieces[sub, member] for sub in range(subs) for member in range(members)], 0)
 
 
-def start_fetches(received_ref, spectrum_ref, sem_ref, per_member):
+def start_fetches(received_ref, spectrum_ref, sem_ref, per_member, steps):
     count = spectrum_ref.shape[1]
     groups = count // (per_member * GROUP)
     copies = []
-    for step, rows in enumerate(row_steps(per_member)):
+    for step, rows in enumerate(steps):
         copies.append([])
         for group in range(groups):
             place = pl.ds((group * per_member + rows[0]) * GROUP, len(rows) * GROUP)
@@ -426,13 +446,13 @@
     rows_sem_ref,
     sem_ref,
 ):
-    steps = row_steps(basis_ref.shape[0])
+    steps = row_steps(basis_ref.shape[0], 16)
     count = spectrum_ref.shape[1]
     rows_copy = pltpu.make_async_copy(
         received_ref.at[:, pl.ds(count, rows_ref.shape[1]), :], rows_ref, rows_sem_ref
     )
     rows_copy.start()
-    copies = start_fetches(received_ref, spectrum_ref, sem_ref, basis_ref.shape[0])
+    copies = start_fetches(received_ref, spectrum_ref, sem_ref, basis_ref.shape[0], steps)
     rows_copy.wait()
     activity = gathered_activity(rows_ref, shape)
     activity_ref[...] = activity
@@ -505,13 +525,14 @@
     numerators = rest[:-6]
     rank = middle_ref.shape[1]
     per_member = basis_ref.shape[0]
-    copies = start_fetches(received_ref, spectrum_ref, sem_ref, per_member)
+    steps = row_steps(per_member)
+    copies = start_fetches(received_ref, spectrum_ref, sem_ref, per_member, steps)
     lanes_ref[...] = lanes_of_activity(middle_ref[...])
     totals = sum(ref[per_member * rank :, :] for ref in numerators)
     totals = jnp.transpose(jnp.concatenate([totals] * (LANES // 8), 0))[:rank]
     scale = 1.0 / totals
     sums = 0.0
-    for step, rows in enumerate(row_steps(per_member)):
+    for step, rows in enumerate(steps):
         blocks = [
             basis_ref[row] * (sum(ref[row * rank : (row + 1) * rank, :] for ref in numerators) * scale)
             for row in rows

time: 151 us -> 148 us (0.980)
  Pallas kernels: 26.9 us -> 24.1 us
    pallas_call x1, Pallas kernels: 11.4 us -> 9.05 us  [spectrum_blocks(): pl.pallas_call(functools.partial(early_kernel, places, per_member, frames...]
  transfers between devices with their start and end apart: 11 -> 11, of which waited for: 8 -> 8; matrix products, arithmetic and copies ran while one was open for 2% -> 2% of each run, Pallas kernels for 10% -> 8%
where the time goes in v7:
time: 148 us; the launch traced here: 147 us
  waiting for transfers between devices  94 us (64%)
  starting transfers between devices  24.5 us (17%)
  Pallas kernels  24.1 us (16%)
  other arithmetic  1.98 us (1%)
  local copies, waits for them, and re-layouts  1.89 us (1%)
    all_to_all x1, waiting for transfers between devices, on_device(): spectrum = lax.all_to_all(spectrum, exchange, 0, 0, tiled=True)  54.7 us
    ppermute x8, waiting for transfers between devices, swap_by(): return lax.ppermute(value, axis, [(i, i ^ mask) for i in range(count)])  33.5 us
    ppermute x8, starting transfers between devices, swap_by(): return lax.ppermute(value, axis, [(i, i ^ mask) for i in range(count)])  14.8 us
    pallas_call x3, Pallas kernels, update_call(): pl.pallas_call(kernel, in_specs=[pl.BlockSpec(memory_space=pltpu.SMEM) fo...  11.6 us
    pallas_call x1, Pallas kernels, spectrum_blocks(): pl.pallas_call(functools.partial(early_kernel, places, per_member, frames...  9.05 us
    all_to_all x1, waiting for transfers between devices, on_device(): lax.all_to_all(payload.reshape(partners, 2, ranks_here, width), exchange,...  5.83 us
    all_to_all x1, starting transfers between devices, on_device(): spectrum = lax.all_to_all(spectrum, exchange, 0, 0, tiled=True)  4.86 us
    all_to_all x1, starting transfers between devices, on_device(): lax.all_to_all(payload.reshape(partners, 2, ranks_here, width), exchange,...  3.54 us
  transfers between devices with their start and end apart: 11, of which 8 were waited for; matrix products, arithmetic and copies ran while one was open for 2% of the time, Pallas kernels for 8%

profile of v7, /device:TPU:0, one launch (start us, length us, event | category | flops | bytes accessed | tf_op | source)
XLA Modules:
  0.0 147.5 jit_solution(15678276106845262492)
XLA Ops:
  0.6 0.9 slice.126
  1.5 1.3 collective-permute-start
  2.8 6.5 %collective-permute-start.1 = (f32[64,1024]{1,0:T(8,128)}, f32[64,1024]{1,0:T(8,128)S(1)}, u32[]{:S(2)}, u32[]{:S(2)}) collective-permute-start(f32[64,1024]{1,0:T(8,128)} %param.10), channel_id=1, source_target_pairs={{0,4},{4,0},{1,5},{5,1},{2,6},{6,2},{3,7},{7,3},{8,12},{12,8},{9,1... | collective-permute-start | bytes 786440 | tf_op jit(solution)/shard_map/ppermute | solution.py:586
  9.3 0.0 copy-start
  9.3 9.0 %shard_map.104 = (f32[16,528,128]{2,1,0:T(8,128)}, f32[2048,128]{1,0:T(8,128)S(1)}, f32[3,16,128,128]{3,2,1,0:T(8,128)S(1)}, f32[2,256,128]{2,1,0:T(8,128)S(1)},...) custom-call(f32[8192,128]{1,0:T(8,128)} %bitcast.115, ...), custom_call_target="tpu_custom_call" | custom-call | flops 4831838208 | bytes 6291456 | tf_op jit(solution)/shard_map/pallas_call | solution.py:318
  18.4 0.0 collective-permute-done.trailing_ref
  18.4 0.0 copy-done
  18.4 3.5 %shard_map.105 = f32[16,528,128]{2,1,0:T(8,128)} custom-call(f32[3,16,128,128]{3,2,1,0:T(8,128)S(1)} %get-tuple-element.21.done_ref, f32[2048,128]{1,0:T(8,128)S(1)} %get-tuple-element.22.tail_ref, f32[256,128]{1,0:T(8,128)S(1)} %collective-permute-done.trailing_ref, f32[16,128]{1,0:T(8,128)S(1)} %copy-done, ...), custom_call_target="tpu_custom_call", output_to_operand_aliasing={{}: (10, {})} | custom-call | flops 1610612736 | bytes 2097152 | tf_op jit(solution)/shard_map/pallas_call | solution.py:332
  21.9 0.0 copy-start.1
  21.9 0.0 collective-permute-done.1
  21.9 4.9 %all-to-all-start = ((f32[16,528,128]{2,1,0:T(8,128)}), f32[16,528,128]{2,1,0:T(8,128)}, u32[]{:S(2)}, u32[]{:S(2)}) async-start(f32[16,528,128]{2,1,0:T(8,128)} %shard_map.105), calls=%async_computation | async-start | bytes 8650752 | tf_op jit(solution)/shard_map/all_to_all | solution.py:630
  26.8 0.1 fusion.6
  26.9 0.0 copy-done.1
  27.0 0.2 slice.163
  27.2 0.2 slice.130
  27.4 0.2 maximum_select_fusion.1
  27.8 54.7 %all-to-all-done.received_ref = f32[16,528,128]{2,1,0:T(8,128)} async-done(((f32[16,528,128]{2,1,0:T(8,128)}), f32[16,528,128]{2,1,0:T(8,128)}, u32[]{:S(2)}, u32[]{:S(2)}) %all-to-all-start) | async-done | bytes 4325408 | tf_op jit(solution)/shard_map/all_to_all | solution.py:630
  82.5 4.8 %shard_map.106 = (f32[136,128]{1,0:T(8,128)S(1)}, f32[136,128]{1,0:T(8,128)S(1)}, f32[512,64]{1,0:T(8,128)S(1)}, f32[16,512,128]{2,1,0:T(8,128)S(1)}) custom-call(s32[1]{0:T(128)} %bitcast.side_ref, f32[16,528,128]{2,1,0:T(8,128)} %all-to-all-done.received_ref, f32[16,64,128]{2,1,0:T(8,128)S(1)} %constant_dynamic-update-slice_fusion.basis_ref), custom_call_target="tpu_custom_call" | custom-call | flops 1107296256 | bytes 4325376 | tf_op jit(solution)/shard_map/pallas_call | solution.py:565
  87.3 2.3 %collective-permute-start.2 = (f32[136,128]{1,0:T(8,128)S(1)}, f32[136,128]{1,0:T(8,128)S(1)}, u32[]{:S(2)}, u32[]{:S(2)}) collective-permute-start(f32[136,128]{1,0:T(8,128)S(1)} %get-tuple-element.35), channel_id=1, source_target_pairs={{0,8},{8,0},{16,24},{24,16},{1,9},{9,1},{17,25},{25,17},{2,10},{10... | collective-permute-start | bytes 208904 | tf_op jit(solution)/shard_map/ppermute | solution.py:586
  89.6 0.9 collective-permute-done.2
  90.5 1.1 collective-permute-start.3
  91.6 3.4 %collective-permute-done.3 = f32[136,128]{1,0:T(8,128)S(1)} collective-permute-done((f32[136,128]{1,0:T(8,128)S(1)}, f32[136,128]{1,0:T(8,128)S(1)}, u32[]{:S(2)}, u32[]{:S(2)}) %collective-permute-start.3) | collective-permute-done | bytes 69664 | tf_op jit(solution)/shard_map/ppermute | solution.py:586
  95.0 0.6 collective-permute-start.4
  95.7 0.0 collective-permute-start.5
  95.7 2.9 %collective-permute-start.6 = (f32[136,128]{1,0:T(8,128)S(1)}, f32[136,128]{1,0:T(8,128)S(1)}, u32[]{:S(2)}, u32[]{:S(2)}) collective-permute-start(f32[136,128]{1,0:T(8,128)S(1)} %add.90), channel_id=1, source_target_pairs={{0,3},{1,2},{2,1},{3,0},{4,7},{5,6},{6,5},{7,4},{8,11},{9,10},{10,... | collective-permute-start | bytes 208904 | tf_op jit(solution)/shard_map/ppermute | solution.py:586
  98.6 1.6 %collective-permute-done.4 = f32[136,128]{1,0:T(8,128)S(1)} collective-permute-done((f32[136,128]{1,0:T(8,128)S(1)}, f32[136,128]{1,0:T(8,128)S(1)}, u32[]{:S(2)}, u32[]{:S(2)}) %collective-permute-start.4) | collective-permute-done | bytes 69664 | tf_op jit(solution)/shard_map/ppermute | solution.py:586
  100.1 0.0 collective-permute-done.5
  100.1 1.5 collective-permute-done.6
  101.6 0.1 collective-permute-start.7
  101.7 1.2 collective-permute-done.7.other_ref
  103.0 1.7 %shard_map.107 = (f32[512,64]{1,0:T(8,128)S(1)}, f32[1032,128]{1,0:T(8,128)S(1)}) custom-call(s32[1]{0:T(128)} %bitcast.side_ref, f32[16,512,128]{2,1,0:T(8,128)S(1)} %get-tuple-element.32.spectrum_ref, f32[16,64,128]{2,1,0:T(8,128)S(1)} %constant_dynamic-update-slice_fusion.basis_ref, f32[512,64]{1,0:T(8,128)S(1)} %get-tuple-element.33.activity_ref, ...), custom_call_target="tpu_custom_call" | custom-call | flops 1073741824 | bytes 4194304 | tf_op jit(solution)/shard_map/pallas_call | solution.py:565
  104.7 1.4 collective-permute-start.8
  106.0 0.1 constant_dynamic-slice_fusion
  106.1 0.1 copy.23
  106.2 24.9 %collective-permute-done.8.rest_1_ = f32[1032,128]{1,0:T(8,128)S(1)} collective-permute-done((f32[1032,128]{1,0:T(8,128)S(1)}, f32[1032,128]{1,0:T(8,128)S(1)}, u32[]{:S(2)}, u32[]{:S(2)}) %collective-permute-start.8) | collective-permute-done | bytes 528416 | tf_op jit(solution)/shard_map/ppermute | solution.py:586
  131.0 5.1 %shard_map.108 = (f32[16,64,128]{2,1,0:T(8,128)S(1)}, f32[4,4,2,16,128]{4,3,2,1,0:T(8,128)}) custom-call(f32[16,528,128]{2,1,0:T(8,128)} %all-to-all-done.received_ref, f32[16,64,128]{2,1,0:T(8,128)S(1)} %constant_dynamic-update-slice_fusion.basis_ref, f32[512,64]{1,0:T(8,128)S(1)} %get-tuple-element.36.middle_ref, ...), custom_call_target="tpu_custom_call" | custom-call | flops 1107296256 | bytes 4325376 | tf_op jit(solution)/shard_map/pallas_call | solution.py:565
  136.2 3.5 %all-to-all-start.1 = ((f32[16,2,16,128]{3,2,1,0:T(8,128)}), f32[16,2,16,128]{3,2,1,0:T(8,128)S(1)}, u32[]{:S(2)}, u32[]{:S(2)}) async-start(f32[16,2,16,128]{3,2,1,0:T(8,128)} %bitcast.28), calls=%async_computation.1 | async-start | bytes 524288 | tf_op jit(solution)/shard_map/all_to_all | solution.py:701
  139.8 0.1 fusion.1
  139.9 0.1 slice.183
  140.0 0.1 slice.161
  140.1 0.9 copy_bitcast_fusion
  141.0 5.8 %all-to-all-done.1 = f32[16,2,16,128]{3,2,1,0:T(8,128)S(1)} async-done(((f32[16,2,16,128]{3,2,1,0:T(8,128)}), f32[16,2,16,128]{3,2,1,0:T(8,128)S(1)}, u32[]{:S(2)}, u32[]{:S(2)}) %all-to-all-start.1) | async-done | bytes 262176 | tf_op jit(solution)/shard_map/all_to_all | solution.py:701
  146.8 0.6 fusion.4
  (30 shorter events, 0.3 us)
Async XLA Ops:
  1.5 16.9 %collective-permute-start = (f32[256,128]{1,0:T(8,128)S(1)}, f32[256,128]{1,0:T(8,128)S(1)}, u32[]{:S(2)}, u32[]{:S(2)}) collective-permute-start(f32[256,128]{1,0:T(8,128)S(1)} %bitcast.114), channel_id=1, source_target_pairs={{8,0},{9,1},{10,2},{11,3},{12,4},{13,5},{14,6},{15,7},{16,8},{17,9... | collective-permute-start | bytes 393224 | tf_op jit(solution)/shard_map/ppermute | solution.py:624
  2.8 19.0 %collective-permute-start.1 = (f32[64,1024]{1,0:T(8,128)}, f32[64,1024]{1,0:T(8,128)S(1)}, u32[]{:S(2)}, u32[]{:S(2)}) collective-permute-start(f32[64,1024]{1,0:T(8,128)} %param.10), channel_id=1, source_target_pairs={{0,4},{4,0},{1,5},{5,1},{2,6},{6,2},{3,7},{7,3},{8,12},{12,8},{9,1... | collective-permute-start | bytes 786440 | tf_op jit(solution)/shard_map/ppermute | solution.py:586
  9.3 9.1 %copy-start = (f32[16,128]{1,0:T(8,128)S(1)}, f32[16,128]{1,0:T(8,128)}, u32[]{:S(2)}) copy-start(f32[16,128]{1,0:T(8,128)} %activity_ref.1) | copy-start | bytes 24580
  21.9 5.0 %copy-start.1 = (f32[64,1024]{1,0:T(8,128)S(1)}, f32[64,1024]{1,0:T(8,128)}, u32[]{:S(2)}) copy-start(f32[64,1024]{1,0:T(8,128)} %param.10) | copy-start | bytes 786436
  21.9 60.6 %all-to-all-start = ((f32[16,528,128]{2,1,0:T(8,128)}), f32[16,528,128]{2,1,0:T(8,128)}, u32[]{:S(2)}, u32[]{:S(2)}) async-start(f32[16,528,128]{2,1,0:T(8,128)} %shard_map.105), calls=%async_computation | async-start | bytes 8650752 | tf_op jit(solution)/shard_map/all_to_all | solution.py:630
  87.3 3.2 %collective-permute-start.2 = (f32[136,128]{1,0:T(8,128)S(1)}, f32[136,128]{1,0:T(8,128)S(1)}, u32[]{:S(2)}, u32[]{:S(2)}) collective-permute-start(f32[136,128]{1,0:T(8,128)S(1)} %get-tuple-element.35), channel_id=1, source_target_pairs={{0,8},{8,0},{16,24},{24,16},{1,9},{9,1},{17,25},{25,17},{2,10},{10... | collective-permute-start | bytes 208904 | tf_op jit(solution)/shard_map/ppermute | solution.py:586
  90.5 4.5 %collective-permute-start.3 = (f32[136,128]{1,0:T(8,128)S(1)}, f32[136,128]{1,0:T(8,128)S(1)}, u32[]{:S(2)}, u32[]{:S(2)}) collective-permute-start(f32[136,128]{1,0:T(8,128)S(1)} %add.89), channel_id=1, source_target_pairs={{0,16},{8,24},{16,0},{24,8},{1,17},{9,25},{17,1},{25,9},{2,18},{10... | collective-permute-start | bytes 208904 | tf_op jit(solution)/shard_map/ppermute | solution.py:586
  95.0 5.1 %collective-permute-start.4 = (f32[136,128]{1,0:T(8,128)S(1)}, f32[136,128]{1,0:T(8,128)S(1)}, u32[]{:S(2)}, u32[]{:S(2)}) collective-permute-start(f32[136,128]{1,0:T(8,128)S(1)} %add.90), channel_id=1, source_target_pairs={{0,1},{1,0},{2,3},{3,2},{4,5},{5,4},{6,7},{7,6},{8,9},{9,8},{10,11... | collective-permute-start | bytes 208904 | tf_op jit(solution)/shard_map/ppermute | solution.py:586
  95.7 4.5 %collective-permute-start.5 = (f32[136,128]{1,0:T(8,128)S(1)}, f32[136,128]{1,0:T(8,128)S(1)}, u32[]{:S(2)}, u32[]{:S(2)}) collective-permute-start(f32[136,128]{1,0:T(8,128)S(1)} %add.90), channel_id=1, source_target_pairs={{0,2},{1,3},{2,0},{3,1},{4,6},{5,7},{6,4},{7,5},{8,10},{9,11},{10,... | collective-permute-start | bytes 208904 | tf_op jit(solution)/shard_map/ppermute | solution.py:586
  95.7 6.0 %collective-permute-start.6 = (f32[136,128]{1,0:T(8,128)S(1)}, f32[136,128]{1,0:T(8,128)S(1)}, u32[]{:S(2)}, u32[]{:S(2)}) collective-permute-start(f32[136,128]{1,0:T(8,128)S(1)} %add.90), channel_id=1, source_target_pairs={{0,3},{1,2},{2,1},{3,0},{4,7},{5,6},{6,5},{7,4},{8,11},{9,10},{10,... | collective-permute-start | bytes 208904 | tf_op jit(solution)/shard_map/ppermute | solution.py:586
  101.6 1.3 collective-permute-start.7
  104.7 26.4 %collective-permute-start.8 = (f32[1032,128]{1,0:T(8,128)S(1)}, f32[1032,128]{1,0:T(8,128)S(1)}, u32[]{:S(2)}, u32[]{:S(2)}) collective-permute-start(f32[1032,128]{1,0:T(8,128)S(1)} %get-tuple-element.37.rest_0_), channel_id=1, source_target_pairs={{0,4},{4,0},{1,5},{5,1},{2,6},{6,2},{3,7},{7,3},{8,12},{12,8},{9,1... | collective-permute-start | bytes 1585160 | tf_op jit(solution)/shard_map/ppermute | solution.py:586
  136.2 10.7 %all-to-all-start.1 = ((f32[16,2,16,128]{3,2,1,0:T(8,128)}), f32[16,2,16,128]{3,2,1,0:T(8,128)S(1)}, u32[]{:S(2)}, u32[]{:S(2)}) async-start(f32[16,2,16,128]{3,2,1,0:T(8,128)} %bitcast.28), calls=%async_computation.1 | async-start | bytes 524288 | tf_op jit(solution)/shard_map/all_to_all | solution.py:701

commit v8 on v7

--- a/solution.py
+++ b/solution.py
@@ -494,7 +494,17 @@
 
 
 def second_kernel(
-    side_ref, spectrum_ref, basis_ref, activity_ref, mine_ref, other_ref, middle_ref, out_ref, lanes_ref, turned_ref
+    side_ref,
+    spectrum_ref,
+    basis_ref,
+    activity_ref,
+    mine_ref,
+    other_ref,
+    middle_ref,
+    early_ref,
+    late_ref,
+    lanes_ref,
+    turned_ref,
 ):
     rank = activity_ref.shape[1]
     quarter = activity_ref.shape[0] // 4
@@ -510,47 +520,60 @@
     turned_ref[...] = jnp.concatenate([high, low], 0)
     totals = jnp.sum(middle, axis=0, keepdims=True)
     totals = jnp.broadcast_to(jnp.concatenate([totals] * (LANES // rank), 1), (8, LANES))
-    out_ref[out_ref.shape[0] - 8 :, :] = totals
+    early_ref[early_ref.shape[0] - 8 :, :] = totals
+    early_rows = early_ref.shape[0] // rank
     for rows in row_steps(basis_ref.shape[0]):
         ratio, _ = ratio_of(spectrum_ref, rows[0], lanes_ref[...], [basis_ref[row] for row in rows])
         high, low = split_values(ratio)
         total = dot(turned_ref[...], high) + dot(turned_ref[...], low)
         total = total[:rank] + total[rank:]
         for place, row in enumerate(rows):
-            out_ref[row * rank : (row + 1) * rank, :] = total[:, place * LANES : (place + 1) * LANES]
-
-
-def third_kernel(received_ref, basis_ref, middle_ref, *rest):
-    new_ref, out_ref, lanes_ref, total_ref, spectrum_ref, sem_ref = rest[-6:]
-    numerators = rest[:-6]
+            out_ref, start = (early_ref, row) if row < early_rows else (late_ref, row - early_rows)
+            out_ref[start * rank : (start + 1) * rank, :] = total[:, place * LANES : (place + 1) * LANES]
+
+
+def renew_and_add(rows, spectrum_ref, basis_ref, lanes_ref, scale, numerators, new_ref, total_ref, sums_ref):
+    rank = basis_ref.shape[1]
+    blocks = [
+        basis_ref[row] * (sum(ref[place * rank : (place + 1) * rank, :] for ref in numerators) * scale)
+        for place, row in enumerate(rows)
+    ]
+    for place, block in enumerate(blocks):
+        new_ref[place] = block
+    ratio, basis = ratio_of(spectrum_ref, rows[0], lanes_ref[...], blocks)
+    total_ref[...] = for_activity(ratio, basis)
+    sums_ref[...] = row_sums(basis)
+
+
+def third_kernel(rows, later, received_ref, basis_ref, middle_ref, *rest):
+    numerators = rest[:-7]
+    new_ref, total_ref, sums_ref, lanes_ref, scale_ref, spectrum_ref, sem_ref = rest[-7:]
     rank = middle_ref.shape[1]
-    per_member = basis_ref.shape[0]
-    steps = row_steps(per_member)
-    copies = start_fetches(received_ref, spectrum_ref, sem_ref, per_member, steps)
+    copies = start_fetches(received_ref, spectrum_ref, sem_ref, basis_ref.shape[0], [rows, later])
     lanes_ref[...] = lanes_of_activity(middle_ref[...])
-    totals = sum(ref[per_member * rank :, :] for ref in numerators)
+    totals = sum(ref[len(rows) * rank :, :] for ref in numerators)
     totals = jnp.transpose(jnp.concatenate([totals] * (LANES // 8), 0))[:rank]
-    scale = 1.0 / totals
-    sums = 0.0
-    for step, rows in enumerate(steps):
-        blocks = [
-            basis_ref[row] * (sum(ref[row * rank : (row + 1) * rank, :] for ref in numerators) * scale)
-            for row in rows
-        ]
-        for row, block in zip(rows, blocks):
-            new_ref[row] = block
-        for copy in copies[step]:
-            copy.wait()
-        ratio, basis = ratio_of(spectrum_ref, rows[0], lanes_ref[...], blocks)
-        part = for_activity(ratio, basis)
-        if step == 0:
-            total_ref[...] = part
-        else:
-            total_ref[...] += part
-        sums += row_sums(basis)
-    total = both_parts(total_ref[...])[:, :rank]
+    scale_ref[...] = 1.0 / totals
+    for copy in copies[0]:
+        copy.wait()
+    renew_and_add(
+        rows, spectrum_ref, basis_ref, lanes_ref, scale_ref[...], numerators, new_ref, total_ref, sums_ref
+    )
+    for copy in copies[1]:
+        copy.wait()
+
+
+def last_kernel(rows, spectrum_ref, basis_ref, lanes_ref, scale_ref, before_ref, sums_before_ref, *rest):
+    numerators = rest[:-4]
+    new_ref, out_ref, total_ref, sums_ref = rest[-4:]
+    rank = basis_ref.shape[1]
+    renew_and_add(
+        rows, spectrum_ref, basis_ref, lanes_ref, scale_ref[...], numerators, new_ref, total_ref, sums_ref
+    )
+    total = both_parts(before_ref[...] + total_ref[...])[:, :rank]
+    sums = both_parts(sums_before_ref[...] + sums_ref[...])
     subs, members, _, ranks, width = out_ref.shape
-    sums = jnp.transpose(jnp.broadcast_to(both_parts(sums)[:1], (LANES, 2 * rank)))[:rank]
+    sums = jnp.transpose(jnp.broadcast_to(sums[:1], (LANES, 2 * rank)))[:rank]
     sums = jnp.concatenate([sums] * (width // LANES), 1).reshape(subs, ranks, width)
     for member, block in enumerate(by_owner(total, (subs, members, ranks, width))):
         out_ref[:, member, 0] = block
@@ -568,7 +591,10 @@
         + [pl.BlockSpec(memory_space=place)]
         + [in_vmem for _ in operands],
         out_specs=[in_vmem for _ in out_shapes],
-        out_shape=[jax.ShapeDtypeStruct(shape, jnp.float32) for shape in out_shapes],
+        out_shape=[
+            shape if hasattr(shape, "dtype") else jax.ShapeDtypeStruct(shape, jnp.float32)
+            for shape in out_shapes
+        ],
         scratch_shapes=scratch,
         compiler_params=pltpu.CompilerParams(vmem_limit_bytes=UPDATE_VMEM),
         cost_estimate=pl.CostEstimate(
@@ -673,31 +699,44 @@
     mine = sum_over(mine, "member", 1)
     other = swap_by(mine, "freq", 1)
 
-    middle, numerator = update_call(
+    early_rows = range(max(1, per_member // 2))
+    late_rows = range(len(early_rows), per_member)
+    middle, *numerators = update_call(
         second_kernel,
         spectrum,
-        [(frames, rank), (per_member * rank + 8, LANES)],
+        [(frames, rank), (len(early_rows) * rank + 8, LANES), (len(late_rows) * rank, LANES)],
         [lanes_scratch, pltpu.VMEM((2 * rank, frames), jnp.bfloat16)],
         (basis, activity, mine, other),
         (side,),
     )
-    numerators = [numerator]
+    numerators = [[numerator] for numerator in numerators]
     if groups == 2:
-        numerators.append(swap_by(numerator, "group", 1))
-    new_basis, payload = update_call(
-        third_kernel,
+        for numerator in numerators:
+            numerator.append(swap_by(numerator[0], "group", 1))
+    early_new, total, sums, lanes, scale, spectrum = update_call(
+        functools.partial(third_kernel, early_rows, late_rows),
         received,
-        [(per_member, rank, LANES), (subs, members, 2, ranks_here, width)],
         [
-            lanes_scratch,
-            total_scratch,
-            pltpu.VMEM((partners, spectrum_rows, LANES), jnp.float32),
-            fetch_sems,
+            (len(early_rows), rank, LANES),
+            (frames, 2 * rank),
+            (16, 2 * rank),
+            jax.ShapeDtypeStruct((frames, 4 * rank), jnp.bfloat16),
+            (rank, LANES),
+            (partners, spectrum_rows, LANES),
         ],
-        (basis, middle, *numerators),
+        [pltpu.SemaphoreType.DMA((2 * row_groups,))],
+        (basis, middle, *numerators[0]),
         (),
         pltpu.HBM,
     )
+    late_new, payload = update_call(
+        functools.partial(last_kernel, late_rows),
+        spectrum,
+        [(len(late_rows), rank, LANES), (subs, members, 2, ranks_here, width)],
+        [total_scratch, pltpu.VMEM((16, 2 * rank), jnp.float32)],
+        (basis, lanes, scale, total, sums, *numerators[1]),
+    )
+    new_basis = [*early_new, *late_new]
     parts = lax.all_to_all(
         payload.reshape(partners, 2, ranks_here, width), exchange, 0, 0, tiled=True
     )

time: 148 us -> 145 us (0.980)
  waiting for transfers between devices: 94 us -> 89.3 us
  starting transfers between devices: 24.5 us -> 26.1 us
    ppermute x8 -> x9, waiting for transfers between devices: 33.5 us -> 28.8 us  [swap_by(): return lax.ppermute(value, axis, [(i, i ^ mask) for i in range(count)])]
    ppermute x8 -> x9, starting transfers between devices: 14.8 us -> 16.4 us  [swap_by(): return lax.ppermute(value, axis, [(i, i ^ mask) for i in range(count)])]
    pallas_call x3 -> x4, Pallas kernels: 11.6 us -> 11.5 us  [update_call(): pl.pallas_call(kernel, in_specs=[pl.BlockSpec(memory_space=pltpu.SMEM) fo...]
  transfers between devices with their start and end apart: 11 -> 12, of which waited for: 8 -> 9; matrix products, arithmetic and copies ran while one was open for 2% -> 2% of each run, Pallas kernels for 8% -> 11%
where the time goes in v8:
time: 145 us; the launch traced here: 144 us
  waiting for transfers between devices  89.3 us (62%)
  starting transfers between devices  26.1 us (18%)
  Pallas kernels  23.9 us (16%)
  other arithmetic  1.97 us (1%)
  local copies, waits for them, and re-layouts  1.89 us (1%)
    all_to_all x1, waiting for transfers between devices, on_device(): spectrum = lax.all_to_all(spectrum, exchange, 0, 0, tiled=True)  54.7 us
    ppermute x9, waiting for transfers between devices, swap_by(): return lax.ppermute(value, axis, [(i, i ^ mask) for i in range(count)])  28.8 us
    ppermute x9, starting transfers between devices, swap_by(): return lax.ppermute(value, axis, [(i, i ^ mask) for i in range(count)])  16.4 us
    pallas_call x4, Pallas kernels, update_call(): pl.pallas_call(kernel, in_specs=[pl.BlockSpec(memory_space=pltpu.SMEM) fo...  11.5 us
    pallas_call x1, Pallas kernels, spectrum_blocks(): pl.pallas_call(functools.partial(early_kernel, places, per_member, frames...  9.05 us
    all_to_all x1, waiting for transfers between devices, on_device(): lax.all_to_all(payload.reshape(partners, 2, ranks_here, width), exchange,...  5.83 us
    all_to_all x1, starting transfers between devices, on_device(): spectrum = lax.all_to_all(spectrum, exchange, 0, 0, tiled=True)  4.86 us
    all_to_all x1, starting transfers between devices, on_device(): lax.all_to_all(payload.reshape(partners, 2, ranks_here, width), exchange,...  3.53 us
  transfers between devices with their start and end apart: 12, of which 9 were waited for; matrix products, arithmetic and copies ran while one was open for 2% of the time, Pallas kernels for 11%

profile of v8, /device:TPU:0, one launch (start us, length us, event | category | flops | bytes accessed | tf_op | source)
XLA Modules:
  0.0 144.2 jit_solution(13916599338861170843)
XLA Ops:
  0.6 0.9 slice.90
  1.5 1.3 collective-permute-start
  2.8 6.5 %collective-permute-start.1 = (f32[64,1024]{1,0:T(8,128)}, f32[64,1024]{1,0:T(8,128)S(1)}, u32[]{:S(2)}, u32[]{:S(2)}) collective-permute-start(f32[64,1024]{1,0:T(8,128)} %param.10), channel_id=1, source_target_pairs={{0,4},{4,0},{1,5},{5,1},{2,6},{6,2},{3,7},{7,3},{8,12},{12,8},{9,1... | collective-permute-start | bytes 786440 | tf_op jit(solution)/shard_map/ppermute | solution.py:612
  9.3 0.0 copy-start
  9.3 9.0 %shard_map.104 = (f32[16,528,128]{2,1,0:T(8,128)}, f32[2048,128]{1,0:T(8,128)S(1)}, f32[3,16,128,128]{3,2,1,0:T(8,128)S(1)}, f32[2,256,128]{2,1,0:T(8,128)S(1)},...) custom-call(f32[8192,128]{1,0:T(8,128)} %bitcast.115, ...), custom_call_target="tpu_custom_call" | custom-call | flops 4831838208 | bytes 6291456 | tf_op jit(solution)/shard_map/pallas_call | solution.py:318
  18.4 0.0 collective-permute-done.trailing_ref
  18.4 0.0 copy-done
  18.4 3.4 %shard_map.105 = f32[16,528,128]{2,1,0:T(8,128)} custom-call(f32[3,16,128,128]{3,2,1,0:T(8,128)S(1)} %get-tuple-element.28.done_ref, f32[2048,128]{1,0:T(8,128)S(1)} %get-tuple-element.29.tail_ref, f32[256,128]{1,0:T(8,128)S(1)} %collective-permute-done.trailing_ref, f32[16,128]{1,0:T(8,128)S(1)} %copy-done, ...), custom_call_target="tpu_custom_call", output_to_operand_aliasing={{}: (10, {})} | custom-call | flops 1610612736 | bytes 2097152 | tf_op jit(solution)/shard_map/pallas_call | solution.py:332
  21.8 0.0 copy-start.1
  21.8 0.0 collective-permute-done.1
  21.8 4.9 %all-to-all-start = ((f32[16,528,128]{2,1,0:T(8,128)}), f32[16,528,128]{2,1,0:T(8,128)}, u32[]{:S(2)}, u32[]{:S(2)}) async-start(f32[16,528,128]{2,1,0:T(8,128)} %shard_map.105), calls=%async_computation | async-start | bytes 8650752 | tf_op jit(solution)/shard_map/all_to_all | solution.py:656
  26.7 0.1 fusion.6
  26.8 0.0 copy-done.1
  26.9 0.2 slice.117
  27.1 0.2 slice.94
  27.3 0.2 maximum_select_fusion.1
  27.8 54.7 %all-to-all-done.received_ref = f32[16,528,128]{2,1,0:T(8,128)} async-done(((f32[16,528,128]{2,1,0:T(8,128)}), f32[16,528,128]{2,1,0:T(8,128)}, u32[]{:S(2)}, u32[]{:S(2)}) %all-to-all-start) | async-done | bytes 4325408 | tf_op jit(solution)/shard_map/all_to_all | solution.py:656
  82.4 4.8 %shard_map.106 = (f32[136,128]{1,0:T(8,128)S(1)}, f32[136,128]{1,0:T(8,128)S(1)}, f32[512,64]{1,0:T(8,128)S(1)}, f32[16,512,128]{2,1,0:T(8,128)S(1)}) custom-call(s32[1]{0:T(128)} %bitcast.side_ref, f32[16,528,128]{2,1,0:T(8,128)} %all-to-all-done.received_ref, f32[16,64,128]{2,1,0:T(8,128)S(1)} %constant_dynamic-update-slice_fusion.basis_ref), custom_call_target="tpu_custom_call" | custom-call | flops 1107296256 | bytes 4325376 | tf_op jit(solution)/shard_map/pallas_call | solution.py:588
  87.3 2.3 %collective-permute-start.2 = (f32[136,128]{1,0:T(8,128)S(1)}, f32[136,128]{1,0:T(8,128)S(1)}, u32[]{:S(2)}, u32[]{:S(2)}) collective-permute-start(f32[136,128]{1,0:T(8,128)S(1)} %get-tuple-element.42), channel_id=1, source_target_pairs={{0,8},{8,0},{16,24},{24,16},{1,9},{9,1},{17,25},{25,17},{2,10},{10... | collective-permute-start | bytes 208904 | tf_op jit(solution)/shard_map/ppermute | solution.py:612
  89.5 0.9 collective-permute-done.2
  90.4 1.1 collective-permute-start.3
  91.5 3.4 %collective-permute-done.3 = f32[136,128]{1,0:T(8,128)S(1)} collective-permute-done((f32[136,128]{1,0:T(8,128)S(1)}, f32[136,128]{1,0:T(8,128)S(1)}, u32[]{:S(2)}, u32[]{:S(2)}) %collective-permute-start.3) | collective-permute-done | bytes 69664 | tf_op jit(solution)/shard_map/ppermute | solution.py:612
  95.0 0.6 collective-permute-start.4
  95.6 0.0 collective-permute-start.5
  95.6 2.9 %collective-permute-start.6 = (f32[136,128]{1,0:T(8,128)S(1)}, f32[136,128]{1,0:T(8,128)S(1)}, u32[]{:S(2)}, u32[]{:S(2)}) collective-permute-start(f32[136,128]{1,0:T(8,128)S(1)} %add.90), channel_id=1, source_target_pairs={{0,3},{1,2},{2,1},{3,0},{4,7},{5,6},{6,5},{7,4},{8,11},{9,10},{10,... | collective-permute-start | bytes 208904 | tf_op jit(solution)/shard_map/ppermute | solution.py:612
  98.5 1.6 %collective-permute-done.4 = f32[136,128]{1,0:T(8,128)S(1)} collective-permute-done((f32[136,128]{1,0:T(8,128)S(1)}, f32[136,128]{1,0:T(8,128)S(1)}, u32[]{:S(2)}, u32[]{:S(2)}) %collective-permute-start.4) | collective-permute-done | bytes 69664 | tf_op jit(solution)/shard_map/ppermute | solution.py:612
  100.1 0.0 collective-permute-done.5
  100.1 1.5 %collective-permute-done.6 = f32[136,128]{1,0:T(8,128)S(1)} collective-permute-done((f32[136,128]{1,0:T(8,128)S(1)}, f32[136,128]{1,0:T(8,128)S(1)}, u32[]{:S(2)}, u32[]{:S(2)}) %collective-permute-start.6) | collective-permute-done | bytes 69664 | tf_op jit(solution)/shard_map/ppermute | solution.py:612
  101.6 0.1 collective-permute-start.7
  101.6 1.2 collective-permute-done.7.other_ref
  102.9 1.7 %shard_map.107 = (f32[512,64]{1,0:T(8,128)S(1)}, f32[520,128]{1,0:T(8,128)S(1)}, f32[512,128]{1,0:T(8,128)S(1)}) custom-call(s32[1]{0:T(128)} %bitcast.side_ref, f32[16,512,128]{2,1,0:T(8,128)S(1)} %get-tuple-element.39.spectrum_ref, f32[16,64,128]{2,1,0:T(8,128)S(1)} %constant_dynamic-update-slice_fusion.basis_ref, ...), custom_call_target="tpu_custom_call" | custom-call | flops 1073741824 | bytes 4194304 | tf_op jit(solution)/shard_map/pallas_call | solution.py:588
  104.6 1.4 collective-permute-start.8
  106.0 1.6 %collective-permute-start.9 = (f32[512,128]{1,0:T(8,128)S(1)}, f32[512,128]{1,0:T(8,128)S(1)}, u32[]{:S(2)}, u32[]{:S(2)}) collective-permute-start(f32[512,128]{1,0:T(8,128)S(1)} %get-tuple-element.50.rest_0_), channel_id=1, source_target_pairs={{0,4},{4,0},{1,5},{5,1},{2,6},{6,2},{3,7},{7,3},{8,12},{12,8},{9,1... | collective-permute-start | bytes 786440 | tf_op jit(solution)/shard_map/ppermute | solution.py:612
  107.6 0.1 constant_dynamic-slice_fusion
  107.7 0.1 copy.23
  107.8 18.4 %collective-permute-done.8.rest_1_ = f32[520,128]{1,0:T(8,128)S(1)} collective-permute-done((f32[520,128]{1,0:T(8,128)S(1)}, f32[520,128]{1,0:T(8,128)S(1)}, u32[]{:S(2)}, u32[]{:S(2)}) %collective-permute-start.8) | collective-permute-done | bytes 266272 | tf_op jit(solution)/shard_map/ppermute | solution.py:612
  126.1 3.0 %shard_map.108 = (f32[8,64,128]{2,1,0:T(8,128)S(1)}, f32[512,128]{1,0:T(8,128)S(1)}, f32[16,128]{1,0:T(8,128)S(1)}, bf16[512,256]{1,0:T(8,128)(2,1)S(1)}, f32[64...) custom-call(f32[16,528,128]{2,1,0:T(8,128)} %all-to-all-done.received_ref, ...), custom_call_target="tpu_custom_call" | custom-call | flops 1107296256 | bytes 4325376 | tf_op jit(solution)/shard_map/pallas_call | solution.py:588
  129.1 1.8 %collective-permute-done.9.rest_1_ = f32[512,128]{1,0:T(8,128)S(1)} collective-permute-done((f32[512,128]{1,0:T(8,128)S(1)}, f32[512,128]{1,0:T(8,128)S(1)}, u32[]{:S(2)}, u32[]{:S(2)}) %collective-permute-start.9) | collective-permute-done | bytes 262176 | tf_op jit(solution)/shard_map/ppermute | solution.py:612
  131.0 2.0 %shard_map.109 = (f32[8,64,128]{2,1,0:T(8,128)S(1)}, f32[4,4,2,16,128]{4,3,2,1,0:T(8,128)}) custom-call(f32[16,512,128]{2,1,0:T(8,128)S(1)} %get-tuple-element.45.spectrum_ref, f32[16,64,128]{2,1,0:T(8,128)S(1)} %constant_dynamic-update-slice_fusion.basis_ref, bf16[512,256]{1,0:T(8,128)(2,1)S(1)} %get-tuple-element.46.lanes_ref, ...), custom_call_target="tpu_custom_call" | custom-call | flops 1073741824 | bytes 4194304 | tf_op jit(solution)/shard_map/pallas_call | solution.py:588
  132.9 3.5 %all-to-all-start.1 = ((f32[16,2,16,128]{3,2,1,0:T(8,128)}), f32[16,2,16,128]{3,2,1,0:T(8,128)S(1)}, u32[]{:S(2)}, u32[]{:S(2)}) async-start(f32[16,2,16,128]{3,2,1,0:T(8,128)} %bitcast.28), calls=%async_computation.1 | async-start | bytes 524288 | tf_op jit(solution)/shard_map/all_to_all | solution.py:740
  136.6 0.1 fusion.1
  136.6 0.1 slice.137
  136.8 0.1 slice.115
  136.9 0.9 copy_bitcast_fusion
  137.8 5.8 %all-to-all-done.1 = f32[16,2,16,128]{3,2,1,0:T(8,128)S(1)} async-done(((f32[16,2,16,128]{3,2,1,0:T(8,128)}), f32[16,2,16,128]{3,2,1,0:T(8,128)S(1)}, u32[]{:S(2)}, u32[]{:S(2)}) %all-to-all-start.1) | async-done | bytes 262176 | tf_op jit(solution)/shard_map/all_to_all | solution.py:740
  143.6 0.6 fusion.4
  (30 shorter events, 0.3 us)
Async XLA Ops:
  1.5 16.9 %collective-permute-start = (f32[256,128]{1,0:T(8,128)S(1)}, f32[256,128]{1,0:T(8,128)S(1)}, u32[]{:S(2)}, u32[]{:S(2)}) collective-permute-start(f32[256,128]{1,0:T(8,128)S(1)} %bitcast.114), channel_id=1, source_target_pairs={{8,0},{9,1},{10,2},{11,3},{12,4},{13,5},{14,6},{15,7},{16,8},{17,9... | collective-permute-start | bytes 393224 | tf_op jit(solution)/shard_map/ppermute | solution.py:650
  2.8 19.0 %collective-permute-start.1 = (f32[64,1024]{1,0:T(8,128)}, f32[64,1024]{1,0:T(8,128)S(1)}, u32[]{:S(2)}, u32[]{:S(2)}) collective-permute-start(f32[64,1024]{1,0:T(8,128)} %param.10), channel_id=1, source_target_pairs={{0,4},{4,0},{1,5},{5,1},{2,6},{6,2},{3,7},{7,3},{8,12},{12,8},{9,1... | collective-permute-start | bytes 786440 | tf_op jit(solution)/shard_map/ppermute | solution.py:612
  9.3 9.1 %copy-start = (f32[16,128]{1,0:T(8,128)S(1)}, f32[16,128]{1,0:T(8,128)}, u32[]{:S(2)}) copy-start(f32[16,128]{1,0:T(8,128)} %activity_ref.1) | copy-start | bytes 24580
  21.8 5.0 %copy-start.1 = (f32[64,1024]{1,0:T(8,128)S(1)}, f32[64,1024]{1,0:T(8,128)}, u32[]{:S(2)}) copy-start(f32[64,1024]{1,0:T(8,128)} %param.10) | copy-start | bytes 786436
  21.8 60.6 %all-to-all-start = ((f32[16,528,128]{2,1,0:T(8,128)}), f32[16,528,128]{2,1,0:T(8,128)}, u32[]{:S(2)}, u32[]{:S(2)}) async-start(f32[16,528,128]{2,1,0:T(8,128)} %shard_map.105), calls=%async_computation | async-start | bytes 8650752 | tf_op jit(solution)/shard_map/all_to_all | solution.py:656
  87.3 3.2 %collective-permute-start.2 = (f32[136,128]{1,0:T(8,128)S(1)}, f32[136,128]{1,0:T(8,128)S(1)}, u32[]{:S(2)}, u32[]{:S(2)}) collective-permute-start(f32[136,128]{1,0:T(8,128)S(1)} %get-tuple-element.42), channel_id=1, source_target_pairs={{0,8},{8,0},{16,24},{24,16},{1,9},{9,1},{17,25},{25,17},{2,10},{10... | collective-permute-start | bytes 208904 | tf_op jit(solution)/shard_map/ppermute | solution.py:612
  90.4 4.5 %collective-permute-start.3 = (f32[136,128]{1,0:T(8,128)S(1)}, f32[136,128]{1,0:T(8,128)S(1)}, u32[]{:S(2)}, u32[]{:S(2)}) collective-permute-start(f32[136,128]{1,0:T(8,128)S(1)} %add.89), channel_id=1, source_target_pairs={{0,16},{8,24},{16,0},{24,8},{1,17},{9,25},{17,1},{25,9},{2,18},{10... | collective-permute-start | bytes 208904 | tf_op jit(solution)/shard_map/ppermute | solution.py:612
  95.0 5.1 %collective-permute-start.4 = (f32[136,128]{1,0:T(8,128)S(1)}, f32[136,128]{1,0:T(8,128)S(1)}, u32[]{:S(2)}, u32[]{:S(2)}) collective-permute-start(f32[136,128]{1,0:T(8,128)S(1)} %add.90), channel_id=1, source_target_pairs={{0,1},{1,0},{2,3},{3,2},{4,5},{5,4},{6,7},{7,6},{8,9},{9,8},{10,11... | collective-permute-start | bytes 208904 | tf_op jit(solution)/shard_map/ppermute | solution.py:612
  95.6 4.5 %collective-permute-start.5 = (f32[136,128]{1,0:T(8,128)S(1)}, f32[136,128]{1,0:T(8,128)S(1)}, u32[]{:S(2)}, u32[]{:S(2)}) collective-permute-start(f32[136,128]{1,0:T(8,128)S(1)} %add.90), channel_id=1, source_target_pairs={{0,2},{1,3},{2,0},{3,1},{4,6},{5,7},{6,4},{7,5},{8,10},{9,11},{10,... | collective-permute-start | bytes 208904 | tf_op jit(solution)/shard_map/ppermute | solution.py:612
  95.6 6.0 %collective-permute-start.6 = (f32[136,128]{1,0:T(8,128)S(1)}, f32[136,128]{1,0:T(8,128)S(1)}, u32[]{:S(2)}, u32[]{:S(2)}) collective-permute-start(f32[136,128]{1,0:T(8,128)S(1)} %add.90), channel_id=1, source_target_pairs={{0,3},{1,2},{2,1},{3,0},{4,7},{5,6},{6,5},{7,4},{8,11},{9,10},{10,... | collective-permute-start | bytes 208904 | tf_op jit(solution)/shard_map/ppermute | solution.py:612
  101.6 1.3 collective-permute-start.7
  104.6 21.5 %collective-permute-start.8 = (f32[520,128]{1,0:T(8,128)S(1)}, f32[520,128]{1,0:T(8,128)S(1)}, u32[]{:S(2)}, u32[]{:S(2)}) collective-permute-start(f32[520,128]{1,0:T(8,128)S(1)} %get-tuple-element.44.rest_0_), channel_id=1, source_target_pairs={{0,4},{4,0},{1,5},{5,1},{2,6},{6,2},{3,7},{7,3},{8,12},{12,8},{9,1... | collective-permute-start | bytes 798728 | tf_op jit(solution)/shard_map/ppermute | solution.py:612
  106.0 24.9 %collective-permute-start.9 = (f32[512,128]{1,0:T(8,128)S(1)}, f32[512,128]{1,0:T(8,128)S(1)}, u32[]{:S(2)}, u32[]{:S(2)}) collective-permute-start(f32[512,128]{1,0:T(8,128)S(1)} %get-tuple-element.50.rest_0_), channel_id=1, source_target_pairs={{0,4},{4,0},{1,5},{5,1},{2,6},{6,2},{3,7},{7,3},{8,12},{12,8},{9,1... | collective-permute-start | bytes 786440 | tf_op jit(solution)/shard_map/ppermute | solution.py:612
  132.9 10.6 %all-to-all-start.1 = ((f32[16,2,16,128]{3,2,1,0:T(8,128)}), f32[16,2,16,128]{3,2,1,0:T(8,128)S(1)}, u32[]{:S(2)}, u32[]{:S(2)}) async-start(f32[16,2,16,128]{3,2,1,0:T(8,128)} %bitcast.28), calls=%async_computation.1 | async-start | bytes 524288 | tf_op jit(solution)/shard_map/all_to_all | solution.py:740

commit v9 on v8

--- a/solution.py
+++ b/solution.py
@@ -130,9 +130,13 @@
             jnp.concatenate([hop_rows(g, side), hop_rows(g + 1, side)], 0) * window_ref[side]
             for side in range(2)
         ]
-        high, low = split_values(jnp.concatenate(columns, 1))
-        section = dot(first_ref[...], high)
-        section = section[:SPLIT] + (section[SPLIT:] + dot(first_ref[:SPLIT, :], low))
+        values = jnp.concatenate(columns, 1)
+        high, low = split_values(values)
+        rest = ((values - high.astype(jnp.float32)) - low.astype(jnp.float32)).astype(jnp.bfloat16)
+        large = dot(first_ref[...], high)
+        small = dot(first_ref[...], low)
+        section = (small[SPLIT:] + dot(first_ref[:SPLIT, :], rest)) + (large[SPLIT:] + small[:SPLIT])
+        section = large[:SPLIT] + section
         a, b = section[:half], section[half:]
         real = a * twiddle_ref[0] + b * twiddle_ref[1]
         imag = b * twiddle_ref[2] - a * twiddle_ref[1]

time: 145 us -> 147 us (1.014)
  Pallas kernels: 23.9 us -> 26.2 us
    pallas_call x1, Pallas kernels: 9.05 us -> 10.8 us  [spectrum_blocks(): pl.pallas_call(functools.partial(early_kernel, places, per_member, frames...]
  transfers between devices with their start and end apart: 12 -> 12, of which waited for: 9 -> 9; matrix products, arithmetic and copies ran while one was open for 2% -> 2% of each run, Pallas kernels for 11% -> 12%
where the time goes in v9:
time: 147 us
  waiting for transfers between devices  89.3 us (61%)
  Pallas kernels  26.2 us (18%)
  starting transfers between devices  26.1 us (18%)
  other arithmetic  1.97 us (1%)
  local copies, waits for them, and re-layouts  1.89 us (1%)
    all_to_all x1, waiting for transfers between devices, on_device(): spectrum = lax.all_to_all(spectrum, exchange, 0, 0, tiled=True)  54.7 us
    ppermute x9, waiting for transfers between devices, swap_by(): return lax.ppermute(value, axis, [(i, i ^ mask) for i in range(count)])  28.8 us
    ppermute x9, starting transfers between devices, swap_by(): return lax.ppermute(value, axis, [(i, i ^ mask) for i in range(count)])  16.4 us
    pallas_call x4, Pallas kernels, update_call(): pl.pallas_call(kernel, in_specs=[pl.BlockSpec(memory_space=pltpu.SMEM) fo...  11.5 us
    pallas_call x1, Pallas kernels, spectrum_blocks(): pl.pallas_call(functools.partial(early_kernel, places, per_member, frames...  10.8 us
    all_to_all x1, waiting for transfers between devices, on_device(): lax.all_to_all(payload.reshape(partners, 2, ranks_here, width), exchange,...  5.83 us
    all_to_all x1, starting transfers between devices, on_device(): spectrum = lax.all_to_all(spectrum, exchange, 0, 0, tiled=True)  4.86 us
    pallas_call x1, Pallas kernels, spectrum_blocks(): pl.pallas_call(functools.partial(late_kernel, places, per_member, frames)...  3.96 us
  transfers between devices with their start and end apart: 12, of which 9 were waited for; matrix products, arithmetic and copies ran while one was open for 2% of the time, Pallas kernels for 12%

profile of v9, /device:TPU:0, one launch (start us, length us, event | category | flops | bytes accessed | tf_op | source)
XLA Modules:
  0.0 146.5 jit_solution(7411323190422989339)
XLA Ops:
  0.6 0.9 slice.90
  1.5 1.3 collective-permute-start
  2.8 6.5 %collective-permute-start.1 = (f32[64,1024]{1,0:T(8,128)}, f32[64,1024]{1,0:T(8,128)S(1)}, u32[]{:S(2)}, u32[]{:S(2)}) collective-permute-start(f32[64,1024]{1,0:T(8,128)} %param.10), channel_id=1, source_target_pairs={{0,4},{4,0},{1,5},{5,1},{2,6},{6,2},{3,7},{7,3},{8,12},{12,8},{9,1... | collective-permute-start | bytes 786440 | tf_op jit(solution)/shard_map/ppermute | solution.py:616
  9.3 0.0 copy-start
  9.3 10.8 %shard_map.104 = (f32[16,528,128]{2,1,0:T(8,128)}, f32[2048,128]{1,0:T(8,128)S(1)}, f32[3,16,128,128]{3,2,1,0:T(8,128)S(1)}, f32[2,256,128]{2,1,0:T(8,128)S(1)},...) custom-call(f32[8192,128]{1,0:T(8,128)} %bitcast.115, ...), custom_call_target="tpu_custom_call" | custom-call | flops 4831838208 | bytes 6291456 | tf_op jit(solution)/shard_map/pallas_call | solution.py:322
  20.2 0.0 collective-permute-done.trailing_ref
  20.2 0.0 copy-done
  20.2 4.0 %shard_map.105 = f32[16,528,128]{2,1,0:T(8,128)} custom-call(f32[3,16,128,128]{3,2,1,0:T(8,128)S(1)} %get-tuple-element.28.done_ref, f32[2048,128]{1,0:T(8,128)S(1)} %get-tuple-element.29.tail_ref, f32[256,128]{1,0:T(8,128)S(1)} %collective-permute-done.trailing_ref, f32[16,128]{1,0:T(8,128)S(1)} %copy-done, ...), custom_call_target="tpu_custom_call", output_to_operand_aliasing={{}: (10, {})} | custom-call | flops 1610612736 | bytes 2097152 | tf_op jit(solution)/shard_map/pallas_call | solution.py:336
  24.1 0.0 copy-start.1
  24.2 0.0 collective-permute-done.1
  24.2 4.9 %all-to-all-start = ((f32[16,528,128]{2,1,0:T(8,128)}), f32[16,528,128]{2,1,0:T(8,128)}, u32[]{:S(2)}, u32[]{:S(2)}) async-start(f32[16,528,128]{2,1,0:T(8,128)} %shard_map.105), calls=%async_computation | async-start | bytes 8650752 | tf_op jit(solution)/shard_map/all_to_all | solution.py:660
  29.1 0.1 fusion.6
  29.1 0.0 copy-done.1
  29.3 0.2 slice.117
  29.5 0.2 slice.94
  29.7 0.2 maximum_select_fusion.1
  30.1 54.7 %all-to-all-done.received_ref = f32[16,528,128]{2,1,0:T(8,128)} async-done(((f32[16,528,128]{2,1,0:T(8,128)}), f32[16,528,128]{2,1,0:T(8,128)}, u32[]{:S(2)}, u32[]{:S(2)}) %all-to-all-start) | async-done | bytes 4325408 | tf_op jit(solution)/shard_map/all_to_all | solution.py:660
  84.8 4.8 %shard_map.106 = (f32[136,128]{1,0:T(8,128)S(1)}, f32[136,128]{1,0:T(8,128)S(1)}, f32[512,64]{1,0:T(8,128)S(1)}, f32[16,512,128]{2,1,0:T(8,128)S(1)}) custom-call(s32[1]{0:T(128)} %bitcast.side_ref, f32[16,528,128]{2,1,0:T(8,128)} %all-to-all-done.received_ref, f32[16,64,128]{2,1,0:T(8,128)S(1)} %constant_dynamic-update-slice_fusion.basis_ref), custom_call_target="tpu_custom_call" | custom-call | flops 1107296256 | bytes 4325376 | tf_op jit(solution)/shard_map/pallas_call | solution.py:592
  89.6 2.3 %collective-permute-start.2 = (f32[136,128]{1,0:T(8,128)S(1)}, f32[136,128]{1,0:T(8,128)S(1)}, u32[]{:S(2)}, u32[]{:S(2)}) collective-permute-start(f32[136,128]{1,0:T(8,128)S(1)} %get-tuple-element.42), channel_id=1, source_target_pairs={{0,8},{8,0},{16,24},{24,16},{1,9},{9,1},{17,25},{25,17},{2,10},{10... | collective-permute-start | bytes 208904 | tf_op jit(solution)/shard_map/ppermute | solution.py:616
  91.9 0.9 collective-permute-done.2
  92.8 1.1 collective-permute-start.3
  93.9 3.4 %collective-permute-done.3 = f32[136,128]{1,0:T(8,128)S(1)} collective-permute-done((f32[136,128]{1,0:T(8,128)S(1)}, f32[136,128]{1,0:T(8,128)S(1)}, u32[]{:S(2)}, u32[]{:S(2)}) %collective-permute-start.3) | collective-permute-done | bytes 69664 | tf_op jit(solution)/shard_map/ppermute | solution.py:616
  97.3 0.6 collective-permute-start.4
  97.9 0.0 collective-permute-start.5
  97.9 2.9 %collective-permute-start.6 = (f32[136,128]{1,0:T(8,128)S(1)}, f32[136,128]{1,0:T(8,128)S(1)}, u32[]{:S(2)}, u32[]{:S(2)}) collective-permute-start(f32[136,128]{1,0:T(8,128)S(1)} %add.90), channel_id=1, source_target_pairs={{0,3},{1,2},{2,1},{3,0},{4,7},{5,6},{6,5},{7,4},{8,11},{9,10},{10,... | collective-permute-start | bytes 208904 | tf_op jit(solution)/shard_map/ppermute | solution.py:616
  100.8 1.6 %collective-permute-done.4 = f32[136,128]{1,0:T(8,128)S(1)} collective-permute-done((f32[136,128]{1,0:T(8,128)S(1)}, f32[136,128]{1,0:T(8,128)S(1)}, u32[]{:S(2)}, u32[]{:S(2)}) %collective-permute-start.4) | collective-permute-done | bytes 69664 | tf_op jit(solution)/shard_map/ppermute | solution.py:616
  102.4 0.0 collective-permute-done.5
  102.4 1.5 collective-permute-done.6
  103.9 0.1 collective-permute-start.7
  104.0 1.2 collective-permute-done.7.other_ref
  105.2 1.7 %shard_map.107 = (f32[512,64]{1,0:T(8,128)S(1)}, f32[520,128]{1,0:T(8,128)S(1)}, f32[512,128]{1,0:T(8,128)S(1)}) custom-call(s32[1]{0:T(128)} %bitcast.side_ref, f32[16,512,128]{2,1,0:T(8,128)S(1)} %get-tuple-element.39.spectrum_ref, f32[16,64,128]{2,1,0:T(8,128)S(1)} %constant_dynamic-update-slice_fusion.basis_ref, ...), custom_call_target="tpu_custom_call" | custom-call | flops 1073741824 | bytes 4194304 | tf_op jit(solution)/shard_map/pallas_call | solution.py:592
  107.0 0.1 collective-permute-start.8
  107.0 2.9 %collective-permute-start.9 = (f32[512,128]{1,0:T(8,128)S(1)}, f32[512,128]{1,0:T(8,128)S(1)}, u32[]{:S(2)}, u32[]{:S(2)}) collective-permute-start(f32[512,128]{1,0:T(8,128)S(1)} %get-tuple-element.50.rest_0_), channel_id=1, source_target_pairs={{0,4},{4,0},{1,5},{5,1},{2,6},{6,2},{3,7},{7,3},{8,12},{12,8},{9,1... | collective-permute-start | bytes 786440 | tf_op jit(solution)/shard_map/ppermute | solution.py:616
  110.0 0.1 constant_dynamic-slice_fusion
  110.0 0.1 copy.23
  110.1 18.4 %collective-permute-done.8.rest_1_ = f32[520,128]{1,0:T(8,128)S(1)} collective-permute-done((f32[520,128]{1,0:T(8,128)S(1)}, f32[520,128]{1,0:T(8,128)S(1)}, u32[]{:S(2)}, u32[]{:S(2)}) %collective-permute-start.8) | collective-permute-done | bytes 266272 | tf_op jit(solution)/shard_map/ppermute | solution.py:616
  128.5 3.0 %shard_map.108 = (f32[8,64,128]{2,1,0:T(8,128)S(1)}, f32[512,128]{1,0:T(8,128)S(1)}, f32[16,128]{1,0:T(8,128)S(1)}, bf16[512,256]{1,0:T(8,128)(2,1)S(1)}, f32[64...) custom-call(f32[16,528,128]{2,1,0:T(8,128)} %all-to-all-done.received_ref, ...), custom_call_target="tpu_custom_call" | custom-call | flops 1107296256 | bytes 4325376 | tf_op jit(solution)/shard_map/pallas_call | solution.py:592
  131.5 1.8 %collective-permute-done.9.rest_1_ = f32[512,128]{1,0:T(8,128)S(1)} collective-permute-done((f32[512,128]{1,0:T(8,128)S(1)}, f32[512,128]{1,0:T(8,128)S(1)}, u32[]{:S(2)}, u32[]{:S(2)}) %collective-permute-start.9) | collective-permute-done | bytes 262176 | tf_op jit(solution)/shard_map/ppermute | solution.py:616
  133.3 2.0 %shard_map.109 = (f32[8,64,128]{2,1,0:T(8,128)S(1)}, f32[4,4,2,16,128]{4,3,2,1,0:T(8,128)}) custom-call(f32[16,512,128]{2,1,0:T(8,128)S(1)} %get-tuple-element.45.spectrum_ref, f32[16,64,128]{2,1,0:T(8,128)S(1)} %constant_dynamic-update-slice_fusion.basis_ref, bf16[512,256]{1,0:T(8,128)(2,1)S(1)} %get-tuple-element.46.lanes_ref, ...), custom_call_target="tpu_custom_call" | custom-call | flops 1073741824 | bytes 4194304 | tf_op jit(solution)/shard_map/pallas_call | solution.py:592
  135.3 3.5 %all-to-all-start.1 = ((f32[16,2,16,128]{3,2,1,0:T(8,128)}), f32[16,2,16,128]{3,2,1,0:T(8,128)S(1)}, u32[]{:S(2)}, u32[]{:S(2)}) async-start(f32[16,2,16,128]{3,2,1,0:T(8,128)} %bitcast.28), calls=%async_computation.1 | async-start | bytes 524288 | tf_op jit(solution)/shard_map/all_to_all | solution.py:744
  138.9 0.1 fusion.1
  139.0 0.1 slice.137
  139.1 0.1 slice.115
  139.2 0.9 copy_bitcast_fusion
  140.1 5.8 %all-to-all-done.1 = f32[16,2,16,128]{3,2,1,0:T(8,128)S(1)} async-done(((f32[16,2,16,128]{3,2,1,0:T(8,128)}), f32[16,2,16,128]{3,2,1,0:T(8,128)S(1)}, u32[]{:S(2)}, u32[]{:S(2)}) %all-to-all-start.1) | async-done | bytes 262176 | tf_op jit(solution)/shard_map/all_to_all | solution.py:744
  145.9 0.6 fusion.4
  (30 shorter events, 0.3 us)
Async XLA Ops:
  1.5 18.6 %collective-permute-start = (f32[256,128]{1,0:T(8,128)S(1)}, f32[256,128]{1,0:T(8,128)S(1)}, u32[]{:S(2)}, u32[]{:S(2)}) collective-permute-start(f32[256,128]{1,0:T(8,128)S(1)} %bitcast.114), channel_id=1, source_target_pairs={{8,0},{9,1},{10,2},{11,3},{12,4},{13,5},{14,6},{15,7},{16,8},{17,9... | collective-permute-start | bytes 393224 | tf_op jit(solution)/shard_map/ppermute | solution.py:654
  2.8 21.3 %collective-permute-start.1 = (f32[64,1024]{1,0:T(8,128)}, f32[64,1024]{1,0:T(8,128)S(1)}, u32[]{:S(2)}, u32[]{:S(2)}) collective-permute-start(f32[64,1024]{1,0:T(8,128)} %param.10), channel_id=1, source_target_pairs={{0,4},{4,0},{1,5},{5,1},{2,6},{6,2},{3,7},{7,3},{8,12},{12,8},{9,1... | collective-permute-start | bytes 786440 | tf_op jit(solution)/shard_map/ppermute | solution.py:616
  9.3 10.8 %copy-start = (f32[16,128]{1,0:T(8,128)S(1)}, f32[16,128]{1,0:T(8,128)}, u32[]{:S(2)}) copy-start(f32[16,128]{1,0:T(8,128)} %activity_ref.1) | copy-start | bytes 24580
  24.1 5.0 %copy-start.1 = (f32[64,1024]{1,0:T(8,128)S(1)}, f32[64,1024]{1,0:T(8,128)}, u32[]{:S(2)}) copy-start(f32[64,1024]{1,0:T(8,128)} %param.10) | copy-start | bytes 786436
  24.2 60.6 %all-to-all-start = ((f32[16,528,128]{2,1,0:T(8,128)}), f32[16,528,128]{2,1,0:T(8,128)}, u32[]{:S(2)}, u32[]{:S(2)}) async-start(f32[16,528,128]{2,1,0:T(8,128)} %shard_map.105), calls=%async_computation | async-start | bytes 8650752 | tf_op jit(solution)/shard_map/all_to_all | solution.py:660
  89.6 3.2 %collective-permute-start.2 = (f32[136,128]{1,0:T(8,128)S(1)}, f32[136,128]{1,0:T(8,128)S(1)}, u32[]{:S(2)}, u32[]{:S(2)}) collective-permute-start(f32[136,128]{1,0:T(8,128)S(1)} %get-tuple-element.42), channel_id=1, source_target_pairs={{0,8},{8,0},{16,24},{24,16},{1,9},{9,1},{17,25},{25,17},{2,10},{10... | collective-permute-start | bytes 208904 | tf_op jit(solution)/shard_map/ppermute | solution.py:616
  92.8 4.5 %collective-permute-start.3 = (f32[136,128]{1,0:T(8,128)S(1)}, f32[136,128]{1,0:T(8,128)S(1)}, u32[]{:S(2)}, u32[]{:S(2)}) collective-permute-start(f32[136,128]{1,0:T(8,128)S(1)} %add.89), channel_id=1, source_target_pairs={{0,16},{8,24},{16,0},{24,8},{1,17},{9,25},{17,1},{25,9},{2,18},{10... | collective-permute-start | bytes 208904 | tf_op jit(solution)/shard_map/ppermute | solution.py:616
  97.3 5.1 %collective-permute-start.4 = (f32[136,128]{1,0:T(8,128)S(1)}, f32[136,128]{1,0:T(8,128)S(1)}, u32[]{:S(2)}, u32[]{:S(2)}) collective-permute-start(f32[136,128]{1,0:T(8,128)S(1)} %add.90), channel_id=1, source_target_pairs={{0,1},{1,0},{2,3},{3,2},{4,5},{5,4},{6,7},{7,6},{8,9},{9,8},{10,11... | collective-permute-start | bytes 208904 | tf_op jit(solution)/shard_map/ppermute | solution.py:616
  97.9 4.5 %collective-permute-start.5 = (f32[136,128]{1,0:T(8,128)S(1)}, f32[136,128]{1,0:T(8,128)S(1)}, u32[]{:S(2)}, u32[]{:S(2)}) collective-permute-start(f32[136,128]{1,0:T(8,128)S(1)} %add.90), channel_id=1, source_target_pairs={{0,2},{1,3},{2,0},{3,1},{4,6},{5,7},{6,4},{7,5},{8,10},{9,11},{10,... | collective-permute-start | bytes 208904 | tf_op jit(solution)/shard_map/ppermute | solution.py:616
  97.9 6.0 %collective-permute-start.6 = (f32[136,128]{1,0:T(8,128)S(1)}, f32[136,128]{1,0:T(8,128)S(1)}, u32[]{:S(2)}, u32[]{:S(2)}) collective-permute-start(f32[136,128]{1,0:T(8,128)S(1)} %add.90), channel_id=1, source_target_pairs={{0,3},{1,2},{2,1},{3,0},{4,7},{5,6},{6,5},{7,4},{8,11},{9,10},{10,... | collective-permute-start | bytes 208904 | tf_op jit(solution)/shard_map/ppermute | solution.py:616
  103.9 1.3 collective-permute-start.7
  107.0 21.5 %collective-permute-start.8 = (f32[520,128]{1,0:T(8,128)S(1)}, f32[520,128]{1,0:T(8,128)S(1)}, u32[]{:S(2)}, u32[]{:S(2)}) collective-permute-start(f32[520,128]{1,0:T(8,128)S(1)} %get-tuple-element.44.rest_0_), channel_id=1, source_target_pairs={{0,4},{4,0},{1,5},{5,1},{2,6},{6,2},{3,7},{7,3},{8,12},{12,8},{9,1... | collective-permute-start | bytes 798728 | tf_op jit(solution)/shard_map/ppermute | solution.py:616
  107.0 26.3 %collective-permute-start.9 = (f32[512,128]{1,0:T(8,128)S(1)}, f32[512,128]{1,0:T(8,128)S(1)}, u32[]{:S(2)}, u32[]{:S(2)}) collective-permute-start(f32[512,128]{1,0:T(8,128)S(1)} %get-tuple-element.50.rest_0_), channel_id=1, source_target_pairs={{0,4},{4,0},{1,5},{5,1},{2,6},{6,2},{3,7},{7,3},{8,12},{12,8},{9,1... | collective-permute-start | bytes 786440 | tf_op jit(solution)/shard_map/ppermute | solution.py:616
  135.3 10.6 %all-to-all-start.1 = ((f32[16,2,16,128]{3,2,1,0:T(8,128)}), f32[16,2,16,128]{3,2,1,0:T(8,128)S(1)}, u32[]{:S(2)}, u32[]{:S(2)}) async-start(f32[16,2,16,128]{3,2,1,0:T(8,128)} %bitcast.28), calls=%async_computation.1 | async-start | bytes 524288 | tf_op jit(solution)/shard_map/all_to_all | solution.py:744

commit v10 on v8

--- a/solution.py
+++ b/solution.py
@@ -46,15 +46,26 @@
     return unit // 2 if unit % 2 == 0 else SPLIT - 1 - unit // 2
 
 
+def lane_order():
+    return np.concatenate([np.arange(0, SPLIT // 2, 2), np.arange(1, SPLIT // 2, 2)])
+
+
 @functools.lru_cache(maxsize=None)
 def tables(unit_order):
     half = SPLIT // 2
     index = np.arange(SPLIT, dtype=np.float64)
     slot = np.arange(half, dtype=np.float64)
-    angle = 2.0 * np.pi / SPLIT * np.mod(np.outer(np.arange(half + 1), np.arange(SPLIT)), SPLIT)
-    cosine, sine = np.cos(angle), np.sin(angle)
-    first = np.concatenate([cosine[:half], cosine[half:], -sine[1:half]], 0)
-    turn = 2.0 * np.pi / (SPLIT * SPLIT) * np.outer(slot, index)
+    firsts = []
+    for parity in range(2):
+        angle = 2.0 * np.pi / SPLIT * np.mod(np.outer(lane_order()[parity * half // 2 :][: half // 2], slot), SPLIT)
+        matrix = np.concatenate([np.cos(angle), -np.sin(angle)], 0)
+        if parity == 0:
+            matrix[half // 2] = np.cos(np.pi * slot)
+        firsts.append(high_low(matrix))
+    zeros = np.zeros_like(firsts[0][0])
+    first = [np.concatenate([np.concatenate([part, part], 1) for part in parts], 0) for parts in firsts]
+    first.append(np.block([[firsts[0][0], zeros], [zeros, firsts[1][0]]]))
+    turn = 2.0 * np.pi / (SPLIT * SPLIT) * np.outer(lane_order(), index)
     twiddle_cos, twiddle_sin = np.cos(turn), np.sin(turn)
     masked_cos = twiddle_cos.copy()
     masked_cos[0] = 0.0
@@ -82,7 +93,7 @@
     window = window.reshape(SPLIT, 2, LANES).transpose(1, 0, 2)
     return (
         np.ascontiguousarray(window),
-        both_parts_below(first),
+        np.stack(first),
         twiddle,
         rows,
         np.stack(seconds),
@@ -126,19 +137,29 @@
         return both[:SPLIT] + (both[SPLIT:] + dot_nt(second_ref[parity, :SPLIT, :], parts[:, SPLIT:]))
 
     for g in range(GROUP):
-        columns = [
-            jnp.concatenate([hop_rows(g, side), hop_rows(g + 1, side)], 0) * window_ref[side]
-            for side in range(2)
-        ]
-        high, low = split_values(jnp.concatenate(columns, 1))
-        section = dot(first_ref[...], high)
-        section = section[:SPLIT] + (section[SPLIT:] + dot(first_ref[:SPLIT, :], low))
-        a, b = section[:half], section[half:]
+        top, bottom = (
+            jnp.concatenate([hop_rows(g + hop, side) * window_ref[side, rows, :] for side in range(2)], 1)
+            for hop, rows in enumerate((slice(0, half), slice(half, SPLIT)))
+        )
+        sections, rests = [], []
+        for parity, values in enumerate((top + bottom, top - bottom)):
+            high, low = split_values(values)
+            rests.append(
+                ((values - high.astype(jnp.float32)) - low.astype(jnp.float32)).astype(jnp.bfloat16)
+            )
+            sections.append(dot(first_ref[parity], jnp.concatenate([high, low], 0)))
+        rest = dot(first_ref[2], jnp.concatenate(rests, 0))
+        even, odd = (
+            section[:half] + (section[half:] + rest[parity * half : (parity + 1) * half])
+            for parity, section in enumerate(sections)
+        )
+        a = jnp.concatenate([even[: half // 2], odd[: half // 2]], 0)
+        b = jnp.concatenate([even[half // 2 :], odd[half // 2 :]], 0)
         real = a * twiddle_ref[0] + b * twiddle_ref[1]
         imag = b * twiddle_ref[2] - a * twiddle_ref[1]
         for parity, values in enumerate(even_odd(real, imag)):
             parts_ref[parity, g * half : (g + 1) * half, :] = in_parts(values)
-        nyquist = section[half : half + 1]
+        nyquist = b[:1]
         for parity, values in enumerate(even_odd(nyquist * rows_ref[0:1], nyquist * rows_ref[1:2])):
             middle_ref[parity, g : g + 1, :] = values
 
@@ -603,8 +624,25 @@
     )(*scalars, spectrum, *operands)
 
 
-def turned_lanes(values):
-    return jnp.roll(jnp.flip(values, -1), 1, -1)
+def reorder(values, is_turned, back):
+    order = lane_order()
+    places = np.stack([order, -order % LANES])
+    moves = np.zeros((2, LANES, LANES), np.float32)
+    for move, place in zip(moves, places):
+        move[place, np.arange(LANES)] = 1.0
+    if back:
+        moves = moves.transpose(0, 2, 1)
+    moved = [
+        lax.dot_general(
+            values,
+            jnp.asarray(move),
+            (((values.ndim - 1,), (0,)), ((), ())),
+            precision=lax.Precision.HIGHEST,
+            preferred_element_type=jnp.float32,
+        )
+        for move in moves
+    ]
+    return jnp.where(is_turned, moved[1], moved[0])
 
 
 def swap_by(value, axis, mask):
@@ -667,7 +705,7 @@
         me_sub * blocks + jnp.arange(groups)[:, None] * members + me_member
     ) + jnp.arange(units_here)[None, :]
     is_turned = (unit_index % 2 == 1)[:, :, None, None]
-    by_group = jnp.where(is_turned, turned_lanes(by_group), by_group)
+    by_group = reorder(by_group, is_turned, False)
     basis = jnp.concatenate([by_group[group, r][None] for group, r in kept], 0)
 
     lanes_scratch = pltpu.VMEM((frames, 4 * rank), jnp.bfloat16)
@@ -757,7 +795,7 @@
     )
     back = lax.dynamic_index_in_dim(back, me_group, 0, keepdims=False)
     turned_here = lax.dynamic_index_in_dim(is_turned, me_group, 0, keepdims=False)
-    back = jnp.where(turned_here, turned_lanes(back), back)
+    back = reorder(back, turned_here, True)
     final_templates = back.transpose(1, 0, 2).reshape(rank, bins_here)
     return (final_activations, final_templates)
 

time: 145 us -> 145 us (level)
  matrix products: 0 us -> 1.86 us
    dot_general x0 -> x4, matrix products: none -> 1.86 us  [reorder(): lax.dot_general(values, jnp.asarray(move), (((values.ndim - 1,), (0,)), (...]
where the time goes in v10:
time: 145 us
  waiting for transfers between devices  88.5 us (61%)
  starting transfers between devices  26.1 us (18%)
  Pallas kernels  24.2 us (17%)
  local copies, waits for them, and re-layouts  1.98 us (1%)
  matrix products  1.86 us (1%)
    all_to_all x1, waiting for transfers between devices, on_device(): spectrum = lax.all_to_all(spectrum, exchange, 0, 0, tiled=True)  54.2 us
    ppermute x9, waiting for transfers between devices, swap_by(): return lax.ppermute(value, axis, [(i, i ^ mask) for i in range(count)])  28.8 us
    ppermute x9, starting transfers between devices, swap_by(): return lax.ppermute(value, axis, [(i, i ^ mask) for i in range(count)])  16.4 us
    pallas_call x4, Pallas kernels, update_call(): pl.pallas_call(kernel, in_specs=[pl.BlockSpec(memory_space=pltpu.SMEM) fo...  11.5 us
    pallas_call x1, Pallas kernels, spectrum_blocks(): pl.pallas_call(functools.partial(early_kernel, places, per_member, frames...  9.33 us
    all_to_all x1, waiting for transfers between devices, on_device(): lax.all_to_all(payload.reshape(partners, 2, ranks_here, width), exchange,...  5.54 us
    all_to_all x1, starting transfers between devices, on_device(): spectrum = lax.all_to_all(spectrum, exchange, 0, 0, tiled=True)  4.86 us
    all_to_all x1, starting transfers between devices, on_device(): lax.all_to_all(payload.reshape(partners, 2, ranks_here, width), exchange,...  3.53 us
  transfers between devices with their start and end apart: 12, of which 9 were waited for; matrix products, arithmetic and copies ran while one was open for 2% of the time, Pallas kernels for 11%

profile of v10, /device:TPU:0, one launch (start us, length us, event | category | flops | bytes accessed | tf_op | source)
XLA Modules:
  0.0 144.5 jit_solution(3953141608692645166)
XLA Ops:
  0.6 0.9 slice.66
  1.5 1.3 collective-permute-start
  2.8 6.5 %collective-permute-start.1 = (f32[64,1024]{1,0:T(8,128)}, f32[64,1024]{1,0:T(8,128)S(1)}, u32[]{:S(2)}, u32[]{:S(2)}) collective-permute-start(f32[64,1024]{1,0:T(8,128)} %param.14), channel_id=1, source_target_pairs={{0,4},{4,0},{1,5},{5,1},{2,6},{6,2},{3,7},{7,3},{8,12},{12,8},{9,1... | collective-permute-start | bytes 786440 | tf_op jit(solution)/shard_map/ppermute | solution.py:650
  9.3 0.0 copy-start
  9.3 9.3 %shard_map.140 = (f32[16,528,128]{2,1,0:T(8,128)}, f32[2048,128]{1,0:T(8,128)S(1)}, f32[3,16,128,128]{3,2,1,0:T(8,128)S(1)}, f32[2,256,128]{2,1,0:T(8,128)S(1)},...) custom-call(f32[8192,128]{1,0:T(8,128)} %bitcast.128, ...), custom_call_target="tpu_custom_call" | custom-call | flops 4831838208 | bytes 6291456 | tf_op jit(solution)/shard_map/pallas_call | solution.py:339
  18.7 0.0 collective-permute-done.trailing_ref
  18.7 0.0 copy-done
  18.7 3.4 %shard_map.141 = f32[16,528,128]{2,1,0:T(8,128)} custom-call(f32[3,16,128,128]{3,2,1,0:T(8,128)S(1)} %get-tuple-element.28.done_ref, f32[2048,128]{1,0:T(8,128)S(1)} %get-tuple-element.29.tail_ref, f32[256,128]{1,0:T(8,128)S(1)} %collective-permute-done.trailing_ref, f32[16,128]{1,0:T(8,128)S(1)} %copy-done, ...), custom_call_target="tpu_custom_call", output_to_operand_aliasing={{}: (10, {})} | custom-call | flops 1610612736 | bytes 2097152 | tf_op jit(solution)/shard_map/pallas_call | solution.py:353
  22.1 0.0 copy-start.1
  22.1 0.0 copy-start.5
  22.1 0.0 copy-start.4
  22.1 0.0 collective-permute-done.1
  22.2 4.9 %all-to-all-start = ((f32[16,528,128]{2,1,0:T(8,128)}), f32[16,528,128]{2,1,0:T(8,128)}, u32[]{:S(2)}, u32[]{:S(2)}) async-start(f32[16,528,128]{2,1,0:T(8,128)} %shard_map.141), calls=%async_computation | async-start | bytes 8650752 | tf_op jit(solution)/shard_map/all_to_all | solution.py:694
  27.1 0.1 fusion.12
  27.1 0.0 copy-done.1
  27.2 0.0 copy-done.5
  27.2 0.6 fusion.1
  27.8 0.0 copy-done.4
  27.8 0.6 convolution_select_fusion
  28.6 54.2 %all-to-all-done.received_ref = f32[16,528,128]{2,1,0:T(8,128)} async-done(((f32[16,528,128]{2,1,0:T(8,128)}), f32[16,528,128]{2,1,0:T(8,128)}, u32[]{:S(2)}, u32[]{:S(2)}) %all-to-all-start) | async-done | bytes 4325408 | tf_op jit(solution)/shard_map/all_to_all | solution.py:694
  82.8 4.8 %shard_map.142 = (f32[136,128]{1,0:T(8,128)S(1)}, f32[136,128]{1,0:T(8,128)S(1)}, f32[512,64]{1,0:T(8,128)S(1)}, f32[16,512,128]{2,1,0:T(8,128)S(1)}) custom-call(s32[1]{0:T(128)} %bitcast.side_ref, f32[16,528,128]{2,1,0:T(8,128)} %all-to-all-done.received_ref, f32[16,64,128]{2,1,0:T(8,128)S(1)} %constant_dynamic-update-slice_fusion.basis_ref), custom_call_target="tpu_custom_call" | custom-call | flops 1107296256 | bytes 4325376 | tf_op jit(solution)/shard_map/pallas_call | solution.py:609
  87.6 2.3 %collective-permute-start.2 = (f32[136,128]{1,0:T(8,128)S(1)}, f32[136,128]{1,0:T(8,128)S(1)}, u32[]{:S(2)}, u32[]{:S(2)}) collective-permute-start(f32[136,128]{1,0:T(8,128)S(1)} %get-tuple-element.42), channel_id=1, source_target_pairs={{0,8},{8,0},{16,24},{24,16},{1,9},{9,1},{17,25},{25,17},{2,10},{10... | collective-permute-start | bytes 208904 | tf_op jit(solution)/shard_map/ppermute | solution.py:650
  89.8 0.9 collective-permute-done.2
  90.8 1.1 collective-permute-start.3
  91.8 3.4 %collective-permute-done.3 = f32[136,128]{1,0:T(8,128)S(1)} collective-permute-done((f32[136,128]{1,0:T(8,128)S(1)}, f32[136,128]{1,0:T(8,128)S(1)}, u32[]{:S(2)}, u32[]{:S(2)}) %collective-permute-start.3) | collective-permute-done | bytes 69664 | tf_op jit(solution)/shard_map/ppermute | solution.py:650
  95.3 0.6 collective-permute-start.4
  95.9 0.0 collective-permute-start.5
  95.9 2.9 %collective-permute-start.6 = (f32[136,128]{1,0:T(8,128)S(1)}, f32[136,128]{1,0:T(8,128)S(1)}, u32[]{:S(2)}, u32[]{:S(2)}) collective-permute-start(f32[136,128]{1,0:T(8,128)S(1)} %add.90), channel_id=1, source_target_pairs={{0,3},{1,2},{2,1},{3,0},{4,7},{5,6},{6,5},{7,4},{8,11},{9,10},{10,... | collective-permute-start | bytes 208904 | tf_op jit(solution)/shard_map/ppermute | solution.py:650
  98.8 1.6 %collective-permute-done.4 = f32[136,128]{1,0:T(8,128)S(1)} collective-permute-done((f32[136,128]{1,0:T(8,128)S(1)}, f32[136,128]{1,0:T(8,128)S(1)}, u32[]{:S(2)}, u32[]{:S(2)}) %collective-permute-start.4) | collective-permute-done | bytes 69664 | tf_op jit(solution)/shard_map/ppermute | solution.py:650
  100.4 0.0 collective-permute-done.5
  100.4 1.5 %collective-permute-done.6 = f32[136,128]{1,0:T(8,128)S(1)} collective-permute-done((f32[136,128]{1,0:T(8,128)S(1)}, f32[136,128]{1,0:T(8,128)S(1)}, u32[]{:S(2)}, u32[]{:S(2)}) %collective-permute-start.6) | collective-permute-done | bytes 69664 | tf_op jit(solution)/shard_map/ppermute | solution.py:650
  101.9 0.1 collective-permute-start.7
  102.0 1.2 collective-permute-done.7.other_ref
  103.2 1.7 %shard_map.143 = (f32[512,64]{1,0:T(8,128)S(1)}, f32[520,128]{1,0:T(8,128)S(1)}, f32[512,128]{1,0:T(8,128)S(1)}) custom-call(s32[1]{0:T(128)} %bitcast.side_ref, f32[16,512,128]{2,1,0:T(8,128)S(1)} %get-tuple-element.39.spectrum_ref, f32[16,64,128]{2,1,0:T(8,128)S(1)} %constant_dynamic-update-slice_fusion.basis_ref, ...), custom_call_target="tpu_custom_call" | custom-call | flops 1073741824 | bytes 4194304 | tf_op jit(solution)/shard_map/pallas_call | solution.py:609
  104.9 1.1 collective-permute-start.8
  106.0 1.9 %collective-permute-start.9 = (f32[512,128]{1,0:T(8,128)S(1)}, f32[512,128]{1,0:T(8,128)S(1)}, u32[]{:S(2)}, u32[]{:S(2)}) collective-permute-start(f32[512,128]{1,0:T(8,128)S(1)} %get-tuple-element.50.rest_0_), channel_id=1, source_target_pairs={{0,4},{4,0},{1,5},{5,1},{2,6},{6,2},{3,7},{7,3},{8,12},{12,8},{9,1... | collective-permute-start | bytes 786440 | tf_op jit(solution)/shard_map/ppermute | solution.py:650
  107.9 0.1 constant_dynamic-slice_fusion
  108.0 0.1 copy.25
  108.1 18.4 %collective-permute-done.8.rest_1_ = f32[520,128]{1,0:T(8,128)S(1)} collective-permute-done((f32[520,128]{1,0:T(8,128)S(1)}, f32[520,128]{1,0:T(8,128)S(1)}, u32[]{:S(2)}, u32[]{:S(2)}) %collective-permute-start.8) | collective-permute-done | bytes 266272 | tf_op jit(solution)/shard_map/ppermute | solution.py:650
  126.4 3.0 %shard_map.144 = (f32[8,64,128]{2,1,0:T(8,128)S(1)}, f32[512,128]{1,0:T(8,128)S(1)}, f32[16,128]{1,0:T(8,128)S(1)}, bf16[512,256]{1,0:T(8,128)(2,1)S(1)}, f32[64...) custom-call(f32[16,528,128]{2,1,0:T(8,128)} %all-to-all-done.received_ref, ...), custom_call_target="tpu_custom_call" | custom-call | flops 1107296256 | bytes 4325376 | tf_op jit(solution)/shard_map/pallas_call | solution.py:609
  129.5 0.0 copy-start.3
  129.5 0.0 copy-start.2
  129.5 1.8 %collective-permute-done.9.rest_1_ = f32[512,128]{1,0:T(8,128)S(1)} collective-permute-done((f32[512,128]{1,0:T(8,128)S(1)}, f32[512,128]{1,0:T(8,128)S(1)}, u32[]{:S(2)}, u32[]{:S(2)}) %collective-permute-start.9) | collective-permute-done | bytes 262176 | tf_op jit(solution)/shard_map/ppermute | solution.py:650
  131.3 2.0 %shard_map.145 = (f32[8,64,128]{2,1,0:T(8,128)S(1)}, f32[4,4,2,16,128]{4,3,2,1,0:T(8,128)}) custom-call(f32[16,512,128]{2,1,0:T(8,128)S(1)} %get-tuple-element.45.spectrum_ref, f32[16,64,128]{2,1,0:T(8,128)S(1)} %constant_dynamic-update-slice_fusion.basis_ref, bf16[512,256]{1,0:T(8,128)(2,1)S(1)} %get-tuple-element.46.lanes_ref, ...), custom_call_target="tpu_custom_call" | custom-call | flops 1073741824 | bytes 4194304 | tf_op jit(solution)/shard_map/pallas_call | solution.py:609
  133.3 3.5 %all-to-all-start.1 = ((f32[16,2,16,128]{3,2,1,0:T(8,128)}), f32[16,2,16,128]{3,2,1,0:T(8,128)S(1)}, u32[]{:S(2)}, u32[]{:S(2)}) async-start(f32[16,2,16,128]{3,2,1,0:T(8,128)} %bitcast.32), calls=%async_computation.1 | async-start | bytes 524288 | tf_op jit(solution)/shard_map/all_to_all | solution.py:778
  136.9 0.0 copy-done.3
  136.9 0.4 fusion.7
  137.3 0.0 copy-done.2
  137.3 0.4 fusion
  137.6 0.7 copy.32
  138.4 5.5 %all-to-all-done.1 = f32[16,2,16,128]{3,2,1,0:T(8,128)S(1)} async-done(((f32[16,2,16,128]{3,2,1,0:T(8,128)}), f32[16,2,16,128]{3,2,1,0:T(8,128)S(1)}, u32[]{:S(2)}, u32[]{:S(2)}) %all-to-all-start.1) | async-done | bytes 262176 | tf_op jit(solution)/shard_map/all_to_all | solution.py:778
  143.9 0.6 fusion.10
  (29 shorter events, 0.2 us)
Async XLA Ops:
  1.5 17.1 %collective-permute-start = (f32[256,128]{1,0:T(8,128)S(1)}, f32[256,128]{1,0:T(8,128)S(1)}, u32[]{:S(2)}, u32[]{:S(2)}) collective-permute-start(f32[256,128]{1,0:T(8,128)S(1)} %bitcast.127), channel_id=1, source_target_pairs={{8,0},{9,1},{10,2},{11,3},{12,4},{13,5},{14,6},{15,7},{16,8},{17,9... | collective-permute-start | bytes 393224 | tf_op jit(solution)/shard_map/ppermute | solution.py:688
  2.8 19.3 %collective-permute-start.1 = (f32[64,1024]{1,0:T(8,128)}, f32[64,1024]{1,0:T(8,128)S(1)}, u32[]{:S(2)}, u32[]{:S(2)}) collective-permute-start(f32[64,1024]{1,0:T(8,128)} %param.14), channel_id=1, source_target_pairs={{0,4},{4,0},{1,5},{5,1},{2,6},{6,2},{3,7},{7,3},{8,12},{12,8},{9,1... | collective-permute-start | bytes 786440 | tf_op jit(solution)/shard_map/ppermute | solution.py:650
  9.3 9.3 %copy-start = (f32[16,128]{1,0:T(8,128)S(1)}, f32[16,128]{1,0:T(8,128)}, u32[]{:S(2)}) copy-start(f32[16,128]{1,0:T(8,128)} %activity_ref.1) | copy-start | bytes 24580
  22.1 5.0 %copy-start.1 = (f32[64,1024]{1,0:T(8,128)S(1)}, f32[64,1024]{1,0:T(8,128)}, u32[]{:S(2)}) copy-start(f32[64,1024]{1,0:T(8,128)} %param.14) | copy-start | bytes 786436
  22.1 5.1 %copy-start.5 = (f32[128,128,1,1]{1,0,3,2:T(8,128)S(1)}, f32[128,128,1,1]{1,0,3,2:T(8,128)}, u32[]{:S(2)}) copy-start(f32[128,128,1,1]{1,0,3,2:T(8,128)} %constant.89) | copy-start | bytes 196612
  22.1 5.6 %copy-start.4 = (f32[128,128,1,1]{1,0,3,2:T(8,128)S(1)}, f32[128,128,1,1]{1,0,3,2:T(8,128)}, u32[]{:S(2)}) copy-start(f32[128,128,1,1]{1,0,3,2:T(8,128)} %constant.90) | copy-start | bytes 196612
  22.2 60.6 %all-to-all-start = ((f32[16,528,128]{2,1,0:T(8,128)}), f32[16,528,128]{2,1,0:T(8,128)}, u32[]{:S(2)}, u32[]{:S(2)}) async-start(f32[16,528,128]{2,1,0:T(8,128)} %shard_map.141), calls=%async_computation | async-start | bytes 8650752 | tf_op jit(solution)/shard_map/all_to_all | solution.py:694
  87.6 3.2 %collective-permute-start.2 = (f32[136,128]{1,0:T(8,128)S(1)}, f32[136,128]{1,0:T(8,128)S(1)}, u32[]{:S(2)}, u32[]{:S(2)}) collective-permute-start(f32[136,128]{1,0:T(8,128)S(1)} %get-tuple-element.42), channel_id=1, source_target_pairs={{0,8},{8,0},{16,24},{24,16},{1,9},{9,1},{17,25},{25,17},{2,10},{10... | collective-permute-start | bytes 208904 | tf_op jit(solution)/shard_map/ppermute | solution.py:650
  90.8 4.5 %collective-permute-start.3 = (f32[136,128]{1,0:T(8,128)S(1)}, f32[136,128]{1,0:T(8,128)S(1)}, u32[]{:S(2)}, u32[]{:S(2)}) collective-permute-start(f32[136,128]{1,0:T(8,128)S(1)} %add.89), channel_id=1, source_target_pairs={{0,16},{8,24},{16,0},{24,8},{1,17},{9,25},{17,1},{25,9},{2,18},{10... | collective-permute-start | bytes 208904 | tf_op jit(solution)/shard_map/ppermute | solution.py:650
  95.3 5.1 %collective-permute-start.4 = (f32[136,128]{1,0:T(8,128)S(1)}, f32[136,128]{1,0:T(8,128)S(1)}, u32[]{:S(2)}, u32[]{:S(2)}) collective-permute-start(f32[136,128]{1,0:T(8,128)S(1)} %add.90), channel_id=1, source_target_pairs={{0,1},{1,0},{2,3},{3,2},{4,5},{5,4},{6,7},{7,6},{8,9},{9,8},{10,11... | collective-permute-start | bytes 208904 | tf_op jit(solution)/shard_map/ppermute | solution.py:650
  95.9 4.5 %collective-permute-start.5 = (f32[136,128]{1,0:T(8,128)S(1)}, f32[136,128]{1,0:T(8,128)S(1)}, u32[]{:S(2)}, u32[]{:S(2)}) collective-permute-start(f32[136,128]{1,0:T(8,128)S(1)} %add.90), channel_id=1, source_target_pairs={{0,2},{1,3},{2,0},{3,1},{4,6},{5,7},{6,4},{7,5},{8,10},{9,11},{10,... | collective-permute-start | bytes 208904 | tf_op jit(solution)/shard_map/ppermute | solution.py:650
  95.9 6.0 %collective-permute-start.6 = (f32[136,128]{1,0:T(8,128)S(1)}, f32[136,128]{1,0:T(8,128)S(1)}, u32[]{:S(2)}, u32[]{:S(2)}) collective-permute-start(f32[136,128]{1,0:T(8,128)S(1)} %add.90), channel_id=1, source_target_pairs={{0,3},{1,2},{2,1},{3,0},{4,7},{5,6},{6,5},{7,4},{8,11},{9,10},{10,... | collective-permute-start | bytes 208904 | tf_op jit(solution)/shard_map/ppermute | solution.py:650
  101.9 1.3 collective-permute-start.7
  104.9 21.5 %collective-permute-start.8 = (f32[520,128]{1,0:T(8,128)S(1)}, f32[520,128]{1,0:T(8,128)S(1)}, u32[]{:S(2)}, u32[]{:S(2)}) collective-permute-start(f32[520,128]{1,0:T(8,128)S(1)} %get-tuple-element.44.rest_0_), channel_id=1, source_target_pairs={{0,4},{4,0},{1,5},{5,1},{2,6},{6,2},{3,7},{7,3},{8,12},{12,8},{9,1... | collective-permute-start | bytes 798728 | tf_op jit(solution)/shard_map/ppermute | solution.py:650
  106.0 25.3 %collective-permute-start.9 = (f32[512,128]{1,0:T(8,128)S(1)}, f32[512,128]{1,0:T(8,128)S(1)}, u32[]{:S(2)}, u32[]{:S(2)}) collective-permute-start(f32[512,128]{1,0:T(8,128)S(1)} %get-tuple-element.50.rest_0_), channel_id=1, source_target_pairs={{0,4},{4,0},{1,5},{5,1},{2,6},{6,2},{3,7},{7,3},{8,12},{12,8},{9,1... | collective-permute-start | bytes 786440 | tf_op jit(solution)/shard_map/ppermute | solution.py:650
  129.5 7.4 %copy-start.3 = (f32[128,128,1]{1,0,2:T(8,128)S(1)}, f32[128,128,1]{1,0,2:T(8,128)}, u32[]{:S(2)}) copy-start(f32[128,128,1]{1,0,2:T(8,128)} %constant.91) | copy-start | bytes 196612
  129.5 7.8 %copy-start.2 = (f32[128,128,1]{1,0,2:T(8,128)S(1)}, f32[128,128,1]{1,0,2:T(8,128)}, u32[]{:S(2)}) copy-start(f32[128,128,1]{1,0,2:T(8,128)} %constant.92) | copy-start | bytes 196612
  133.3 10.6 %all-to-all-start.1 = ((f32[16,2,16,128]{3,2,1,0:T(8,128)}), f32[16,2,16,128]{3,2,1,0:T(8,128)S(1)}, u32[]{:S(2)}, u32[]{:S(2)}) async-start(f32[16,2,16,128]{3,2,1,0:T(8,128)} %bitcast.32), calls=%async_computation.1 | async-start | bytes 524288 | tf_op jit(solution)/shard_map/all_to_all | solution.py:778

commit v11 on v10

--- a/solution.py
+++ b/solution.py
@@ -15,6 +15,7 @@
 SPLIT = 256
 LANES = 128
 GROUP = 8
+SPARE = 8
 HOP_ROWS = FRAME_LEN // 2 // LANES
 SPECTRUM_VMEM = 24 * 1024 * 1024
 UPDATE_VMEM = 24 * 1024 * 1024
@@ -248,9 +249,9 @@
         return carry
 
     def send(i):
-        count = group_ref.shape[2]
+        count = per_member * GROUP
         return pltpu.make_async_copy(
-            group_ref.at[i],
+            group_ref.at[i, :, pl.ds(0, count), :],
             out_ref.at[:, pl.ds(pl.multiple_of(i * count, count), count), :],
             out_sem_ref.at[i],
         )
@@ -266,7 +267,7 @@
     count = per_member * GROUP
     before = frames // GROUP - 1
     pass_on = pltpu.make_async_copy(
-        done_ref.at[before - 1], out_ref.at[:, pl.ds((before - 1) * count, count), :], sem_ref.at[0]
+        done_ref.at[before - 1, :, pl.ds(0, count), :], out_ref.at[:, pl.ds((before - 1) * count, count), :], sem_ref.at[0]
     )
     pass_on.start()
 
@@ -315,7 +316,7 @@
     frames = samples.shape[0] // HOP_ROWS
     groups = frames // GROUP - 1
     constants = [jnp.asarray(t) for t in values]
-    group_shape = (members, per_member * GROUP, LANES)
+    group_shape = (members, per_member * GROUP + SPARE, LANES)
     last_shape = (members, per_member * GROUP + activity.shape[0], LANES)
     out_shape = pltpu.HBM((members, per_member * frames + activity.shape[0], LANES), jnp.float32)
     tail_shape = jax.ShapeDtypeStruct((GROUP * HOP_ROWS, LANES), jnp.float32)
@@ -342,7 +343,7 @@
         out_specs=[in_hbm] + [in_vmem] * (2 + len(constants)),
         out_shape=[out_shape, tail_shape, jax.ShapeDtypeStruct((groups, *group_shape), jnp.float32)]
         + [jax.ShapeDtypeStruct(t.shape, t.dtype) for t in constants],
-        scratch_shapes=[pltpu.VMEM(((groups * GROUP + 1) * HOP_ROWS, LANES), jnp.float32)]
+        scratch_shapes=[pltpu.VMEM(((groups * GROUP + 1) * HOP_ROWS + SPARE, LANES), jnp.float32)]
         + scratch
         + [
             pltpu.SemaphoreType.DMA((8 + groups,)),

time: 145 us -> 145 us (level)
  no operation moved by 1% of the time
where the time goes in v11:
time: 145 us
  waiting for transfers between devices  88.5 us (61%)
  starting transfers between devices  26.1 us (18%)
  Pallas kernels  24.3 us (17%)
  local copies, waits for them, and re-layouts  1.98 us (1%)
  matrix products  1.86 us (1%)
    all_to_all x1, waiting for transfers between devices, on_device(): spectrum = lax.all_to_all(spectrum, exchange, 0, 0, tiled=True)  54.2 us
    ppermute x9, waiting for transfers between devices, swap_by(): return lax.ppermute(value, axis, [(i, i ^ mask) for i in range(count)])  28.8 us
    ppermute x9, starting transfers between devices, swap_by(): return lax.ppermute(value, axis, [(i, i ^ mask) for i in range(count)])  16.4 us
    pallas_call x4, Pallas kernels, update_call(): pl.pallas_call(kernel, in_specs=[pl.BlockSpec(memory_space=pltpu.SMEM) fo...  11.5 us
    pallas_call x1, Pallas kernels, spectrum_blocks(): pl.pallas_call(functools.partial(early_kernel, places, per_member, frames...  9.39 us
    all_to_all x1, waiting for transfers between devices, on_device(): lax.all_to_all(payload.reshape(partners, 2, ranks_here, width), exchange,...  5.54 us
    all_to_all x1, starting transfers between devices, on_device(): spectrum = lax.all_to_all(spectrum, exchange, 0, 0, tiled=True)  4.86 us
    all_to_all x1, starting transfers between devices, on_device(): lax.all_to_all(payload.reshape(partners, 2, ranks_here, width), exchange,...  3.53 us
  transfers between devices with their start and end apart: 12, of which 9 were waited for; matrix products, arithmetic and copies ran while one was open for 2% of the time, Pallas kernels for 11%

profile of v11, /device:TPU:0, one launch (start us, length us, event | category | flops | bytes accessed | tf_op | source)
XLA Modules:
  0.0 144.6 jit_solution(8539930284850974594)
XLA Ops:
  0.6 0.9 slice.66
  1.5 1.3 collective-permute-start
  2.8 6.5 %collective-permute-start.1 = (f32[64,1024]{1,0:T(8,128)}, f32[64,1024]{1,0:T(8,128)S(1)}, u32[]{:S(2)}, u32[]{:S(2)}) collective-permute-start(f32[64,1024]{1,0:T(8,128)} %param.14), channel_id=1, source_target_pairs={{0,4},{4,0},{1,5},{5,1},{2,6},{6,2},{3,7},{7,3},{8,12},{12,8},{9,1... | collective-permute-start | bytes 786440 | tf_op jit(solution)/shard_map/ppermute | solution.py:651
  9.3 0.0 copy-start
  9.3 9.4 %shard_map.140 = (f32[16,528,128]{2,1,0:T(8,128)}, f32[2048,128]{1,0:T(8,128)S(1)}, f32[3,16,136,128]{3,2,1,0:T(8,128)S(1)}, f32[2,256,128]{2,1,0:T(8,128)S(1)},...) custom-call(f32[8192,128]{1,0:T(8,128)} %bitcast.128, ...), custom_call_target="tpu_custom_call" | custom-call | flops 4831838208 | bytes 6291456 | tf_op jit(solution)/shard_map/pallas_call | solution.py:340
  18.7 0.0 collective-permute-done.trailing_ref
  18.7 0.0 copy-done
  18.8 3.4 %shard_map.141 = f32[16,528,128]{2,1,0:T(8,128)} custom-call(f32[3,16,136,128]{3,2,1,0:T(8,128)S(1)} %get-tuple-element.28.done_ref, f32[2048,128]{1,0:T(8,128)S(1)} %get-tuple-element.29.tail_ref, f32[256,128]{1,0:T(8,128)S(1)} %collective-permute-done.trailing_ref, f32[16,128]{1,0:T(8,128)S(1)} %copy-done, ...), custom_call_target="tpu_custom_call", output_to_operand_aliasing={{}: (10, {})} | custom-call | flops 1610612736 | bytes 2097152 | tf_op jit(solution)/shard_map/pallas_call | solution.py:354
  22.2 0.0 copy-start.1
  22.2 0.0 copy-start.5
  22.2 0.0 copy-start.4
  22.2 0.0 collective-permute-done.1
  22.2 4.9 %all-to-all-start = ((f32[16,528,128]{2,1,0:T(8,128)}), f32[16,528,128]{2,1,0:T(8,128)}, u32[]{:S(2)}, u32[]{:S(2)}) async-start(f32[16,528,128]{2,1,0:T(8,128)} %shard_map.141), calls=%async_computation | async-start | bytes 8650752 | tf_op jit(solution)/shard_map/all_to_all | solution.py:695
  27.1 0.1 fusion.12
  27.2 0.0 copy-done.1
  27.3 0.0 copy-done.5
  27.3 0.6 fusion.1
  27.8 0.0 copy-done.4
  27.9 0.6 convolution_select_fusion
  28.6 54.2 %all-to-all-done.received_ref = f32[16,528,128]{2,1,0:T(8,128)} async-done(((f32[16,528,128]{2,1,0:T(8,128)}), f32[16,528,128]{2,1,0:T(8,128)}, u32[]{:S(2)}, u32[]{:S(2)}) %all-to-all-start) | async-done | bytes 4325408 | tf_op jit(solution)/shard_map/all_to_all | solution.py:695
  82.8 4.8 %shard_map.142 = (f32[136,128]{1,0:T(8,128)S(1)}, f32[136,128]{1,0:T(8,128)S(1)}, f32[512,64]{1,0:T(8,128)S(1)}, f32[16,512,128]{2,1,0:T(8,128)S(1)}) custom-call(s32[1]{0:T(128)} %bitcast.side_ref, f32[16,528,128]{2,1,0:T(8,128)} %all-to-all-done.received_ref, f32[16,64,128]{2,1,0:T(8,128)S(1)} %constant_dynamic-update-slice_fusion.basis_ref), custom_call_target="tpu_custom_call" | custom-call | flops 1107296256 | bytes 4325376 | tf_op jit(solution)/shard_map/pallas_call | solution.py:610
  87.6 2.3 %collective-permute-start.2 = (f32[136,128]{1,0:T(8,128)S(1)}, f32[136,128]{1,0:T(8,128)S(1)}, u32[]{:S(2)}, u32[]{:S(2)}) collective-permute-start(f32[136,128]{1,0:T(8,128)S(1)} %get-tuple-element.42), channel_id=1, source_target_pairs={{0,8},{8,0},{16,24},{24,16},{1,9},{9,1},{17,25},{25,17},{2,10},{10... | collective-permute-start | bytes 208904 | tf_op jit(solution)/shard_map/ppermute | solution.py:651
  89.9 0.9 collective-permute-done.2
  90.8 1.1 collective-permute-start.3
  91.9 3.4 %collective-permute-done.3 = f32[136,128]{1,0:T(8,128)S(1)} collective-permute-done((f32[136,128]{1,0:T(8,128)S(1)}, f32[136,128]{1,0:T(8,128)S(1)}, u32[]{:S(2)}, u32[]{:S(2)}) %collective-permute-start.3) | collective-permute-done | bytes 69664 | tf_op jit(solution)/shard_map/ppermute | solution.py:651
  95.3 0.6 collective-permute-start.4
  96.0 0.0 collective-permute-start.5
  96.0 2.9 %collective-permute-start.6 = (f32[136,128]{1,0:T(8,128)S(1)}, f32[136,128]{1,0:T(8,128)S(1)}, u32[]{:S(2)}, u32[]{:S(2)}) collective-permute-start(f32[136,128]{1,0:T(8,128)S(1)} %add.90), channel_id=1, source_target_pairs={{0,3},{1,2},{2,1},{3,0},{4,7},{5,6},{6,5},{7,4},{8,11},{9,10},{10,... | collective-permute-start | bytes 208904 | tf_op jit(solution)/shard_map/ppermute | solution.py:651
  98.9 1.6 %collective-permute-done.4 = f32[136,128]{1,0:T(8,128)S(1)} collective-permute-done((f32[136,128]{1,0:T(8,128)S(1)}, f32[136,128]{1,0:T(8,128)S(1)}, u32[]{:S(2)}, u32[]{:S(2)}) %collective-permute-start.4) | collective-permute-done | bytes 69664 | tf_op jit(solution)/shard_map/ppermute | solution.py:651
  100.5 0.0 collective-permute-done.5
  100.5 1.5 %collective-permute-done.6 = f32[136,128]{1,0:T(8,128)S(1)} collective-permute-done((f32[136,128]{1,0:T(8,128)S(1)}, f32[136,128]{1,0:T(8,128)S(1)}, u32[]{:S(2)}, u32[]{:S(2)}) %collective-permute-start.6) | collective-permute-done | bytes 69664 | tf_op jit(solution)/shard_map/ppermute | solution.py:651
  102.0 0.1 collective-permute-start.7
  102.0 1.2 collective-permute-done.7.other_ref
  103.3 1.7 %shard_map.143 = (f32[512,64]{1,0:T(8,128)S(1)}, f32[520,128]{1,0:T(8,128)S(1)}, f32[512,128]{1,0:T(8,128)S(1)}) custom-call(s32[1]{0:T(128)} %bitcast.side_ref, f32[16,512,128]{2,1,0:T(8,128)S(1)} %get-tuple-element.39.spectrum_ref, f32[16,64,128]{2,1,0:T(8,128)S(1)} %constant_dynamic-update-slice_fusion.basis_ref, ...), custom_call_target="tpu_custom_call" | custom-call | flops 1073741824 | bytes 4194304 | tf_op jit(solution)/shard_map/pallas_call | solution.py:610
  105.0 1.0 collective-permute-start.8
  106.0 2.0 %collective-permute-start.9 = (f32[512,128]{1,0:T(8,128)S(1)}, f32[512,128]{1,0:T(8,128)S(1)}, u32[]{:S(2)}, u32[]{:S(2)}) collective-permute-start(f32[512,128]{1,0:T(8,128)S(1)} %get-tuple-element.50.rest_0_), channel_id=1, source_target_pairs={{0,4},{4,0},{1,5},{5,1},{2,6},{6,2},{3,7},{7,3},{8,12},{12,8},{9,1... | collective-permute-start | bytes 786440 | tf_op jit(solution)/shard_map/ppermute | solution.py:651
  108.0 0.1 constant_dynamic-slice_fusion
  108.1 0.1 copy.25
  108.1 18.4 %collective-permute-done.8.rest_1_ = f32[520,128]{1,0:T(8,128)S(1)} collective-permute-done((f32[520,128]{1,0:T(8,128)S(1)}, f32[520,128]{1,0:T(8,128)S(1)}, u32[]{:S(2)}, u32[]{:S(2)}) %collective-permute-start.8) | collective-permute-done | bytes 266272 | tf_op jit(solution)/shard_map/ppermute | solution.py:651
  126.5 3.0 %shard_map.144 = (f32[8,64,128]{2,1,0:T(8,128)S(1)}, f32[512,128]{1,0:T(8,128)S(1)}, f32[16,128]{1,0:T(8,128)S(1)}, bf16[512,256]{1,0:T(8,128)(2,1)S(1)}, f32[64...) custom-call(f32[16,528,128]{2,1,0:T(8,128)} %all-to-all-done.received_ref, ...), custom_call_target="tpu_custom_call" | custom-call | flops 1107296256 | bytes 4325376 | tf_op jit(solution)/shard_map/pallas_call | solution.py:610
  129.5 0.0 copy-start.3
  129.5 0.0 copy-start.2
  129.6 1.8 %collective-permute-done.9.rest_1_ = f32[512,128]{1,0:T(8,128)S(1)} collective-permute-done((f32[512,128]{1,0:T(8,128)S(1)}, f32[512,128]{1,0:T(8,128)S(1)}, u32[]{:S(2)}, u32[]{:S(2)}) %collective-permute-start.9) | collective-permute-done | bytes 262176 | tf_op jit(solution)/shard_map/ppermute | solution.py:651
  131.4 2.0 %shard_map.145 = (f32[8,64,128]{2,1,0:T(8,128)S(1)}, f32[4,4,2,16,128]{4,3,2,1,0:T(8,128)}) custom-call(f32[16,512,128]{2,1,0:T(8,128)S(1)} %get-tuple-element.45.spectrum_ref, f32[16,64,128]{2,1,0:T(8,128)S(1)} %constant_dynamic-update-slice_fusion.basis_ref, bf16[512,256]{1,0:T(8,128)(2,1)S(1)} %get-tuple-element.46.lanes_ref, ...), custom_call_target="tpu_custom_call" | custom-call | flops 1073741824 | bytes 4194304 | tf_op jit(solution)/shard_map/pallas_call | solution.py:610
  133.3 3.5 %all-to-all-start.1 = ((f32[16,2,16,128]{3,2,1,0:T(8,128)}), f32[16,2,16,128]{3,2,1,0:T(8,128)S(1)}, u32[]{:S(2)}, u32[]{:S(2)}) async-start(f32[16,2,16,128]{3,2,1,0:T(8,128)} %bitcast.32), calls=%async_computation.1 | async-start | bytes 524288 | tf_op jit(solution)/shard_map/all_to_all | solution.py:779
  136.9 0.0 copy-done.3
  137.0 0.4 fusion.7
  137.3 0.0 copy-done.2
  137.3 0.4 fusion
  137.7 0.7 copy.32
  138.4 5.5 %all-to-all-done.1 = f32[16,2,16,128]{3,2,1,0:T(8,128)S(1)} async-done(((f32[16,2,16,128]{3,2,1,0:T(8,128)}), f32[16,2,16,128]{3,2,1,0:T(8,128)S(1)}, u32[]{:S(2)}, u32[]{:S(2)}) %all-to-all-start.1) | async-done | bytes 262176 | tf_op jit(solution)/shard_map/all_to_all | solution.py:779
  144.0 0.6 fusion.10
  (29 shorter events, 0.2 us)
Async XLA Ops:
  1.5 17.2 %collective-permute-start = (f32[256,128]{1,0:T(8,128)S(1)}, f32[256,128]{1,0:T(8,128)S(1)}, u32[]{:S(2)}, u32[]{:S(2)}) collective-permute-start(f32[256,128]{1,0:T(8,128)S(1)} %bitcast.127), channel_id=1, source_target_pairs={{8,0},{9,1},{10,2},{11,3},{12,4},{13,5},{14,6},{15,7},{16,8},{17,9... | collective-permute-start | bytes 393224 | tf_op jit(solution)/shard_map/ppermute | solution.py:689
  2.8 19.4 %collective-permute-start.1 = (f32[64,1024]{1,0:T(8,128)}, f32[64,1024]{1,0:T(8,128)S(1)}, u32[]{:S(2)}, u32[]{:S(2)}) collective-permute-start(f32[64,1024]{1,0:T(8,128)} %param.14), channel_id=1, source_target_pairs={{0,4},{4,0},{1,5},{5,1},{2,6},{6,2},{3,7},{7,3},{8,12},{12,8},{9,1... | collective-permute-start | bytes 786440 | tf_op jit(solution)/shard_map/ppermute | solution.py:651
  9.3 9.4 %copy-start = (f32[16,128]{1,0:T(8,128)S(1)}, f32[16,128]{1,0:T(8,128)}, u32[]{:S(2)}) copy-start(f32[16,128]{1,0:T(8,128)} %activity_ref.1) | copy-start | bytes 24580
  22.2 5.0 %copy-start.1 = (f32[64,1024]{1,0:T(8,128)S(1)}, f32[64,1024]{1,0:T(8,128)}, u32[]{:S(2)}) copy-start(f32[64,1024]{1,0:T(8,128)} %param.14) | copy-start | bytes 786436
  22.2 5.1 %copy-start.5 = (f32[128,128,1,1]{1,0,3,2:T(8,128)S(1)}, f32[128,128,1,1]{1,0,3,2:T(8,128)}, u32[]{:S(2)}) copy-start(f32[128,128,1,1]{1,0,3,2:T(8,128)} %constant.89) | copy-start | bytes 196612
  22.2 5.6 %copy-start.4 = (f32[128,128,1,1]{1,0,3,2:T(8,128)S(1)}, f32[128,128,1,1]{1,0,3,2:T(8,128)}, u32[]{:S(2)}) copy-start(f32[128,128,1,1]{1,0,3,2:T(8,128)} %constant.90) | copy-start | bytes 196612
  22.2 60.6 %all-to-all-start = ((f32[16,528,128]{2,1,0:T(8,128)}), f32[16,528,128]{2,1,0:T(8,128)}, u32[]{:S(2)}, u32[]{:S(2)}) async-start(f32[16,528,128]{2,1,0:T(8,128)} %shard_map.141), calls=%async_computation | async-start | bytes 8650752 | tf_op jit(solution)/shard_map/all_to_all | solution.py:695
  87.6 3.2 %collective-permute-start.2 = (f32[136,128]{1,0:T(8,128)S(1)}, f32[136,128]{1,0:T(8,128)S(1)}, u32[]{:S(2)}, u32[]{:S(2)}) collective-permute-start(f32[136,128]{1,0:T(8,128)S(1)} %get-tuple-element.42), channel_id=1, source_target_pairs={{0,8},{8,0},{16,24},{24,16},{1,9},{9,1},{17,25},{25,17},{2,10},{10... | collective-permute-start | bytes 208904 | tf_op jit(solution)/shard_map/ppermute | solution.py:651
  90.8 4.5 %collective-permute-start.3 = (f32[136,128]{1,0:T(8,128)S(1)}, f32[136,128]{1,0:T(8,128)S(1)}, u32[]{:S(2)}, u32[]{:S(2)}) collective-permute-start(f32[136,128]{1,0:T(8,128)S(1)} %add.89), channel_id=1, source_target_pairs={{0,16},{8,24},{16,0},{24,8},{1,17},{9,25},{17,1},{25,9},{2,18},{10... | collective-permute-start | bytes 208904 | tf_op jit(solution)/shard_map/ppermute | solution.py:651
  95.3 5.1 %collective-permute-start.4 = (f32[136,128]{1,0:T(8,128)S(1)}, f32[136,128]{1,0:T(8,128)S(1)}, u32[]{:S(2)}, u32[]{:S(2)}) collective-permute-start(f32[136,128]{1,0:T(8,128)S(1)} %add.90), channel_id=1, source_target_pairs={{0,1},{1,0},{2,3},{3,2},{4,5},{5,4},{6,7},{7,6},{8,9},{9,8},{10,11... | collective-permute-start | bytes 208904 | tf_op jit(solution)/shard_map/ppermute | solution.py:651
  96.0 4.5 %collective-permute-start.5 = (f32[136,128]{1,0:T(8,128)S(1)}, f32[136,128]{1,0:T(8,128)S(1)}, u32[]{:S(2)}, u32[]{:S(2)}) collective-permute-start(f32[136,128]{1,0:T(8,128)S(1)} %add.90), channel_id=1, source_target_pairs={{0,2},{1,3},{2,0},{3,1},{4,6},{5,7},{6,4},{7,5},{8,10},{9,11},{10,... | collective-permute-start | bytes 208904 | tf_op jit(solution)/shard_map/ppermute | solution.py:651
  96.0 6.0 %collective-permute-start.6 = (f32[136,128]{1,0:T(8,128)S(1)}, f32[136,128]{1,0:T(8,128)S(1)}, u32[]{:S(2)}, u32[]{:S(2)}) collective-permute-start(f32[136,128]{1,0:T(8,128)S(1)} %add.90), channel_id=1, source_target_pairs={{0,3},{1,2},{2,1},{3,0},{4,7},{5,6},{6,5},{7,4},{8,11},{9,10},{10,... | collective-permute-start | bytes 208904 | tf_op jit(solution)/shard_map/ppermute | solution.py:651
  102.0 1.3 collective-permute-start.7
  105.0 21.5 %collective-permute-start.8 = (f32[520,128]{1,0:T(8,128)S(1)}, f32[520,128]{1,0:T(8,128)S(1)}, u32[]{:S(2)}, u32[]{:S(2)}) collective-permute-start(f32[520,128]{1,0:T(8,128)S(1)} %get-tuple-element.44.rest_0_), channel_id=1, source_target_pairs={{0,4},{4,0},{1,5},{5,1},{2,6},{6,2},{3,7},{7,3},{8,12},{12,8},{9,1... | collective-permute-start | bytes 798728 | tf_op jit(solution)/shard_map/ppermute | solution.py:651
  106.0 25.3 %collective-permute-start.9 = (f32[512,128]{1,0:T(8,128)S(1)}, f32[512,128]{1,0:T(8,128)S(1)}, u32[]{:S(2)}, u32[]{:S(2)}) collective-permute-start(f32[512,128]{1,0:T(8,128)S(1)} %get-tuple-element.50.rest_0_), channel_id=1, source_target_pairs={{0,4},{4,0},{1,5},{5,1},{2,6},{6,2},{3,7},{7,3},{8,12},{12,8},{9,1... | collective-permute-start | bytes 786440 | tf_op jit(solution)/shard_map/ppermute | solution.py:651
  129.5 7.4 %copy-start.3 = (f32[128,128,1]{1,0,2:T(8,128)S(1)}, f32[128,128,1]{1,0,2:T(8,128)}, u32[]{:S(2)}) copy-start(f32[128,128,1]{1,0,2:T(8,128)} %constant.91) | copy-start | bytes 196612
  129.5 7.8 %copy-start.2 = (f32[128,128,1]{1,0,2:T(8,128)S(1)}, f32[128,128,1]{1,0,2:T(8,128)}, u32[]{:S(2)}) copy-start(f32[128,128,1]{1,0,2:T(8,128)} %constant.92) | copy-start | bytes 196612
  133.3 10.6 %all-to-all-start.1 = ((f32[16,2,16,128]{3,2,1,0:T(8,128)}), f32[16,2,16,128]{3,2,1,0:T(8,128)S(1)}, u32[]{:S(2)}, u32[]{:S(2)}) async-start(f32[16,2,16,128]{3,2,1,0:T(8,128)} %bitcast.32), calls=%async_computation.1 | async-start | bytes 524288 | tf_op jit(solution)/shard_map/all_to_all | solution.py:779

commit v12 on v11

--- a/solution.py
+++ b/solution.py
@@ -515,7 +515,18 @@
     return blocks
 
 
+def sums_for_basis(rows, spectrum_ref, basis_ref, lanes_ref, turned_ref, out_ref):
+    rank = basis_ref.shape[1]
+    ratio, _ = ratio_of(spectrum_ref, rows[0], lanes_ref[...], [basis_ref[row] for row in rows])
+    high, low = split_values(ratio)
+    total = dot(turned_ref[...], high) + dot(turned_ref[...], low)
+    total = total[:rank] + total[rank:]
+    for place in range(len(rows)):
+        out_ref[place * rank : (place + 1) * rank, :] = total[:, place * LANES : (place + 1) * LANES]
+
+
 def second_kernel(
+    rows,
     side_ref,
     spectrum_ref,
     basis_ref,
@@ -524,7 +535,6 @@
     other_ref,
     middle_ref,
     early_ref,
-    late_ref,
     lanes_ref,
     turned_ref,
 ):
@@ -543,15 +553,11 @@
     totals = jnp.sum(middle, axis=0, keepdims=True)
     totals = jnp.broadcast_to(jnp.concatenate([totals] * (LANES // rank), 1), (8, LANES))
     early_ref[early_ref.shape[0] - 8 :, :] = totals
-    early_rows = early_ref.shape[0] // rank
-    for rows in row_steps(basis_ref.shape[0]):
-        ratio, _ = ratio_of(spectrum_ref, rows[0], lanes_ref[...], [basis_ref[row] for row in rows])
-        high, low = split_values(ratio)
-        total = dot(turned_ref[...], high) + dot(turned_ref[...], low)
-        total = total[:rank] + total[rank:]
-        for place, row in enumerate(rows):
-            out_ref, start = (early_ref, row) if row < early_rows else (late_ref, row - early_rows)
-            out_ref[start * rank : (start + 1) * rank, :] = total[:, place * LANES : (place + 1) * LANES]
+    sums_for_basis(rows, spectrum_ref, basis_ref, lanes_ref, turned_ref, early_ref)
+
+
+def second_late_kernel(rows, spectrum_ref, basis_ref, lanes_ref, turned_ref, late_ref):
+    sums_for_basis(rows, spectrum_ref, basis_ref, lanes_ref, turned_ref, late_ref)
 
 
 def renew_and_add(rows, spectrum_ref, basis_ref, lanes_ref, scale, numerators, new_ref, total_ref, sums_ref):
@@ -740,14 +746,27 @@
 
     early_rows = range(max(1, per_member // 2))
     late_rows = range(len(early_rows), per_member)
-    middle, *numerators = update_call(
-        second_kernel,
+    middle, early_sums, lanes, turned = update_call(
+        functools.partial(second_kernel, early_rows),
         spectrum,
-        [(frames, rank), (len(early_rows) * rank + 8, LANES), (len(late_rows) * rank, LANES)],
-        [lanes_scratch, pltpu.VMEM((2 * rank, frames), jnp.bfloat16)],
+        [
+            (frames, rank),
+            (len(early_rows) * rank + 8, LANES),
+            jax.ShapeDtypeStruct((frames, 4 * rank), jnp.bfloat16),
+            jax.ShapeDtypeStruct((2 * rank, frames), jnp.bfloat16),
+        ],
+        [],
         (basis, activity, mine, other),
         (side,),
     )
+    (late_sums,) = update_call(
+        functools.partial(second_late_kernel, late_rows),
+        spectrum,
+        [(len(late_rows) * rank, LANES)],
+        [],
+        (basis, lanes, turned),
+    )
+    numerators = [early_sums, late_sums]
     numerators = [[numerator] for numerator in numerators]
     if groups == 2:
         for numerator in numerators:

time: 145 us -> 148 us (1.021)
  local copies, waits for them, and re-layouts: 1.98 us -> 8.37 us
  waiting for transfers between devices: 88.5 us -> 85.4 us
    unnamed x31 -> x37, local copies, waits for them, and re-layouts: 0.16 us -> 6.54 us
    ppermute x9, waiting for transfers between devices: 28.8 us -> 25.6 us  [swap_by(): return lax.ppermute(value, axis, [(i, i ^ mask) for i in range(count)])]
    pallas_call x4 -> x5, Pallas kernels: 11.5 us -> 11.7 us  [update_call(): pl.pallas_call(kernel, in_specs=[pl.BlockSpec(memory_space=pltpu.SMEM) fo...]
where the time goes in v12:
time: 148 us
  waiting for transfers between devices  85.4 us (58%)
  starting transfers between devices  26.1 us (18%)
  Pallas kernels  24.5 us (17%)
  local copies, waits for them, and re-layouts  8.37 us (6%)
  matrix products  1.86 us (1%)
    all_to_all x1, waiting for transfers between devices, on_device(): spectrum = lax.all_to_all(spectrum, exchange, 0, 0, tiled=True)  54.2 us
    ppermute x9, waiting for transfers between devices, swap_by(): return lax.ppermute(value, axis, [(i, i ^ mask) for i in range(count)])  25.6 us
    ppermute x9, starting transfers between devices, swap_by(): return lax.ppermute(value, axis, [(i, i ^ mask) for i in range(count)])  16.4 us
    pallas_call x5, Pallas kernels, update_call(): pl.pallas_call(kernel, in_specs=[pl.BlockSpec(memory_space=pltpu.SMEM) fo...  11.7 us
    pallas_call x1, Pallas kernels, spectrum_blocks(): pl.pallas_call(functools.partial(early_kernel, places, per_member, frames...  9.39 us
    unnamed x37, local copies, waits for them, and re-layouts  6.54 us
    all_to_all x1, waiting for transfers between devices, on_device(): lax.all_to_all(payload.reshape(partners, 2, ranks_here, width), exchange,...  5.54 us
    all_to_all x1, starting transfers between devices, on_device(): spectrum = lax.all_to_all(spectrum, exchange, 0, 0, tiled=True)  4.87 us
  transfers between devices with their start and end apart: 12, of which 9 were waited for; matrix products, arithmetic and copies ran while one was open for 2% of the time, Pallas kernels for 11%

profile of v12, /device:TPU:0, one launch (start us, length us, event | category | flops | bytes accessed | tf_op | source)
XLA Modules:
  0.0 148.1 jit_solution(11706804869084848977)
XLA Ops:
  0.6 0.9 slice.66
  1.5 1.3 collective-permute-start
  2.8 6.5 %collective-permute-start.1 = (f32[64,1024]{1,0:T(8,128)}, f32[64,1024]{1,0:T(8,128)S(1)}, u32[]{:S(2)}, u32[]{:S(2)}) collective-permute-start(f32[64,1024]{1,0:T(8,128)} %param.14), channel_id=1, source_target_pairs={{0,4},{4,0},{1,5},{5,1},{2,6},{6,2},{3,7},{7,3},{8,12},{12,8},{9,1... | collective-permute-start | bytes 786440 | tf_op jit(solution)/shard_map/ppermute | solution.py:657
  9.3 0.0 copy-start.3
  9.3 9.4 %shard_map.140 = (f32[16,528,128]{2,1,0:T(8,128)}, f32[2048,128]{1,0:T(8,128)S(1)}, f32[3,16,136,128]{3,2,1,0:T(8,128)S(1)}, f32[2,256,128]{2,1,0:T(8,128)S(1)},...) custom-call(f32[8192,128]{1,0:T(8,128)} %bitcast.128, ...), custom_call_target="tpu_custom_call" | custom-call | flops 4831838208 | bytes 6291456 | tf_op jit(solution)/shard_map/pallas_call | solution.py:340
  18.7 0.0 collective-permute-done.trailing_ref
  18.7 0.0 copy-done.3
  18.8 3.4 %shard_map.141 = f32[16,528,128]{2,1,0:T(8,128)} custom-call(f32[3,16,136,128]{3,2,1,0:T(8,128)S(1)} %get-tuple-element.29.done_ref, f32[2048,128]{1,0:T(8,128)S(1)} %get-tuple-element.30.tail_ref, f32[256,128]{1,0:T(8,128)S(1)} %collective-permute-done.trailing_ref, f32[16,128]{1,0:T(8,128)S(1)} %copy-done.3, ...), custom_call_target="tpu_custom_call", output_to_operand_aliasing={{}: (10, {})} | custom-call | flops 1610612736 | bytes 2097152 | tf_op jit(solution)/shard_map/pallas_call | solution.py:354
  22.1 0.0 copy-start.4
  22.2 0.0 copy-start.8
  22.2 0.0 copy-start.7
  22.2 0.0 collective-permute-done.1
  22.2 4.9 %all-to-all-start = ((f32[16,528,128]{2,1,0:T(8,128)}), f32[16,528,128]{2,1,0:T(8,128)}, u32[]{:S(2)}, u32[]{:S(2)}) async-start(f32[16,528,128]{2,1,0:T(8,128)} %shard_map.141), calls=%async_computation | async-start | bytes 8650752 | tf_op jit(solution)/shard_map/all_to_all | solution.py:701
  27.1 0.1 fusion.12
  27.2 0.0 copy-done.4
  27.2 0.0 copy-done.8
  27.2 0.6 fusion.1
  27.8 0.0 copy-done.7
  27.8 0.6 convolution_select_fusion
  28.6 54.2 %all-to-all-done.received_ref = f32[16,528,128]{2,1,0:T(8,128)} async-done(((f32[16,528,128]{2,1,0:T(8,128)}), f32[16,528,128]{2,1,0:T(8,128)}, u32[]{:S(2)}, u32[]{:S(2)}) %all-to-all-start) | async-done | bytes 4325408 | tf_op jit(solution)/shard_map/all_to_all | solution.py:701
  82.8 4.8 %shard_map.142 = (f32[136,128]{1,0:T(8,128)S(1)}, f32[136,128]{1,0:T(8,128)S(1)}, f32[512,64]{1,0:T(8,128)S(1)}, f32[16,512,128]{2,1,0:T(8,128)S(1)}) custom-call(s32[1]{0:T(128)} %bitcast.side_ref, f32[16,528,128]{2,1,0:T(8,128)} %all-to-all-done.received_ref, f32[16,64,128]{2,1,0:T(8,128)S(1)} %constant_dynamic-update-slice_fusion.basis_ref), custom_call_target="tpu_custom_call" | custom-call | flops 1107296256 | bytes 4325376 | tf_op jit(solution)/shard_map/pallas_call | solution.py:616
  87.7 0.0 copy-start
  87.7 2.0 %copy-done = f32[16,512,128]{2,1,0:T(8,128)} copy-done((f32[16,512,128]{2,1,0:T(8,128)}, f32[16,512,128]{2,1,0:T(8,128)S(1)}, u32[]{:S(2)}) %copy-start) | copy-done | bytes 4194328
  89.7 2.2 %collective-permute-start.2 = (f32[136,128]{1,0:T(8,128)S(1)}, f32[136,128]{1,0:T(8,128)S(1)}, u32[]{:S(2)}, u32[]{:S(2)}) collective-permute-start(f32[136,128]{1,0:T(8,128)S(1)} %get-tuple-element.43), channel_id=1, source_target_pairs={{0,8},{8,0},{16,24},{24,16},{1,9},{9,1},{17,25},{25,17},{2,10},{10... | collective-permute-start | bytes 208904 | tf_op jit(solution)/shard_map/ppermute | solution.py:657
  91.9 0.9 collective-permute-done.2
  92.8 1.1 collective-permute-start.3
  93.9 3.4 %collective-permute-done.3 = f32[136,128]{1,0:T(8,128)S(1)} collective-permute-done((f32[136,128]{1,0:T(8,128)S(1)}, f32[136,128]{1,0:T(8,128)S(1)}, u32[]{:S(2)}, u32[]{:S(2)}) %collective-permute-start.3) | collective-permute-done | bytes 69664 | tf_op jit(solution)/shard_map/ppermute | solution.py:657
  97.3 0.6 collective-permute-start.4
  97.9 0.0 collective-permute-start.5
  97.9 2.9 %collective-permute-start.6 = (f32[136,128]{1,0:T(8,128)S(1)}, f32[136,128]{1,0:T(8,128)S(1)}, u32[]{:S(2)}, u32[]{:S(2)}) collective-permute-start(f32[136,128]{1,0:T(8,128)S(1)} %add.90), channel_id=1, source_target_pairs={{0,3},{1,2},{2,1},{3,0},{4,7},{5,6},{6,5},{7,4},{8,11},{9,10},{10,... | collective-permute-start | bytes 208904 | tf_op jit(solution)/shard_map/ppermute | solution.py:657
  100.9 1.6 %collective-permute-done.4 = f32[136,128]{1,0:T(8,128)S(1)} collective-permute-done((f32[136,128]{1,0:T(8,128)S(1)}, f32[136,128]{1,0:T(8,128)S(1)}, u32[]{:S(2)}, u32[]{:S(2)}) %collective-permute-start.4) | collective-permute-done | bytes 69664 | tf_op jit(solution)/shard_map/ppermute | solution.py:657
  102.4 0.0 collective-permute-done.5
  102.4 1.5 collective-permute-done.6
  103.9 0.1 collective-permute-start.7
  104.0 1.2 collective-permute-done.7.other_ref
  105.3 0.0 copy-start.1
  105.3 2.2 %copy-done.1 = f32[16,512,128]{2,1,0:T(8,128)S(1)} copy-done((f32[16,512,128]{2,1,0:T(8,128)S(1)}, f32[16,512,128]{2,1,0:T(8,128)}, u32[]{:S(2)}) %copy-start.1) | copy-done | bytes 4194328
  107.4 1.0 shard_map.143
  108.5 1.0 collective-permute-start.8
  109.5 0.0 copy-start.2
  109.5 2.2 %copy-done.2 = f32[16,512,128]{2,1,0:T(8,128)S(1)} copy-done((f32[16,512,128]{2,1,0:T(8,128)S(1)}, f32[16,512,128]{2,1,0:T(8,128)}, u32[]{:S(2)}) %copy-start.2) | copy-done | bytes 4194328
  111.7 0.9 shard_map.145.rest_0_
  112.6 2.0 %collective-permute-start.9 = (f32[512,128]{1,0:T(8,128)S(1)}, f32[512,128]{1,0:T(8,128)S(1)}, u32[]{:S(2)}, u32[]{:S(2)}) collective-permute-start(f32[512,128]{1,0:T(8,128)S(1)} %shard_map.145.rest_0_), channel_id=1, source_target_pairs={{0,4},{4,0},{1,5},{5,1},{2,6},{6,2},{3,7},{7,3},{8,12},{12,8},{9,1... | collective-permute-start | bytes 786440 | tf_op jit(solution)/shard_map/ppermute | solution.py:657
  114.6 0.1 constant_dynamic-slice_fusion
  114.7 0.1 copy.25
  114.7 15.2 %collective-permute-done.8.rest_1_ = f32[520,128]{1,0:T(8,128)S(1)} collective-permute-done((f32[520,128]{1,0:T(8,128)S(1)}, f32[520,128]{1,0:T(8,128)S(1)}, u32[]{:S(2)}, u32[]{:S(2)}) %collective-permute-start.8) | collective-permute-done | bytes 266272 | tf_op jit(solution)/shard_map/ppermute | solution.py:657
  130.0 3.0 %shard_map.144 = (f32[8,64,128]{2,1,0:T(8,128)S(1)}, f32[512,128]{1,0:T(8,128)S(1)}, f32[16,128]{1,0:T(8,128)S(1)}, bf16[512,256]{1,0:T(8,128)(2,1)S(1)}, f32[64...) custom-call(f32[16,528,128]{2,1,0:T(8,128)} %all-to-all-done.received_ref, ...), custom_call_target="tpu_custom_call" | custom-call | flops 1107296256 | bytes 4325376 | tf_op jit(solution)/shard_map/pallas_call | solution.py:616
  133.0 0.0 copy-start.6
  133.0 0.0 copy-start.5
  133.0 1.8 %collective-permute-done.9.rest_1_ = f32[512,128]{1,0:T(8,128)S(1)} collective-permute-done((f32[512,128]{1,0:T(8,128)S(1)}, f32[512,128]{1,0:T(8,128)S(1)}, u32[]{:S(2)}, u32[]{:S(2)}) %collective-permute-start.9) | collective-permute-done | bytes 262176 | tf_op jit(solution)/shard_map/ppermute | solution.py:657
  134.8 2.0 %shard_map.146 = (f32[8,64,128]{2,1,0:T(8,128)S(1)}, f32[4,4,2,16,128]{4,3,2,1,0:T(8,128)}) custom-call(f32[16,512,128]{2,1,0:T(8,128)S(1)} %get-tuple-element.46.spectrum_ref, f32[16,64,128]{2,1,0:T(8,128)S(1)} %constant_dynamic-update-slice_fusion.basis_ref, bf16[512,256]{1,0:T(8,128)(2,1)S(1)} %get-tuple-element.47.lanes_ref, ...), custom_call_target="tpu_custom_call" | custom-call | flops 1073741824 | bytes 4194304 | tf_op jit(solution)/shard_map/pallas_call | solution.py:616
  136.8 3.5 %all-to-all-start.1 = ((f32[16,2,16,128]{3,2,1,0:T(8,128)}), f32[16,2,16,128]{3,2,1,0:T(8,128)S(1)}, u32[]{:S(2)}, u32[]{:S(2)}) async-start(f32[16,2,16,128]{3,2,1,0:T(8,128)} %bitcast.32), calls=%async_computation.1 | async-start | bytes 524288 | tf_op jit(solution)/shard_map/all_to_all | solution.py:798
  140.4 0.0 copy-done.6
  140.4 0.4 fusion.7
  140.8 0.0 copy-done.5
  140.8 0.4 fusion
  141.2 0.7 copy.32
  141.9 5.5 %all-to-all-done.1 = f32[16,2,16,128]{3,2,1,0:T(8,128)S(1)} async-done(((f32[16,2,16,128]{3,2,1,0:T(8,128)}), f32[16,2,16,128]{3,2,1,0:T(8,128)S(1)}, u32[]{:S(2)}, u32[]{:S(2)}) %all-to-all-start.1) | async-done | bytes 262176 | tf_op jit(solution)/shard_map/all_to_all | solution.py:798
  147.5 0.6 fusion.10
  (29 shorter events, 0.3 us)
Async XLA Ops:
  1.5 17.2 %collective-permute-start = (f32[256,128]{1,0:T(8,128)S(1)}, f32[256,128]{1,0:T(8,128)S(1)}, u32[]{:S(2)}, u32[]{:S(2)}) collective-permute-start(f32[256,128]{1,0:T(8,128)S(1)} %bitcast.127), channel_id=1, source_target_pairs={{8,0},{9,1},{10,2},{11,3},{12,4},{13,5},{14,6},{15,7},{16,8},{17,9... | collective-permute-start | bytes 393224 | tf_op jit(solution)/shard_map/ppermute | solution.py:695
  2.8 19.3 %collective-permute-start.1 = (f32[64,1024]{1,0:T(8,128)}, f32[64,1024]{1,0:T(8,128)S(1)}, u32[]{:S(2)}, u32[]{:S(2)}) collective-permute-start(f32[64,1024]{1,0:T(8,128)} %param.14), channel_id=1, source_target_pairs={{0,4},{4,0},{1,5},{5,1},{2,6},{6,2},{3,7},{7,3},{8,12},{12,8},{9,1... | collective-permute-start | bytes 786440 | tf_op jit(solution)/shard_map/ppermute | solution.py:657
  9.3 9.4 %copy-start.3 = (f32[16,128]{1,0:T(8,128)S(1)}, f32[16,128]{1,0:T(8,128)}, u32[]{:S(2)}) copy-start(f32[16,128]{1,0:T(8,128)} %activity_ref.1) | copy-start | bytes 24580
  22.1 5.0 %copy-start.4 = (f32[64,1024]{1,0:T(8,128)S(1)}, f32[64,1024]{1,0:T(8,128)}, u32[]{:S(2)}) copy-start(f32[64,1024]{1,0:T(8,128)} %param.14) | copy-start | bytes 786436
  22.2 5.1 %copy-start.8 = (f32[128,128,1,1]{1,0,3,2:T(8,128)S(1)}, f32[128,128,1,1]{1,0,3,2:T(8,128)}, u32[]{:S(2)}) copy-start(f32[128,128,1,1]{1,0,3,2:T(8,128)} %constant.89) | copy-start | bytes 196612
  22.2 5.7 %copy-start.7 = (f32[128,128,1,1]{1,0,3,2:T(8,128)S(1)}, f32[128,128,1,1]{1,0,3,2:T(8,128)}, u32[]{:S(2)}) copy-start(f32[128,128,1,1]{1,0,3,2:T(8,128)} %constant.90) | copy-start | bytes 196612
  22.2 60.6 %all-to-all-start = ((f32[16,528,128]{2,1,0:T(8,128)}), f32[16,528,128]{2,1,0:T(8,128)}, u32[]{:S(2)}, u32[]{:S(2)}) async-start(f32[16,528,128]{2,1,0:T(8,128)} %shard_map.141), calls=%async_computation | async-start | bytes 8650752 | tf_op jit(solution)/shard_map/all_to_all | solution.py:701
  87.7 2.0 %copy-start = (f32[16,512,128]{2,1,0:T(8,128)}, f32[16,512,128]{2,1,0:T(8,128)S(1)}, u32[]{:S(2)}) copy-start(f32[16,512,128]{2,1,0:T(8,128)S(1)} %get-tuple-element.40.spectrum_ref) | copy-start | bytes 12582916
  89.7 3.1 %collective-permute-start.2 = (f32[136,128]{1,0:T(8,128)S(1)}, f32[136,128]{1,0:T(8,128)S(1)}, u32[]{:S(2)}, u32[]{:S(2)}) collective-permute-start(f32[136,128]{1,0:T(8,128)S(1)} %get-tuple-element.43), channel_id=1, source_target_pairs={{0,8},{8,0},{16,24},{24,16},{1,9},{9,1},{17,25},{25,17},{2,10},{10... | collective-permute-start | bytes 208904 | tf_op jit(solution)/shard_map/ppermute | solution.py:657
  92.8 4.5 %collective-permute-start.3 = (f32[136,128]{1,0:T(8,128)S(1)}, f32[136,128]{1,0:T(8,128)S(1)}, u32[]{:S(2)}, u32[]{:S(2)}) collective-permute-start(f32[136,128]{1,0:T(8,128)S(1)} %add.89), channel_id=1, source_target_pairs={{0,16},{8,24},{16,0},{24,8},{1,17},{9,25},{17,1},{25,9},{2,18},{10... | collective-permute-start | bytes 208904 | tf_op jit(solution)/shard_map/ppermute | solution.py:657
  97.3 5.1 %collective-permute-start.4 = (f32[136,128]{1,0:T(8,128)S(1)}, f32[136,128]{1,0:T(8,128)S(1)}, u32[]{:S(2)}, u32[]{:S(2)}) collective-permute-start(f32[136,128]{1,0:T(8,128)S(1)} %add.90), channel_id=1, source_target_pairs={{0,1},{1,0},{2,3},{3,2},{4,5},{5,4},{6,7},{7,6},{8,9},{9,8},{10,11... | collective-permute-start | bytes 208904 | tf_op jit(solution)/shard_map/ppermute | solution.py:657
  97.9 4.5 %collective-permute-start.5 = (f32[136,128]{1,0:T(8,128)S(1)}, f32[136,128]{1,0:T(8,128)S(1)}, u32[]{:S(2)}, u32[]{:S(2)}) collective-permute-start(f32[136,128]{1,0:T(8,128)S(1)} %add.90), channel_id=1, source_target_pairs={{0,2},{1,3},{2,0},{3,1},{4,6},{5,7},{6,4},{7,5},{8,10},{9,11},{10,... | collective-permute-start | bytes 208904 | tf_op jit(solution)/shard_map/ppermute | solution.py:657
  97.9 6.0 %collective-permute-start.6 = (f32[136,128]{1,0:T(8,128)S(1)}, f32[136,128]{1,0:T(8,128)S(1)}, u32[]{:S(2)}, u32[]{:S(2)}) collective-permute-start(f32[136,128]{1,0:T(8,128)S(1)} %add.90), channel_id=1, source_target_pairs={{0,3},{1,2},{2,1},{3,0},{4,7},{5,6},{6,5},{7,4},{8,11},{9,10},{10,... | collective-permute-start | bytes 208904 | tf_op jit(solution)/shard_map/ppermute | solution.py:657
  103.9 1.3 collective-permute-start.7
  105.3 2.2 %copy-start.1 = (f32[16,512,128]{2,1,0:T(8,128)S(1)}, f32[16,512,128]{2,1,0:T(8,128)}, u32[]{:S(2)}) copy-start(f32[16,512,128]{2,1,0:T(8,128)} %copy-done) | copy-start | bytes 12582916
  108.5 21.5 %collective-permute-start.8 = (f32[520,128]{1,0:T(8,128)S(1)}, f32[520,128]{1,0:T(8,128)S(1)}, u32[]{:S(2)}, u32[]{:S(2)}) collective-permute-start(f32[520,128]{1,0:T(8,128)S(1)} %get-tuple-element.45.rest_0_), channel_id=1, source_target_pairs={{0,4},{4,0},{1,5},{5,1},{2,6},{6,2},{3,7},{7,3},{8,12},{12,8},{9,1... | collective-permute-start | bytes 798728 | tf_op jit(solution)/shard_map/ppermute | solution.py:657
  109.5 2.2 %copy-start.2 = (f32[16,512,128]{2,1,0:T(8,128)S(1)}, f32[16,512,128]{2,1,0:T(8,128)}, u32[]{:S(2)}) copy-start(f32[16,512,128]{2,1,0:T(8,128)} %copy-done) | copy-start | bytes 12582916
  112.6 22.2 %collective-permute-start.9 = (f32[512,128]{1,0:T(8,128)S(1)}, f32[512,128]{1,0:T(8,128)S(1)}, u32[]{:S(2)}, u32[]{:S(2)}) collective-permute-start(f32[512,128]{1,0:T(8,128)S(1)} %shard_map.145.rest_0_), channel_id=1, source_target_pairs={{0,4},{4,0},{1,5},{5,1},{2,6},{6,2},{3,7},{7,3},{8,12},{12,8},{9,1... | collective-permute-start | bytes 786440 | tf_op jit(solution)/shard_map/ppermute | solution.py:657
  133.0 7.4 %copy-start.6 = (f32[128,128,1]{1,0,2:T(8,128)S(1)}, f32[128,128,1]{1,0,2:T(8,128)}, u32[]{:S(2)}) copy-start(f32[128,128,1]{1,0,2:T(8,128)} %constant.91) | copy-start | bytes 196612
  133.0 7.8 %copy-start.5 = (f32[128,128,1]{1,0,2:T(8,128)S(1)}, f32[128,128,1]{1,0,2:T(8,128)}, u32[]{:S(2)}) copy-start(f32[128,128,1]{1,0,2:T(8,128)} %constant.92) | copy-start | bytes 196612
  136.8 10.6 %all-to-all-start.1 = ((f32[16,2,16,128]{3,2,1,0:T(8,128)}), f32[16,2,16,128]{3,2,1,0:T(8,128)S(1)}, u32[]{:S(2)}, u32[]{:S(2)}) async-start(f32[16,2,16,128]{3,2,1,0:T(8,128)} %bitcast.32), calls=%async_computation.1 | async-start | bytes 524288 | tf_op jit(solution)/shard_map/all_to_all | solution.py:798

commit v13 on v12

--- a/solution.py
+++ b/solution.py
@@ -556,7 +556,9 @@
     sums_for_basis(rows, spectrum_ref, basis_ref, lanes_ref, turned_ref, early_ref)
 
 
-def second_late_kernel(rows, spectrum_ref, basis_ref, lanes_ref, turned_ref, late_ref):
+def second_late_kernel(rows, received_ref, basis_ref, lanes_ref, turned_ref, late_ref, spectrum_ref, sem_ref):
+    for copy in start_fetches(received_ref, spectrum_ref, sem_ref, basis_ref.shape[0], [rows])[0]:
+        copy.wait()
     sums_for_basis(rows, spectrum_ref, basis_ref, lanes_ref, turned_ref, late_ref)
 
 
@@ -761,10 +763,15 @@
     )
     (late_sums,) = update_call(
         functools.partial(second_late_kernel, late_rows),
-        spectrum,
+        received,
         [(len(late_rows) * rank, LANES)],
-        [],
+        [
+            pltpu.VMEM((partners, spectrum_rows, LANES), jnp.float32),
+            pltpu.SemaphoreType.DMA((row_groups,)),
+        ],
         (basis, lanes, turned),
+        (),
+        pltpu.HBM,
     )
     numerators = [early_sums, late_sums]
     numerators = [[numerator] for numerator in numerators]

time: 148 us -> 148 us (level)
  local copies, waits for them, and re-layouts: 8.37 us -> 6.19 us
  Pallas kernels: 24.5 us -> 26 us
    unnamed x37 -> x35, local copies, waits for them, and re-layouts: 6.54 us -> 4.36 us
    pallas_call x5, Pallas kernels: 11.7 us -> 13.3 us  [update_call(): pl.pallas_call(kernel, in_specs=[pl.BlockSpec(memory_space=pltpu.SMEM) fo...]
  transfers between devices with their start and end apart: 12 -> 12, of which waited for: 9 -> 9; matrix products, arithmetic and copies ran while one was open for 2% -> 2% of each run, Pallas kernels for 11% -> 12%
where the time goes in v13:
time: 148 us
  waiting for transfers between devices  86 us (58%)
  starting transfers between devices  26.1 us (18%)
  Pallas kernels  26 us (18%)
  local copies, waits for them, and re-layouts  6.19 us (4%)
  matrix products  1.85 us (1%)
    all_to_all x1, waiting for transfers between devices, on_device(): spectrum = lax.all_to_all(spectrum, exchange, 0, 0, tiled=True)  54.2 us
    ppermute x9, waiting for transfers between devices, swap_by(): return lax.ppermute(value, axis, [(i, i ^ mask) for i in range(count)])  26.3 us
    ppermute x9, starting transfers between devices, swap_by(): return lax.ppermute(value, axis, [(i, i ^ mask) for i in range(count)])  16.4 us
    pallas_call x5, Pallas kernels, update_call(): pl.pallas_call(kernel, in_specs=[pl.BlockSpec(memory_space=pltpu.SMEM) fo...  13.3 us
    pallas_call x1, Pallas kernels, spectrum_blocks(): pl.pallas_call(functools.partial(early_kernel, places, per_member, frames...  9.39 us
    all_to_all x1, waiting for transfers between devices, on_device(): lax.all_to_all(payload.reshape(partners, 2, ranks_here, width), exchange,...  5.55 us
    all_to_all x1, starting transfers between devices, on_device(): spectrum = lax.all_to_all(spectrum, exchange, 0, 0, tiled=True)  4.86 us
    unnamed x35, local copies, waits for them, and re-layouts  4.36 us
  transfers between devices with their start and end apart: 12, of which 9 were waited for; matrix products, arithmetic and copies ran while one was open for 2% of the time, Pallas kernels for 12%

profile of v13, /device:TPU:0, one launch (start us, length us, event | category | flops | bytes accessed | tf_op | source)
XLA Modules:
  0.0 148.0 jit_solution(14442199218362571568)
XLA Ops:
  0.6 0.9 slice.66
  1.5 1.3 collective-permute-start
  2.8 6.5 %collective-permute-start.1 = (f32[64,1024]{1,0:T(8,128)}, f32[64,1024]{1,0:T(8,128)S(1)}, u32[]{:S(2)}, u32[]{:S(2)}) collective-permute-start(f32[64,1024]{1,0:T(8,128)} %param.14), channel_id=1, source_target_pairs={{0,4},{4,0},{1,5},{5,1},{2,6},{6,2},{3,7},{7,3},{8,12},{12,8},{9,1... | collective-permute-start | bytes 786440 | tf_op jit(solution)/shard_map/ppermute | solution.py:659
  9.3 0.0 copy-start.2
  9.3 9.4 %shard_map.140 = (f32[16,528,128]{2,1,0:T(8,128)}, f32[2048,128]{1,0:T(8,128)S(1)}, f32[3,16,136,128]{3,2,1,0:T(8,128)S(1)}, f32[2,256,128]{2,1,0:T(8,128)S(1)},...) custom-call(f32[8192,128]{1,0:T(8,128)} %bitcast.128, ...), custom_call_target="tpu_custom_call" | custom-call | flops 4831838208 | bytes 6291456 | tf_op jit(solution)/shard_map/pallas_call | solution.py:340
  18.7 0.0 collective-permute-done.trailing_ref
  18.7 0.0 copy-done.2
  18.8 3.4 %shard_map.141 = f32[16,528,128]{2,1,0:T(8,128)} custom-call(f32[3,16,136,128]{3,2,1,0:T(8,128)S(1)} %get-tuple-element.29.done_ref, f32[2048,128]{1,0:T(8,128)S(1)} %get-tuple-element.30.tail_ref, f32[256,128]{1,0:T(8,128)S(1)} %collective-permute-done.trailing_ref, f32[16,128]{1,0:T(8,128)S(1)} %copy-done.2, ...), custom_call_target="tpu_custom_call", output_to_operand_aliasing={{}: (10, {})} | custom-call | flops 1610612736 | bytes 2097152 | tf_op jit(solution)/shard_map/pallas_call | solution.py:354
  22.1 0.0 copy-start.3
  22.2 0.0 copy-start.7
  22.2 0.0 copy-start.6
  22.2 0.0 collective-permute-done.1
  22.2 4.9 %all-to-all-start = ((f32[16,528,128]{2,1,0:T(8,128)}), f32[16,528,128]{2,1,0:T(8,128)}, u32[]{:S(2)}, u32[]{:S(2)}) async-start(f32[16,528,128]{2,1,0:T(8,128)} %shard_map.141), calls=%async_computation | async-start | bytes 8650752 | tf_op jit(solution)/shard_map/all_to_all | solution.py:703
  27.1 0.1 fusion.12
  27.2 0.0 copy-done.3
  27.2 0.0 copy-done.7
  27.2 0.6 fusion.1
  27.8 0.0 copy-done.6
  27.8 0.6 convolution_select_fusion
  28.6 54.2 %all-to-all-done.received_ref = f32[16,528,128]{2,1,0:T(8,128)} async-done(((f32[16,528,128]{2,1,0:T(8,128)}), f32[16,528,128]{2,1,0:T(8,128)}, u32[]{:S(2)}, u32[]{:S(2)}) %all-to-all-start) | async-done | bytes 4325408 | tf_op jit(solution)/shard_map/all_to_all | solution.py:703
  82.8 4.8 %shard_map.142 = (f32[136,128]{1,0:T(8,128)S(1)}, f32[136,128]{1,0:T(8,128)S(1)}, f32[512,64]{1,0:T(8,128)S(1)}, f32[16,512,128]{2,1,0:T(8,128)S(1)}) custom-call(s32[1]{0:T(128)} %bitcast.side_ref, f32[16,528,128]{2,1,0:T(8,128)} %all-to-all-done.received_ref, f32[16,64,128]{2,1,0:T(8,128)S(1)} %constant_dynamic-update-slice_fusion.basis_ref), custom_call_target="tpu_custom_call" | custom-call | flops 1107296256 | bytes 4325376 | tf_op jit(solution)/shard_map/pallas_call | solution.py:618
  87.7 0.0 copy-start
  87.7 2.0 %copy-done = f32[16,512,128]{2,1,0:T(8,128)} copy-done((f32[16,512,128]{2,1,0:T(8,128)}, f32[16,512,128]{2,1,0:T(8,128)S(1)}, u32[]{:S(2)}) %copy-start) | copy-done | bytes 4194328
  89.7 2.2 %collective-permute-start.2 = (f32[136,128]{1,0:T(8,128)S(1)}, f32[136,128]{1,0:T(8,128)S(1)}, u32[]{:S(2)}, u32[]{:S(2)}) collective-permute-start(f32[136,128]{1,0:T(8,128)S(1)} %get-tuple-element.43), channel_id=1, source_target_pairs={{0,8},{8,0},{16,24},{24,16},{1,9},{9,1},{17,25},{25,17},{2,10},{10... | collective-permute-start | bytes 208904 | tf_op jit(solution)/shard_map/ppermute | solution.py:659
  91.9 0.9 collective-permute-done.2
  92.8 1.1 collective-permute-start.3
  93.9 3.4 %collective-permute-done.3 = f32[136,128]{1,0:T(8,128)S(1)} collective-permute-done((f32[136,128]{1,0:T(8,128)S(1)}, f32[136,128]{1,0:T(8,128)S(1)}, u32[]{:S(2)}, u32[]{:S(2)}) %collective-permute-start.3) | collective-permute-done | bytes 69664 | tf_op jit(solution)/shard_map/ppermute | solution.py:659
  97.3 0.6 collective-permute-start.4
  97.9 0.0 collective-permute-start.5
  97.9 2.9 %collective-permute-start.6 = (f32[136,128]{1,0:T(8,128)S(1)}, f32[136,128]{1,0:T(8,128)S(1)}, u32[]{:S(2)}, u32[]{:S(2)}) collective-permute-start(f32[136,128]{1,0:T(8,128)S(1)} %add.90), channel_id=1, source_target_pairs={{0,3},{1,2},{2,1},{3,0},{4,7},{5,6},{6,5},{7,4},{8,11},{9,10},{10,... | collective-permute-start | bytes 208904 | tf_op jit(solution)/shard_map/ppermute | solution.py:659
  100.9 1.6 %collective-permute-done.4 = f32[136,128]{1,0:T(8,128)S(1)} collective-permute-done((f32[136,128]{1,0:T(8,128)S(1)}, f32[136,128]{1,0:T(8,128)S(1)}, u32[]{:S(2)}, u32[]{:S(2)}) %collective-permute-start.4) | collective-permute-done | bytes 69664 | tf_op jit(solution)/shard_map/ppermute | solution.py:659
  102.4 0.0 collective-permute-done.5
  102.4 1.5 collective-permute-done.6
  103.9 0.1 collective-permute-start.7
  104.0 1.2 collective-permute-done.7.other_ref
  105.3 0.0 copy-start.1
  105.3 2.2 %copy-done.1 = f32[16,512,128]{2,1,0:T(8,128)S(1)} copy-done((f32[16,512,128]{2,1,0:T(8,128)S(1)}, f32[16,512,128]{2,1,0:T(8,128)}, u32[]{:S(2)}) %copy-start.1) | copy-done | bytes 4194328
  107.4 1.0 shard_map.143
  108.5 1.1 collective-permute-start.8
  109.5 2.4 %shard_map.145.rest_0_ = f32[512,128]{1,0:T(8,128)S(1)} custom-call(f32[16,528,128]{2,1,0:T(8,128)} %all-to-all-done.received_ref, f32[16,64,128]{2,1,0:T(8,128)S(1)} %constant_dynamic-update-slice_fusion.basis_ref, bf16[512,256]{1,0:T(8,128)(2,1)S(1)} %get-tuple-element.51.lanes_ref, bf16[128,512]{1,0:T(8,128)(2,1)S(1)} %get-tuple-element.52.turned_ref), custom_call_target="tpu_custom_call" | custom-call | flops 1107296256 | bytes 4325376 | tf_op jit(solution)/shard_map/pallas_call | solution.py:618
  112.0 2.0 %collective-permute-start.9 = (f32[512,128]{1,0:T(8,128)S(1)}, f32[512,128]{1,0:T(8,128)S(1)}, u32[]{:S(2)}, u32[]{:S(2)}) collective-permute-start(f32[512,128]{1,0:T(8,128)S(1)} %shard_map.145.rest_0_), channel_id=1, source_target_pairs={{0,4},{4,0},{1,5},{5,1},{2,6},{6,2},{3,7},{7,3},{8,12},{12,8},{9,1... | collective-permute-start | bytes 786440 | tf_op jit(solution)/shard_map/ppermute | solution.py:659
  114.0 0.1 constant_dynamic-slice_fusion
  114.1 0.1 copy.25
  114.1 15.9 %collective-permute-done.8.rest_1_ = f32[520,128]{1,0:T(8,128)S(1)} collective-permute-done((f32[520,128]{1,0:T(8,128)S(1)}, f32[520,128]{1,0:T(8,128)S(1)}, u32[]{:S(2)}, u32[]{:S(2)}) %collective-permute-start.8) | collective-permute-done | bytes 266272 | tf_op jit(solution)/shard_map/ppermute | solution.py:659
  130.0 3.0 %shard_map.144 = (f32[8,64,128]{2,1,0:T(8,128)S(1)}, f32[512,128]{1,0:T(8,128)S(1)}, f32[16,128]{1,0:T(8,128)S(1)}, bf16[512,256]{1,0:T(8,128)(2,1)S(1)}, f32[64...) custom-call(f32[16,528,128]{2,1,0:T(8,128)} %all-to-all-done.received_ref, ...), custom_call_target="tpu_custom_call" | custom-call | flops 1107296256 | bytes 4325376 | tf_op jit(solution)/shard_map/pallas_call | solution.py:618
  133.0 0.0 copy-start.5
  133.0 0.0 copy-start.4
  133.0 1.8 %collective-permute-done.9.rest_1_ = f32[512,128]{1,0:T(8,128)S(1)} collective-permute-done((f32[512,128]{1,0:T(8,128)S(1)}, f32[512,128]{1,0:T(8,128)S(1)}, u32[]{:S(2)}, u32[]{:S(2)}) %collective-permute-start.9) | collective-permute-done | bytes 262176 | tf_op jit(solution)/shard_map/ppermute | solution.py:659
  134.8 2.0 %shard_map.146 = (f32[8,64,128]{2,1,0:T(8,128)S(1)}, f32[4,4,2,16,128]{4,3,2,1,0:T(8,128)}) custom-call(f32[16,512,128]{2,1,0:T(8,128)S(1)} %get-tuple-element.46.spectrum_ref, f32[16,64,128]{2,1,0:T(8,128)S(1)} %constant_dynamic-update-slice_fusion.basis_ref, bf16[512,256]{1,0:T(8,128)(2,1)S(1)} %get-tuple-element.47.lanes_ref, ...), custom_call_target="tpu_custom_call" | custom-call | flops 1073741824 | bytes 4194304 | tf_op jit(solution)/shard_map/pallas_call | solution.py:618
  136.8 3.5 %all-to-all-start.1 = ((f32[16,2,16,128]{3,2,1,0:T(8,128)}), f32[16,2,16,128]{3,2,1,0:T(8,128)S(1)}, u32[]{:S(2)}, u32[]{:S(2)}) async-start(f32[16,2,16,128]{3,2,1,0:T(8,128)} %bitcast.32), calls=%async_computation.1 | async-start | bytes 524288 | tf_op jit(solution)/shard_map/all_to_all | solution.py:805
  140.4 0.0 copy-done.5
  140.4 0.4 fusion.7
  140.8 0.0 copy-done.4
  140.8 0.4 fusion
  141.1 0.7 copy.32
  141.9 5.5 %all-to-all-done.1 = f32[16,2,16,128]{3,2,1,0:T(8,128)S(1)} async-done(((f32[16,2,16,128]{3,2,1,0:T(8,128)}), f32[16,2,16,128]{3,2,1,0:T(8,128)S(1)}, u32[]{:S(2)}, u32[]{:S(2)}) %all-to-all-start.1) | async-done | bytes 262176 | tf_op jit(solution)/shard_map/all_to_all | solution.py:805
  147.4 0.6 fusion.10
  (29 shorter events, 0.3 us)
Async XLA Ops:
  1.5 17.2 %collective-permute-start = (f32[256,128]{1,0:T(8,128)S(1)}, f32[256,128]{1,0:T(8,128)S(1)}, u32[]{:S(2)}, u32[]{:S(2)}) collective-permute-start(f32[256,128]{1,0:T(8,128)S(1)} %bitcast.127), channel_id=1, source_target_pairs={{8,0},{9,1},{10,2},{11,3},{12,4},{13,5},{14,6},{15,7},{16,8},{17,9... | collective-permute-start | bytes 393224 | tf_op jit(solution)/shard_map/ppermute | solution.py:697
  2.8 19.3 %collective-permute-start.1 = (f32[64,1024]{1,0:T(8,128)}, f32[64,1024]{1,0:T(8,128)S(1)}, u32[]{:S(2)}, u32[]{:S(2)}) collective-permute-start(f32[64,1024]{1,0:T(8,128)} %param.14), channel_id=1, source_target_pairs={{0,4},{4,0},{1,5},{5,1},{2,6},{6,2},{3,7},{7,3},{8,12},{12,8},{9,1... | collective-permute-start | bytes 786440 | tf_op jit(solution)/shard_map/ppermute | solution.py:659
  9.3 9.4 %copy-start.2 = (f32[16,128]{1,0:T(8,128)S(1)}, f32[16,128]{1,0:T(8,128)}, u32[]{:S(2)}) copy-start(f32[16,128]{1,0:T(8,128)} %activity_ref.1) | copy-start | bytes 24580
  22.1 5.0 %copy-start.3 = (f32[64,1024]{1,0:T(8,128)S(1)}, f32[64,1024]{1,0:T(8,128)}, u32[]{:S(2)}) copy-start(f32[64,1024]{1,0:T(8,128)} %param.14) | copy-start | bytes 786436
  22.2 5.1 %copy-start.7 = (f32[128,128,1,1]{1,0,3,2:T(8,128)S(1)}, f32[128,128,1,1]{1,0,3,2:T(8,128)}, u32[]{:S(2)}) copy-start(f32[128,128,1,1]{1,0,3,2:T(8,128)} %constant.89) | copy-start | bytes 196612
  22.2 5.6 %copy-start.6 = (f32[128,128,1,1]{1,0,3,2:T(8,128)S(1)}, f32[128,128,1,1]{1,0,3,2:T(8,128)}, u32[]{:S(2)}) copy-start(f32[128,128,1,1]{1,0,3,2:T(8,128)} %constant.90) | copy-start | bytes 196612
  22.2 60.6 %all-to-all-start = ((f32[16,528,128]{2,1,0:T(8,128)}), f32[16,528,128]{2,1,0:T(8,128)}, u32[]{:S(2)}, u32[]{:S(2)}) async-start(f32[16,528,128]{2,1,0:T(8,128)} %shard_map.141), calls=%async_computation | async-start | bytes 8650752 | tf_op jit(solution)/shard_map/all_to_all | solution.py:703
  87.7 2.0 %copy-start = (f32[16,512,128]{2,1,0:T(8,128)}, f32[16,512,128]{2,1,0:T(8,128)S(1)}, u32[]{:S(2)}) copy-start(f32[16,512,128]{2,1,0:T(8,128)S(1)} %get-tuple-element.40.spectrum_ref) | copy-start | bytes 12582916
  89.7 3.1 %collective-permute-start.2 = (f32[136,128]{1,0:T(8,128)S(1)}, f32[136,128]{1,0:T(8,128)S(1)}, u32[]{:S(2)}, u32[]{:S(2)}) collective-permute-start(f32[136,128]{1,0:T(8,128)S(1)} %get-tuple-element.43), channel_id=1, source_target_pairs={{0,8},{8,0},{16,24},{24,16},{1,9},{9,1},{17,25},{25,17},{2,10},{10... | collective-permute-start | bytes 208904 | tf_op jit(solution)/shard_map/ppermute | solution.py:659
  92.8 4.5 %collective-permute-start.3 = (f32[136,128]{1,0:T(8,128)S(1)}, f32[136,128]{1,0:T(8,128)S(1)}, u32[]{:S(2)}, u32[]{:S(2)}) collective-permute-start(f32[136,128]{1,0:T(8,128)S(1)} %add.89), channel_id=1, source_target_pairs={{0,16},{8,24},{16,0},{24,8},{1,17},{9,25},{17,1},{25,9},{2,18},{10... | collective-permute-start | bytes 208904 | tf_op jit(solution)/shard_map/ppermute | solution.py:659
  97.3 5.1 %collective-permute-start.4 = (f32[136,128]{1,0:T(8,128)S(1)}, f32[136,128]{1,0:T(8,128)S(1)}, u32[]{:S(2)}, u32[]{:S(2)}) collective-permute-start(f32[136,128]{1,0:T(8,128)S(1)} %add.90), channel_id=1, source_target_pairs={{0,1},{1,0},{2,3},{3,2},{4,5},{5,4},{6,7},{7,6},{8,9},{9,8},{10,11... | collective-permute-start | bytes 208904 | tf_op jit(solution)/shard_map/ppermute | solution.py:659
  97.9 4.5 %collective-permute-start.5 = (f32[136,128]{1,0:T(8,128)S(1)}, f32[136,128]{1,0:T(8,128)S(1)}, u32[]{:S(2)}, u32[]{:S(2)}) collective-permute-start(f32[136,128]{1,0:T(8,128)S(1)} %add.90), channel_id=1, source_target_pairs={{0,2},{1,3},{2,0},{3,1},{4,6},{5,7},{6,4},{7,5},{8,10},{9,11},{10,... | collective-permute-start | bytes 208904 | tf_op jit(solution)/shard_map/ppermute | solution.py:659
  97.9 6.0 %collective-permute-start.6 = (f32[136,128]{1,0:T(8,128)S(1)}, f32[136,128]{1,0:T(8,128)S(1)}, u32[]{:S(2)}, u32[]{:S(2)}) collective-permute-start(f32[136,128]{1,0:T(8,128)S(1)} %add.90), channel_id=1, source_target_pairs={{0,3},{1,2},{2,1},{3,0},{4,7},{5,6},{6,5},{7,4},{8,11},{9,10},{10,... | collective-permute-start | bytes 208904 | tf_op jit(solution)/shard_map/ppermute | solution.py:659
  103.9 1.3 collective-permute-start.7
  105.3 2.2 %copy-start.1 = (f32[16,512,128]{2,1,0:T(8,128)S(1)}, f32[16,512,128]{2,1,0:T(8,128)}, u32[]{:S(2)}) copy-start(f32[16,512,128]{2,1,0:T(8,128)} %copy-done) | copy-start | bytes 12582916
  108.5 21.5 %collective-permute-start.8 = (f32[520,128]{1,0:T(8,128)S(1)}, f32[520,128]{1,0:T(8,128)S(1)}, u32[]{:S(2)}, u32[]{:S(2)}) collective-permute-start(f32[520,128]{1,0:T(8,128)S(1)} %get-tuple-element.45.rest_0_), channel_id=1, source_target_pairs={{0,4},{4,0},{1,5},{5,1},{2,6},{6,2},{3,7},{7,3},{8,12},{12,8},{9,1... | collective-permute-start | bytes 798728 | tf_op jit(solution)/shard_map/ppermute | solution.py:659
  112.0 22.8 %collective-permute-start.9 = (f32[512,128]{1,0:T(8,128)S(1)}, f32[512,128]{1,0:T(8,128)S(1)}, u32[]{:S(2)}, u32[]{:S(2)}) collective-permute-start(f32[512,128]{1,0:T(8,128)S(1)} %shard_map.145.rest_0_), channel_id=1, source_target_pairs={{0,4},{4,0},{1,5},{5,1},{2,6},{6,2},{3,7},{7,3},{8,12},{12,8},{9,1... | collective-permute-start | bytes 786440 | tf_op jit(solution)/shard_map/ppermute | solution.py:659
  133.0 7.4 %copy-start.5 = (f32[128,128,1]{1,0,2:T(8,128)S(1)}, f32[128,128,1]{1,0,2:T(8,128)}, u32[]{:S(2)}) copy-start(f32[128,128,1]{1,0,2:T(8,128)} %constant.91) | copy-start | bytes 196612
  133.0 7.8 %copy-start.4 = (f32[128,128,1]{1,0,2:T(8,128)S(1)}, f32[128,128,1]{1,0,2:T(8,128)}, u32[]{:S(2)}) copy-start(f32[128,128,1]{1,0,2:T(8,128)} %constant.92) | copy-start | bytes 196612
  136.8 10.6 %all-to-all-start.1 = ((f32[16,2,16,128]{3,2,1,0:T(8,128)}), f32[16,2,16,128]{3,2,1,0:T(8,128)S(1)}, u32[]{:S(2)}, u32[]{:S(2)}) async-start(f32[16,2,16,128]{3,2,1,0:T(8,128)} %bitcast.32), calls=%async_computation.1 | async-start | bytes 524288 | tf_op jit(solution)/shard_map/all_to_all | solution.py:805

commit v14 on v13

--- a/solution.py
+++ b/solution.py
@@ -18,7 +18,7 @@
 SPARE = 8
 HOP_ROWS = FRAME_LEN // 2 // LANES
 SPECTRUM_VMEM = 24 * 1024 * 1024
-UPDATE_VMEM = 24 * 1024 * 1024
+UPDATE_VMEM = 16 * 1024 * 1024
 NT = (((1,), (1,)), ((), ()))
 
 

time: 148 us -> 148 us (level)
  no operation moved by 1% of the time
where the time goes in v14:
time: 148 us
  waiting for transfers between devices  86 us (58%)
  starting transfers between devices  26.1 us (18%)
  Pallas kernels  26 us (18%)
  local copies, waits for them, and re-layouts  6.19 us (4%)
  matrix products  1.85 us (1%)
    all_to_all x1, waiting for transfers between devices, on_device(): spectrum = lax.all_to_all(spectrum, exchange, 0, 0, tiled=True)  54.2 us
    ppermute x9, waiting for transfers between devices, swap_by(): return lax.ppermute(value, axis, [(i, i ^ mask) for i in range(count)])  26.3 us
    ppermute x9, starting transfers between devices, swap_by(): return lax.ppermute(value, axis, [(i, i ^ mask) for i in range(count)])  16.4 us
    pallas_call x5, Pallas kernels, update_call(): pl.pallas_call(kernel, in_specs=[pl.BlockSpec(memory_space=pltpu.SMEM) fo...  13.3 us
    pallas_call x1, Pallas kernels, spectrum_blocks(): pl.pallas_call(functools.partial(early_kernel, places, per_member, frames...  9.39 us
    all_to_all x1, waiting for transfers between devices, on_device(): lax.all_to_all(payload.reshape(partners, 2, ranks_here, width), exchange,...  5.55 us
    all_to_all x1, starting transfers between devices, on_device(): spectrum = lax.all_to_all(spectrum, exchange, 0, 0, tiled=True)  4.86 us
    unnamed x35, local copies, waits for them, and re-layouts  4.36 us
  transfers between devices with their start and end apart: 12, of which 9 were waited for; matrix products, arithmetic and copies ran while one was open for 2% of the time, Pallas kernels for 12%

profile of v14, /device:TPU:0, one launch (start us, length us, event | category | flops | bytes accessed | tf_op | source)
XLA Modules:
  0.0 148.0 jit_solution(15596265475563381769)
XLA Ops:
  0.6 0.9 slice.66
  1.5 1.3 collective-permute-start
  2.8 6.5 %collective-permute-start.1 = (f32[64,1024]{1,0:T(8,128)}, f32[64,1024]{1,0:T(8,128)S(1)}, u32[]{:S(2)}, u32[]{:S(2)}) collective-permute-start(f32[64,1024]{1,0:T(8,128)} %param.14), channel_id=1, source_target_pairs={{0,4},{4,0},{1,5},{5,1},{2,6},{6,2},{3,7},{7,3},{8,12},{12,8},{9,1... | collective-permute-start | bytes 786440 | tf_op jit(solution)/shard_map/ppermute | solution.py:659
  9.3 0.0 copy-start.2
  9.3 9.4 %shard_map.140 = (f32[16,528,128]{2,1,0:T(8,128)}, f32[2048,128]{1,0:T(8,128)S(1)}, f32[3,16,136,128]{3,2,1,0:T(8,128)S(1)}, f32[2,256,128]{2,1,0:T(8,128)S(1)},...) custom-call(f32[8192,128]{1,0:T(8,128)} %bitcast.128, ...), custom_call_target="tpu_custom_call" | custom-call | flops 4831838208 | bytes 6291456 | tf_op jit(solution)/shard_map/pallas_call | solution.py:340
  18.7 0.0 collective-permute-done.trailing_ref
  18.7 0.0 copy-done.2
  18.8 3.4 %shard_map.141 = f32[16,528,128]{2,1,0:T(8,128)} custom-call(f32[3,16,136,128]{3,2,1,0:T(8,128)S(1)} %get-tuple-element.29.done_ref, f32[2048,128]{1,0:T(8,128)S(1)} %get-tuple-element.30.tail_ref, f32[256,128]{1,0:T(8,128)S(1)} %collective-permute-done.trailing_ref, f32[16,128]{1,0:T(8,128)S(1)} %copy-done.2, ...), custom_call_target="tpu_custom_call", output_to_operand_aliasing={{}: (10, {})} | custom-call | flops 1610612736 | bytes 2097152 | tf_op jit(solution)/shard_map/pallas_call | solution.py:354
  22.1 0.0 copy-start.3
  22.2 0.0 copy-start.7
  22.2 0.0 copy-start.6
  22.2 0.0 collective-permute-done.1
  22.2 4.9 %all-to-all-start = ((f32[16,528,128]{2,1,0:T(8,128)}), f32[16,528,128]{2,1,0:T(8,128)}, u32[]{:S(2)}, u32[]{:S(2)}) async-start(f32[16,528,128]{2,1,0:T(8,128)} %shard_map.141), calls=%async_computation | async-start | bytes 8650752 | tf_op jit(solution)/shard_map/all_to_all | solution.py:703
  27.1 0.1 fusion.12
  27.2 0.0 copy-done.3
  27.2 0.0 copy-done.7
  27.2 0.6 fusion.1
  27.8 0.0 copy-done.6
  27.8 0.6 convolution_select_fusion
  28.6 54.2 %all-to-all-done.received_ref = f32[16,528,128]{2,1,0:T(8,128)} async-done(((f32[16,528,128]{2,1,0:T(8,128)}), f32[16,528,128]{2,1,0:T(8,128)}, u32[]{:S(2)}, u32[]{:S(2)}) %all-to-all-start) | async-done | bytes 4325408 | tf_op jit(solution)/shard_map/all_to_all | solution.py:703
  82.8 4.8 %shard_map.142 = (f32[136,128]{1,0:T(8,128)S(1)}, f32[136,128]{1,0:T(8,128)S(1)}, f32[512,64]{1,0:T(8,128)S(1)}, f32[16,512,128]{2,1,0:T(8,128)S(1)}) custom-call(s32[1]{0:T(128)} %bitcast.side_ref, f32[16,528,128]{2,1,0:T(8,128)} %all-to-all-done.received_ref, f32[16,64,128]{2,1,0:T(8,128)S(1)} %constant_dynamic-update-slice_fusion.basis_ref), custom_call_target="tpu_custom_call" | custom-call | flops 1107296256 | bytes 4325376 | tf_op jit(solution)/shard_map/pallas_call | solution.py:618
  87.7 0.0 copy-start
  87.7 2.0 %copy-done = f32[16,512,128]{2,1,0:T(8,128)} copy-done((f32[16,512,128]{2,1,0:T(8,128)}, f32[16,512,128]{2,1,0:T(8,128)S(1)}, u32[]{:S(2)}) %copy-start) | copy-done | bytes 4194328
  89.7 2.2 %collective-permute-start.2 = (f32[136,128]{1,0:T(8,128)S(1)}, f32[136,128]{1,0:T(8,128)S(1)}, u32[]{:S(2)}, u32[]{:S(2)}) collective-permute-start(f32[136,128]{1,0:T(8,128)S(1)} %get-tuple-element.43), channel_id=1, source_target_pairs={{0,8},{8,0},{16,24},{24,16},{1,9},{9,1},{17,25},{25,17},{2,10},{10... | collective-permute-start | bytes 208904 | tf_op jit(solution)/shard_map/ppermute | solution.py:659
  91.9 0.9 collective-permute-done.2
  92.8 1.1 collective-permute-start.3
  93.9 3.4 %collective-permute-done.3 = f32[136,128]{1,0:T(8,128)S(1)} collective-permute-done((f32[136,128]{1,0:T(8,128)S(1)}, f32[136,128]{1,0:T(8,128)S(1)}, u32[]{:S(2)}, u32[]{:S(2)}) %collective-permute-start.3) | collective-permute-done | bytes 69664 | tf_op jit(solution)/shard_map/ppermute | solution.py:659
  97.3 0.6 collective-permute-start.4
  97.9 0.0 collective-permute-start.5
  97.9 2.9 %collective-permute-start.6 = (f32[136,128]{1,0:T(8,128)S(1)}, f32[136,128]{1,0:T(8,128)S(1)}, u32[]{:S(2)}, u32[]{:S(2)}) collective-permute-start(f32[136,128]{1,0:T(8,128)S(1)} %add.90), channel_id=1, source_target_pairs={{0,3},{1,2},{2,1},{3,0},{4,7},{5,6},{6,5},{7,4},{8,11},{9,10},{10,... | collective-permute-start | bytes 208904 | tf_op jit(solution)/shard_map/ppermute | solution.py:659
  100.9 1.6 %collective-permute-done.4 = f32[136,128]{1,0:T(8,128)S(1)} collective-permute-done((f32[136,128]{1,0:T(8,128)S(1)}, f32[136,128]{1,0:T(8,128)S(1)}, u32[]{:S(2)}, u32[]{:S(2)}) %collective-permute-start.4) | collective-permute-done | bytes 69664 | tf_op jit(solution)/shard_map/ppermute | solution.py:659
  102.4 0.0 collective-permute-done.5
  102.4 1.5 collective-permute-done.6
  103.9 0.1 collective-permute-start.7
  104.0 1.2 collective-permute-done.7.other_ref
  105.3 0.0 copy-start.1
  105.3 2.2 %copy-done.1 = f32[16,512,128]{2,1,0:T(8,128)S(1)} copy-done((f32[16,512,128]{2,1,0:T(8,128)S(1)}, f32[16,512,128]{2,1,0:T(8,128)}, u32[]{:S(2)}) %copy-start.1) | copy-done | bytes 4194328
  107.4 1.0 shard_map.143
  108.5 1.1 collective-permute-start.8
  109.5 2.4 %shard_map.145.rest_0_ = f32[512,128]{1,0:T(8,128)S(1)} custom-call(f32[16,528,128]{2,1,0:T(8,128)} %all-to-all-done.received_ref, f32[16,64,128]{2,1,0:T(8,128)S(1)} %constant_dynamic-update-slice_fusion.basis_ref, bf16[512,256]{1,0:T(8,128)(2,1)S(1)} %get-tuple-element.51.lanes_ref, bf16[128,512]{1,0:T(8,128)(2,1)S(1)} %get-tuple-element.52.turned_ref), custom_call_target="tpu_custom_call" | custom-call | flops 1107296256 | bytes 4325376 | tf_op jit(solution)/shard_map/pallas_call | solution.py:618
  112.0 2.0 %collective-permute-start.9 = (f32[512,128]{1,0:T(8,128)S(1)}, f32[512,128]{1,0:T(8,128)S(1)}, u32[]{:S(2)}, u32[]{:S(2)}) collective-permute-start(f32[512,128]{1,0:T(8,128)S(1)} %shard_map.145.rest_0_), channel_id=1, source_target_pairs={{0,4},{4,0},{1,5},{5,1},{2,6},{6,2},{3,7},{7,3},{8,12},{12,8},{9,1... | collective-permute-start | bytes 786440 | tf_op jit(solution)/shard_map/ppermute | solution.py:659
  114.0 0.1 constant_dynamic-slice_fusion
  114.1 0.1 copy.25
  114.1 15.9 %collective-permute-done.8.rest_1_ = f32[520,128]{1,0:T(8,128)S(1)} collective-permute-done((f32[520,128]{1,0:T(8,128)S(1)}, f32[520,128]{1,0:T(8,128)S(1)}, u32[]{:S(2)}, u32[]{:S(2)}) %collective-permute-start.8) | collective-permute-done | bytes 266272 | tf_op jit(solution)/shard_map/ppermute | solution.py:659
  130.0 3.0 %shard_map.144 = (f32[8,64,128]{2,1,0:T(8,128)S(1)}, f32[512,128]{1,0:T(8,128)S(1)}, f32[16,128]{1,0:T(8,128)S(1)}, bf16[512,256]{1,0:T(8,128)(2,1)S(1)}, f32[64...) custom-call(f32[16,528,128]{2,1,0:T(8,128)} %all-to-all-done.received_ref, ...), custom_call_target="tpu_custom_call" | custom-call | flops 1107296256 | bytes 4325376 | tf_op jit(solution)/shard_map/pallas_call | solution.py:618
  133.0 0.0 copy-start.5
  133.0 0.0 copy-start.4
  133.0 1.8 %collective-permute-done.9.rest_1_ = f32[512,128]{1,0:T(8,128)S(1)} collective-permute-done((f32[512,128]{1,0:T(8,128)S(1)}, f32[512,128]{1,0:T(8,128)S(1)}, u32[]{:S(2)}, u32[]{:S(2)}) %collective-permute-start.9) | collective-permute-done | bytes 262176 | tf_op jit(solution)/shard_map/ppermute | solution.py:659
  134.8 2.0 %shard_map.146 = (f32[8,64,128]{2,1,0:T(8,128)S(1)}, f32[4,4,2,16,128]{4,3,2,1,0:T(8,128)}) custom-call(f32[16,512,128]{2,1,0:T(8,128)S(1)} %get-tuple-element.46.spectrum_ref, f32[16,64,128]{2,1,0:T(8,128)S(1)} %constant_dynamic-update-slice_fusion.basis_ref, bf16[512,256]{1,0:T(8,128)(2,1)S(1)} %get-tuple-element.47.lanes_ref, ...), custom_call_target="tpu_custom_call" | custom-call | flops 1073741824 | bytes 4194304 | tf_op jit(solution)/shard_map/pallas_call | solution.py:618
  136.8 3.5 %all-to-all-start.1 = ((f32[16,2,16,128]{3,2,1,0:T(8,128)}), f32[16,2,16,128]{3,2,1,0:T(8,128)S(1)}, u32[]{:S(2)}, u32[]{:S(2)}) async-start(f32[16,2,16,128]{3,2,1,0:T(8,128)} %bitcast.32), calls=%async_computation.1 | async-start | bytes 524288 | tf_op jit(solution)/shard_map/all_to_all | solution.py:805
  140.4 0.0 copy-done.5
  140.4 0.4 fusion.7
  140.8 0.0 copy-done.4
  140.8 0.4 fusion
  141.1 0.7 copy.32
  141.9 5.5 %all-to-all-done.1 = f32[16,2,16,128]{3,2,1,0:T(8,128)S(1)} async-done(((f32[16,2,16,128]{3,2,1,0:T(8,128)}), f32[16,2,16,128]{3,2,1,0:T(8,128)S(1)}, u32[]{:S(2)}, u32[]{:S(2)}) %all-to-all-start.1) | async-done | bytes 262176 | tf_op jit(solution)/shard_map/all_to_all | solution.py:805
  147.4 0.6 fusion.10
  (29 shorter events, 0.3 us)
Async XLA Ops:
  1.5 17.2 %collective-permute-start = (f32[256,128]{1,0:T(8,128)S(1)}, f32[256,128]{1,0:T(8,128)S(1)}, u32[]{:S(2)}, u32[]{:S(2)}) collective-permute-start(f32[256,128]{1,0:T(8,128)S(1)} %bitcast.127), channel_id=1, source_target_pairs={{8,0},{9,1},{10,2},{11,3},{12,4},{13,5},{14,6},{15,7},{16,8},{17,9... | collective-permute-start | bytes 393224 | tf_op jit(solution)/shard_map/ppermute | solution.py:697
  2.8 19.3 %collective-permute-start.1 = (f32[64,1024]{1,0:T(8,128)}, f32[64,1024]{1,0:T(8,128)S(1)}, u32[]{:S(2)}, u32[]{:S(2)}) collective-permute-start(f32[64,1024]{1,0:T(8,128)} %param.14), channel_id=1, source_target_pairs={{0,4},{4,0},{1,5},{5,1},{2,6},{6,2},{3,7},{7,3},{8,12},{12,8},{9,1... | collective-permute-start | bytes 786440 | tf_op jit(solution)/shard_map/ppermute | solution.py:659
  9.3 9.4 %copy-start.2 = (f32[16,128]{1,0:T(8,128)S(1)}, f32[16,128]{1,0:T(8,128)}, u32[]{:S(2)}) copy-start(f32[16,128]{1,0:T(8,128)} %activity_ref.1) | copy-start | bytes 24580
  22.1 5.0 %copy-start.3 = (f32[64,1024]{1,0:T(8,128)S(1)}, f32[64,1024]{1,0:T(8,128)}, u32[]{:S(2)}) copy-start(f32[64,1024]{1,0:T(8,128)} %param.14) | copy-start | bytes 786436
  22.2 5.1 %copy-start.7 = (f32[128,128,1,1]{1,0,3,2:T(8,128)S(1)}, f32[128,128,1,1]{1,0,3,2:T(8,128)}, u32[]{:S(2)}) copy-start(f32[128,128,1,1]{1,0,3,2:T(8,128)} %constant.89) | copy-start | bytes 196612
  22.2 5.6 %copy-start.6 = (f32[128,128,1,1]{1,0,3,2:T(8,128)S(1)}, f32[128,128,1,1]{1,0,3,2:T(8,128)}, u32[]{:S(2)}) copy-start(f32[128,128,1,1]{1,0,3,2:T(8,128)} %constant.90) | copy-start | bytes 196612
  22.2 60.6 %all-to-all-start = ((f32[16,528,128]{2,1,0:T(8,128)}), f32[16,528,128]{2,1,0:T(8,128)}, u32[]{:S(2)}, u32[]{:S(2)}) async-start(f32[16,528,128]{2,1,0:T(8,128)} %shard_map.141), calls=%async_computation | async-start | bytes 8650752 | tf_op jit(solution)/shard_map/all_to_all | solution.py:703
  87.7 2.0 %copy-start = (f32[16,512,128]{2,1,0:T(8,128)}, f32[16,512,128]{2,1,0:T(8,128)S(1)}, u32[]{:S(2)}) copy-start(f32[16,512,128]{2,1,0:T(8,128)S(1)} %get-tuple-element.40.spectrum_ref) | copy-start | bytes 12582916
  89.7 3.1 %collective-permute-start.2 = (f32[136,128]{1,0:T(8,128)S(1)}, f32[136,128]{1,0:T(8,128)S(1)}, u32[]{:S(2)}, u32[]{:S(2)}) collective-permute-start(f32[136,128]{1,0:T(8,128)S(1)} %get-tuple-element.43), channel_id=1, source_target_pairs={{0,8},{8,0},{16,24},{24,16},{1,9},{9,1},{17,25},{25,17},{2,10},{10... | collective-permute-start | bytes 208904 | tf_op jit(solution)/shard_map/ppermute | solution.py:659
  92.8 4.5 %collective-permute-start.3 = (f32[136,128]{1,0:T(8,128)S(1)}, f32[136,128]{1,0:T(8,128)S(1)}, u32[]{:S(2)}, u32[]{:S(2)}) collective-permute-start(f32[136,128]{1,0:T(8,128)S(1)} %add.89), channel_id=1, source_target_pairs={{0,16},{8,24},{16,0},{24,8},{1,17},{9,25},{17,1},{25,9},{2,18},{10... | collective-permute-start | bytes 208904 | tf_op jit(solution)/shard_map/ppermute | solution.py:659
  97.3 5.1 %collective-permute-start.4 = (f32[136,128]{1,0:T(8,128)S(1)}, f32[136,128]{1,0:T(8,128)S(1)}, u32[]{:S(2)}, u32[]{:S(2)}) collective-permute-start(f32[136,128]{1,0:T(8,128)S(1)} %add.90), channel_id=1, source_target_pairs={{0,1},{1,0},{2,3},{3,2},{4,5},{5,4},{6,7},{7,6},{8,9},{9,8},{10,11... | collective-permute-start | bytes 208904 | tf_op jit(solution)/shard_map/ppermute | solution.py:659
  97.9 4.5 %collective-permute-start.5 = (f32[136,128]{1,0:T(8,128)S(1)}, f32[136,128]{1,0:T(8,128)S(1)}, u32[]{:S(2)}, u32[]{:S(2)}) collective-permute-start(f32[136,128]{1,0:T(8,128)S(1)} %add.90), channel_id=1, source_target_pairs={{0,2},{1,3},{2,0},{3,1},{4,6},{5,7},{6,4},{7,5},{8,10},{9,11},{10,... | collective-permute-start | bytes 208904 | tf_op jit(solution)/shard_map/ppermute | solution.py:659
  97.9 6.0 %collective-permute-start.6 = (f32[136,128]{1,0:T(8,128)S(1)}, f32[136,128]{1,0:T(8,128)S(1)}, u32[]{:S(2)}, u32[]{:S(2)}) collective-permute-start(f32[136,128]{1,0:T(8,128)S(1)} %add.90), channel_id=1, source_target_pairs={{0,3},{1,2},{2,1},{3,0},{4,7},{5,6},{6,5},{7,4},{8,11},{9,10},{10,... | collective-permute-start | bytes 208904 | tf_op jit(solution)/shard_map/ppermute | solution.py:659
  103.9 1.3 collective-permute-start.7
  105.3 2.2 %copy-start.1 = (f32[16,512,128]{2,1,0:T(8,128)S(1)}, f32[16,512,128]{2,1,0:T(8,128)}, u32[]{:S(2)}) copy-start(f32[16,512,128]{2,1,0:T(8,128)} %copy-done) | copy-start | bytes 12582916
  108.5 21.5 %collective-permute-start.8 = (f32[520,128]{1,0:T(8,128)S(1)}, f32[520,128]{1,0:T(8,128)S(1)}, u32[]{:S(2)}, u32[]{:S(2)}) collective-permute-start(f32[520,128]{1,0:T(8,128)S(1)} %get-tuple-element.45.rest_0_), channel_id=1, source_target_pairs={{0,4},{4,0},{1,5},{5,1},{2,6},{6,2},{3,7},{7,3},{8,12},{12,8},{9,1... | collective-permute-start | bytes 798728 | tf_op jit(solution)/shard_map/ppermute | solution.py:659
  112.0 22.8 %collective-permute-start.9 = (f32[512,128]{1,0:T(8,128)S(1)}, f32[512,128]{1,0:T(8,128)S(1)}, u32[]{:S(2)}, u32[]{:S(2)}) collective-permute-start(f32[512,128]{1,0:T(8,128)S(1)} %shard_map.145.rest_0_), channel_id=1, source_target_pairs={{0,4},{4,0},{1,5},{5,1},{2,6},{6,2},{3,7},{7,3},{8,12},{12,8},{9,1... | collective-permute-start | bytes 786440 | tf_op jit(solution)/shard_map/ppermute | solution.py:659
  133.0 7.4 %copy-start.5 = (f32[128,128,1]{1,0,2:T(8,128)S(1)}, f32[128,128,1]{1,0,2:T(8,128)}, u32[]{:S(2)}) copy-start(f32[128,128,1]{1,0,2:T(8,128)} %constant.91) | copy-start | bytes 196612
  133.0 7.8 %copy-start.4 = (f32[128,128,1]{1,0,2:T(8,128)S(1)}, f32[128,128,1]{1,0,2:T(8,128)}, u32[]{:S(2)}) copy-start(f32[128,128,1]{1,0,2:T(8,128)} %constant.92) | copy-start | bytes 196612
  136.8 10.6 %all-to-all-start.1 = ((f32[16,2,16,128]{3,2,1,0:T(8,128)}), f32[16,2,16,128]{3,2,1,0:T(8,128)S(1)}, u32[]{:S(2)}, u32[]{:S(2)}) async-start(f32[16,2,16,128]{3,2,1,0:T(8,128)} %bitcast.32), calls=%async_computation.1 | async-start | bytes 524288 | tf_op jit(solution)/shard_map/all_to_all | solution.py:805
